TPU v7x, 32 devices: a whole 2x2x4 slice. The times are simulated.
32 devices in a mesh: seq: 8 (over z, x), tp: 4 (over y, core).
Axes of the slice: x: 2, y: 2, z: 4, core: 2. Of those that a mesh axis runs over, the one named last changes fastest.
Arguments:
- tokens: bfloat16 [4096, 1536], P('seq'), may hold values from -6 to 6
- cotangent: bfloat16 [4096, 1536], P('seq'), may hold values from -6 to 6
- doc_lengths: int32 [4], replicated, may hold values from 1 to 4096, as said below
- norm_gains: float32 [4, 1536], replicated, may hold values from 0.5 to 1.5
- input_branch: bfloat16 [1536, 2048], P('seq', 'tp'), may hold values from -0.15625 to 0.15625
- gate_branch: bfloat16 [1536, 2048], P('seq', 'tp'), may hold values from -0.15625 to 0.15625
- conv_taps: float32 [4, 2048], P(None, 'tp'), may hold values from -3 to 3
- conv_bias: float32 [2048], P('tp'), may hold values from -2 to 2
- recur_gate: bfloat16 [2048, 128], P('tp', 'seq'), may hold values from -0.5 to 0.5
- input_gate: bfloat16 [2048, 128], P('tp', 'seq'), may hold values from -0.5 to 0.5
- gate_biases: float32 [2, 2048], P(None, 'tp'), may hold values from -4 to 4
- decay_param: float32 [2048], P('tp'), may hold values from 2 to 12
- recur_output: bfloat16 [2048, 1536], P('tp', 'seq'), may hold values from -0.125 to 0.125
- dense_gate_one: bfloat16 [1536, 4608], P('seq', 'tp'), may hold values from -0.15625 to 0.15625
- dense_up_one: bfloat16 [1536, 4608], P('seq', 'tp'), may hold values from -0.15625 to 0.15625
- dense_down_one: bfloat16 [4608, 1536], P('tp', 'seq'), may hold values from -0.09375 to 0.09375
- query_weight: bfloat16 [1536, 1536], P('seq', 'tp'), may hold values from -0.15625 to 0.15625
- keyvalue_weight: bfloat16 [1536, 256], P(('seq', 'tp')), may hold values from -0.15625 to 0.15625
- attention_out: bfloat16 [1536, 1536], P('tp', 'seq'), may hold values from -0.875 to 0.875
- dense_gate_two: bfloat16 [1536, 4608], P('seq', 'tp'), may hold values from -0.15625 to 0.15625
- dense_up_two: bfloat16 [1536, 4608], P('seq', 'tp'), may hold values from -0.15625 to 0.15625
- dense_down_two: bfloat16 [4608, 1536], P('tp', 'seq'), may hold values from -0.09375 to 0.09375
Outputs:
- layer_out: bfloat16 [4096, 1536], P('seq')
- input_grad: float32 [4096, 1536], P('seq')
- norm_gains_grad: float32 [4, 1536], replicated
- input_branch_grad: float32 [1536, 2048], P('seq', 'tp')
- gate_branch_grad: float32 [1536, 2048], P('seq', 'tp')
- conv_taps_grad: float32 [4, 2048], P(None, 'tp')
- conv_bias_grad: float32 [2048], P('tp')
- recur_gate_grad: float32 [2048, 128], P('tp', 'seq')
- input_gate_grad: float32 [2048, 128], P('tp', 'seq')
- gate_biases_grad: float32 [2, 2048], P(None, 'tp')
- decay_param_grad: float32 [2048], P('tp')
- recur_output_grad: float32 [2048, 1536], P('tp', 'seq')
- dense_gate_one_grad: float32 [1536, 4608], P('seq', 'tp')
- dense_up_one_grad: float32 [1536, 4608], P('seq', 'tp')
- dense_down_one_grad: float32 [4608, 1536], P('tp', 'seq')
- query_weight_grad: float32 [1536, 1536], P('seq', 'tp')
- keyvalue_weight_grad: float32 [1536, 256], P(('seq', 'tp'))
- attention_out_grad: float32 [1536, 1536], P('tp', 'seq')
- dense_gate_two_grad: float32 [1536, 4608], P('seq', 'tp')
- dense_up_two_grad: float32 [1536, 4608], P('seq', 'tp')
- dense_down_two_grad: float32 [4608, 1536], P('tp', 'seq')
Inputs may be any that keep to these rules, and one draw needn't show every extreme that they name: `doc_lengths`: lengths of 4 documents packed in order from slot 0; they sum to less than 4096, and the slots after them are padding.
All inputs are finite; a program needn't handle non-finite values.
Results may differ from a plain program's by a relative error of at most 0.02.
Values may be sent and summed in bfloat16 or wider, within the bound.
A program may use at most 192 MiB of HBM per device.

v0:
```python
import functools

import jax
import jax.numpy as jnp
from jax import lax
from jax.sharding import PartitionSpec as P

HD = 128
CONV = 4
WINDOW = 1024


def passed_along(block, axis, distance):
    devices = range(lax.axis_size(axis))
    route = [(i - distance, i) for i in devices if i - distance in devices]
    return lax.ppermute(block, axis, route)


def prefix(x, axis, combine, identity, reverse):
    length, mine = (lax.axis_size(axis), lax.axis_index(axis))
    everything = jax.tree.map(lambda part: lax.all_gather(part, axis), x)
    start = jax.tree.map(
        lambda part, zero: jnp.broadcast_to(jnp.asarray(zero, part.dtype), part.shape), x, identity
    )

    def turn(k, before):
        at = length - 1 - k if reverse else k
        reached = at > mine if reverse else at < mine
        new = combine(before, jax.tree.map(lambda part: part[at], everything))
        return jax.tree.map(lambda a, b: jnp.where(reached, a, b), new, before)

    return lax.fori_loop(0, length, turn, start)


def product(left, right):
    return jnp.dot(left, right, preferred_element_type=jnp.float32)


def product_left(left, right):
    return lax.dot_general(
        left, right, (((0,), (0,)), ((), ())), preferred_element_type=jnp.float32
    )


def product_right(left, right):
    return lax.dot_general(
        left, right, (((1,), (1,)), ((), ())), preferred_element_type=jnp.float32
    )


def lowered(values):
    return values.astype(jnp.bfloat16)


def rms_norm(values, gain):
    return values * lax.rsqrt(jnp.mean(values * values, axis=-1, keepdims=True) + 1e-06) * gain


def gated(gate_values, up_values):
    return jax.nn.gelu(gate_values) * up_values


def layout(doc_lengths, first_slot, count):
    ends = jnp.cumsum(doc_lengths, dtype=jnp.int32)
    slots = first_slot + jnp.arange(count, dtype=jnp.int32)
    passed = slots[:, None] >= ends[None, :]
    segment = jnp.sum(passed.astype(jnp.int32), axis=1)
    begin = jnp.max(jnp.where(passed, ends[None, :], 0), axis=1)
    segment = jnp.where(slots < 0, -1, segment)
    position = slots - begin
    reset = (slots != begin).astype(jnp.float32)
    valid = (segment < doc_lengths.shape[0]).astype(jnp.float32)
    return (segment, position, reset, valid)


def rotate(values, position):
    half_width = values.shape[-1] // 2
    frequency = 10000.0 ** (-jnp.arange(half_width, dtype=jnp.float32) / half_width)
    angle = position.astype(jnp.float32)[:, None] * frequency[None, :]
    if values.ndim == 3:
        angle = angle[:, None, :]
    cosine = jnp.cos(angle)
    sine = jnp.sin(angle)
    first_half = values[..., :half_width]
    second_half = values[..., half_width:]
    return jnp.concatenate(
        [first_half * cosine - second_half * sine, second_half * cosine + first_half * sine],
        axis=-1,
    )


def convolve(extended, taps, bias, segment):
    leading = CONV - 1
    total_rows = extended.shape[0] - leading
    result = bias[None, :] + taps[0][None, :] * extended[leading:]
    for lag_index in range(1, CONV):
        same = (
            segment[leading:] == segment[leading - lag_index : leading - lag_index + total_rows]
        ).astype(jnp.float32)
        result = (
            result
            + same[:, None]
            * taps[lag_index][None, :]
            * extended[leading - lag_index : leading - lag_index + total_rows]
        )
    return result


def coefficients(recur_raw, input_raw, conv_values, bias_pair, decay_values, reset):
    recur_rate = jax.nn.sigmoid(recur_raw + bias_pair[0][None, :])
    input_rate = jax.nn.sigmoid(input_raw + bias_pair[1][None, :])
    log_decay = -8.0 * recur_rate * jax.nn.softplus(-decay_values)[None, :]
    multiplier = jnp.sqrt(jnp.maximum(-jnp.expm1(2.0 * log_decay), 0.01))
    return (jnp.exp(log_decay) * reset[:, None], multiplier * input_rate * conv_values)


def combine_state(earlier, later):
    return (earlier[0] * later[0], later[0] * earlier[1] + later[1])


def block_product(values, weight):
    total_rows = values.shape[0]
    block_width = weight.shape[1]
    block_count = weight.shape[0] // block_width
    left = values.reshape(total_rows, block_count, block_width)
    right = weight.reshape(block_count, block_width, block_width)
    result = jnp.einsum("tni,nic->tnc", left, right, preferred_element_type=jnp.float32)
    return result.reshape(total_rows, block_count * block_width)


def block_grads(values, weight, upstream_low):
    total_rows = values.shape[0]
    block_width = weight.shape[1]
    block_count = weight.shape[0] // block_width
    left = values.reshape(total_rows, block_count, block_width)
    right = weight.reshape(block_count, block_width, block_width)
    upstream = upstream_low.reshape(total_rows, block_count, block_width)
    weight_grad = jnp.einsum("tni,tnc->nic", left, upstream, preferred_element_type=jnp.float32)
    values_grad = jnp.einsum("tnc,nic->tni", upstream, right, preferred_element_type=jnp.float32)
    return (
        weight_grad.reshape(block_count * block_width, block_width),
        values_grad.reshape(total_rows, block_count * block_width),
    )


def head_sum(values):
    return lax.psum(values, "tp")


def gather_first(
    branch_weight,
    gating_weight,
    recur_weight,
    input_weight,
    output_weight,
    gate_one,
    up_one,
    down_one,
):
    return (
        lax.all_gather(branch_weight, "seq", axis=0, tiled=True),
        lax.all_gather(gating_weight, "seq", axis=0, tiled=True),
        lax.all_gather(recur_weight, "seq", axis=1, tiled=True),
        lax.all_gather(input_weight, "seq", axis=1, tiled=True),
        lax.all_gather(output_weight, "seq", axis=1, tiled=True),
        lax.all_gather(gate_one, "seq", axis=0, tiled=True),
        lax.all_gather(up_one, "seq", axis=0, tiled=True),
        lax.all_gather(down_one, "seq", axis=1, tiled=True),
    )


def gather_second(query_part, attn_part, gate_two, up_two, down_two):
    return (
        lax.all_gather(query_part, "seq", axis=0, tiled=True),
        lax.all_gather(attn_part, "seq", axis=1, tiled=True),
        lax.all_gather(gate_two, "seq", axis=0, tiled=True),
        lax.all_gather(up_two, "seq", axis=0, tiled=True),
        lax.all_gather(down_two, "seq", axis=1, tiled=True),
    )


def gather_keyvalue(keyvalue_part):
    return lax.all_gather(keyvalue_part, ("seq", "tp"), axis=0, tiled=True)


def dense_forward(stream, gain, gate_full, up_full, down_full):
    normed = lowered(rms_norm(stream, gain))
    gate_values = product(normed, gate_full)
    up_values = product(normed, up_full)
    hidden = lowered(gated(gate_values, up_values))
    return (head_sum(product(hidden, down_full)), (normed, gate_values, up_values, hidden))


def dense_backward(stream, gain, grad_out, kept, gate_full, up_full, down_full):
    normed, gate_values, up_values, hidden = kept
    grad_low = lowered(grad_out)
    grad_down = product_left(hidden, grad_low)
    grad_hidden = product_right(grad_low, down_full)
    gate_grad, up_grad = jax.vjp(gated, gate_values, up_values)[1](grad_hidden)
    gate_low = lowered(gate_grad)
    up_low = lowered(up_grad)
    grad_gate = product_left(normed, gate_low)
    grad_up = product_left(normed, up_low)
    grad_normed = head_sum(product_right(gate_low, gate_full) + product_right(up_low, up_full))
    stream_grad, gain_grad = jax.vjp(rms_norm, stream, gain)[1](grad_normed)
    return (grad_out + stream_grad, gain_grad, grad_gate, grad_up, grad_down)


def score_block(query_rot, keys_ext, allowed, score_scale):
    raw = jnp.einsum("qhd,kd->hqk", query_rot, keys_ext, preferred_element_type=jnp.float32)
    return jnp.where(allowed[None], raw * score_scale, -1e30)


def local(
    tokens,
    cotangent,
    doc_lengths,
    norm_gains,
    input_branch,
    gate_branch,
    conv_taps,
    conv_bias,
    recur_gate,
    input_gate,
    gate_biases,
    decay_param,
    recur_output,
    dense_gate_one,
    dense_up_one,
    dense_down_one,
    query_weight,
    keyvalue_weight,
    attention_out,
    dense_gate_two,
    dense_up_two,
    dense_down_two,
):
    shard_rows = tokens.shape[0]
    channels = conv_bias.shape[0]
    leading = CONV - 1
    halo_shards = WINDOW // shard_rows
    first_slot = lax.axis_index("seq") * shard_rows
    segment, position, reset, valid = layout(doc_lengths, first_slot, shard_rows)
    conv_segment = layout(doc_lengths, first_slot - leading, shard_rows + leading)[0]
    key_segment = layout(
        doc_lengths, first_slot - halo_shards * shard_rows, (halo_shards + 1) * shard_rows
    )[0]
    ones_state = jnp.ones((channels,), jnp.float32)
    zeros_state = jnp.zeros((channels,), jnp.float32)
    (
        branch_full,
        gating_full,
        recur_full,
        input_gate_full,
        output_full,
        gate_one,
        up_one,
        down_one,
    ) = gather_first(
        input_branch,
        gate_branch,
        recur_gate,
        input_gate,
        recur_output,
        dense_gate_one,
        dense_up_one,
        dense_down_one,
    )
    query_full, attn_full, gate_two, up_two, down_two = gather_second(
        query_weight, attention_out, dense_gate_two, dense_up_two, dense_down_two
    )
    keyvalue_full = gather_keyvalue(keyvalue_weight)
    stream_in = tokens.astype(jnp.float32)
    normed_one = lowered(rms_norm(stream_in, norm_gains[0]))
    branch = product(normed_one, branch_full)
    gating = product(normed_one, gating_full)
    rim = passed_along(branch[shard_rows - leading :], "seq", 1)
    branch_ext = jnp.concatenate([rim, branch], axis=0)
    conv_local = functools.partial(convolve, segment=conv_segment)
    conv_out, conv_pull = jax.vjp(conv_local, branch_ext, conv_taps, conv_bias)
    conv_low = lowered(conv_out)
    recur_raw = block_product(conv_low, recur_full)
    input_raw = block_product(conv_low, input_gate_full)
    rate_local = functools.partial(coefficients, reset=reset)
    (decay, drive), rate_pull = jax.vjp(
        rate_local, recur_raw, input_raw, conv_out, gate_biases, decay_param
    )
    cumulative, local_state = lax.associative_scan(combine_state, (decay, drive), axis=0)
    carried = prefix(
        (cumulative[-1], local_state[-1]), "seq", combine_state, (ones_state, zeros_state), False
    )
    state_in = carried[1]
    state = local_state + cumulative * state_in[None, :]
    gate_act, gate_pull = jax.vjp(jax.nn.gelu, gating)
    mixed = lowered(state * gate_act)
    stream_one = stream_in + head_sum(product(mixed, output_full))
    dense_out, kept_one = dense_forward(stream_one, norm_gains[1], gate_one, up_one, down_one)
    stream_two = stream_one + dense_out
    normed_three = lowered(rms_norm(stream_two, norm_gains[2]))
    query = product(normed_three, query_full)
    keyval = product(normed_three, keyvalue_full)
    local_heads = query.shape[1] // HD
    query_heads = query.reshape(shard_rows, local_heads, HD)
    rotate_here = functools.partial(rotate, position=position)
    query_rot = lowered(rotate_here(query_heads))
    key_rot = lowered(rotate_here(keyval[:, :HD]))
    packed = jnp.concatenate([key_rot, lowered(keyval[:, HD:])], axis=1)
    earlier = [passed_along(packed, "seq", offset) for offset in range(halo_shards, 0, -1)]
    extended = jnp.concatenate(earlier + [packed], axis=0)
    keys_ext = extended[:, :HD]
    values_ext = extended[:, HD:]
    query_slots = first_slot + jnp.arange(shard_rows, dtype=jnp.int32)
    key_slots = (
        first_slot
        - halo_shards * shard_rows
        + jnp.arange((halo_shards + 1) * shard_rows, dtype=jnp.int32)
    )
    distance = query_slots[:, None] - key_slots[None, :]
    allowed = (segment[:, None] == key_segment[None, :]) & (distance >= 0) & (distance < WINDOW)
    score_scale = HD ** (-0.5)
    scores = score_block(query_rot, keys_ext, allowed, score_scale)
    row_top = jnp.max(scores, axis=-1, keepdims=True)
    row_total = jnp.sum(jnp.exp(scores - row_top), axis=-1, keepdims=True)
    log_total = row_top + jnp.log(row_total)
    probs_low = lowered(jnp.exp(scores - row_top) / row_total)
    attended = lowered(
        jnp.einsum("hqk,kd->qhd", probs_low, values_ext, preferred_element_type=jnp.float32)
    ).reshape(shard_rows, local_heads * HD)
    stream_three = stream_two + head_sum(product(attended, attn_full))
    dense_out, kept_two = dense_forward(stream_three, norm_gains[3], gate_two, up_two, down_two)
    stream_four = stream_three + dense_out
    layer_out = lowered(stream_four * valid[:, None])
    grad_stream = cotangent.astype(jnp.float32) * valid[:, None]
    grad_stream, gain_four, grad_gate_two, grad_up_two, grad_down_two = dense_backward(
        stream_three, norm_gains[3], grad_stream, kept_two, gate_two, up_two, down_two
    )
    grad_attn_low = lowered(grad_stream)
    grad_attn_out = product_left(attended, grad_attn_low)
    grad_attended = lowered(product_right(grad_attn_low, attn_full)).reshape(
        shard_rows, local_heads, HD
    )
    scores = score_block(query_rot, keys_ext, allowed, score_scale)
    probs = jnp.exp(scores - log_total)
    grad_probs = jnp.einsum(
        "qhd,kd->hqk", grad_attended, values_ext, preferred_element_type=jnp.float32
    )
    grad_scores = lowered(
        probs * (grad_probs - jnp.sum(probs * grad_probs, axis=-1, keepdims=True)) * score_scale
    )
    grad_query_rot = jnp.einsum(
        "hqk,kd->qhd", grad_scores, keys_ext, preferred_element_type=jnp.float32
    )
    grad_keys = jnp.einsum(
        "hqk,qhd->kd", grad_scores, query_rot, preferred_element_type=jnp.float32
    )
    grad_values = jnp.einsum(
        "hqk,qhd->kd", lowered(probs), grad_attended, preferred_element_type=jnp.float32
    )
    grad_ext = jnp.concatenate([grad_keys, grad_values], axis=1)
    grad_own = grad_ext[halo_shards * shard_rows :]
    for offset in range(1, halo_shards + 1):
        grad_piece = grad_ext[
            (halo_shards - offset) * shard_rows : (halo_shards - offset + 1) * shard_rows
        ]
        grad_own = grad_own + passed_along(grad_piece, "seq", -offset)
    key_pre_grad = jax.vjp(rotate_here, keyval[:, :HD])[1](grad_own[:, :HD])[0]
    query_pre_grad = jax.vjp(rotate_here, query_heads)[1](grad_query_rot)[0]
    grad_query_low = lowered(query_pre_grad).reshape(shard_rows, local_heads * HD)
    keyvalue_partial = jnp.concatenate([key_pre_grad, grad_own[:, HD:]], axis=1)
    keyvalue_total, normed_part = head_sum(
        (keyvalue_partial, product_right(grad_query_low, query_full))
    )
    keyvalue_low = lowered(keyvalue_total)
    grad_normed = normed_part + product_right(keyvalue_low, keyvalue_full)
    grad_query = product_left(normed_three, grad_query_low)
    grad_keyvalue = product_left(normed_three, keyvalue_low)
    stream_grad, gain_three = jax.vjp(rms_norm, stream_two, norm_gains[2])[1](grad_normed)
    grad_stream = grad_stream + stream_grad
    grad_stream, gain_two, grad_gate_one, grad_up_one, grad_down_one = dense_backward(
        stream_one, norm_gains[1], grad_stream, kept_one, gate_one, up_one, down_one
    )
    grad_out_low = lowered(grad_stream)
    grad_recur_out = product_left(mixed, grad_out_low)
    grad_mixed = product_right(grad_out_low, output_full)
    grad_state = grad_mixed * gate_act
    grad_gating = lowered(gate_pull(grad_mixed * state)[0])
    decay_next = jnp.concatenate([decay[1:], jnp.ones((1, channels), jnp.float32)], axis=0)
    after_decay, grad_local = lax.associative_scan(
        combine_state, (decay_next, grad_state), axis=0, reverse=True
    )
    returned = prefix(
        (cumulative[-1], decay[0] * grad_local[0]),
        "seq",
        combine_state,
        (ones_state, zeros_state),
        True,
    )
    grad_drive = grad_local + after_decay * returned[1][None, :]
    state_prev = jnp.concatenate([state_in[None, :], state[:-1]], axis=0)
    grad_decay = grad_drive * state_prev
    grad_recur_raw, grad_input_raw, grad_conv, grad_biases, grad_decay_param = rate_pull(
        (grad_decay, grad_drive)
    )
    grad_recur_gate, conv_back_recur = block_grads(conv_low, recur_full, lowered(grad_recur_raw))
    grad_input_gate, conv_back_input = block_grads(
        conv_low, input_gate_full, lowered(grad_input_raw)
    )
    grad_branch_ext, grad_taps, grad_conv_bias = conv_pull(
        grad_conv + conv_back_recur + conv_back_input
    )
    returned_rim = passed_along(grad_branch_ext[:leading], "seq", -1)
    grad_branch = grad_branch_ext[leading:] + jnp.pad(
        returned_rim, ((shard_rows - leading, 0), (0, 0))
    )
    branch_low = lowered(grad_branch)
    grad_input_branch = product_left(normed_one, branch_low)
    grad_gate_branch = product_left(normed_one, grad_gating)
    grad_normed = head_sum(
        product_right(branch_low, branch_full) + product_right(grad_gating, gating_full)
    )
    stream_grad, gain_one = jax.vjp(rms_norm, stream_in, norm_gains[0])[1](grad_normed)
    input_grad = grad_stream + stream_grad
    layer_one = (
        lax.psum_scatter(grad_input_branch, "seq", scatter_dimension=0, tiled=True),
        lax.psum_scatter(grad_gate_branch, "seq", scatter_dimension=0, tiled=True),
        lax.psum_scatter(grad_recur_gate, "seq", scatter_dimension=1, tiled=True),
        lax.psum_scatter(grad_input_gate, "seq", scatter_dimension=1, tiled=True),
        lax.psum_scatter(grad_recur_out, "seq", scatter_dimension=1, tiled=True),
        lax.psum_scatter(grad_gate_one, "seq", scatter_dimension=0, tiled=True),
        lax.psum_scatter(grad_up_one, "seq", scatter_dimension=0, tiled=True),
        lax.psum_scatter(grad_down_one, "seq", scatter_dimension=1, tiled=True),
    )
    layer_two = (
        lax.psum_scatter(grad_query, "seq", scatter_dimension=0, tiled=True),
        lax.psum_scatter(grad_attn_out, "seq", scatter_dimension=1, tiled=True),
        lax.psum_scatter(grad_gate_two, "seq", scatter_dimension=0, tiled=True),
        lax.psum_scatter(grad_up_two, "seq", scatter_dimension=0, tiled=True),
        lax.psum_scatter(grad_down_two, "seq", scatter_dimension=1, tiled=True),
        lax.psum_scatter(grad_keyvalue, "seq", scatter_dimension=0, tiled=True),
    )
    small_sums = lax.psum(
        (
            jnp.stack([gain_one, gain_two, gain_three, gain_four]),
            grad_taps,
            grad_conv_bias,
            grad_biases,
            grad_decay_param,
        ),
        "seq",
    )
    keyvalue_rows = keyvalue_weight.shape[0]
    keyvalue_grad = lax.dynamic_slice_in_dim(
        layer_two[5], lax.axis_index("tp") * keyvalue_rows, keyvalue_rows, 0
    )
    return (
        layer_out,
        input_grad,
        small_sums[0],
        layer_one[0],
        layer_one[1],
        small_sums[1],
        small_sums[2],
        layer_one[2],
        layer_one[3],
        small_sums[3],
        small_sums[4],
        layer_one[4],
        layer_one[5],
        layer_one[6],
        layer_one[7],
        layer_two[0],
        keyvalue_grad,
        layer_two[1],
        layer_two[2],
        layer_two[3],
        layer_two[4],
    )


def solution(mesh):
    placed = (
        P("seq", None),
        P("seq", None),
        P(),
        P(),
        P("seq", "tp"),
        P("seq", "tp"),
        P(None, "tp"),
        P("tp"),
        P("tp", "seq"),
        P("tp", "seq"),
        P(None, "tp"),
        P("tp"),
        P("tp", "seq"),
        P("seq", "tp"),
        P("seq", "tp"),
        P("tp", "seq"),
        P("seq", "tp"),
        P(("seq", "tp"), None),
        P("tp", "seq"),
        P("seq", "tp"),
        P("seq", "tp"),
        P("tp", "seq"),
    )
    return jax.shard_map(
        local,
        mesh=mesh,
        in_specs=placed,
        out_specs=(
            P("seq", None),
            P("seq", None),
            P(),
            P("seq", "tp"),
            P("seq", "tp"),
            P(None, "tp"),
            P("tp"),
            P("tp", "seq"),
            P("tp", "seq"),
            P(None, "tp"),
            P("tp"),
            P("tp", "seq"),
            P("seq", "tp"),
            P("seq", "tp"),
            P("tp", "seq"),
            P("seq", "tp"),
            P(("seq", "tp"), None),
            P("tp", "seq"),
            P("seq", "tp"),
            P("seq", "tp"),
            P("tp", "seq"),
        ),
        check_vma=False,
    )
```

profile of v0, /device:TPU:0, one launch (start us, length us, event | category | flops | bytes accessed | tf_op | source)
XLA Modules:
  0.0 2992.0 jit_solution(1368379546579131861)
XLA Ops:
  17.5 32.9 %all_gather.54 = bf16[512,128]{0,1:T(8,128)(2,1)S(1)} all-gather(bf16[512,16]{0,1:T(8,128)(2,1)} %param.34), channel_id=1, replica_groups=mesh['seq'=8,'tp'=4] {'seq'}, dimensions={1}, use_global_device_ids=true | all-gather | bytes 147456 | tf_op jit(solution)/shard_map/all_gather | solution.py:163
  50.5 7.0 all-gather.15.cloned.1.call-done
  62.9 30.9 %all_gather.55 = bf16[512,128]{0,1:T(8,128)(2,1)S(1)} all-gather(bf16[512,16]{0,1:T(8,128)(2,1)S(1)} %copy-done.120), channel_id=1, replica_groups=mesh['seq'=8,'tp'=4] {'seq'}, dimensions={1}, use_global_device_ids=true | all-gather | bytes 147456 | tf_op jit(solution)/shard_map/all_gather | solution.py:164
  145.2 26.0 all-gather
  175.7 26.2 all-gather.1
  202.4 5.0 multiply_convert_fusion.8
  213.7 64.1 %all-reduce.100.cloned.1.call-done = f32[512,1536]{1,0:T(8,128)} async-done(((f32[512,1536]{1,0:T(8,128)}), f32[512,1536]{1,0:T(8,128)}) %all-reduce.100.cloned.1.call-update) | async-done | bytes 3145744 | tf_op jit(solution)/shard_map/psum | solution.py:147
  283.6 61.5 %all-gather.21.cloned.1.call-done = bf16[1536,1152]{1,0:T(8,128)(2,1)} async-done(((bf16[192,1152]{1,0:T(8,128)(2,1)}), bf16[1536,1152]{1,0:T(8,128)(2,1)}) %all-gather.21.cloned.1.call-update) | async-done | bytes 3538960 | tf_op jit(solution)/shard_map/all_gather | solution.py:166
  345.1 6.1 fusion.199
  351.2 59.6 %all-gather.23.cloned.1.call-done = bf16[1536,1152]{1,0:T(8,128)(2,1)} async-done(((bf16[192,1152]{1,0:T(8,128)(2,1)}), bf16[1536,1152]{1,0:T(8,128)(2,1)}) %all-gather.23.cloned.1.call-update) | async-done | bytes 3538960 | tf_op jit(solution)/shard_map/all_gather | solution.py:167
  410.8 7.3 multiply_convert_fusion.7
  418.1 58.6 %all-gather.25.cloned.1.call-done = bf16[1152,1536]{0,1:T(8,128)(2,1)} async-done(((bf16[1152,192]{0,1:T(8,128)(2,1)}), bf16[1152,1536]{0,1:T(8,128)(2,1)}) %all-gather.25.cloned.1.call-update) | async-done | bytes 3538960 | tf_op jit(solution)/shard_map/all_gather | solution.py:168
  476.7 6.3 fusion.200
  485.2 44.4 %all_gather.63 = bf16[1536,256]{1,0:T(8,128)(2,1)} all-gather(bf16[48,256]{1,0:T(8,128)(2,1)S(1)} %copy-done.95), channel_id=1, replica_groups=mesh['seq'=8,'tp'=4] {'seq','tp'}, dimensions={0}, use_global_device_ids=true | all-gather | bytes 811008 | tf_op jit(solution)/shard_map/all_gather | solution.py:183
  531.6 25.3 all-reduce.102.cloned.1.call-done
  570.9 31.2 %all-gather.27.cloned.1.call-done = bf16[1536,384]{1,0:T(8,128)(2,1)} async-done(((bf16[192,384]{1,0:T(8,128)(2,1)}), bf16[1536,384]{1,0:T(8,128)(2,1)}) %all-gather.27.cloned.1.call-update) | async-done | bytes 1179664 | tf_op jit(solution)/shard_map/all_gather | solution.py:174
  614.4 29.7 all-gather.29.cloned.1.call-done
  650.4 65.0 %all-reduce.104.cloned.1.call-done = f32[512,1536]{1,0:T(8,128)} async-done(((f32[512,1536]{1,0:T(8,128)}), f32[512,1536]{1,0:T(8,128)}) %all-reduce.104.cloned.1.call-update) | async-done | bytes 3145744 | tf_op jit(solution)/shard_map/psum | solution.py:147
  720.2 62.6 %all-gather.33.cloned.1.call-done = bf16[1536,1152]{1,0:T(8,128)(2,1)} async-done(((bf16[192,1152]{1,0:T(8,128)(2,1)}), bf16[1536,1152]{1,0:T(8,128)(2,1)}) %all-gather.33.cloned.1.call-update) | async-done | bytes 3538960 | tf_op jit(solution)/shard_map/all_gather | solution.py:177
  782.7 6.1 fusion.205
  788.9 59.7 %all-gather.31.cloned.1.call-done = bf16[1536,1152]{1,0:T(8,128)(2,1)} async-done(((bf16[192,1152]{1,0:T(8,128)(2,1)}), bf16[1536,1152]{1,0:T(8,128)(2,1)}) %all-gather.31.cloned.1.call-update) | async-done | bytes 3538960 | tf_op jit(solution)/shard_map/all_gather | solution.py:176
  848.6 6.1 fusion.204
  854.7 59.7 %all-gather.35.cloned.1.call-done = bf16[1152,1536]{0,1:T(8,128)(2,1)} async-done(((bf16[1152,192]{0,1:T(8,128)(2,1)}), bf16[1152,1536]{0,1:T(8,128)(2,1)}) %all-gather.35.cloned.1.call-update) | async-done | bytes 3538960 | tf_op jit(solution)/shard_map/all_gather | solution.py:178
  914.4 8.7 multiply_convert_fusion.5
  930.0 66.9 %all-reduce.106.cloned.1.call-done = f32[512,1536]{1,0:T(8,128)} async-done(((f32[512,1536]{1,0:T(8,128)}), f32[512,1536]{1,0:T(8,128)}) %all-reduce.106.cloned.1.call-update) | async-done | bytes 3145744 | tf_op jit(solution)/shard_map/psum | solution.py:147
  1004.5 4.9 fusion.99
  1012.0 15.0 fusion.26
  1027.1 15.2 fusion.44
  1054.2 10.1 collective-permute-done.3
  1064.3 12.1 collective-permute-done.4
  1079.4 21.7 all-reduce.113
  1101.1 33.1 %all-reduce.108.cloned.1.call-done = f32[512,1536]{1,0:T(8,128)} async-done(((f32[512,1536]{1,0:T(8,128)}), f32[512,1536]{1,0:T(8,128)}) %all-reduce.108.cloned.1.call-update) | async-done | bytes 3145744 | tf_op jit(solution)/shard_map/psum | solution.py:147
  1134.1 5.1 multiply_reduce_fusion.1
  1172.6 4.9 slice.780
  1182.3 6.4 fusion.206
  1191.0 32.1 %all-reduce.110.cloned.1.call-done = f32[512,1536]{1,0:T(8,128)} async-done(((f32[512,1536]{1,0:T(8,128)}), f32[512,1536]{1,0:T(8,128)}) %all-reduce.110.cloned.1.call-update) | async-done | bytes 3145744 | tf_op jit(solution)/shard_map/psum | solution.py:147
  1464.3 8.9 rev.8
  1473.2 26.2 all-gather.2
  1500.0 6.2 while.31
  1518.3 8.9 rev.9
  1527.2 5.3 fusion.175
  1537.2 5.2 multiply_reduce_fusion.9
  1547.5 5.7 multiply_reduce_fusion.13
  1594.8 7.0 fusion.76
  1601.9 6.8 fusion.215
  1608.8 6.9 fusion.214
  1616.0 7.5 fusion.69
  1623.6 7.2 fusion.212
  1630.9 6.9 fusion.211
  1640.1 40.7 %all-reduce.112.cloned.1.call-done = (f32[512,1536]{1,0:T(8,128)}, f32[512,1536]{1,0:T(8,128)}) async-done(((f32[512,1536]{1,0:T(8,128)}, f32[512,1536]{1,0:T(8,128)}), (f32[512,1536]{1,0:T(8,128)}, f32[512,1536]{1,0:T(8,128)})) %all-reduce.112.cloned.1.call-update) | async-done | bytes 6291472 | tf_op jit(solution)/shard_map/psum | solution.py:147
  1684.2 38.2 %all-reduce.89 = (f32[4,1536]{1,0:T(4,128)}, f32[4,512]{1,0:T(4,128)}, f32[512]{0:T(512)}, f32[2,512]{1,0:T(2,128)}, f32[512]{0:T(512)}) all-reduce(f32[4,1536]{1,0:T(4,128)S(1)} %pad_maximum_fusion.26, f32[4,512]{1,0:T(4,128)S(1)} %pad_add_fusion.3, f32[512]{0:T(512)S(1)} %copy-done.124, ...), channel_id=1, replica_groups=mesh['seq'=8,'tp'=4] {'seq'}, use_global_device_ids=true, to_apply=%region_33.34 | all-reduce | flops 10240 | bytes 81920 | tf_op jit(solution)/shard_map/psum | solution.py:441
  1729.7 16.6 reduce-scatter.21.cloned.1.call-done
  1746.3 64.5 %reduce-scatter.19.cloned.1.call-done = f32[512,16]{0,1:T(8,128)} async-done(((f32[512,128]{0,1:T(8,128)}), f32[512,16]{0,1:T(8,128)}) %reduce-scatter.19.cloned.1.call-update) | async-done | bytes 32784 | tf_op jit(solution)/shard_map/reduce_scatter | solution.py:426
  1810.9 72.6 %reduce-scatter.35.cloned.1.call-done = f32[384,192]{0,1:T(8,128)} async-done(((f32[384,1536]{0,1:T(8,128)}), f32[384,192]{0,1:T(8,128)}) %reduce-scatter.35.cloned.1.call-update) | async-done | bytes 294928 | tf_op jit(solution)/shard_map/reduce_scatter | solution.py:435
  1883.5 72.7 %reduce-scatter.31.cloned.1.call-done = f32[192,384]{1,0:T(8,128)} async-done(((f32[1536,384]{1,0:T(8,128)}), f32[192,384]{1,0:T(8,128)}) %reduce-scatter.31.cloned.1.call-update) | async-done | bytes 294928 | tf_op jit(solution)/shard_map/reduce_scatter | solution.py:434
  1956.2 77.8 %reduce-scatter.17.cloned.1.call-done = f32[192,512]{1,0:T(8,128)} async-done(((f32[1536,512]{1,0:T(8,128)}), f32[192,512]{1,0:T(8,128)}) %reduce-scatter.17.cloned.1.call-update) | async-done | bytes 393232 | tf_op jit(solution)/shard_map/reduce_scatter | solution.py:425
  2033.9 78.1 %reduce-scatter.23.cloned.1.call-done = f32[512,192]{0,1:T(8,128)} async-done(((f32[512,1536]{0,1:T(8,128)}), f32[512,192]{0,1:T(8,128)}) %reduce-scatter.23.cloned.1.call-update) | async-done | bytes 393232 | tf_op jit(solution)/shard_map/reduce_scatter | solution.py:428
  2112.0 77.7 %reduce-scatter.15.cloned.1.call-done = f32[192,512]{1,0:T(8,128)} async-done(((f32[1536,512]{1,0:T(8,128)}), f32[192,512]{1,0:T(8,128)}) %reduce-scatter.15.cloned.1.call-update) | async-done | bytes 393232 | tf_op jit(solution)/shard_map/reduce_scatter | solution.py:424
  2189.8 132.7 %reduce-scatter.41.cloned.1.call-done = f32[1152,192]{0,1:T(8,128)} async-done(((f32[1152,1536]{0,1:T(8,128)}), f32[1152,192]{0,1:T(8,128)}) %reduce-scatter.41.cloned.1.call-update) | async-done | bytes 884752 | tf_op jit(solution)/shard_map/reduce_scatter | solution.py:438
  2322.5 132.4 %reduce-scatter.39.cloned.1.call-done = f32[192,1152]{1,0:T(8,128)} async-done(((f32[1536,1152]{1,0:T(8,128)}), f32[192,1152]{1,0:T(8,128)}) %reduce-scatter.39.cloned.1.call-update) | async-done | bytes 884752 | tf_op jit(solution)/shard_map/reduce_scatter | solution.py:437
  2454.8 132.8 %reduce-scatter.37.cloned.1.call-done = f32[192,1152]{1,0:T(8,128)} async-done(((f32[1536,1152]{1,0:T(8,128)}), f32[192,1152]{1,0:T(8,128)}) %reduce-scatter.37.cloned.1.call-update) | async-done | bytes 884752 | tf_op jit(solution)/shard_map/reduce_scatter | solution.py:436
  2587.7 132.2 %reduce-scatter.29.cloned.1.call-done = f32[1152,192]{0,1:T(8,128)} async-done(((f32[1152,1536]{0,1:T(8,128)}), f32[1152,192]{0,1:T(8,128)}) %reduce-scatter.29.cloned.1.call-update) | async-done | bytes 884752 | tf_op jit(solution)/shard_map/reduce_scatter | solution.py:431
  2719.9 132.8 %reduce-scatter.27.cloned.1.call-done = f32[192,1152]{1,0:T(8,128)} async-done(((f32[1536,1152]{1,0:T(8,128)}), f32[192,1152]{1,0:T(8,128)}) %reduce-scatter.27.cloned.1.call-update) | async-done | bytes 884752 | tf_op jit(solution)/shard_map/reduce_scatter | solution.py:430
  2852.7 132.3 %reduce-scatter.25.cloned.1.call-done = f32[192,1152]{1,0:T(8,128)} async-done(((f32[1536,1152]{1,0:T(8,128)}), f32[192,1152]{1,0:T(8,128)}) %reduce-scatter.25.cloned.1.call-update) | async-done | bytes 884752 | tf_op jit(solution)/shard_map/reduce_scatter | solution.py:429
  (851 shorter events, 520.5 us)
Async XLA Ops:
  7.2 50.2 %all-gather.15.cloned.1.call-start = ((), (), s32[]{:S(2)}) async-start(), calls=%async_computation.14 | async-start | bytes 1769472 | tf_op jit(solution)/shard_map/all_gather | solution.py:161
  7.9 194.4 %all-gather.17.cloned.1.call-start = ((), (), s32[]{:S(2)}) async-start(), calls=%async_computation.15 | async-start | bytes 1769472 | tf_op jit(solution)/shard_map/all_gather | solution.py:162
  8.7 198.7 %all-gather.19.cloned.1.call-start = ((), (), s32[]{:S(2)}) async-start(), calls=%async_computation.16 | async-start | bytes 1769472 | tf_op jit(solution)/shard_map/all_gather | solution.py:165
  9.4 268.3 %all-reduce.100.cloned.1.call-start = ((), (), s32[]{:S(2)}) async-start(), calls=%async_computation.17 | async-start | bytes 6291456 | tf_op jit(solution)/shard_map/psum | solution.py:147
  9.5 50.9 %copy-start.116 = (s32[512]{0:T(512)}, s32[512]{0:T(512)S(1)}, u32[]{:S(2)}) copy-start(s32[512]{0:T(512)S(1)} %iota_add_fusion.2) | copy-start | bytes 6148
  11.3 49.1 %copy-start.92 = (f32[512]{0:T(512)}, f32[512]{0:T(512)S(1)}, u32[]{:S(2)}) copy-start(f32[512]{0:T(512)S(1)} %fusion.156) | copy-start | bytes 6148
  12.1 45.3 %copy-start.144 = (s32[4,1]{0,1:T(1,128)}, s32[4,1]{0,1:T(1,128)S(1)}, u32[]{:S(2)}) copy-start(s32[4,1]{0,1:T(1,128)S(1)} %reduce-window.8) | copy-start | bytes 52
  12.3 81.8 %copy-start.79 = (f32[512]{0:T(512)}, f32[512]{0:T(512)S(1)}, u32[]{:S(2)}) copy-start(f32[512]{0:T(512)S(1)} %get-tuple-element.461) | copy-start | bytes 6148
  12.3 81.8 %copy-start.81 = (f32[512]{0:T(512)}, f32[512]{0:T(512)S(1)}, u32[]{:S(2)}) copy-start(f32[512]{0:T(512)S(1)} %get-tuple-element.462) | copy-start | bytes 6148
  12.3 81.8 %copy-start.83 = (f32[512]{0:T(512)}, f32[512]{0:T(512)S(1)}, u32[]{:S(2)}) copy-start(f32[512]{0:T(512)S(1)} %get-tuple-element.463) | copy-start | bytes 6148
  13.0 47.4 %copy-start.118 = (s32[512]{0:T(512)}, s32[512]{0:T(512)S(1)}, u32[]{:S(2)}) copy-start(s32[512]{0:T(512)S(1)} %get-tuple-element.305) | copy-start | bytes 6148
  13.0 87.9 %copy-start.96 = (f32[512]{0:T(512)}, f32[512]{0:T(512)S(1)}, u32[]{:S(2)}) copy-start(f32[512]{0:T(512)S(1)} %fusion.155) | copy-start | bytes 6148
  13.8 87.2 %copy-start.71 = (f32[1,512]{1,0:T(1,128)}, f32[1,512]{1,0:T(1,128)S(1)}, u32[]{:S(2)}) copy-start(f32[1,512]{1,0:T(1,128)S(1)} %get-tuple-element.460) | copy-start | bytes 6148
  13.8 87.2 %copy-start.76 = (f32[1,512]{1,0:T(1,128)}, f32[1,512]{1,0:T(1,128)S(1)}, u32[]{:S(2)}) copy-start(f32[1,512]{1,0:T(1,128)S(1)} %get-tuple-element.459) | copy-start | bytes 6148
  15.1 85.9 %copy-start.74 = (f32[512]{0:T(512)}, f32[512]{0:T(512)S(1)}, u32[]{:S(2)}) copy-start(f32[512]{0:T(512)S(1)} %get-tuple-element.469) | copy-start | bytes 6148
  15.9 78.2 %copy-start.102 = (f32[1,512]{1,0:T(1,128)}, f32[1,512]{1,0:T(1,128)S(1)}, u32[]{:S(2)}) copy-start(f32[1,512]{1,0:T(1,128)S(1)} %get-tuple-element.443) | copy-start | bytes 6148
  15.9 78.2 %copy-start.104 = (f32[1,512]{1,0:T(1,128)}, f32[1,512]{1,0:T(1,128)S(1)}, u32[]{:S(2)}) copy-start(f32[1,512]{1,0:T(1,128)S(1)} %get-tuple-element.444) | copy-start | bytes 6148
  15.9 78.2 %copy-start.106 = (f32[1,512]{1,0:T(1,128)}, f32[1,512]{1,0:T(1,128)S(1)}, u32[]{:S(2)}) copy-start(f32[1,512]{1,0:T(1,128)S(1)} %get-tuple-element.445) | copy-start | bytes 6148
  16.0 78.2 %copy-start.108 = (f32[1,512]{1,0:T(1,128)}, f32[1,512]{1,0:T(1,128)S(1)}, u32[]{:S(2)}) copy-start(f32[1,512]{1,0:T(1,128)S(1)} %get-tuple-element.446) | copy-start | bytes 6148
  17.5 184.8 %copy-start.65 = (f32[1536]{0:T(1024)}, f32[1536]{0:T(1024)S(1)}, u32[]{:S(2)}) copy-start(f32[1536]{0:T(1024)S(1)} %get-tuple-element.302) | copy-start | bytes 18436
  60.4 33.7 %collective-permute-start = (f32[3,512]{1,0:T(4,128)S(1)}, f32[3,512]{1,0:T(4,128)S(1)}, u32[]{:S(2)}, u32[]{:S(2)}) collective-permute-start(f32[3,512]{1,0:T(4,128)S(1)} %slice.871), channel_id=1, source_target_pairs={{0,4},{4,8},{8,12},{12,16},{16,20},{20,24},{24,28},{1,5},{5,9},{9,... | collective-permute-start | bytes 18440 | tf_op jit(solution)/shard_map/ppermute | solution.py:16
  141.7 60.7 %copy-start.7 = (bf16[512,1536]{1,0:T(8,128)(2,1)S(1)}, bf16[512,1536]{1,0:T(8,128)(2,1)}, u32[]{:S(2)}) copy-start(bf16[512,1536]{1,0:T(8,128)(2,1)} %param.26) | copy-start | bytes 4718596
  141.7 60.7 %copy-start.93 = (f32[512]{0:T(512)S(1)}, f32[512]{0:T(512)}, u32[]{:S(2)}) copy-start(f32[512]{0:T(512)} %copy-done.92) | copy-start | bytes 6148
  211.7 133.4 %all-gather.21.cloned.1.call-start = ((), (), s32[]{:S(2)}) async-start(), calls=%async_computation.18 | async-start | bytes 3981312 | tf_op jit(solution)/shard_map/all_gather | solution.py:166
  212.3 198.5 %all-gather.23.cloned.1.call-start = ((), (), s32[]{:S(2)}) async-start(), calls=%async_computation.19 | async-start | bytes 3981312 | tf_op jit(solution)/shard_map/all_gather | solution.py:167
  212.9 263.8 %all-gather.25.cloned.1.call-start = ((), (), s32[]{:S(2)}) async-start(), calls=%async_computation.20 | async-start | bytes 3981312 | tf_op jit(solution)/shard_map/all_gather | solution.py:168
  213.6 343.3 %all-reduce.102.cloned.1.call-start = ((), (), s32[]{:S(2)}) async-start(), calls=%async_computation.21 | async-start | bytes 6291456 | tf_op jit(solution)/shard_map/psum | solution.py:147
  280.6 276.4 %copy-start = (f32[512,1536]{1,0:T(8,128)}, f32[512,1536]{1,0:T(8,128)S(1)}, u32[]{:S(2)}) copy-start(f32[512,1536]{1,0:T(8,128)S(1)} %get-tuple-element.345) | copy-start | bytes 9437188
  483.0 46.6 %copy-start.117 = (s32[512]{0:T(512)S(1)}, s32[512]{0:T(512)}, u32[]{:S(2)}) copy-start(s32[512]{0:T(512)} %copy-done.116) | copy-start | bytes 6148
  483.0 119.1 %all-gather.27.cloned.1.call-start = ((), (), s32[]{:S(2)}) async-start(), calls=%async_computation.22 | async-start | bytes 1327104 | tf_op jit(solution)/shard_map/all_gather | solution.py:174
  483.7 160.3 %all-gather.29.cloned.1.call-start = ((), (), s32[]{:S(2)}) async-start(), calls=%async_computation.23 | async-start | bytes 1327104 | tf_op jit(solution)/shard_map/all_gather | solution.py:175
  484.3 231.1 %all-reduce.104.cloned.1.call-start = ((), (), s32[]{:S(2)}) async-start(), calls=%async_computation.24 | async-start | bytes 6291456 | tf_op jit(solution)/shard_map/psum | solution.py:147
  484.4 77.3 %copy-start.147 = (f32[64]{0:T(128)}, f32[64]{0:T(128)S(1)}, u32[]{:S(2)}) copy-start(f32[64]{0:T(128)S(1)} %multiply_power_fusion) | copy-start | bytes 772
  484.4 77.3 %copy-start.100 = (f32[512]{0:T(512)}, f32[512]{0:T(512)S(1)}, u32[]{:S(2)}) copy-start(f32[512]{0:T(512)S(1)} %subtract_convert_fusion.1) | copy-start | bytes 6148
  563.0 42.2 %collective-permute-start.2 = (bf16[512,256]{0,1:T(8,128)(2,1)}, bf16[512,256]{0,1:T(8,128)(2,1)}, u32[]{:S(2)}, u32[]{:S(2)}) collective-permute-start(bf16[512,256]{0,1:T(8,128)(2,1)} %pad_maximum_fusion.9), channel_id=1, source_target_pairs={{0,4},{4,8},{8,12},{12,16},{16,20},{20,24},{24,28},{1,5},{5,9},{9,... | collective-permute-start | bytes 786440 | tf_op jit(solution)/shard_map/ppermute | solution.py:16
  567.0 38.1 %collective-permute-start.1 = (bf16[512,256]{0,1:T(8,128)(2,1)}, bf16[512,256]{0,1:T(8,128)(2,1)}, u32[]{:S(2)}, u32[]{:S(2)}) collective-permute-start(bf16[512,256]{0,1:T(8,128)(2,1)} %pad_maximum_fusion.9), channel_id=1, source_target_pairs={{0,8},{4,12},{8,16},{12,20},{16,24},{20,28},{1,9},{5,13},{9,17},{1... | collective-permute-start | bytes 786440 | tf_op jit(solution)/shard_map/ppermute | solution.py:16
  648.0 134.7 %all-gather.33.cloned.1.call-start = ((), (), s32[]{:S(2)}) async-start(), calls=%async_computation.26 | async-start | bytes 3981312 | tf_op jit(solution)/shard_map/all_gather | solution.py:177
  648.6 200.0 %all-gather.31.cloned.1.call-start = ((), (), s32[]{:S(2)}) async-start(), calls=%async_computation.25 | async-start | bytes 3981312 | tf_op jit(solution)/shard_map/all_gather | solution.py:176
  649.3 265.0 %all-gather.35.cloned.1.call-start = ((), (), s32[]{:S(2)}) async-start(), calls=%async_computation.27 | async-start | bytes 3981312 | tf_op jit(solution)/shard_map/all_gather | solution.py:178
  649.9 68.7 %copy-start.64 = (f32[1536]{0:T(1024)S(1)}, f32[1536]{0:T(1024)}, u32[]{:S(2)}) copy-start(f32[1536]{0:T(1024)} %get-tuple-element.300) | copy-start | bytes 18436
  649.9 347.0 %all-reduce.106.cloned.1.call-start = ((), (), s32[]{:S(2)}) async-start(), calls=%async_computation.28 | async-start | bytes 6291456 | tf_op jit(solution)/shard_map/psum | solution.py:147
  788.9 125.5 %copy-start.98 = (f32[512]{0:T(512)S(1)}, f32[512]{0:T(512)}, u32[]{:S(2)}) copy-start(f32[512]{0:T(512)} %get-tuple-element.338) | copy-start | bytes 6148
  929.8 204.3 %all-reduce.108.cloned.1.call-start = ((), (), s32[]{:S(2)}) async-start(), calls=%async_computation.29 | async-start | bytes 6291456 | tf_op jit(solution)/shard_map/psum | solution.py:147
  1048.5 15.8 collective-permute-start.3
  1049.8 26.6 collective-permute-start.4
  1053.9 169.2 %all-reduce.110.cloned.1.call-start = ((), (), s32[]{:S(2)}) async-start(), calls=%async_computation.30 | async-start | bytes 6291456 | tf_op jit(solution)/shard_map/psum | solution.py:147
  1154.4 484.2 %reduce-scatter.33.cloned.1.call-start = ((), (), s32[]{:S(2)}) async-start(), calls=%async_computation.40 | async-start | bytes 1769472 | tf_op jit(solution)/shard_map/reduce_scatter | solution.py:439
  1190.5 490.3 %all-reduce.112.cloned.1.call-start = ((), (), s32[]{:S(2)}) async-start(), calls=%async_computation.45 | async-start | bytes 12582912 | tf_op jit(solution)/shard_map/psum | solution.py:147
  1553.6 5.7 collective-permute-start.5
  1562.6 183.7 %reduce-scatter.21.cloned.1.call-start = ((), (), s32[]{:S(2)}) async-start(), calls=%async_computation.34 | async-start | bytes 294912 | tf_op jit(solution)/shard_map/reduce_scatter | solution.py:427
  1566.7 244.2 %reduce-scatter.19.cloned.1.call-start = ((), (), s32[]{:S(2)}) async-start(), calls=%async_computation.33 | async-start | bytes 294912 | tf_op jit(solution)/shard_map/reduce_scatter | solution.py:426
  1570.9 312.6 %reduce-scatter.35.cloned.1.call-start = ((), (), s32[]{:S(2)}) async-start(), calls=%async_computation.41 | async-start | bytes 2654208 | tf_op jit(solution)/shard_map/reduce_scatter | solution.py:435
  1575.5 380.7 %reduce-scatter.31.cloned.1.call-start = ((), (), s32[]{:S(2)}) async-start(), calls=%async_computation.39 | async-start | bytes 2654208 | tf_op jit(solution)/shard_map/reduce_scatter | solution.py:434
  1579.6 454.3 %reduce-scatter.17.cloned.1.call-start = ((), (), s32[]{:S(2)}) async-start(), calls=%async_computation.32 | async-start | bytes 3538944 | tf_op jit(solution)/shard_map/reduce_scatter | solution.py:425
  1584.0 528.0 %reduce-scatter.23.cloned.1.call-start = ((), (), s32[]{:S(2)}) async-start(), calls=%async_computation.35 | async-start | bytes 3538944 | tf_op jit(solution)/shard_map/reduce_scatter | solution.py:428
  1589.0 600.8 %reduce-scatter.15.cloned.1.call-start = ((), (), s32[]{:S(2)}) async-start(), calls=%async_computation.31 | async-start | bytes 3538944 | tf_op jit(solution)/shard_map/reduce_scatter | solution.py:424
  1594.1 728.4 %reduce-scatter.41.cloned.1.call-start = ((), (), s32[]{:S(2)}) async-start(), calls=%async_computation.44 | async-start | bytes 7962624 | tf_op jit(solution)/shard_map/reduce_scatter | solution.py:438
  1601.8 853.0 %reduce-scatter.39.cloned.1.call-start = ((), (), s32[]{:S(2)}) async-start(), calls=%async_computation.43 | async-start | bytes 7962624 | tf_op jit(solution)/shard_map/reduce_scatter | solution.py:437
  1608.7 978.9 %reduce-scatter.37.cloned.1.call-start = ((), (), s32[]{:S(2)}) async-start(), calls=%async_computation.42 | async-start | bytes 7962624 | tf_op jit(solution)/shard_map/reduce_scatter | solution.py:436
  1615.7 1104.2 %reduce-scatter.29.cloned.1.call-start = ((), (), s32[]{:S(2)}) async-start(), calls=%async_computation.38 | async-start | bytes 7962624 | tf_op jit(solution)/shard_map/reduce_scatter | solution.py:431
  1623.5 1229.2 %reduce-scatter.27.cloned.1.call-start = ((), (), s32[]{:S(2)}) async-start(), calls=%async_computation.37 | async-start | bytes 7962624 | tf_op jit(solution)/shard_map/reduce_scatter | solution.py:430
  1630.8 1354.2 %reduce-scatter.25.cloned.1.call-start = ((), (), s32[]{:S(2)}) async-start(), calls=%async_computation.36 | async-start | bytes 7962624 | tf_op jit(solution)/shard_map/reduce_scatter | solution.py:429
  1637.8 46.3 %copy-start.124 = (f32[512]{0:T(512)S(1)}, f32[512]{0:T(512)}, u32[]{:S(2)}) copy-start(f32[512]{0:T(512)} %get-tuple-element.299) | copy-start | bytes 6148
  1637.9 84.5 %copy-start.111 = (f32[512]{0:T(512)S(1)}, f32[512]{0:T(512)}, u32[]{:S(2)}) copy-start(f32[512]{0:T(512)} %copy-done.110) | copy-start | bytes 6148
  (137 other events, 951.6 us)
Sparse Core Ops, SparseCore 0:
  10.2 47.1 all-gather.14
  59.6 43.4 all-gather.16
  105.3 42.7 all-gather.18
  211.8 65.8 all-reduce.99
  279.7 65.2 all-gather.20
  347.1 63.6 all-gather.22
  413.0 63.6 all-gather.24
  483.1 73.7 all-reduce.101
  559.1 42.9 all-gather.26
  604.2 39.8 all-gather.28
  648.1 67.2 all-reduce.103
  717.4 65.2 all-gather.32
  784.9 63.6 all-gather.30
  850.7 63.6 all-gather.34
  929.9 66.9 all-reduce.105
  1054.0 80.0 all-reduce.107
  1154.6 68.4 all-reduce.109
  1226.4 64.8 reduce-scatter.32
  1562.7 118.0 all-reduce.111
  1684.9 61.3 reduce-scatter.20
  1750.6 60.2 reduce-scatter.18
  1815.3 68.1 reduce-scatter.34
  1888.0 68.1 reduce-scatter.30
  1960.6 73.2 reduce-scatter.16
  2038.5 73.4 reduce-scatter.22
  2116.5 73.2 reduce-scatter.14
  2194.3 128.1 reduce-scatter.40
  2326.7 128.0 reduce-scatter.38
  2459.6 128.0 reduce-scatter.36
  2591.8 128.0 reduce-scatter.28
  2724.6 128.0 reduce-scatter.26
  2856.9 128.0 reduce-scatter.24
where the time goes:
time: 3010 us; the launch traced here: 2990 us
  waiting for transfers between devices  2040 us (68%)
  local copies, waits for them, and re-layouts  300 us (10%)
  blocking collectives  246 us (8%)
  matrix products  214 us (7%)
  other arithmetic  152 us (5%)
    psum x7, waiting for transfers between devices, head_sum(): return lax.psum(values, 'tp')  327 us
    reduce_scatter x1, waiting for transfers between devices, local(): lax.psum_scatter(grad_gate_two, 'seq', scatter_dimension=0, tiled=True)  133 us
    reduce_scatter x1, waiting for transfers between devices, local(): lax.psum_scatter(grad_up_one, 'seq', scatter_dimension=0, tiled=True)  133 us
    reduce_scatter x1, waiting for transfers between devices, local(): lax.psum_scatter(grad_down_two, 'seq', scatter_dimension=1, tiled=True)  133 us
    reduce_scatter x1, waiting for transfers between devices, local(): lax.psum_scatter(grad_up_two, 'seq', scatter_dimension=0, tiled=True)  132 us
    reduce_scatter x1, waiting for transfers between devices, local(): lax.psum_scatter(grad_gate_one, 'seq', scatter_dimension=0, tiled=True)  132 us
    reduce_scatter x1, waiting for transfers between devices, local(): lax.psum_scatter(grad_down_one, 'seq', scatter_dimension=1, tiled=True)  132 us
    slice x65, local copies, waits for them, and re-layouts, local(): lax.associative_scan(combine_state, (decay_next, grad_state), axis=0, rev...  121 us
  transfers between devices with their start and end apart: 38, of which 32 were waited for; matrix products, arithmetic and copies ran while one was open for 18% of the time, Pallas kernels for 0%

commit v1 on v0

v1 whole, which is shorter than its diff:
```python
import functools

import jax
import jax.numpy as jnp
from jax import lax
from jax.experimental import pallas as pl
from jax.experimental.pallas import tpu as pltpu
from jax.sharding import PartitionSpec as P

HD = 128
CONV = 4
WINDOW = 1024


def product(left, right):
    return jnp.dot(left, right, preferred_element_type=jnp.float32)


def product_left(left, right):
    return lax.dot_general(
        left, right, (((0,), (0,)), ((), ())), preferred_element_type=jnp.float32
    )


def product_right(left, right):
    return lax.dot_general(
        left, right, (((1,), (1,)), ((), ())), preferred_element_type=jnp.float32
    )


def lowered(values):
    return values.astype(jnp.bfloat16)


def rms_norm(values, gain):
    return values * lax.rsqrt(jnp.mean(values * values, axis=-1, keepdims=True) + 1e-06) * gain


def gated(gate_values, up_values):
    return jax.nn.gelu(gate_values) * up_values


def layout(doc_lengths, first_slot, count):
    ends = jnp.cumsum(doc_lengths, dtype=jnp.int32)
    slots = first_slot + jnp.arange(count, dtype=jnp.int32)
    passed = slots[:, None] >= ends[None, :]
    segment = jnp.sum(passed.astype(jnp.int32), axis=1)
    begin = jnp.max(jnp.where(passed, ends[None, :], 0), axis=1)
    segment = jnp.where(slots < 0, -1, segment)
    position = slots - begin
    reset = (slots != begin).astype(jnp.float32)
    valid = (segment < doc_lengths.shape[0]).astype(jnp.float32)
    return (segment, position, reset, valid)


def rotate(values, position):
    half_width = values.shape[-1] // 2
    frequency = 10000.0 ** (-jnp.arange(half_width, dtype=jnp.float32) / half_width)
    angle = position.astype(jnp.float32)[:, None] * frequency[None, :]
    if values.ndim == 3:
        angle = angle[:, None, :]
    cosine = jnp.cos(angle)
    sine = jnp.sin(angle)
    first_half = values[..., :half_width]
    second_half = values[..., half_width:]
    return jnp.concatenate(
        [first_half * cosine - second_half * sine, second_half * cosine + first_half * sine],
        axis=-1,
    )


def convolve(extended, taps, bias, segment):
    leading = CONV - 1
    total_rows = extended.shape[0] - leading
    result = bias[None, :] + taps[0][None, :] * extended[leading:]
    for lag_index in range(1, CONV):
        same = (
            segment[leading:] == segment[leading - lag_index : leading - lag_index + total_rows]
        ).astype(jnp.float32)
        result = (
            result
            + same[:, None]
            * taps[lag_index][None, :]
            * extended[leading - lag_index : leading - lag_index + total_rows]
        )
    return result


def coefficients(recur_raw, input_raw, conv_values, bias_pair, decay_values, reset):
    recur_rate = jax.nn.sigmoid(recur_raw + bias_pair[0][None, :])
    input_rate = jax.nn.sigmoid(input_raw + bias_pair[1][None, :])
    log_decay = -8.0 * recur_rate * jax.nn.softplus(-decay_values)[None, :]
    multiplier = jnp.sqrt(jnp.maximum(-jnp.expm1(2.0 * log_decay), 0.01))
    return (jnp.exp(log_decay) * reset[:, None], multiplier * input_rate * conv_values)


def combine_state(earlier, later):
    return (earlier[0] * later[0], later[0] * earlier[1] + later[1])


MESH = pl.DeviceIdType.MESH
LO = 2
EIGHTEEN_US = pl.CostEstimate(flops=0, bytes_accessed=60_000_000, transcendentals=0)
TEN_US = pl.CostEstimate(flops=0, bytes_accessed=33_000_000, transcendentals=0)
ANY = pl.BlockSpec(memory_space=pl.ANY)
VMEM = pl.BlockSpec(memory_space=pltpu.VMEM)


def cube():
    seq = lax.axis_index("seq")
    tp = lax.axis_index("tp")
    a = lax.rem(seq, LO)
    b = tp // 2
    c = lax.rem(tp, 2)
    across_a = (seq - a + 1 - a, tp)
    across_b = (seq, (1 - b) * 2 + c)
    across_c = (seq, b * 2 + 1 - c)
    return (a, b, c, across_a, across_b, across_c)


def greet(devices):
    barrier = pltpu.get_barrier_semaphore()
    for device in devices:
        pl.semaphore_signal(barrier, inc=1, device_id=device, device_id_type=MESH)
    pl.semaphore_wait(barrier, len(devices))


def remote(src, dst, send_sem, recv_sem, slot, device):
    return pltpu.make_async_remote_copy(
        src_ref=src,
        dst_ref=dst,
        send_sem=send_sem.at[slot],
        recv_sem=recv_sem.at[slot],
        device_id=device,
        device_id_type=MESH,
    )


def gather_kernel(full, in_ref, out_ref, send_sem, recv_sem, local_sem):
    a, b, c, across_a, across_b, across_c = cube()
    half = in_ref.shape[0] // 2

    def index(pa, pb, pc):
        return pa * 4 + pb * 2 + pc if full else pb * 2 + pc

    me, an, bn, dn = (
        index(a, b, c),
        index(1 - a, b, c),
        index(a, 1 - b, c),
        index(1 - a, 1 - b, c),
    )
    greet([across_c, across_b] + ([across_a] if full else []))
    low, high = (pl.ds(0, half), pl.ds(half, half))

    def own(part, slot, device):
        return remote(in_ref.at[part], out_ref.at[me, part], send_sem, recv_sem, slot, device)

    def onward(block, part, slot, device):
        here = out_ref.at[block, part]
        return remote(here, here, send_sem, recv_sem, slot, device)

    sent = {}

    def go(slot, copy):
        copy.start()
        sent[slot] = copy

    if full:
        go(0, own(low, 0, across_a))
    go(1, own(high, 1, across_b))
    if full:
        go(2, own(high, 2, across_a))
    go(3, own(low, 3, across_b))
    go(4, remote(in_ref, out_ref.at[me], send_sem, recv_sem, 4, across_c))
    mine = pltpu.make_async_copy(in_ref, out_ref.at[me], local_sem)
    mine.start()
    if full:
        sent[0].wait_recv()
        go(5, onward(an, low, 5, across_b))
        go(6, onward(an, low, 6, across_c))
    sent[1].wait_recv()
    if full:
        go(7, onward(bn, high, 7, across_a))
    go(8, onward(bn, high, 8, across_c))
    if full:
        sent[2].wait_recv()
        go(9, onward(an, high, 9, across_c))
    sent[3].wait_recv()
    go(10, onward(bn, low, 10, across_c))
    if full:
        sent[5].wait_recv()
        go(11, onward(dn, low, 11, across_c))
        sent[7].wait_recv()
        go(12, onward(dn, high, 12, across_c))
    for slot in (4, 6, 8, 9, 10, 11, 12):
        if slot in sent:
            sent[slot].wait_recv()
    for copy in sent.values():
        copy.wait_send()
    mine.wait()


def gather(block, full, collective_id):
    count = 8 if full else 4
    rows, width = block.shape
    result = pl.pallas_call(
        functools.partial(gather_kernel, full),
        out_shape=jax.ShapeDtypeStruct((count, rows, width), block.dtype),
        in_specs=[ANY],
        out_specs=ANY,
        scratch_shapes=[
            pltpu.SemaphoreType.DMA((13,)),
            pltpu.SemaphoreType.DMA((13,)),
            pltpu.SemaphoreType.DMA,
        ],
        name="gather_full" if full else "gather_half",
        cost_estimate=EIGHTEEN_US,
        compiler_params=pltpu.CompilerParams(collective_id=collective_id, has_side_effects=True),
    )(block)
    return result.reshape(count * rows, width)


def scatter_kernel(
    full, part_ref, out_ref, cbuf, sx, sy, tx, ty, ax, by, rx, ry, csend, crecv, send_sem, recv_sem
):
    a, b, c, across_a, across_b, across_c = cube()
    half = part_ref.shape[1] // 2

    def index(pa, pb, pc):
        return pa * 4 + pb * 2 + pc if full else pb * 2 + pc

    def pair(pa, pb):
        return pa * 2 + pb if full else pb

    low, high = (pl.ds(0, half), pl.ds(half, half))
    if full:
        order = [
            (1 - a, 1 - b, low),
            (1 - a, 1 - b, high),
            (1 - a, b, low),
            (a, 1 - b, high),
            (a, 1 - b, low),
            (1 - a, b, high),
            (a, b, low),
            (a, b, high),
        ]
    else:
        order = [(a, 1 - b, low), (a, 1 - b, high), (a, b, low), (a, b, high)]
    greet([across_c, across_b] + ([across_a] if full else []))
    core = []
    for k, (pa, pb, part) in enumerate(order):
        copy = remote(
            part_ref.at[index(pa, pb, 1 - c), part],
            cbuf.at[pair(pa, pb), part],
            csend,
            crecv,
            k,
            across_c,
        )
        copy.start()
        core.append(copy)

    def summed(k):
        pa, pb, part = order[k]
        core[k].wait_recv()
        return part_ref[index(pa, pb, c), part].astype(jnp.float32) + cbuf[
            pair(pa, pb), part
        ].astype(jnp.float32)

    sent = []

    def go(src, dst, slot, device):
        copy = remote(src, dst, send_sem, recv_sem, slot, device)
        copy.start()
        sent.append(copy)
        return copy

    if full:
        sx[0] = lowered(summed(0))
        x0 = go(sx.at[0], ax.at[0], 0, across_a)
        sy[0] = lowered(summed(1))
        y0 = go(sy.at[0], by.at[0], 1, across_b)
        sx[1] = lowered(summed(2))
        x1 = go(sx.at[1], ax.at[1], 2, across_a)
        sy[1] = lowered(summed(3))
        y1 = go(sy.at[1], by.at[1], 3, across_b)
        total = summed(4)
        x0.wait_recv()
        ty[...] = lowered(total + ax[0].astype(jnp.float32))
        last_y = go(ty, ry, 4, across_b)
        total = summed(5)
        y0.wait_recv()
        tx[...] = lowered(total + by[0].astype(jnp.float32))
        last_x = go(tx, rx, 5, across_a)
        total = summed(6)
        x1.wait_recv()
        total = total + ax[1].astype(jnp.float32)
        last_y.wait_recv()
        out_ref[low] = total + ry[...].astype(jnp.float32)
        total = summed(7)
        y1.wait_recv()
        total = total + by[1].astype(jnp.float32)
        last_x.wait_recv()
        out_ref[high] = total + rx[...].astype(jnp.float32)
    else:
        sy[0] = lowered(summed(0))
        y0 = go(sy.at[0], by.at[0], 1, across_b)
        sy[1] = lowered(summed(1))
        y1 = go(sy.at[1], by.at[1], 3, across_b)
        total = summed(2)
        y0.wait_recv()
        out_ref[low] = total + by[0].astype(jnp.float32)
        total = summed(3)
        y1.wait_recv()
        out_ref[high] = total + by[1].astype(jnp.float32)
    for copy in core + sent:
        copy.wait_send()


def scatter(partial, full, collective_id):
    count = 8 if full else 4
    rows, width = (partial.shape[0] // count, partial.shape[1])
    half = rows // 2
    low = jnp.bfloat16
    return pl.pallas_call(
        functools.partial(scatter_kernel, full),
        out_shape=jax.ShapeDtypeStruct((rows, width), jnp.float32),
        in_specs=[VMEM],
        out_specs=VMEM,
        scratch_shapes=[
            pltpu.VMEM((count // 2, rows, width), low),
            pltpu.VMEM((2, half, width), low),
            pltpu.VMEM((2, half, width), low),
            pltpu.VMEM((half, width), low),
            pltpu.VMEM((half, width), low),
            pltpu.VMEM((2, half, width), low),
            pltpu.VMEM((2, half, width), low),
            pltpu.VMEM((half, width), low),
            pltpu.VMEM((half, width), low),
            pltpu.SemaphoreType.DMA((8,)),
            pltpu.SemaphoreType.DMA((8,)),
            pltpu.SemaphoreType.DMA((6,)),
            pltpu.SemaphoreType.DMA((6,)),
        ],
        name="scatter_full" if full else "scatter_half",
        cost_estimate=EIGHTEEN_US,
        compiler_params=pltpu.CompilerParams(
            collective_id=collective_id, has_side_effects=True, vmem_limit_bytes=40 * 2**20
        ),
    )(lowered(partial).reshape(count, rows, width))


def scan_kernel(
    high, reverse, decay_ref, drive_ref, end_ref, state_ref, carry_ref, cum, strips, sendbuf, recvbuf, send_sem, recv_sem
):
    rows, width = decay_ref.shape
    strands = 8
    steps = rows // strands
    lanes = 128
    blocks = width // lanes
    seq = lax.axis_index("seq")
    tp = lax.axis_index("tp")
    lo = lax.rem(seq, LO)
    mine = seq // LO
    peers = [(lax.rem(mine + k, high) * LO + lo, tp) for k in range(1, high)]
    greet(peers)
    for n in range(blocks):
        cum[n] = decay_ref[:, n * lanes : (n + 1) * lanes]
        strips[n] = drive_ref[:, n * lanes : (n + 1) * lanes]

    def step(i, carry):
        r = steps - 1 - i if reverse else i
        at = pl.ds(r, strands, stride=steps)
        new = []
        for n in range(blocks):
            a = cum[n, at, :]
            product_now = carry[2 * n] * a
            state_now = carry[2 * n + 1] * a + strips[n, at, :]
            cum[n, at, :] = product_now
            strips[n, at, :] = state_now
            new += [product_now, state_now]
        return tuple(new)

    ones = jnp.ones((strands, lanes), jnp.float32)
    ends = lax.fori_loop(0, steps, step, (ones, jnp.zeros_like(ones)) * blocks, unroll=8)
    strand_order = list(range(strands - 1, -1, -1)) if reverse else list(range(strands))
    before = {}
    for n in range(blocks):
        total_a = jnp.ones((1, lanes), jnp.float32)
        total_h = jnp.zeros((1, lanes), jnp.float32)
        for k in strand_order:
            before[n, k] = (total_a, total_h)
            a, h = (ends[2 * n][k : k + 1], ends[2 * n + 1][k : k + 1])
            total_h = a * total_h + h
            total_a = a * total_a
        scale = end_ref[0:1, n * lanes : (n + 1) * lanes]
        sendbuf[n, 0:1, :] = total_a * scale
        sendbuf[n, 1:2, :] = total_h * scale
        sendbuf[n, 2:8, :] = jnp.zeros((6, lanes), jnp.float32)
    copies = []
    for k, peer in enumerate(peers):
        copy = remote(sendbuf, recvbuf.at[k], send_sem, recv_sem, k, peer)
        copy.start()
        copies.append(copy)
    for copy in copies:
        copy.wait_recv()
    for n in range(blocks):
        carry = jnp.zeros((1, lanes), jnp.float32)
        for turn in range(high - 1):
            plane = high - 1 - turn if reverse else turn
            away = lax.rem(mine - plane + high, high)
            reached = plane > mine if reverse else plane < mine
            got = recvbuf[jnp.where(reached, away - 1, 0), n]
            carry = jnp.where(reached, got[0:1] * carry + got[1:2], carry)
        span = pl.ds(n * lanes, lanes)
        carry_ref[:, span] = jnp.broadcast_to(carry, (carry_ref.shape[0], lanes))
        for k in range(strands):
            enter = before[n, k][0] * carry + before[n, k][1]
            at = pl.ds(k * steps, steps)
            state_ref[at, span] = strips[n, at, :] + cum[n, at, :] * enter
    for copy in copies:
        copy.wait_send()


def plane_scan(decay, drive, end_scale, high, reverse, collective_id):
    rows, width = decay.shape
    return pl.pallas_call(
        functools.partial(scan_kernel, high, reverse),
        out_shape=(
            jax.ShapeDtypeStruct((rows, width), jnp.float32),
            jax.ShapeDtypeStruct((8, width), jnp.float32),
        ),
        in_specs=[VMEM] * 3,
        out_specs=(VMEM, VMEM),
        scratch_shapes=[
            pltpu.VMEM((width // 128, rows, 128), jnp.float32),
            pltpu.VMEM((width // 128, rows, 128), jnp.float32),
            pltpu.VMEM((width // 128, 8, 128), jnp.float32),
            pltpu.VMEM((high - 1, width // 128, 8, 128), jnp.float32),
            pltpu.SemaphoreType.DMA((high - 1,)),
            pltpu.SemaphoreType.DMA((high - 1,)),
        ],
        name="scan_back" if reverse else "scan",
        cost_estimate=TEN_US,
        compiler_params=pltpu.CompilerParams(
            collective_id=collective_id, has_side_effects=True, vmem_limit_bytes=32 * 2**20
        ),
    )(decay, drive, end_scale)


def small_kernel(high, gains_ref, rest_ref, gains_out, rest_out, gbuf, rbuf, ghold, rhold, gpair, rpair, send_sem, recv_sem):
    a, b, c, across_a, across_b, across_c = cube()
    seq = lax.axis_index("seq")
    tp = lax.axis_index("tp")
    mine = seq // LO
    peers = [(lax.rem(mine + k, high) * LO + a, tp) for k in range(1, high)]
    greet(peers + [across_a, across_b, across_c])
    copies = []
    for k, peer in enumerate(peers):
        for n, (src, dst) in enumerate(((gains_ref, gbuf.at[k]), (rest_ref, rbuf.at[k]))):
            copy = remote(src, dst, send_sem, recv_sem, 2 * k + n, peer)
            copy.start()
            copies.append(copy)
    for copy in copies:
        copy.wait_recv()
    gains = gains_ref[...]
    rest = rest_ref[...]
    for k in range(high - 1):
        gains = gains + gbuf[k]
        rest = rest + rbuf[k]
    rhold[...] = rest
    slot = 2 * (high - 1)
    swap = remote(rhold, rpair, send_sem, recv_sem, slot, across_a)
    swap.start()
    copies.append(swap)
    for n, device in enumerate((across_a, across_b, across_c)):
        ghold[n] = gains
        copy = remote(ghold.at[n], gpair.at[n], send_sem, recv_sem, slot + 1 + n, device)
        copy.start()
        copies.append(copy)
        copy.wait_recv()
        gains = gains + gpair[n]
    swap.wait_recv()
    gains_out[...] = gains
    other = rpair[...]
    width = rest.shape[1]
    rest_out[:, :width] = jnp.where(a == 0, rest, other)
    rest_out[:, width:] = jnp.where(a == 0, other, rest)
    for copy in copies:
        copy.wait_send()


def small_sums(gains, rest, high, collective_id):
    count = 2 * (high - 1) + 4
    return pl.pallas_call(
        functools.partial(small_kernel, high),
        out_shape=(
            jax.ShapeDtypeStruct(gains.shape, jnp.float32),
            jax.ShapeDtypeStruct((rest.shape[0], LO * rest.shape[1]), jnp.float32),
        ),
        in_specs=[VMEM] * 2,
        out_specs=(VMEM, VMEM),
        scratch_shapes=[
            pltpu.VMEM((high - 1, *gains.shape), jnp.float32),
            pltpu.VMEM((high - 1, *rest.shape), jnp.float32),
            pltpu.VMEM((3, *gains.shape), jnp.float32),
            pltpu.VMEM(rest.shape, jnp.float32),
            pltpu.VMEM((3, *gains.shape), jnp.float32),
            pltpu.VMEM(rest.shape, jnp.float32),
            pltpu.SemaphoreType.DMA((count,)),
            pltpu.SemaphoreType.DMA((count,)),
        ],
        name="small_sums",
        cost_estimate=TEN_US,
        compiler_params=pltpu.CompilerParams(collective_id=collective_id, has_side_effects=True),
    )(gains, rest)


def stacked_by_low(mine, other):
    lo = lax.rem(lax.axis_index("seq"), LO)
    return jnp.stack([jnp.where(lo == 0, mine, other), jnp.where(lo == 0, other, mine)])


def swap_low(block):
    count = lax.axis_size("seq")
    return lax.ppermute(block, "seq", [(s, s // LO * LO + (1 - s % LO)) for s in range(count)])


def high_groups():
    count = lax.axis_size("seq")
    return [[h * LO + l for h in range(count // LO)] for l in range(LO)]


def gather_weight(halves):
    lo = lax.rem(lax.axis_index("seq"), LO)
    kept = jnp.where(lo == 0, halves[0], halves[1])
    given = jnp.where(lo == 0, halves[1], halves[0])
    both = stacked_by_low(kept, swap_low(given))
    rows = both.shape[1]
    return lax.all_gather(
        both.reshape(LO * rows, both.shape[2]),
        "seq",
        axis=0,
        tiled=True,
        axis_index_groups=high_groups(),
    )


def reduce_weight(grad):
    lo = lax.rem(lax.axis_index("seq"), LO)
    both = lax.psum_scatter(
        lowered(grad), "seq", scatter_dimension=0, tiled=True, axis_index_groups=high_groups()
    )
    rows = both.shape[0] // LO
    both = both.reshape(LO, rows, both.shape[1])
    kept = jnp.where(lo == 0, both[0], both[1])
    given = jnp.where(lo == 0, both[1], both[0])
    return stacked_by_low(kept, swap_low(given))


def split_columns(block):
    width = block.shape[1] // LO
    return [block[:, l * width : (l + 1) * width] for l in range(LO)]


def joined(blocks):
    return jnp.concatenate([blocks[l] for l in range(LO)], axis=1).astype(jnp.float32)


def dense_forward(stream, gain, weights, cid):
    gate_up, down = weights
    width = down.shape[1]
    normed = gather(lowered(rms_norm(stream, gain)), True, cid["gather_full"])
    both = product(normed, gate_up)
    hidden = lowered(gated(both[:, :width], both[:, width:]))
    out = scatter(product_right(hidden, down), True, cid["scatter_full"])
    return (out, (normed, both, hidden))


def dense_backward(stream, gain, grad_out, kept, weights, cid):
    gate_up, down = weights
    width = down.shape[1]
    normed, both, hidden = kept
    grad_low = gather(lowered(grad_out), True, cid["gather_full"])
    grad_down = product_left(grad_low, hidden)
    grad_hidden = product(grad_low, down)
    gate_grad, up_grad = jax.vjp(gated, both[:, :width], both[:, width:])[1](grad_hidden)
    both_low = jnp.concatenate([lowered(gate_grad), lowered(up_grad)], axis=1)
    grad_both = product_left(normed, both_low)
    partial = product_right(both_low, gate_up)
    partial, grad_both, grad_down = lax.optimization_barrier(
        (lowered(partial), lowered(grad_both), lowered(grad_down))
    )
    grad_normed = scatter(partial, True, cid["scatter_full"])
    stream_grad, gain_grad = jax.vjp(rms_norm, stream, gain)[1](grad_normed)
    return (grad_out + stream_grad, gain_grad, grad_both, grad_down)


def block_product(values, weight):
    block_width = weight.shape[0]
    blocks = weight.shape[1] // block_width
    return jnp.concatenate(
        [
            product_right(
                values[:, n * block_width : (n + 1) * block_width],
                weight[:, n * block_width : (n + 1) * block_width],
            )
            for n in range(blocks)
        ],
        axis=1,
    )


def block_grads(values, weight, upstream):
    block_width = weight.shape[0]
    cuts = [slice(n * block_width, (n + 1) * block_width) for n in range(weight.shape[1] // block_width)]
    return (
        jnp.concatenate([product_left(upstream[:, s], values[:, s]) for s in cuts], axis=1),
        jnp.concatenate([product(upstream[:, s], weight[:, s]) for s in cuts], axis=1),
    )


def shifted(block, distance):
    count = lax.axis_size("seq")
    route = [(i - distance, i) for i in range(count) if 0 <= i - distance < count]
    return lax.ppermute(block, "seq", route)


def score_block(query_rot, keys_ext, allowed, score_scale):
    raw = jnp.einsum("qhd,kd->hqk", query_rot, keys_ext, preferred_element_type=jnp.float32)
    return jnp.where(allowed[None], raw * score_scale, -1e30)


CIDS = {
    "gather_full": 0,
    "gather_half": 1,
    "scatter_full": 2,
    "scatter_half": 3,
    "scan": 4,
    "scan_back": 5,
    "scatter_wide": 6,
    "small_sums": 7,
    "gather_narrow": 8,
}


def dense_weights(gate_part, up_part, down_part, *more):
    pieces = [split_columns(part) for part in (gate_part, up_part, *more)]
    wide = gather_weight([jnp.concatenate(each, axis=1) for each in zip(*pieces)])
    down = gather_weight(split_columns(down_part.T))
    width = 2 * down.shape[1]
    return (wide[:, :width], down) + ((wide[:, width:],) if more else ())


def dense_grads(grad_both, grad_down):
    width = grad_down.shape[1]
    both = reduce_weight(jnp.concatenate([grad_both, grad_down], axis=1))
    return (
        joined(both[:, :, :width]),
        joined(both[:, :, width : 2 * width]),
        joined(both[:, :, 2 * width :]).T,
    )


def gather_whole(part):
    count = lax.axis_size("seq")
    lanes = lax.all_gather(part, "seq", axis_index_groups=high_groups())
    other = swap_low(lanes)
    lo = lax.rem(lax.axis_index("seq"), LO)
    both = jnp.stack([jnp.where(lo == 0, lanes, other), jnp.where(lo == 0, other, lanes)], axis=1)
    return both.reshape(count * part.shape[0], part.shape[1])


def reduce_whole(blocks):
    count, rows, width = blocks.shape
    lo = lax.rem(lax.axis_index("seq"), LO)
    pairs = blocks.reshape(count // LO, LO, rows, width)
    kept = jnp.where(lo == 0, pairs[:, 0], pairs[:, 1])
    given = jnp.where(lo == 0, pairs[:, 1], pairs[:, 0])
    total = lowered(kept.astype(jnp.float32) + swap_low(given).astype(jnp.float32))
    return lax.psum_scatter(
        total.reshape(-1, width),
        "seq",
        scatter_dimension=0,
        tiled=True,
        axis_index_groups=high_groups(),
    )


def local(
    tokens,
    cotangent,
    doc_lengths,
    norm_gains,
    input_branch,
    gate_branch,
    conv_taps,
    conv_bias,
    recur_gate,
    input_gate,
    gate_biases,
    decay_param,
    recur_output,
    dense_gate_one,
    dense_up_one,
    dense_down_one,
    query_weight,
    keyvalue_weight,
    attention_out,
    dense_gate_two,
    dense_up_two,
    dense_down_two,
):
    cid = CIDS
    shard_rows = tokens.shape[0]
    seq = lax.axis_index("seq")
    tp = lax.axis_index("tp")
    lo = lax.rem(seq, LO)
    high = lax.axis_size("seq") // LO
    ways = lax.axis_size("tp")
    own_rows = shard_rows // ways
    plane_rows = shard_rows * LO
    channels = conv_bias.shape[0] // LO
    leading = CONV - 1
    halo_shards = WINDOW // shard_rows
    first_slot = seq * shard_rows
    plane_slot = (seq // LO) * plane_rows
    own_slot = first_slot + tp * own_rows
    valid = layout(doc_lengths, own_slot, own_rows)[3]
    segment, position, _, _ = layout(doc_lengths, first_slot, shard_rows)
    plane_reset = layout(doc_lengths, plane_slot, plane_rows)[2]
    conv_segment = layout(doc_lengths, plane_slot - leading, plane_rows + leading)[0]
    key_segment = layout(
        doc_lengths, first_slot - halo_shards * shard_rows, (halo_shards + 1) * shard_rows
    )[0]

    def ours(block, axis):
        return lax.dynamic_slice_in_dim(block, lo * channels, channels, axis)

    taps, bias = (ours(conv_taps, 1), ours(conv_bias, 0))
    bias_pair, decay_values = (ours(gate_biases, 1), ours(decay_param, 0))

    gate_rows = recur_gate.shape[1]
    weight_rows = input_branch.shape[0]
    ins = zip(split_columns(input_branch), split_columns(gate_branch))
    gates = zip(split_columns(recur_gate.T), split_columns(input_gate.T))
    first = gather_weight(
        [
            jnp.concatenate(
                [jnp.concatenate(pair, axis=1), jnp.concatenate(gate, axis=1)], axis=0
            )
            for pair, gate in zip(ins, gates)
        ]
    ).reshape(high * LO, weight_rows + gate_rows, 2 * channels)
    in_full = first[:, :weight_rows].reshape(-1, 2 * channels)
    recur_full = first[:, weight_rows:, :channels].reshape(-1, channels)
    input_gate_full = first[:, weight_rows:, channels:].reshape(-1, channels)
    *weights_one, output_full = dense_weights(
        dense_gate_one, dense_up_one, dense_down_one, recur_output.T
    )

    stream_in = lax.dynamic_slice_in_dim(tokens, tp * own_rows, own_rows, 0).astype(jnp.float32)
    normed_one = gather(lowered(rms_norm(stream_in, norm_gains[0])), True, cid["gather_full"])
    normed_one, query_weight, keyvalue_weight, attention_out = lax.optimization_barrier(
        (normed_one, query_weight, keyvalue_weight, attention_out)
    )
    both = product(normed_one, in_full)
    both, dense_gate_two, dense_up_two, dense_down_two = lax.optimization_barrier(
        (both, dense_gate_two, dense_up_two, dense_down_two)
    )

    keyvalue_part = keyvalue_weight[None]
    for step in (1, 2):
        other = lax.ppermute(keyvalue_part, "tp", [(i, i ^ step) for i in range(ways)])
        low_bit = lax.rem(tp // step, 2)
        keyvalue_part = jnp.concatenate(
            [
                jnp.where(low_bit == 0, keyvalue_part, other),
                jnp.where(low_bit == 0, other, keyvalue_part),
            ],
            axis=0,
        )
    keyvalue_part = keyvalue_part.reshape(weight_rows, keyvalue_weight.shape[1])
    third = gather_whole(
        jnp.concatenate([query_weight, attention_out.T, keyvalue_part], axis=1)
    )
    query_width = query_weight.shape[1]
    attn_width = attention_out.shape[0]
    query_full = third[:, :query_width]
    attn_full = third[:, query_width : query_width + attn_width]
    keyvalue_full = third[:, query_width + attn_width :]
    weights_two = dense_weights(dense_gate_two, dense_up_two, dense_down_two)

    branch = both[:, :channels]
    gating = both[:, channels:]
    rim = shifted(branch[plane_rows - leading :], LO)
    branch_ext = jnp.concatenate([rim, branch], axis=0)
    conv_local = functools.partial(convolve, segment=conv_segment)
    conv_out, conv_pull = jax.vjp(conv_local, branch_ext, taps, bias)
    conv_low = lowered(conv_out)
    recur_raw = block_product(conv_low, recur_full)
    input_raw = block_product(conv_low, input_gate_full)
    rate_local = functools.partial(coefficients, reset=plane_reset)
    (decay, drive), rate_pull = jax.vjp(
        rate_local, recur_raw, input_raw, conv_out, bias_pair, decay_values
    )
    ones = jnp.ones((8, channels), jnp.float32)
    state, state_in = plane_scan(decay, drive, ones, high, False, cid["scan"])
    gate_act, gate_pull = jax.vjp(jax.nn.gelu, gating)
    mixed = lowered(state * gate_act)
    stream_one = stream_in + scatter(product_right(mixed, output_full), True, cid["scatter_full"])

    dense_out, kept_one = dense_forward(stream_one, norm_gains[1], weights_one, cid)
    stream_two = stream_one + dense_out

    normed_own = lowered(rms_norm(stream_two, norm_gains[2]))
    normed_three = gather(normed_own, False, cid["gather_half"])
    query = product(normed_three, query_full)
    keyval = product(normed_three, keyvalue_full)
    local_heads = query.shape[1] // HD
    query_heads = query.reshape(shard_rows, local_heads, HD)
    rotate_here = functools.partial(rotate, position=position)
    query_rot = lowered(rotate_here(query_heads))
    key_rot = lowered(rotate_here(keyval[:, :HD]))
    packed = jnp.concatenate([key_rot, lowered(keyval[:, HD:])], axis=1)
    earlier = [shifted(packed, offset) for offset in range(halo_shards, 0, -1)]
    extended = jnp.concatenate(earlier + [packed], axis=0)
    keys_ext = extended[:, :HD]
    values_ext = extended[:, HD:]
    query_slots = first_slot + jnp.arange(shard_rows, dtype=jnp.int32)
    key_slots = (
        first_slot
        - halo_shards * shard_rows
        + jnp.arange((halo_shards + 1) * shard_rows, dtype=jnp.int32)
    )
    distance = query_slots[:, None] - key_slots[None, :]
    allowed = (segment[:, None] == key_segment[None, :]) & (distance >= 0) & (distance < WINDOW)
    score_scale = HD ** (-0.5)
    scores = score_block(query_rot, keys_ext, allowed, score_scale)
    row_top = jnp.max(scores, axis=-1, keepdims=True)
    row_total = jnp.sum(jnp.exp(scores - row_top), axis=-1, keepdims=True)
    log_total = row_top + jnp.log(row_total)
    probs_low = lowered(jnp.exp(scores - row_top) / row_total)
    attended = lowered(
        jnp.einsum("hqk,kd->qhd", probs_low, values_ext, preferred_element_type=jnp.float32)
    ).reshape(shard_rows, local_heads * HD)
    stream_three = stream_two + scatter(
        product_right(attended, attn_full), False, cid["scatter_half"]
    )

    dense_out, kept_two = dense_forward(stream_three, norm_gains[3], weights_two, cid)
    stream_four = stream_three + dense_out
    out_own = lowered(stream_four * valid[:, None])
    layer_out = gather(out_own, False, cid["gather_half"])

    grad_stream = (
        lax.dynamic_slice_in_dim(cotangent, tp * own_rows, own_rows, 0).astype(jnp.float32)
        * valid[:, None]
    )
    grad_stream, gain_four, grad_both_two, grad_down_two = dense_backward(
        stream_three, norm_gains[3], grad_stream, kept_two, weights_two, cid
    )

    done_two = dense_grads(grad_both_two, grad_down_two)
    grad_attn_low = gather(lowered(grad_stream), False, cid["gather_half"])
    grad_attn_out = product_left(grad_attn_low, attended)
    grad_attended = lowered(product(grad_attn_low, attn_full)).reshape(
        shard_rows, local_heads, HD
    )
    scores = score_block(query_rot, keys_ext, allowed, score_scale)
    probs = jnp.exp(scores - log_total)
    grad_probs = jnp.einsum(
        "qhd,kd->hqk", grad_attended, values_ext, preferred_element_type=jnp.float32
    )
    grad_scores = lowered(
        probs * (grad_probs - jnp.sum(probs * grad_probs, axis=-1, keepdims=True)) * score_scale
    )
    grad_query_rot = jnp.einsum(
        "hqk,kd->qhd", grad_scores, keys_ext, preferred_element_type=jnp.float32
    )
    grad_keys = jnp.einsum(
        "hqk,qhd->kd", grad_scores, query_rot, preferred_element_type=jnp.float32
    )
    grad_values = jnp.einsum(
        "hqk,qhd->kd", lowered(probs), grad_attended, preferred_element_type=jnp.float32
    )
    grad_ext = jnp.concatenate([grad_keys, grad_values], axis=1)
    grad_own = grad_ext[halo_shards * shard_rows :]
    for offset in range(1, halo_shards + 1):
        grad_piece = grad_ext[
            (halo_shards - offset) * shard_rows : (halo_shards - offset + 1) * shard_rows
        ]
        grad_own = grad_own + shifted(lowered(grad_piece), -offset).astype(jnp.float32)
    key_pre_grad = jax.vjp(rotate_here, keyval[:, :HD])[1](grad_own[:, :HD])[0]
    query_pre_grad = jax.vjp(rotate_here, query_heads)[1](grad_query_rot)[0]
    grad_query_low = lowered(query_pre_grad).reshape(shard_rows, local_heads * HD)
    keyvalue_partial = jnp.concatenate([key_pre_grad, grad_own[:, HD:]], axis=1)
    grad_query = product_left(normed_three, grad_query_low)
    partial = lowered(
        jnp.concatenate([product_right(grad_query_low, query_full), keyvalue_partial], axis=1)
    )
    partial, grad_query, grad_attn_out = lax.optimization_barrier(
        (partial, lowered(grad_query), lowered(grad_attn_out))
    )
    summed = scatter(partial, False, cid["scatter_wide"])
    width = normed_own.shape[1]
    keyvalue_low = lowered(summed[:, width:])
    grad_normed = summed[:, :width] + product_right(keyvalue_low, keyvalue_full)
    keyvalue_grads = gather(keyvalue_low, False, cid["gather_narrow"])
    part_rows = keyvalue_weight.shape[0]
    ways_view = normed_three.reshape(shard_rows, high * LO, ways, part_rows)
    ours_only = lax.dynamic_slice_in_dim(ways_view, tp, 1, 2).reshape(shard_rows, -1)
    grad_keyvalue = lowered(product_left(ours_only, keyvalue_grads))
    attn_wire = jnp.concatenate([grad_query, grad_attn_out], axis=1)
    attn_wire = attn_wire.reshape(high * LO, weight_rows, attn_wire.shape[1])
    keyvalue_wire = grad_keyvalue.reshape(high * LO, -1, attn_wire.shape[2])
    done_attn = reduce_whole(jnp.concatenate([attn_wire, keyvalue_wire], axis=1))
    stream_grad, gain_three = jax.vjp(rms_norm, stream_two, norm_gains[2])[1](grad_normed)
    grad_stream = grad_stream + stream_grad

    grad_stream, gain_two, grad_both_one, grad_down_one = dense_backward(
        stream_one, norm_gains[1], grad_stream, kept_one, weights_one, cid
    )

    done_one = dense_grads(grad_both_one, grad_down_one)
    grad_stream, done_two = lax.optimization_barrier((grad_stream, done_two))
    grad_out_low = gather(lowered(grad_stream), True, cid["gather_full"])
    grad_recur_out = product_left(grad_out_low, mixed)
    grad_mixed = product(grad_out_low, output_full)
    grad_mixed, done_attn = lax.optimization_barrier((grad_mixed, done_attn))
    grad_state = grad_mixed * gate_act
    grad_gating = lowered(gate_pull(grad_mixed * state)[0])
    decay_next = jnp.concatenate([decay[1:], jnp.ones((1, channels), jnp.float32)], axis=0)
    first_decay = jnp.broadcast_to(decay[:1], (8, channels))
    grad_drive, _ = plane_scan(decay_next, grad_state, first_decay, high, True, cid["scan_back"])
    state_prev = jnp.concatenate([state_in[:1], state[:-1]], axis=0)
    grad_decay = grad_drive * state_prev
    grad_recur_raw, grad_input_raw, grad_conv, grad_biases, grad_decay_param = rate_pull(
        (grad_decay, grad_drive)
    )
    grad_recur_gate, conv_back_recur = block_grads(conv_low, recur_full, lowered(grad_recur_raw))
    grad_input_gate, conv_back_input = block_grads(
        conv_low, input_gate_full, lowered(grad_input_raw)
    )
    grad_branch_ext, grad_taps, grad_conv_bias = conv_pull(
        grad_conv + conv_back_recur + conv_back_input
    )
    returned_rim = shifted(grad_branch_ext[:leading], -LO)
    grad_branch = grad_branch_ext[leading:] + jnp.pad(
        returned_rim, ((plane_rows - leading, 0), (0, 0))
    )
    both_low = jnp.concatenate([lowered(grad_branch), grad_gating], axis=1)
    grad_in = product_left(normed_one, both_low)
    partial = lowered(product_right(both_low, in_full))
    partial, grad_in, grad_recur_out = lax.optimization_barrier(
        (partial, lowered(grad_in), lowered(grad_recur_out))
    )
    grad_normed = scatter(partial, True, cid["scatter_full"])
    stream_grad, gain_one = jax.vjp(rms_norm, stream_in, norm_gains[0])[1](grad_normed)
    input_own = grad_stream + stream_grad
    input_grad = gather(lowered(input_own), False, cid["gather_half"]).astype(jnp.float32)

    in_grad = reduce_weight(grad_in)
    rest_grad = jnp.concatenate(
        [
            grad_recur_out.reshape(high * LO, weight_rows, channels),
            lowered(grad_recur_gate).reshape(high * LO, gate_rows, channels),
            lowered(grad_input_gate).reshape(high * LO, gate_rows, channels),
        ],
        axis=1,
    )
    rest_grad = joined(reduce_weight(rest_grad.reshape(-1, channels))).T
    gains_sum, small = small_sums(
        jnp.concatenate(
            [jnp.stack([gain_one, gain_two, gain_three, gain_four]), jnp.zeros_like(norm_gains)]
        ),
        jnp.concatenate(
            [grad_taps, grad_conv_bias[None], grad_biases, grad_decay_param[None]], axis=0
        ),
        high,
        cid["small_sums"],
    )
    gains_sum = gains_sum[: norm_gains.shape[0]]
    return (
        layer_out,
        input_grad,
        gains_sum,
        joined(in_grad[:, :, :channels]),
        joined(in_grad[:, :, channels:]),
        small[:CONV],
        small[CONV],
        rest_grad[:, weight_rows : weight_rows + gate_rows],
        rest_grad[:, weight_rows + gate_rows :],
        small[CONV + 1 : CONV + 3],
        small[CONV + 3],
        rest_grad[:, :weight_rows],
        *done_one,
        done_attn[:weight_rows, :query_width].astype(jnp.float32),
        done_attn[weight_rows:].reshape(keyvalue_weight.shape).astype(jnp.float32),
        done_attn[:weight_rows, query_width:].astype(jnp.float32).T,
        *done_two,
    )


def solution(mesh):
    placed = (
        P("seq", None),
        P("seq", None),
        P(),
        P(),
        P("seq", "tp"),
        P("seq", "tp"),
        P(None, "tp"),
        P("tp"),
        P("tp", "seq"),
        P("tp", "seq"),
        P(None, "tp"),
        P("tp"),
        P("tp", "seq"),
        P("seq", "tp"),
        P("seq", "tp"),
        P("tp", "seq"),
        P("seq", "tp"),
        P(("seq", "tp"), None),
        P("tp", "seq"),
        P("seq", "tp"),
        P("seq", "tp"),
        P("tp", "seq"),
    )
    return jax.shard_map(
        local,
        mesh=mesh,
        in_specs=placed,
        out_specs=(
            P("seq", None),
            P("seq", None),
            P(),
            P("seq", "tp"),
            P("seq", "tp"),
            P(None, "tp"),
            P("tp"),
            P("tp", "seq"),
            P("tp", "seq"),
            P(None, "tp"),
            P("tp"),
            P("tp", "seq"),
            P("seq", "tp"),
            P("seq", "tp"),
            P("tp", "seq"),
            P("seq", "tp"),
            P(("seq", "tp"), None),
            P("tp", "seq"),
            P("seq", "tp"),
            P("seq", "tp"),
            P("tp", "seq"),
        ),
        check_vma=False,
    )
```

time: 3010 us -> 844 us (0.28)
  waiting for transfers between devices: 2040 us -> 119 us
  Pallas kernels: 0 us -> 386 us
  local copies, waits for them, and re-layouts: 300 us -> 41.7 us
  blocking collectives: 246 us -> 0 us
  other arithmetic: 152 us -> 88.2 us
  matrix products: 214 us -> 152 us
    reduce_scatter x14 -> x5, waiting for transfers between devices: 1260 us -> 20.6 us  [the longest x4 20.6 us: reduce_weight(): lax.psum_scatter(lowered(grad), 'seq', scatter_dimension=0, tiled=True, a...]
    all_gather x11 -> x6, waiting for transfers between devices: 429 us -> 24.9 us  [the longest x5 24.9 us: gather_weight(): lax.all_gather(both.reshape(LO * rows, both.shape[2]), 'seq', axis=0, til...]
    pallas_call x0 -> x22, Pallas kernels: none -> 386 us  [the longest x11 188 us: gather(): pl.pallas_call(functools.partial(gather_kernel, full), out_shape=jax.Shap...]
    psum x7 -> x0, waiting for transfers between devices: 327 us -> none  [head_sum(): return lax.psum(values, 'tp')]
    all_gather x6 -> x0, blocking collectives: 187 us -> none  [the longest x3 78.4 us: prefix(): everything = jax.tree.map(lambda part: lax.all_gather(part, axis), x)]
    slice x128 -> x20, local copies, waits for them, and re-layouts: 144 us -> 14.4 us  [the longest x6 2.47 us: split_columns(): return [block[:, l * width:(l + 1) * width] for l in range(LO)]]
    pad x64 -> x0, local copies, waits for them, and re-layouts: 85.2 us -> none  [the longest x32 72.4 us: local(): lax.associative_scan(combine_state, (decay_next, grad_state), axis=0, rev...]
    psum x2 -> x0, blocking collectives: 59.8 us -> none  [the longest x1 38.2 us: local(): lax.psum((jnp.stack([gain_one, gain_two, gain_three, gain_four]), grad_ta...]
  transfers between devices with their start and end apart: 38 -> 30, of which waited for: 32 -> 14; matrix products, arithmetic and copies ran while one was open for 18% -> 29% of each run, Pallas kernels for 0% -> 46%
where the time goes in v1:
time: 844 us; the launch traced here: 835 us
  Pallas kernels  386 us (46%)
  matrix products  152 us (18%)
  waiting for transfers between devices  119 us (14%)
  other arithmetic  88.2 us (10%)
  local copies, waits for them, and re-layouts  41.7 us (5%)
  starting transfers between devices  29.9 us (4%)
  between operations  17.1 us (2%)
    pallas_call x11, Pallas kernels, gather(): pl.pallas_call(functools.partial(gather_kernel, full), out_shape=jax.Shap...  188 us
    pallas_call x8, Pallas kernels, scatter(): pl.pallas_call(functools.partial(scatter_kernel, full), out_shape=jax.Sha...  158 us
    ppermute x11, waiting for transfers between devices, swap_low(): lax.ppermute(block, 'seq', [(s, s // LO * LO + (1 - s % LO)) for s in ran...  56.6 us
    dot_general x13, matrix products, product(): return jnp.dot(left, right, preferred_element_type=jnp.float32)  44.2 us
    dot_general x13, matrix products, product_right(): lax.dot_general(left, right, (((1,), (1,)), ((), ())), preferred_element_...  35 us
    dot_general x13, matrix products, product_left(): lax.dot_general(left, right, (((0,), (0,)), ((), ())), preferred_element_...  30.3 us
    all_gather x5, waiting for transfers between devices, gather_weight(): lax.all_gather(both.reshape(LO * rows, both.shape[2]), 'seq', axis=0, til...  24.9 us
    pallas_call x2, Pallas kernels, plane_scan(): pl.pallas_call(functools.partial(scan_kernel, high, reverse), out_shape=(...  22.1 us
  transfers between devices with their start and end apart: 30, of which 14 were waited for; matrix products, arithmetic and copies ran while one was open for 29% of the time, Pallas kernels for 46%

profile of v1, /device:TPU:0, one launch (start us, length us, event | category | flops | bytes accessed | tf_op | source)
XLA Modules:
  0.0 834.7 jit_solution(742010474446704296)
XLA Ops:
  9.2 3.0 collective-permute-start
  12.3 5.3 collective-permute-done
  20.8 18.0 %gather_full.6 = bf16[8,128,1536]{2,1,0:T(8,128)(2,1)} custom-call(bf16[128,1536]{1,0:T(8,128)(2,1)} %fusion.76.in_ref), custom_call_target="tpu_custom_call" | custom-call | bytes 60000000 | tf_op jit(solution)/shard_map/gather_full/pallas_call | solution.py:206
  41.5 2.9 collective-permute-done.5
  48.1 12.3 %collective-permute-done.2 = bf16[192,1408]{1,0:T(8,128)(2,1)S(1)} collective-permute-done((bf16[192,1408]{1,0:T(8,128)(2,1)S(1)}, bf16[192,1408]{1,0:T(8,128)(2,1)S(1)}, u32[]{:S(2)}, u32[]{:S(2)}) %collective-permute-start.2) | collective-permute-done | bytes 540704 | tf_op jit(solution)/shard_map/ppermute | solution.py:526
  64.5 4.1 collective-permute-done.3
  71.3 4.2 fusion.197
  79.6 6.6 collective-permute-done.9
  87.8 17.5 %gather_full.9 = bf16[8,128,1536]{2,1,0:T(8,128)(2,1)} custom-call(bf16[128,1536]{1,0:T(8,128)(2,1)} %fusion.85.in_ref), custom_call_target="tpu_custom_call" | custom-call | bytes 60000000 | tf_op jit(solution)/shard_map/gather_full/pallas_call | solution.py:206
  108.8 3.3 collective-permute-start.1
  117.9 11.2 %scan.1 = (f32[1024,256]{1,0:T(8,128)S(1)}, f32[8,256]{1,0:T(8,128)S(1)}) custom-call(f32[1024,256]{1,0:T(8,128)S(1)} %get-tuple-element.144.decay_ref, f32[1024,256]{1,0:T(8,128)S(1)} %get-tuple-element.143.drive_ref, f32[8,256]{1,0:T(8,128)S(1)} %broadcast_in_dim.76.end_ref), custom_call_target="tpu_custom_call" | custom-call | bytes 33000000 | tf_op jit(solution)/shard_map/scan/pallas_call | solution.py:427
  129.5 20.7 %collective-permute-done.10 = bf16[192,576]{1,0:T(8,128)(2,1)S(1)} collective-permute-done((bf16[192,576]{1,0:T(8,128)(2,1)S(1)}, bf16[192,576]{1,0:T(8,128)(2,1)S(1)}, u32[]{:S(2)}, u32[]{:S(2)}) %collective-permute-start.10) | collective-permute-done | bytes 221216 | tf_op jit(solution)/shard_map/ppermute | solution.py:526
  156.7 24.8 %all-gather.10.cloned.1.call-done = bf16[1536,1408]{1,0:T(8,128)(2,1)} async-done(((bf16[384,1408]{1,0:T(8,128)(2,1)}), bf16[1536,1408]{1,0:T(8,128)(2,1)}) %all-gather.10.cloned.1.call-update) | async-done | bytes 4325392 | tf_op jit(solution)/shard_map/all_gather | solution.py:540
  183.7 18.2 %scatter_full.6 = f32[128,1536]{1,0:T(8,128)S(1)} custom-call(bf16[8,128,1536]{2,1,0:T(8,128)(2,1)S(1)} %bitcast.270), custom_call_target="tpu_custom_call" | custom-call | bytes 60000000 | tf_op jit(solution)/shard_map/scatter_full/pallas_call | solution.py:325
  204.0 18.0 %gather_full.7 = bf16[8,128,1536]{2,1,0:T(8,128)(2,1)} custom-call(bf16[128,1536]{1,0:T(8,128)(2,1)} %multiply_convert_fusion.8.in_ref), custom_call_target="tpu_custom_call" | custom-call | bytes 60000000 | tf_op jit(solution)/shard_map/gather_full/pallas_call | solution.py:206
  222.0 7.2 fusion.16
  232.6 5.1 convolution_convert_fusion.3
  237.7 17.8 %scatter_full.7 = f32[128,1536]{1,0:T(8,128)S(1)} custom-call(bf16[8,128,1536]{2,1,0:T(8,128)(2,1)S(1)} %bitcast.277), custom_call_target="tpu_custom_call" | custom-call | bytes 60000000 | tf_op jit(solution)/shard_map/scatter_full/pallas_call | solution.py:325
  256.7 13.9 %gather_half.5 = bf16[4,128,1536]{2,1,0:T(8,128)(2,1)} custom-call(bf16[128,1536]{1,0:T(8,128)(2,1)} %multiply_convert_fusion.7.in_ref), custom_call_target="tpu_custom_call" | custom-call | bytes 60000000 | tf_op jit(solution)/shard_map/gather_half/pallas_call | solution.py:206
  275.0 3.7 collective-permute-start.8
  279.7 7.2 collective-permute-done.7
  297.1 13.0 %scatter_half.2 = f32[128,1536]{1,0:T(8,128)S(1)} custom-call(bf16[4,128,1536]{2,1,0:T(8,128)(2,1)S(1)} %bitcast.278), custom_call_target="tpu_custom_call" | custom-call | bytes 60000000 | tf_op jit(solution)/shard_map/scatter_half/pallas_call | solution.py:325
  312.1 29.0 %gather_full.8 = bf16[8,128,1536]{2,1,0:T(8,128)(2,1)} custom-call(bf16[128,1536]{1,0:T(8,128)(2,1)} %multiply_convert_fusion.6.in_ref), custom_call_target="tpu_custom_call" | custom-call | bytes 60000000 | tf_op jit(solution)/shard_map/gather_full/pallas_call | solution.py:206
  341.7 9.4 %fusion.199 = f32[1024,1152]{1,0:T(8,128)} fusion(bf16[1024,1536]{1,0:T(8,128)(2,1)} %bitcast.303, bf16[1536,1152]{1,0:T(8,128)(2,1)} %all-gather.14.cloned.1.call-done), kind=kOutput, calls=%fused_computation.449 | convolution fusion | flops 3623878656 | bytes 11403264 | tf_op jit(solution)/shard_map/dot_general | solution.py:16
  351.2 6.5 fusion.31
  360.4 4.8 convolution_convert_fusion.1
  365.3 4.7 convolution_convert_fusion.7
  370.0 2.9 pad_maximum_fusion
  373.1 4.6 convolution_convert_fusion.2
  377.7 17.8 %scatter_full.8 = f32[128,1536]{1,0:T(8,128)S(1)} custom-call(bf16[8,128,1536]{2,1,0:T(8,128)(2,1)S(1)} %bitcast.276), custom_call_target="tpu_custom_call" | custom-call | bytes 60000000 | tf_op jit(solution)/shard_map/scatter_full/pallas_call | solution.py:325
  395.6 17.5 %scatter_full.9 = f32[128,1536]{1,0:T(8,128)S(1)} custom-call(bf16[8,128,1536]{2,1,0:T(8,128)(2,1)S(1)} %bitcast.275), custom_call_target="tpu_custom_call" | custom-call | bytes 60000000 | tf_op jit(solution)/shard_map/scatter_full/pallas_call | solution.py:325
  416.3 14.2 %gather_half.7 = bf16[4,128,1536]{2,1,0:T(8,128)(2,1)} custom-call(bf16[128,1536]{1,0:T(8,128)(2,1)} %get-tuple-element.110.in_ref), custom_call_target="tpu_custom_call" | custom-call | bytes 60000000 | tf_op jit(solution)/shard_map/gather_half/pallas_call | solution.py:206
  433.2 4.9 fusion.96
  438.2 14.2 %fusion.33 = f32[1536,128]{0,1:T(8,128)S(1)} fusion(f32[1536,512,3]{1,0,2:T(8,128)} %fusion.96, f32[3,512,1536]{1,2,0:T(8,128)} %copy-done.5, f32[3,512]{1,0:T(4,128)S(1)} %copy-done.86, bf16[512,3,64]{0,2,1:T(8,128)(2,1)S(1)} %copy-done.78, bf16[512,3,64]{0,2,1:T(8,128)(2,1)S(1)} %copy-done.76), kind=kOutput, calls=%fused_computation.72 | convolution fusion | flops 621284352 | bytes 20060160 | tf_op jit(solution)/shard_map/hqk,qhd->kd/dot_general | solution.py:881
  452.4 5.5 fusion.34
  461.9 14.2 %fusion.38 = f32[512,3,128]{0,2,1:T(8,128)S(1)} fusion(f32[1536,512,3]{1,0,2:T(8,128)} %fusion.96, f32[3,512,1536]{1,2,0:T(8,128)} %copy-done.5, f32[3,512]{1,0:T(4,128)S(1)} %copy-done.86, bf16[1536,256]{0,1:T(8,128)(2,1)S(1)} %copy-done.52), kind=kOutput, calls=%fused_computation.104 | convolution fusion | flops 620497920 | bytes 38944768 | tf_op jit(solution)/shard_map/hqk,kd->qhd/dot_general | solution.py:878
  481.7 3.5 convolution_convert_fusion.11
  485.2 2.8 collective-permute-done.12
  491.7 14.6 %scatter_half.3 = f32[128,1792]{1,0:T(8,128)S(1)} custom-call(bf16[4,128,1792]{2,1,0:T(8,128)(2,1)S(1)} %bitcast.272), custom_call_target="tpu_custom_call" | custom-call | bytes 60000000 | tf_op jit(solution)/shard_map/scatter_half/pallas_call | solution.py:325
  509.9 17.5 %gather_full.10 = bf16[8,128,1536]{2,1,0:T(8,128)(2,1)} custom-call(bf16[128,1536]{1,0:T(8,128)(2,1)} %get-tuple-element.108.in_ref), custom_call_target="tpu_custom_call" | custom-call | bytes 60000000 | tf_op jit(solution)/shard_map/gather_full/pallas_call | solution.py:206
  527.4 5.1 convolution_convert_fusion.8
  532.5 6.1 fusion.24
  538.6 5.0 convolution_convert_fusion
  543.6 5.8 convolution_convert_fusion.6
  549.5 2.8 pad_maximum_fusion.1
  560.3 14.7 %gather_half.6 = bf16[4,128,1536]{2,1,0:T(8,128)(2,1)} custom-call(bf16[128,1536]{1,0:T(8,128)(2,1)} %get-tuple-element.153.in_ref), custom_call_target="tpu_custom_call" | custom-call | bytes 60000000 | tf_op jit(solution)/shard_map/gather_half/pallas_call | solution.py:206
  575.6 6.0 gather_half.8
  588.1 42.5 %scatter_full.10 = f32[128,1536]{1,0:T(8,128)S(1)} custom-call(bf16[8,128,1536]{2,1,0:T(8,128)(2,1)S(1)} %bitcast.273), custom_call_target="tpu_custom_call" | custom-call | bytes 60000000 | tf_op jit(solution)/shard_map/scatter_full/pallas_call | solution.py:325
  634.9 2.9 fusion.32
  637.8 20.6 %reduce-scatter.14.cloned.1.call-done = bf16[384,1728]{1,0:T(8,128)(2,1)} async-done(((bf16[1536,1728]{1,0:T(8,128)(2,1)}), bf16[384,1728]{1,0:T(8,128)(2,1)}) %reduce-scatter.14.cloned.1.call-update) | async-done | bytes 1327120 | tf_op jit(solution)/shard_map/reduce_scatter | solution.py:551
  667.6 24.9 %gather_full.11 = bf16[8,128,1536]{2,1,0:T(8,128)(2,1)} custom-call(bf16[128,1536]{1,0:T(8,128)(2,1)} %convert_element_type.305.in_ref), custom_call_target="tpu_custom_call" | custom-call | bytes 60000000 | tf_op jit(solution)/shard_map/gather_full/pallas_call | solution.py:206
  692.5 4.1 fusion.89
  699.3 10.9 %scan_back.1 = (f32[1024,256]{1,0:T(8,128)S(1)}, f32[8,256]{1,0:T(8,128)}) custom-call(f32[1024,256]{1,0:T(8,128)S(1)} %concatenate.187.decay_ref, f32[1024,256]{1,0:T(8,128)S(1)} %get-tuple-element.129.drive_ref, f32[8,256]{1,0:T(8,128)S(1)} %broadcast_in_dim.88.end_ref), custom_call_target="tpu_custom_call" | custom-call | bytes 33000000 | tf_op jit(solution)/shard_map/scan_back/pallas_call | solution.py:427
  710.4 3.4 fusion.109
  715.9 2.9 multiply_reduce_fusion.4
  726.8 3.3 collective-permute-done.15
  731.1 3.0 convolution_convert_fusion.10
  734.1 3.6 convolution_convert_fusion.5
  744.3 17.1 %scatter_full.11 = f32[128,1536]{1,0:T(8,128)S(1)} custom-call(bf16[8,128,1536]{2,1,0:T(8,128)(2,1)S(1)} %bitcast.274), custom_call_target="tpu_custom_call" | custom-call | bytes 60000000 | tf_op jit(solution)/shard_map/scatter_full/pallas_call | solution.py:325
  764.1 17.5 %small_sums.1 = (f32[8,1536]{1,0:T(8,128)}, f32[8,512]{1,0:T(8,128)}) custom-call(f32[8,1536]{1,0:T(8,128)} %concatenate.196.gains_ref, f32[8,256]{1,0:T(8,128)} %pad_maximum_fusion.31.rest_ref), custom_call_target="tpu_custom_call" | custom-call | bytes 33000000 | tf_op jit(solution)/shard_map/small_sums/pallas_call | solution.py:495
  787.0 14.5 %gather_half.9 = bf16[4,128,1536]{2,1,0:T(8,128)(2,1)} custom-call(bf16[128,1536]{1,0:T(8,128)(2,1)} %fusion.82.in_ref), custom_call_target="tpu_custom_call" | custom-call | bytes 60000000 | tf_op jit(solution)/shard_map/gather_half/pallas_call | solution.py:206
  801.5 3.6 bitcast_convert_fusion
  811.7 3.2 collective-permute-done.17
  819.4 4.5 collective-permute-done.16
  (551 shorter events, 163.2 us)
Async XLA Ops:
  7.2 62.5 %all-gather.8.cloned.1.call-start = ((), (), s32[]{:S(2)}) async-start(), calls=%async_computation.5 | async-start | bytes 2129920 | tf_op jit(solution)/shard_map/all_gather | solution.py:540
  9.2 8.3 collective-permute-start
  18.4 89.5 %all-gather.18.cloned.1.call-start = ((), (), s32[]{:S(2)}) async-start(), calls=%async_computation.15 | async-start | bytes 1966080 | tf_op jit(solution)/shard_map/all_gather | solution.py:667
  18.7 25.7 %copy-start.79 = (bf16[384,192]{0,1:T(8,128)(2,1)S(1)}, bf16[384,192]{0,1:T(8,128)(2,1)}, u32[]{:S(2)}) copy-start(bf16[384,192]{0,1:T(8,128)(2,1)} %param.40) | copy-start | bytes 442372
  18.7 25.7 %copy-start.80 = (bf16[192,384]{1,0:T(8,128)(2,1)S(1)}, bf16[192,384]{1,0:T(8,128)(2,1)}, u32[]{:S(2)}) copy-start(bf16[192,384]{1,0:T(8,128)(2,1)} %param.38) | copy-start | bytes 442372
  19.3 183.7 %copy-start.83 = (f32[1536]{0:T(1024)}, f32[1536]{0:T(1024)S(1)}, u32[]{:S(2)}) copy-start(f32[1536]{0:T(1024)S(1)} %get-tuple-element.99) | copy-start | bytes 18436
  20.8 24.5 %copy-start.74 = (bf16[512,192]{0,1:T(8,128)(2,1)S(1)}, bf16[512,192]{0,1:T(8,128)(2,1)}, u32[]{:S(2)}) copy-start(bf16[512,192]{0,1:T(8,128)(2,1)} %param.34) | copy-start | bytes 589828
  20.8 24.5 %copy-start.69 = (bf16[192,1152]{1,0:T(8,128)(2,1)S(1)}, bf16[192,1152]{1,0:T(8,128)(2,1)}, u32[]{:S(2)}) copy-start(bf16[192,1152]{1,0:T(8,128)(2,1)} %param.36) | copy-start | bytes 1327108
  20.8 24.5 %copy-start.70 = (bf16[192,1152]{1,0:T(8,128)(2,1)S(1)}, bf16[192,1152]{1,0:T(8,128)(2,1)}, u32[]{:S(2)}) copy-start(bf16[192,1152]{1,0:T(8,128)(2,1)} %param.35) | copy-start | bytes 1327108
  38.9 1.3 collective-permute-start.4
  40.2 4.2 collective-permute-start.5
  45.2 136.3 %all-gather.10.cloned.1.call-start = ((), (), s32[]{:S(2)}) async-start(), calls=%async_computation.6 | async-start | bytes 5406720 | tf_op jit(solution)/shard_map/all_gather | solution.py:540
  46.5 13.8 %collective-permute-start.2 = (bf16[192,1408]{1,0:T(8,128)(2,1)S(1)}, bf16[192,1408]{1,0:T(8,128)(2,1)S(1)}, u32[]{:S(2)}, u32[]{:S(2)}) collective-permute-start(bf16[192,1408]{1,0:T(8,128)(2,1)S(1)} %broadcast_select_fusion.4), channel_id=1, source_target_pairs={{0,4},{4,0},{8,12},{12,8},{16,20},{20,16},{24,28},{28,24},{1,5},{5... | collective-permute-start | bytes 1622024 | tf_op jit(solution)/shard_map/ppermute | solution.py:526
  61.7 170.9 %all-gather.12.cloned.1.call-start = ((), (), s32[]{:S(2)}) async-start(), calls=%async_computation.7 | async-start | bytes 2457600 | tf_op jit(solution)/shard_map/all_gather | solution.py:540
  61.9 6.7 collective-permute-start.3
  64.3 52.3 %copy-start.109 = (f32[256]{0:T(256)}, f32[256]{0:T(256)S(1)}, u32[]{:S(2)}) copy-start(f32[256]{0:T(256)S(1)} %get-tuple-element.120) | copy-start | bytes 3076
  64.4 50.2 %copy-start.112 = (f32[1,256]{1,0:T(1,128)}, f32[1,256]{1,0:T(1,128)S(1)}, u32[]{:S(2)}) copy-start(f32[1,256]{1,0:T(1,128)S(1)} %get-tuple-element.214) | copy-start | bytes 3076
  64.4 50.2 %copy-start.114 = (f32[1,256]{1,0:T(1,128)}, f32[1,256]{1,0:T(1,128)S(1)}, u32[]{:S(2)}) copy-start(f32[1,256]{1,0:T(1,128)S(1)} %get-tuple-element.215) | copy-start | bytes 3076
  64.4 50.2 %copy-start.116 = (f32[1,256]{1,0:T(1,128)}, f32[1,256]{1,0:T(1,128)S(1)}, u32[]{:S(2)}) copy-start(f32[1,256]{1,0:T(1,128)S(1)} %get-tuple-element.216) | copy-start | bytes 3076
  64.4 50.2 %copy-start.118 = (f32[1,256]{1,0:T(1,128)}, f32[1,256]{1,0:T(1,128)S(1)}, u32[]{:S(2)}) copy-start(f32[1,256]{1,0:T(1,128)S(1)} %get-tuple-element.217) | copy-start | bytes 3076
  64.4 52.2 %copy-start.99 = (f32[1,256]{1,0:T(1,128)}, f32[1,256]{1,0:T(1,128)S(1)}, u32[]{:S(2)}) copy-start(f32[1,256]{1,0:T(1,128)S(1)} %get-tuple-element.234) | copy-start | bytes 3076
  64.4 52.2 %copy-start.107 = (f32[1,256]{1,0:T(1,128)}, f32[1,256]{1,0:T(1,128)S(1)}, u32[]{:S(2)}) copy-start(f32[1,256]{1,0:T(1,128)S(1)} %get-tuple-element.235) | copy-start | bytes 3076
  69.6 272.1 %all-gather.14.cloned.1.call-start = ((), (), s32[]{:S(2)}) async-start(), calls=%async_computation.8 | async-start | bytes 4423680 | tf_op jit(solution)/shard_map/all_gather | solution.py:540
  75.5 53.5 %copy-start.23 = (f32[1024,512]{1,0:T(8,128)}, f32[1024,512]{1,0:T(8,128)S(1)}, u32[]{:S(2)}) copy-start(f32[1024,512]{1,0:T(8,128)S(1)} %fusion.197) | copy-start | bytes 6291460
  76.1 10.1 %collective-permute-start.9 = (bf16[192,1152]{1,0:T(8,128)(2,1)S(1)}, bf16[192,1152]{1,0:T(8,128)(2,1)S(1)}, u32[]{:S(2)}, u32[]{:S(2)}) collective-permute-start(bf16[192,1152]{1,0:T(8,128)(2,1)S(1)} %broadcast_select_fusion.6), channel_id=1, source_target_pairs={{0,4},{4,0},{8,12},{12,8},{16,20},{20,16},{24,28},{28,24},{1,5},{5... | collective-permute-start | bytes 1327112 | tf_op jit(solution)/shard_map/ppermute | solution.py:526
  87.6 24.5 %copy-start.50 = (bf16[1152,192]{0,1:T(8,128)(2,1)S(1)}, bf16[1152,192]{0,1:T(8,128)(2,1)}, u32[]{:S(2)}) copy-start(bf16[1152,192]{0,1:T(8,128)(2,1)} %param.43) | copy-start | bytes 1327108
  87.6 263.5 %all-gather.16.cloned.1.call-start = ((), (), s32[]{:S(2)}) async-start(), calls=%async_computation.9 | async-start | bytes 2457600 | tf_op jit(solution)/shard_map/all_gather | solution.py:540
  87.7 185.3 %copy-start.130 = (f32[64]{0:T(128)}, f32[64]{0:T(128)S(1)}, u32[]{:S(2)}) copy-start(f32[64]{0:T(128)S(1)} %multiply_power_fusion) | copy-start | bytes 772
  105.7 167.4 %copy-start.103 = (f32[512]{0:T(512)}, f32[512]{0:T(512)S(1)}, u32[]{:S(2)}) copy-start(f32[512]{0:T(512)S(1)} %subtract_convert_fusion.1) | copy-start | bytes 6148
  108.0 43.5 %collective-permute-start.6 = (bf16[4,192,1024]{2,1,0:T(8,128)(2,1)}, bf16[4,192,1024]{2,1,0:T(8,128)(2,1)}, u32[]{:S(2)}, u32[]{:S(2)}) collective-permute-start(bf16[4,192,1024]{2,1,0:T(8,128)(2,1)} %bitcast.320), channel_id=1, source_target_pairs={{0,4},{4,0},{8,12},{12,8},{16,20},{20,16},{24,28},{28,24},{1,5},{5... | collective-permute-start | bytes 4718600 | tf_op jit(solution)/shard_map/ppermute | solution.py:526
  108.8 5.8 collective-permute-start.1
  113.3 36.9 %collective-permute-start.10 = (bf16[192,576]{1,0:T(8,128)(2,1)S(1)}, bf16[192,576]{1,0:T(8,128)(2,1)S(1)}, u32[]{:S(2)}, u32[]{:S(2)}) collective-permute-start(bf16[192,576]{1,0:T(8,128)(2,1)S(1)} %broadcast_select_fusion.8), channel_id=1, source_target_pairs={{0,4},{4,0},{8,12},{12,8},{16,20},{20,16},{24,28},{28,24},{1,5},{5... | collective-permute-start | bytes 663560 | tf_op jit(solution)/shard_map/ppermute | solution.py:526
  117.8 32.4 %copy-start = (f32[1024,256]{1,0:T(8,128)}, f32[1024,256]{1,0:T(8,128)S(1)}, u32[]{:S(2)}) copy-start(f32[1024,256]{1,0:T(8,128)S(1)} %get-tuple-element.144.decay_ref) | copy-start | bytes 3145732
  129.5 52.0 %copy-start.37 = (bf16[1024,256]{1,0:T(8,128)(2,1)}, bf16[1024,256]{1,0:T(8,128)(2,1)S(1)}, u32[]{:S(2)}) copy-start(bf16[1024,256]{1,0:T(8,128)(2,1)S(1)} %multiply_convert_fusion.4) | copy-start | bytes 1572868
  129.5 22.0 %copy-start.55 = (bf16[768,1024]{1,0:T(8,128)(2,1)S(1)}, bf16[768,1024]{1,0:T(8,128)(2,1)}, u32[]{:S(2)}) copy-start(bf16[768,1024]{1,0:T(8,128)(2,1)} %all-gather.18.cloned.1.call-done) | copy-start | bytes 4718596
  151.2 480.8 %reduce-scatter.6.cloned.1.call-start = ((), (), s32[]{:S(2)}) async-start(), calls=%async_computation.10 | async-start | bytes 6881280 | tf_op jit(solution)/shard_map/reduce_scatter | solution.py:551
  203.0 26.2 %copy-start.137 = (f32[128]{0:T(128)}, f32[128]{0:T(128)S(1)}, u32[]{:S(2)}) copy-start(f32[128]{0:T(128)S(1)} %get-tuple-element.116) | copy-start | bytes 1540
  203.0 52.4 %copy-start.6 = (f32[128,1536]{1,0:T(8,128)}, f32[128,1536]{1,0:T(8,128)S(1)}, u32[]{:S(2)}) copy-start(f32[128,1536]{1,0:T(8,128)S(1)} %get-tuple-element.117) | copy-start | bytes 2359300
  203.1 26.2 %copy-start.122 = (f32[128]{0:T(128)}, f32[128]{0:T(128)S(1)}, u32[]{:S(2)}) copy-start(f32[128]{0:T(128)S(1)} %fusion.158) | copy-start | bytes 1540
  255.7 54.4 %copy-start.8 = (f32[128,1536]{1,0:T(8,128)}, f32[128,1536]{1,0:T(8,128)S(1)}, u32[]{:S(2)}) copy-start(f32[128,1536]{1,0:T(8,128)S(1)} %get-tuple-element.115) | copy-start | bytes 2359300
  273.7 13.3 %collective-permute-start.7 = (bf16[512,256]{0,1:T(8,128)(2,1)S(1)}, bf16[512,256]{0,1:T(8,128)(2,1)S(1)}, u32[]{:S(2)}, u32[]{:S(2)}) collective-permute-start(bf16[512,256]{0,1:T(8,128)(2,1)S(1)} %pad_maximum_fusion.26), channel_id=1, source_target_pairs={{0,8},{4,12},{8,16},{12,20},{16,24},{20,28},{1,9},{5,13},{9,17},{1... | collective-permute-start | bytes 786440 | tf_op jit(solution)/shard_map/ppermute | solution.py:626
  275.0 12.0 %collective-permute-start.8 = (bf16[512,256]{0,1:T(8,128)(2,1)S(1)}, bf16[512,256]{0,1:T(8,128)(2,1)S(1)}, u32[]{:S(2)}, u32[]{:S(2)}) collective-permute-start(bf16[512,256]{0,1:T(8,128)(2,1)S(1)} %pad_maximum_fusion.26), channel_id=1, source_target_pairs={{0,4},{4,8},{8,12},{12,16},{16,20},{20,24},{24,28},{1,5},{5,9},{9,... | collective-permute-start | bytes 786440 | tf_op jit(solution)/shard_map/ppermute | solution.py:626
  372.9 285.6 %reduce-scatter.14.cloned.1.call-start = ((), (), s32[]{:S(2)}) async-start(), calls=%async_computation.14 | async-start | bytes 6881280 | tf_op jit(solution)/shard_map/reduce_scatter | solution.py:551
  458.8 26.4 %collective-permute-start.11 = (bf16[512,256]{0,1:T(8,128)(2,1)}, bf16[512,256]{0,1:T(8,128)(2,1)}, u32[]{:S(2)}, u32[]{:S(2)}) collective-permute-start(bf16[512,256]{0,1:T(8,128)(2,1)} %get-tuple-element.154), channel_id=1, source_target_pairs={{4,0},{8,4},{12,8},{16,12},{20,16},{24,20},{28,24},{5,1},{9,5},{13... | collective-permute-start | bytes 786440 | tf_op jit(solution)/shard_map/ppermute | solution.py:626
  460.1 27.9 %collective-permute-start.12 = (bf16[512,256]{0,1:T(8,128)(2,1)}, bf16[512,256]{0,1:T(8,128)(2,1)}, u32[]{:S(2)}, u32[]{:S(2)}) collective-permute-start(bf16[512,256]{0,1:T(8,128)(2,1)} %get-tuple-element.155), channel_id=1, source_target_pairs={{8,0},{12,4},{16,8},{20,12},{24,16},{28,20},{9,1},{13,5},{17,9},{2... | collective-permute-start | bytes 786440 | tf_op jit(solution)/shard_map/ppermute | solution.py:626
  552.3 144.4 %reduce-scatter.8.cloned.1.call-start = ((), (), s32[]{:S(2)}) async-start(), calls=%async_computation.11 | async-start | bytes 1597440 | tf_op jit(solution)/shard_map/reduce_scatter | solution.py:681
  587.1 43.5 %copy-start.7 = (f32[128,1536]{1,0:T(8,128)S(1)}, f32[128,1536]{1,0:T(8,128)}, u32[]{:S(2)}) copy-start(f32[128,1536]{1,0:T(8,128)} %copy-done.6) | copy-start | bytes 2359300
  587.1 43.5 %copy-start.84 = (f32[1536]{0:T(1024)S(1)}, f32[1536]{0:T(1024)}, u32[]{:S(2)}) copy-start(f32[1536]{0:T(1024)} %copy-done.83) | copy-start | bytes 18436
  587.1 43.5 %copy-start.123 = (f32[128]{0:T(128)S(1)}, f32[128]{0:T(128)}, u32[]{:S(2)}) copy-start(f32[128]{0:T(128)} %copy-done.122) | copy-start | bytes 1540
  587.1 47.8 %collective-permute-start.14 = (bf16[4,208,768]{2,1,0:T(8,128)(2,1)}, bf16[4,208,768]{2,1,0:T(8,128)(2,1)}, u32[]{:S(2)}, u32[]{:S(2)}) collective-permute-start(bf16[4,208,768]{2,1,0:T(8,128)(2,1)} %fusion.39), channel_id=1, source_target_pairs={{0,4},{4,0},{8,12},{12,8},{16,20},{20,16},{24,28},{28,24},{1,5},{5... | collective-permute-start | bytes 3833864 | tf_op jit(solution)/shard_map/ppermute | solution.py:526
  588.1 42.7 %copy-start.98 = (f32[1536]{0:T(1024)S(1)}, f32[1536]{0:T(1024)}, u32[]{:S(2)}) copy-start(f32[1536]{0:T(1024)} %get-tuple-element.92) | copy-start | bytes 18436
  588.1 42.8 %copy-start.138 = (f32[128]{0:T(128)S(1)}, f32[128]{0:T(128)}, u32[]{:S(2)}) copy-start(f32[128]{0:T(128)} %copy-done.137) | copy-start | bytes 1540
  588.1 42.8 %copy-start.45 = (f32[128,1536]{1,0:T(8,128)S(1)}, f32[128,1536]{1,0:T(8,128)}, u32[]{:S(2)}) copy-start(f32[128,1536]{1,0:T(8,128)} %get-tuple-element.109) | copy-start | bytes 2359300
  634.2 27.9 %collective-permute-start.13 = (bf16[192,1728]{1,0:T(8,128)(2,1)}, bf16[192,1728]{1,0:T(8,128)(2,1)}, u32[]{:S(2)}, u32[]{:S(2)}) collective-permute-start(bf16[192,1728]{1,0:T(8,128)(2,1)} %broadcast_select_fusion.2), channel_id=1, source_target_pairs={{0,4},{4,0},{8,12},{12,8},{16,20},{20,16},{24,28},{28,24},{1,5},{5... | collective-permute-start | bytes 1990664 | tf_op jit(solution)/shard_map/ppermute | solution.py:526
  637.7 24.4 %copy-start.34 = (bf16[384,1728]{1,0:T(8,128)(2,1)S(1)}, bf16[384,1728]{1,0:T(8,128)(2,1)}, u32[]{:S(2)}) copy-start(bf16[384,1728]{1,0:T(8,128)(2,1)} %reduce-scatter.6.cloned.1.call-done) | copy-start | bytes 3981316
  637.8 171.0 %reduce-scatter.12.cloned.1.call-start = ((), (), s32[]{:S(2)}) async-start(), calls=%async_computation.13 | async-start | bytes 1146880 | tf_op jit(solution)/shard_map/reduce_scatter | solution.py:551
  660.7 144.5 %collective-permute-start.18 = (bf16[192,1728]{1,0:T(8,128)(2,1)}, bf16[192,1728]{1,0:T(8,128)(2,1)}, u32[]{:S(2)}, u32[]{:S(2)}) collective-permute-start(bf16[192,1728]{1,0:T(8,128)(2,1)} %broadcast_select_fusion), channel_id=1, source_target_pairs={{0,4},{4,0},{8,12},{12,8},{16,20},{20,16},{24,28},{28,24},{1,5},{5... | collective-permute-start | bytes 1990664 | tf_op jit(solution)/shard_map/ppermute | solution.py:526
  699.3 31.0 %copy-start.71 = (bf16[1024,256]{1,0:T(8,128)(2,1)}, bf16[1024,256]{1,0:T(8,128)(2,1)S(1)}, u32[]{:S(2)}) copy-start(bf16[1024,256]{1,0:T(8,128)(2,1)S(1)} %get-tuple-element.130) | copy-start | bytes 1572868
  724.7 5.5 collective-permute-start.15
  738.8 22.6 %copy-start.82 = (f32[1536]{0:T(1024)S(1)}, f32[1536]{0:T(1024)}, u32[]{:S(2)}) copy-start(f32[1536]{0:T(1024)} %copy-done.81) | copy-start | bytes 18436
  738.8 77.9 %reduce-scatter.10.cloned.1.call-start = ((), (), s32[]{:S(2)}) async-start(), calls=%async_computation.12 | async-start | bytes 1966080 | tf_op jit(solution)/shard_map/reduce_scatter | solution.py:551
  739.8 21.7 %copy-start.48 = (bf16[512,1536]{1,0:T(8,128)(2,1)S(1)}, bf16[512,1536]{1,0:T(8,128)(2,1)}, u32[]{:S(2)}) copy-start(bf16[512,1536]{1,0:T(8,128)(2,1)} %param.22) | copy-start | bytes 4718596
  809.7 5.2 collective-permute-start.17
  817.8 6.1 collective-permute-start.16
  (116 other events, 838.1 us)
Sparse Core Ops, SparseCore 0:
  18.6 40.7 all-gather.7
  61.5 35.9 all-gather.17
  99.0 82.4 all-gather.9
  183.5 42.0 all-gather.11
  227.6 70.5 all-gather.13
  300.1 49.6 all-gather.15
  373.0 108.7 reduce-scatter.5
  552.4 105.9 reduce-scatter.13
  661.3 31.1 reduce-scatter.7
  738.9 24.2 reduce-scatter.11
  766.2 34.2 reduce-scatter.9

commit v2 on v1

--- a/solution.py
+++ b/solution.py
@@ -136,7 +136,20 @@
     )
 
 
-def gather_kernel(full, in_ref, out_ref, send_sem, recv_sem, local_sem):
+def in_turn(*runs):
+    runs = list(runs)
+    while runs:
+        for run in list(runs):
+            if next(run, "end") == "end":
+                runs.remove(run)
+
+
+def neighbours(full):
+    across_a, across_b, across_c = cube()[3:]
+    return [across_c, across_b] + ([across_a] if full else [])
+
+
+def gather_steps(full, in_ref, out_ref, send_sem, recv_sem, local_sem):
     a, b, c, across_a, across_b, across_c = cube()
     half = in_ref.shape[0] // 2
 
@@ -149,49 +162,54 @@
         index(a, 1 - b, c),
         index(1 - a, 1 - b, c),
     )
-    greet([across_c, across_b] + ([across_a] if full else []))
     low, high = (pl.ds(0, half), pl.ds(half, half))
-
-    def own(part, slot, device):
-        return remote(in_ref.at[part], out_ref.at[me, part], send_sem, recv_sem, slot, device)
-
-    def onward(block, part, slot, device):
-        here = out_ref.at[block, part]
-        return remote(here, here, send_sem, recv_sem, slot, device)
-
     sent = {}
 
-    def go(slot, copy):
+    def go(slot, src, dst, device):
+        copy = remote(src, dst, send_sem, recv_sem, slot, device)
         copy.start()
         sent[slot] = copy
 
+    def own(slot, part, device):
+        go(slot, in_ref.at[part], out_ref.at[me, part], device)
+
+    def onward(slot, block, part, device):
+        go(slot, out_ref.at[block, part], out_ref.at[block, part], device)
+
     if full:
-        go(0, own(low, 0, across_a))
-    go(1, own(high, 1, across_b))
+        own(0, low, across_a)
+    own(1, high, across_b)
     if full:
-        go(2, own(high, 2, across_a))
-    go(3, own(low, 3, across_b))
-    go(4, remote(in_ref, out_ref.at[me], send_sem, recv_sem, 4, across_c))
+        own(2, high, across_a)
+    own(3, low, across_b)
+    go(4, in_ref, out_ref.at[me], across_c)
     mine = pltpu.make_async_copy(in_ref, out_ref.at[me], local_sem)
     mine.start()
+    yield
     if full:
         sent[0].wait_recv()
-        go(5, onward(an, low, 5, across_b))
-        go(6, onward(an, low, 6, across_c))
+        onward(5, an, low, across_b)
+        onward(6, an, low, across_c)
+        yield
     sent[1].wait_recv()
     if full:
-        go(7, onward(bn, high, 7, across_a))
-    go(8, onward(bn, high, 8, across_c))
+        onward(7, bn, high, across_a)
+    onward(8, bn, high, across_c)
+    yield
     if full:
         sent[2].wait_recv()
-        go(9, onward(an, high, 9, across_c))
+        onward(9, an, high, across_c)
+        yield
     sent[3].wait_recv()
-    go(10, onward(bn, low, 10, across_c))
+    onward(10, bn, low, across_c)
+    yield
     if full:
         sent[5].wait_recv()
-        go(11, onward(dn, low, 11, across_c))
+        onward(11, dn, low, across_c)
+        yield
         sent[7].wait_recv()
-        go(12, onward(dn, high, 12, across_c))
+        onward(12, dn, high, across_c)
+        yield
     for slot in (4, 6, 8, 9, 10, 11, 12):
         if slot in sent:
             sent[slot].wait_recv()
@@ -200,27 +218,46 @@
     mine.wait()
 
 
-def gather(block, full, collective_id):
-    count = 8 if full else 4
-    rows, width = block.shape
-    result = pl.pallas_call(
-        functools.partial(gather_kernel, full),
-        out_shape=jax.ShapeDtypeStruct((count, rows, width), block.dtype),
-        in_specs=[ANY],
-        out_specs=ANY,
+def gather_kernel(full, count, *refs):
+    in_refs, out_refs = (refs[:count], refs[count : 2 * count])
+    send_sem, recv_sem, local_sem = refs[2 * count :]
+    greet(neighbours(full))
+    in_turn(
+        *[
+            gather_steps(
+                full, in_refs[k], out_refs[k], send_sem.at[k], recv_sem.at[k], local_sem.at[k]
+            )
+            for k in range(count)
+        ]
+    )
+
+
+def gather(blocks, full, collective_id):
+    ways = 8 if full else 4
+    count = len(blocks)
+    results = pl.pallas_call(
+        functools.partial(gather_kernel, full, count),
+        out_shape=[
+            jax.ShapeDtypeStruct((ways, *block.shape), block.dtype) for block in blocks
+        ],
+        in_specs=[ANY] * count,
+        out_specs=[ANY] * count,
         scratch_shapes=[
-            pltpu.SemaphoreType.DMA((13,)),
-            pltpu.SemaphoreType.DMA((13,)),
-            pltpu.SemaphoreType.DMA,
+            pltpu.SemaphoreType.DMA((count, 13)),
+            pltpu.SemaphoreType.DMA((count, 13)),
+            pltpu.SemaphoreType.DMA((count,)),
         ],
         name="gather_full" if full else "gather_half",
         cost_estimate=EIGHTEEN_US,
         compiler_params=pltpu.CompilerParams(collective_id=collective_id, has_side_effects=True),
-    )(block)
-    return result.reshape(count * rows, width)
-
-
-def scatter_kernel(
+    )(*blocks)
+    return [
+        result.reshape(ways * block.shape[0], block.shape[1])
+        for result, block in zip(results, blocks)
+    ]
+
+
+def scatter_steps(
     full, part_ref, out_ref, cbuf, sx, sy, tx, ty, ax, by, rx, ry, csend, crecv, send_sem, recv_sem
 ):
     a, b, c, across_a, across_b, across_c = cube()
@@ -246,7 +283,6 @@
         ]
     else:
         order = [(a, 1 - b, low), (a, 1 - b, high), (a, b, low), (a, b, high)]
-    greet([across_c, across_b] + ([across_a] if full else []))
     core = []
     for k, (pa, pb, part) in enumerate(order):
         copy = remote(
@@ -259,6 +295,7 @@
         )
         copy.start()
         core.append(copy)
+    yield
 
     def summed(k):
         pa, pb, part = order[k]
@@ -280,10 +317,12 @@
         x0 = go(sx.at[0], ax.at[0], 0, across_a)
         sy[0] = lowered(summed(1))
         y0 = go(sy.at[0], by.at[0], 1, across_b)
+        yield
         sx[1] = lowered(summed(2))
         x1 = go(sx.at[1], ax.at[1], 2, across_a)
         sy[1] = lowered(summed(3))
         y1 = go(sy.at[1], by.at[1], 3, across_b)
+        yield
         total = summed(4)
         x0.wait_recv()
         ty[...] = lowered(total + ax[0].astype(jnp.float32))
@@ -292,6 +331,7 @@
         y0.wait_recv()
         tx[...] = lowered(total + by[0].astype(jnp.float32))
         last_x = go(tx, rx, 5, across_a)
+        yield
         total = summed(6)
         x1.wait_recv()
         total = total + ax[1].astype(jnp.float32)
@@ -302,52 +342,64 @@
         total = total + by[1].astype(jnp.float32)
         last_x.wait_recv()
         out_ref[high] = total + rx[...].astype(jnp.float32)
+        yield
     else:
         sy[0] = lowered(summed(0))
         y0 = go(sy.at[0], by.at[0], 1, across_b)
         sy[1] = lowered(summed(1))
         y1 = go(sy.at[1], by.at[1], 3, across_b)
+        yield
         total = summed(2)
         y0.wait_recv()
         out_ref[low] = total + by[0].astype(jnp.float32)
         total = summed(3)
         y1.wait_recv()
         out_ref[high] = total + by[1].astype(jnp.float32)
+        yield
     for copy in core + sent:
         copy.wait_send()
 
 
-def scatter(partial, full, collective_id):
-    count = 8 if full else 4
-    rows, width = (partial.shape[0] // count, partial.shape[1])
+def scatter_kernel(full, count, *refs):
+    greet(neighbours(full))
+    in_turn(
+        *[
+            scatter_steps(full, refs[k], refs[count + k], *refs[2 * count + 13 * k :][:13])
+            for k in range(count)
+        ]
+    )
+
+
+def scatter_scratch(ways, rows, width):
     half = rows // 2
-    low = jnp.bfloat16
+    shapes = [(ways // 2, rows, width)] + [(2, half, width)] * 2 + [(half, width)] * 2
+    shapes += [(2, half, width)] * 2 + [(half, width)] * 2
+    return [pltpu.VMEM(shape, jnp.bfloat16) for shape in shapes] + [
+        pltpu.SemaphoreType.DMA((k,)) for k in (8, 8, 6, 6)
+    ]
+
+
+def scatter(partials, full, collective_id):
+    ways = 8 if full else 4
+    count = len(partials)
+    rows = partials[0].shape[0] // ways
+    scratch = []
+    for partial in partials:
+        scratch += scatter_scratch(ways, rows, partial.shape[1])
     return pl.pallas_call(
-        functools.partial(scatter_kernel, full),
-        out_shape=jax.ShapeDtypeStruct((rows, width), jnp.float32),
-        in_specs=[VMEM],
-        out_specs=VMEM,
-        scratch_shapes=[
-            pltpu.VMEM((count // 2, rows, width), low),
-            pltpu.VMEM((2, half, width), low),
-            pltpu.VMEM((2, half, width), low),
-            pltpu.VMEM((half, width), low),
-            pltpu.VMEM((half, width), low),
-            pltpu.VMEM((2, half, width), low),
-            pltpu.VMEM((2, half, width), low),
-            pltpu.VMEM((half, width), low),
-            pltpu.VMEM((half, width), low),
-            pltpu.SemaphoreType.DMA((8,)),
-            pltpu.SemaphoreType.DMA((8,)),
-            pltpu.SemaphoreType.DMA((6,)),
-            pltpu.SemaphoreType.DMA((6,)),
+        functools.partial(scatter_kernel, full, count),
+        out_shape=[
+            jax.ShapeDtypeStruct((rows, partial.shape[1]), jnp.float32) for partial in partials
         ],
+        in_specs=[VMEM] * count,
+        out_specs=[VMEM] * count,
+        scratch_shapes=scratch,
         name="scatter_full" if full else "scatter_half",
         cost_estimate=EIGHTEEN_US,
         compiler_params=pltpu.CompilerParams(
-            collective_id=collective_id, has_side_effects=True, vmem_limit_bytes=40 * 2**20
+            collective_id=collective_id, has_side_effects=True, vmem_limit_bytes=48 * 2**20
         ),
-    )(lowered(partial).reshape(count, rows, width))
+    )(*[lowered(partial).reshape(ways, rows, -1) for partial in partials])
 
 
 def scan_kernel(
@@ -358,11 +410,8 @@
     steps = rows // strands
     lanes = 128
     blocks = width // lanes
-    seq = lax.axis_index("seq")
-    tp = lax.axis_index("tp")
-    lo = lax.rem(seq, LO)
-    mine = seq // LO
-    peers = [(lax.rem(mine + k, high) * LO + lo, tp) for k in range(1, high)]
+    mine = lax.axis_index("seq") // LO
+    peers = high_peers(high)
     greet(peers)
     for n in range(blocks):
         cum[n] = decay_ref[:, n * lanes : (n + 1) * lanes]
@@ -448,19 +497,16 @@
     )(decay, drive, end_scale)
 
 
-def small_kernel(high, gains_ref, rest_ref, gains_out, rest_out, gbuf, rbuf, ghold, rhold, gpair, rpair, send_sem, recv_sem):
+def small_steps(high, gains_ref, rest_ref, gains_out, rest_out, gbuf, rbuf, ghold, rhold, gpair, rpair, send_sem, recv_sem):
     a, b, c, across_a, across_b, across_c = cube()
-    seq = lax.axis_index("seq")
-    tp = lax.axis_index("tp")
-    mine = seq // LO
-    peers = [(lax.rem(mine + k, high) * LO + a, tp) for k in range(1, high)]
-    greet(peers + [across_a, across_b, across_c])
+    peers = high_peers(high)
     copies = []
     for k, peer in enumerate(peers):
         for n, (src, dst) in enumerate(((gains_ref, gbuf.at[k]), (rest_ref, rbuf.at[k]))):
             copy = remote(src, dst, send_sem, recv_sem, 2 * k + n, peer)
             copy.start()
             copies.append(copy)
+    yield
     for copy in copies:
         copy.wait_recv()
     gains = gains_ref[...]
@@ -478,6 +524,7 @@
         copy = remote(ghold.at[n], gpair.at[n], send_sem, recv_sem, slot + 1 + n, device)
         copy.start()
         copies.append(copy)
+        yield
         copy.wait_recv()
         gains = gains + gpair[n]
     swap.wait_recv()
@@ -490,30 +537,125 @@
         copy.wait_send()
 
 
-def small_sums(gains, rest, high, collective_id):
-    count = 2 * (high - 1) + 4
+def high_peers(high):
+    seq = lax.axis_index("seq")
+    tp = lax.axis_index("tp")
+    return [(lax.rem(seq // LO + k, high) * LO + lax.rem(seq, LO), tp) for k in range(1, high)]
+
+
+def last_kernel(high, part_ref, gains_ref, rest_ref, out_ref, gains_out, rest_out, *more):
+    greet(high_peers(high) + neighbours(True))
+    in_turn(
+        scatter_steps(True, part_ref, out_ref, *more[:13]),
+        small_steps(high, gains_ref, rest_ref, gains_out, rest_out, *more[13:]),
+    )
+
+
+def scatter_and_sums(partial, gains, rest, high, collective_id):
+    slots = 2 * (high - 1) + 4
+    ways = 8
+    width = partial.shape[1]
+    rows = partial.shape[0] // ways
     return pl.pallas_call(
-        functools.partial(small_kernel, high),
-        out_shape=(
+        functools.partial(last_kernel, high),
+        out_shape=[
+            jax.ShapeDtypeStruct((rows, width), jnp.float32),
             jax.ShapeDtypeStruct(gains.shape, jnp.float32),
             jax.ShapeDtypeStruct((rest.shape[0], LO * rest.shape[1]), jnp.float32),
-        ),
-        in_specs=[VMEM] * 2,
-        out_specs=(VMEM, VMEM),
-        scratch_shapes=[
+        ],
+        in_specs=[VMEM] * 3,
+        out_specs=[VMEM] * 3,
+        scratch_shapes=scatter_scratch(ways, rows, width)
+        + [
             pltpu.VMEM((high - 1, *gains.shape), jnp.float32),
             pltpu.VMEM((high - 1, *rest.shape), jnp.float32),
             pltpu.VMEM((3, *gains.shape), jnp.float32),
             pltpu.VMEM(rest.shape, jnp.float32),
             pltpu.VMEM((3, *gains.shape), jnp.float32),
             pltpu.VMEM(rest.shape, jnp.float32),
-            pltpu.SemaphoreType.DMA((count,)),
-            pltpu.SemaphoreType.DMA((count,)),
+            pltpu.SemaphoreType.DMA((slots,)),
+            pltpu.SemaphoreType.DMA((slots,)),
         ],
-        name="small_sums",
-        cost_estimate=TEN_US,
-        compiler_params=pltpu.CompilerParams(collective_id=collective_id, has_side_effects=True),
-    )(gains, rest)
+        name="scatter_and_sums",
+        cost_estimate=EIGHTEEN_US,
+        compiler_params=pltpu.CompilerParams(
+            collective_id=collective_id, has_side_effects=True, vmem_limit_bytes=40 * 2**20
+        ),
+    )(lowered(partial).reshape(ways, rows, width), gains, rest)
+
+
+def attention_back_kernel(
+    shift, query_ref, ext_ref, grad_ref, log_ref, here_ref, there_ref, cos_ref, sin_ref, dquery_ref, dext_ref, total
+):
+    tile = 256
+    rows, width = query_ref.shape
+    heads = width // HD
+    reach = shift + tile
+    scale = HD ** (-0.5)
+    total[...] = jnp.zeros_like(total)
+
+    def turn(n, carry):
+        h = n // (rows // tile)
+        first = pl.multiple_of(lax.rem(n, rows // tile) * tile, tile)
+        lanes = pl.ds(pl.multiple_of(h * HD, HD), HD)
+        at = pl.ds(first, tile)
+        seen = pl.ds(first, reach)
+        query = query_ref[at, lanes]
+        grad = grad_ref[at, lanes]
+        keys = ext_ref[seen, :HD]
+        values = ext_ref[seen, HD:]
+        distance = (
+            lax.broadcasted_iota(jnp.int32, (reach, tile), 1)
+            - lax.broadcasted_iota(jnp.int32, (reach, tile), 0)
+            + shift
+        )
+        allowed = (
+            (there_ref[seen, :] == here_ref[0:1, at]) & (distance >= 0) & (distance < WINDOW)
+        )
+        scores = jnp.where(allowed, product_right(keys, query) * scale, -1e30)
+        probs = jnp.exp(scores - log_ref[pl.ds(h, 1), at])
+        grad_probs = product_right(values, grad)
+        mean = jnp.sum(probs * grad_probs, axis=0, keepdims=True)
+        grad_scores = lowered(probs * (grad_probs - mean) * scale)
+        total[seen, :HD] += product(grad_scores, query)
+        total[seen, HD:] += product(lowered(probs), grad)
+        turned = product_left(grad_scores, keys)
+        turned = turned * cos_ref[at, :] - pltpu.roll(turned, HD // 2, 1) * sin_ref[at, :]
+        dquery_ref[at, lanes] = lowered(turned)
+        return carry
+
+    lax.fori_loop(0, heads * (rows // tile), turn, 0)
+    dext_ref[...] = lowered(total[...])
+
+
+def attention_back(query_rot, extended, grad, log_total, segment, key_segment, cosine, sine):
+    rows, width = query_rot.shape
+    seen = extended.shape[0]
+    log_rows = jnp.concatenate(
+        [log_total, jnp.zeros((8 - log_total.shape[0], rows), jnp.float32)], axis=0
+    )
+    return pl.pallas_call(
+        functools.partial(attention_back_kernel, seen - rows),
+        out_shape=[
+            jax.ShapeDtypeStruct((rows, width), jnp.bfloat16),
+            jax.ShapeDtypeStruct((seen, 2 * HD), jnp.bfloat16),
+        ],
+        in_specs=[VMEM] * 8,
+        out_specs=[VMEM] * 2,
+        scratch_shapes=[pltpu.VMEM((seen, 2 * HD), jnp.float32)],
+        name="attention_back",
+        cost_estimate=EIGHTEEN_US,
+        compiler_params=pltpu.CompilerParams(vmem_limit_bytes=48 * 2**20),
+    )(
+        query_rot,
+        extended,
+        grad,
+        log_rows,
+        jnp.broadcast_to(segment[None], (8, rows)),
+        key_segment[:, None],
+        cosine,
+        sine,
+    )
 
 
 def stacked_by_low(mine, other):
@@ -531,28 +673,28 @@
     return [[h * LO + l for h in range(count // LO)] for l in range(LO)]
 
 
-def gather_weight(halves):
+def swap_columns(*parts):
     lo = lax.rem(lax.axis_index("seq"), LO)
+    halves = [jnp.concatenate(each, axis=1) for each in zip(*map(split_columns, parts))]
     kept = jnp.where(lo == 0, halves[0], halves[1])
     given = jnp.where(lo == 0, halves[1], halves[0])
     both = stacked_by_low(kept, swap_low(given))
-    rows = both.shape[1]
-    return lax.all_gather(
-        both.reshape(LO * rows, both.shape[2]),
-        "seq",
-        axis=0,
-        tiled=True,
-        axis_index_groups=high_groups(),
-    )
-
-
-def reduce_weight(grad):
+    return both.reshape(-1, both.shape[2])
+
+
+def gather_high(rows):
+    return lax.all_gather(rows, "seq", axis=0, tiled=True, axis_index_groups=high_groups())
+
+
+def reduce_high(grad):
+    return lax.psum_scatter(
+        lowered(grad), "seq", scatter_dimension=0, tiled=True, axis_index_groups=high_groups()
+    )
+
+
+def exchanged(both):
     lo = lax.rem(lax.axis_index("seq"), LO)
-    both = lax.psum_scatter(
-        lowered(grad), "seq", scatter_dimension=0, tiled=True, axis_index_groups=high_groups()
-    )
-    rows = both.shape[0] // LO
-    both = both.reshape(LO, rows, both.shape[1])
+    both = both.reshape(LO, -1, both.shape[1])
     kept = jnp.where(lo == 0, both[0], both[1])
     given = jnp.where(lo == 0, both[1], both[0])
     return stacked_by_low(kept, swap_low(given))
@@ -567,33 +709,30 @@
     return jnp.concatenate([blocks[l] for l in range(LO)], axis=1).astype(jnp.float32)
 
 
-def dense_forward(stream, gain, weights, cid):
+def dense_forward(normed, weights):
     gate_up, down = weights
     width = down.shape[1]
-    normed = gather(lowered(rms_norm(stream, gain)), True, cid["gather_full"])
     both = product(normed, gate_up)
     hidden = lowered(gated(both[:, :width], both[:, width:]))
-    out = scatter(product_right(hidden, down), True, cid["scatter_full"])
-    return (out, (normed, both, hidden))
-
-
-def dense_backward(stream, gain, grad_out, kept, weights, cid):
+    return (lowered(product_right(hidden, down)), (normed, both, hidden))
+
+
+def dense_backward(stream, gain, grad_out, grad_low, kept, weights, cid, tied=()):
     gate_up, down = weights
     width = down.shape[1]
     normed, both, hidden = kept
-    grad_low = gather(lowered(grad_out), True, cid["gather_full"])
     grad_down = product_left(grad_low, hidden)
     grad_hidden = product(grad_low, down)
     gate_grad, up_grad = jax.vjp(gated, both[:, :width], both[:, width:])[1](grad_hidden)
     both_low = jnp.concatenate([lowered(gate_grad), lowered(up_grad)], axis=1)
     grad_both = product_left(normed, both_low)
     partial = product_right(both_low, gate_up)
-    partial, grad_both, grad_down = lax.optimization_barrier(
-        (lowered(partial), lowered(grad_both), lowered(grad_down))
-    )
-    grad_normed = scatter(partial, True, cid["scatter_full"])
+    partial, grad_both, grad_down, tied = lax.optimization_barrier(
+        (lowered(partial), lowered(grad_both), lowered(grad_down), tied)
+    )
+    (grad_normed,) = scatter([partial], True, cid["scatter_full"])
     stream_grad, gain_grad = jax.vjp(rms_norm, stream, gain)[1](grad_normed)
-    return (grad_out + stream_grad, gain_grad, grad_both, grad_down)
+    return (grad_out + stream_grad, gain_grad, grad_both, grad_down, tied)
 
 
 def block_product(values, weight):
@@ -639,22 +778,16 @@
     "scan": 4,
     "scan_back": 5,
     "scatter_wide": 6,
-    "small_sums": 7,
+    "last": 7,
     "gather_narrow": 8,
+    "gather_two": 9,
+    "scatter_two": 10,
 }
 
 
-def dense_weights(gate_part, up_part, down_part, *more):
-    pieces = [split_columns(part) for part in (gate_part, up_part, *more)]
-    wide = gather_weight([jnp.concatenate(each, axis=1) for each in zip(*pieces)])
-    down = gather_weight(split_columns(down_part.T))
-    width = 2 * down.shape[1]
-    return (wide[:, :width], down) + ((wide[:, width:],) if more else ())
-
-
-def dense_grads(grad_both, grad_down):
-    width = grad_down.shape[1]
-    both = reduce_weight(jnp.concatenate([grad_both, grad_down], axis=1))
+def dense_grads(both):
+    width = both.shape[1] // 3
+    both = exchanged(both)
     return (
         joined(both[:, :, :width]),
         joined(both[:, :, width : 2 * width]),
@@ -662,29 +795,35 @@
     )
 
 
-def gather_whole(part):
-    count = lax.axis_size("seq")
-    lanes = lax.all_gather(part, "seq", axis_index_groups=high_groups())
+def turns(position):
+    half_width = HD // 2
+    frequency = 10000.0 ** (-jnp.arange(half_width, dtype=jnp.float32) / half_width)
+    angle = position.astype(jnp.float32)[:, None] * frequency[None, :]
+    cosine, sine = (jnp.cos(angle), jnp.sin(angle))
+    return (
+        jnp.concatenate([cosine, cosine], axis=1),
+        jnp.concatenate([-sine, sine], axis=1),
+    )
+
+
+def both_lows(lanes):
     other = swap_low(lanes)
     lo = lax.rem(lax.axis_index("seq"), LO)
     both = jnp.stack([jnp.where(lo == 0, lanes, other), jnp.where(lo == 0, other, lanes)], axis=1)
-    return both.reshape(count * part.shape[0], part.shape[1])
-
-
-def reduce_whole(blocks):
-    count, rows, width = blocks.shape
+    return both.reshape(-1, lanes.shape[2])
+
+
+def dense_weights(wide):
+    width = wide.shape[1] // 3
+    return (wide[:, : 2 * width], wide[:, 2 * width :])
+
+
+def summed_low(both):
     lo = lax.rem(lax.axis_index("seq"), LO)
-    pairs = blocks.reshape(count // LO, LO, rows, width)
-    kept = jnp.where(lo == 0, pairs[:, 0], pairs[:, 1])
-    given = jnp.where(lo == 0, pairs[:, 1], pairs[:, 0])
-    total = lowered(kept.astype(jnp.float32) + swap_low(given).astype(jnp.float32))
-    return lax.psum_scatter(
-        total.reshape(-1, width),
-        "seq",
-        scatter_dimension=0,
-        tiled=True,
-        axis_index_groups=high_groups(),
-    )
+    both = both.reshape(LO, -1, both.shape[1])
+    kept = jnp.where(lo == 0, both[0], both[1])
+    given = jnp.where(lo == 0, both[1], both[0])
+    return kept.astype(jnp.float32) + swap_low(given).astype(jnp.float32)
 
 
 def local(
@@ -742,28 +881,31 @@
 
     gate_rows = recur_gate.shape[1]
     weight_rows = input_branch.shape[0]
-    ins = zip(split_columns(input_branch), split_columns(gate_branch))
-    gates = zip(split_columns(recur_gate.T), split_columns(input_gate.T))
-    first = gather_weight(
-        [
-            jnp.concatenate(
-                [jnp.concatenate(pair, axis=1), jnp.concatenate(gate, axis=1)], axis=0
-            )
-            for pair, gate in zip(ins, gates)
-        ]
-    ).reshape(high * LO, weight_rows + gate_rows, 2 * channels)
-    in_full = first[:, :weight_rows].reshape(-1, 2 * channels)
-    recur_full = first[:, weight_rows:, :channels].reshape(-1, channels)
-    input_gate_full = first[:, weight_rows:, channels:].reshape(-1, channels)
-    *weights_one, output_full = dense_weights(
-        dense_gate_one, dense_up_one, dense_down_one, recur_output.T
-    )
-
-    stream_in = lax.dynamic_slice_in_dim(tokens, tp * own_rows, own_rows, 0).astype(jnp.float32)
-    normed_one = gather(lowered(rms_norm(stream_in, norm_gains[0])), True, cid["gather_full"])
-    normed_one, query_weight, keyvalue_weight, attention_out = lax.optimization_barrier(
-        (normed_one, query_weight, keyvalue_weight, attention_out)
-    )
+    first = swap_columns(
+        jnp.concatenate([input_branch, recur_gate.T], axis=0),
+        jnp.concatenate([gate_branch, input_gate.T], axis=0),
+        jnp.concatenate([recur_output.T, jnp.zeros_like(recur_gate.T)], axis=0),
+    )
+    first_full = gather_high(first).reshape(high * LO, weight_rows + gate_rows, 3 * channels)
+    in_full = first_full[:, :weight_rows, : 2 * channels].reshape(-1, 2 * channels)
+    output_full = first_full[:, :weight_rows, 2 * channels :].reshape(-1, channels)
+    recur_full = first_full[:, weight_rows:, :channels].reshape(-1, channels)
+    input_gate_full = first_full[:, weight_rows:, channels : 2 * channels].reshape(-1, channels)
+    second = swap_columns(dense_gate_one, dense_up_one, dense_down_one.T)
+
+    own_tokens = lax.dynamic_slice_in_dim(tokens, tp * own_rows, own_rows, 0)
+    own_cotangent = lax.dynamic_slice_in_dim(cotangent, tp * own_rows, own_rows, 0)
+    stream_in = own_tokens.astype(jnp.float32)
+    grad_stream = own_cotangent.astype(jnp.float32) * valid[:, None]
+    normed_one, grad_low = gather(
+        [lowered(rms_norm(stream_in, norm_gains[0])), lowered(grad_stream)],
+        True,
+        cid["gather_two"],
+    )
+    normed_one, second, query_weight, keyvalue_weight, attention_out = lax.optimization_barrier(
+        (normed_one, second, query_weight, keyvalue_weight, attention_out)
+    )
+    weights_one = dense_weights(gather_high(second))
     both = product(normed_one, in_full)
     both, dense_gate_two, dense_up_two, dense_down_two = lax.optimization_barrier(
         (both, dense_gate_two, dense_up_two, dense_down_two)
@@ -781,15 +923,8 @@
             axis=0,
         )
     keyvalue_part = keyvalue_part.reshape(weight_rows, keyvalue_weight.shape[1])
-    third = gather_whole(
-        jnp.concatenate([query_weight, attention_out.T, keyvalue_part], axis=1)
-    )
-    query_width = query_weight.shape[1]
-    attn_width = attention_out.shape[0]
-    query_full = third[:, :query_width]
-    attn_full = third[:, query_width : query_width + attn_width]
-    keyvalue_full = third[:, query_width + attn_width :]
-    weights_two = dense_weights(dense_gate_two, dense_up_two, dense_down_two)
+    third = jnp.concatenate([query_weight, keyvalue_part, attention_out.T], axis=1)
+    fourth = swap_columns(dense_gate_two, dense_up_two, dense_down_two.T)
 
     branch = both[:, :channels]
     gating = both[:, channels:]
@@ -808,13 +943,27 @@
     state, state_in = plane_scan(decay, drive, ones, high, False, cid["scan"])
     gate_act, gate_pull = jax.vjp(jax.nn.gelu, gating)
     mixed = lowered(state * gate_act)
-    stream_one = stream_in + scatter(product_right(mixed, output_full), True, cid["scatter_full"])
-
-    dense_out, kept_one = dense_forward(stream_one, norm_gains[1], weights_one, cid)
-    stream_two = stream_one + dense_out
+    (summed,) = scatter([product_right(mixed, output_full)], True, cid["scatter_full"])
+    stream_one = stream_in + summed
+    (normed_two,) = gather([lowered(rms_norm(stream_one, norm_gains[1]))], True, cid["gather_full"])
+    normed_two, weights_one, third = lax.optimization_barrier((normed_two, weights_one, third))
+    third = lax.all_gather(third, "seq", axis_index_groups=high_groups())
+
+    partial, kept_one = dense_forward(normed_two, weights_one)
+    partial, fourth = lax.optimization_barrier((partial, fourth))
+    weights_two = dense_weights(gather_high(fourth))
+    query_width = query_weight.shape[1]
+    early_width = query_width + keyvalue_part.shape[1]
+    early_full = both_lows(third[:, :, :early_width])
+    query_full = early_full[:, :query_width]
+    keyvalue_full = early_full[:, query_width:]
+    attn_full = both_lows(third[:, :, early_width:])
+
+    (summed,) = scatter([partial], True, cid["scatter_full"])
+    stream_two = stream_one + summed
 
     normed_own = lowered(rms_norm(stream_two, norm_gains[2]))
-    normed_three = gather(normed_own, False, cid["gather_half"])
+    (normed_three,) = gather([normed_own], False, cid["gather_half"])
     query = product(normed_three, query_full)
     keyval = product(normed_three, keyvalue_full)
     local_heads = query.shape[1] // HD
@@ -844,90 +993,91 @@
     attended = lowered(
         jnp.einsum("hqk,kd->qhd", probs_low, values_ext, preferred_element_type=jnp.float32)
     ).reshape(shard_rows, local_heads * HD)
-    stream_three = stream_two + scatter(
-        product_right(attended, attn_full), False, cid["scatter_half"]
-    )
-
-    dense_out, kept_two = dense_forward(stream_three, norm_gains[3], weights_two, cid)
-    stream_four = stream_three + dense_out
-    out_own = lowered(stream_four * valid[:, None])
-    layer_out = gather(out_own, False, cid["gather_half"])
-
-    grad_stream = (
-        lax.dynamic_slice_in_dim(cotangent, tp * own_rows, own_rows, 0).astype(jnp.float32)
-        * valid[:, None]
-    )
-    grad_stream, gain_four, grad_both_two, grad_down_two = dense_backward(
-        stream_three, norm_gains[3], grad_stream, kept_two, weights_two, cid
-    )
-
-    done_two = dense_grads(grad_both_two, grad_down_two)
-    grad_attn_low = gather(lowered(grad_stream), False, cid["gather_half"])
+    (summed,) = scatter([product_right(attended, attn_full)], False, cid["scatter_half"])
+    stream_three = stream_two + summed
+
+    (normed_four,) = gather(
+        [lowered(rms_norm(stream_three, norm_gains[3]))], True, cid["gather_full"]
+    )
+    partial_four, kept_two = dense_forward(normed_four, weights_two)
+    grad_stream, gain_four, grad_both_two, grad_down_two, _ = dense_backward(
+        stream_three, norm_gains[3], grad_stream, grad_low, kept_two, weights_two, cid
+    )
+
+    done_two = reduce_high(jnp.concatenate([grad_both_two, grad_down_two], axis=1))
+    (grad_attn_low,) = gather([lowered(grad_stream)], False, cid["gather_half"])
     grad_attn_out = product_left(grad_attn_low, attended)
-    grad_attended = lowered(product(grad_attn_low, attn_full)).reshape(
-        shard_rows, local_heads, HD
-    )
-    scores = score_block(query_rot, keys_ext, allowed, score_scale)
-    probs = jnp.exp(scores - log_total)
-    grad_probs = jnp.einsum(
-        "qhd,kd->hqk", grad_attended, values_ext, preferred_element_type=jnp.float32
-    )
-    grad_scores = lowered(
-        probs * (grad_probs - jnp.sum(probs * grad_probs, axis=-1, keepdims=True)) * score_scale
-    )
-    grad_query_rot = jnp.einsum(
-        "hqk,kd->qhd", grad_scores, keys_ext, preferred_element_type=jnp.float32
-    )
-    grad_keys = jnp.einsum(
-        "hqk,qhd->kd", grad_scores, query_rot, preferred_element_type=jnp.float32
-    )
-    grad_values = jnp.einsum(
-        "hqk,qhd->kd", lowered(probs), grad_attended, preferred_element_type=jnp.float32
-    )
-    grad_ext = jnp.concatenate([grad_keys, grad_values], axis=1)
-    grad_own = grad_ext[halo_shards * shard_rows :]
-    for offset in range(1, halo_shards + 1):
-        grad_piece = grad_ext[
-            (halo_shards - offset) * shard_rows : (halo_shards - offset + 1) * shard_rows
-        ]
-        grad_own = grad_own + shifted(lowered(grad_piece), -offset).astype(jnp.float32)
-    key_pre_grad = jax.vjp(rotate_here, keyval[:, :HD])[1](grad_own[:, :HD])[0]
-    query_pre_grad = jax.vjp(rotate_here, query_heads)[1](grad_query_rot)[0]
-    grad_query_low = lowered(query_pre_grad).reshape(shard_rows, local_heads * HD)
-    keyvalue_partial = jnp.concatenate([key_pre_grad, grad_own[:, HD:]], axis=1)
+    grad_attended = lowered(product(grad_attn_low, attn_full))
+    grad_query_low, grad_ext = attention_back(
+        query_rot.reshape(shard_rows, local_heads * HD),
+        extended,
+        grad_attended,
+        log_total[:, :, 0],
+        segment,
+        key_segment,
+        *turns(position),
+    )
     grad_query = product_left(normed_three, grad_query_low)
-    partial = lowered(
-        jnp.concatenate([product_right(grad_query_low, query_full), keyvalue_partial], axis=1)
+    grad_pieces = grad_ext.reshape(halo_shards + 1, shard_rows, 2 * HD)
+    partial = jnp.concatenate(
+        [lowered(product_right(grad_query_low, query_full))] + list(grad_pieces), axis=1
     )
     partial, grad_query, grad_attn_out = lax.optimization_barrier(
         (partial, lowered(grad_query), lowered(grad_attn_out))
     )
-    summed = scatter(partial, False, cid["scatter_wide"])
+    attn_wire = jnp.concatenate([grad_query, grad_attn_out], axis=1)
+    (summed,) = scatter([partial], False, cid["scatter_wide"])
+    summed, partial_four = lax.optimization_barrier((summed, partial_four))
+    (summed_four,) = scatter([partial_four], True, cid["scatter_full"])
     width = normed_own.shape[1]
-    keyvalue_low = lowered(summed[:, width:])
+    pieces = [
+        summed[:, width + 2 * HD * k : width + 2 * HD * (k + 1)] for k in range(halo_shards + 1)
+    ]
+    keyvalue_total = pieces[halo_shards]
+    for offset in range(1, halo_shards + 1):
+        piece = shifted(lowered(pieces[halo_shards - offset]), -offset)
+        keyvalue_total = keyvalue_total + piece.astype(jnp.float32)
+    keyvalue_total, attn_wire, done_two, summed_four = lax.optimization_barrier(
+        (keyvalue_total, attn_wire, done_two, summed_four)
+    )
+    done_attn = reduce_high(attn_wire)
+    own_position = lax.dynamic_slice_in_dim(position, tp * own_rows, own_rows, 0)
+    rotate_own = functools.partial(rotate, position=own_position)
+    key_grad = jax.vjp(rotate_own, keyvalue_total[:, :HD])[1](keyvalue_total[:, :HD])[0]
+    keyvalue_low = lowered(jnp.concatenate([key_grad, keyvalue_total[:, HD:]], axis=1))
     grad_normed = summed[:, :width] + product_right(keyvalue_low, keyvalue_full)
-    keyvalue_grads = gather(keyvalue_low, False, cid["gather_narrow"])
+    (keyvalue_grads,) = gather([keyvalue_low], False, cid["gather_narrow"])
     part_rows = keyvalue_weight.shape[0]
     ways_view = normed_three.reshape(shard_rows, high * LO, ways, part_rows)
     ours_only = lax.dynamic_slice_in_dim(ways_view, tp, 1, 2).reshape(shard_rows, -1)
     grad_keyvalue = lowered(product_left(ours_only, keyvalue_grads))
-    attn_wire = jnp.concatenate([grad_query, grad_attn_out], axis=1)
-    attn_wire = attn_wire.reshape(high * LO, weight_rows, attn_wire.shape[1])
-    keyvalue_wire = grad_keyvalue.reshape(high * LO, -1, attn_wire.shape[2])
-    done_attn = reduce_whole(jnp.concatenate([attn_wire, keyvalue_wire], axis=1))
     stream_grad, gain_three = jax.vjp(rms_norm, stream_two, norm_gains[2])[1](grad_normed)
     grad_stream = grad_stream + stream_grad
 
-    grad_stream, gain_two, grad_both_one, grad_down_one = dense_backward(
-        stream_one, norm_gains[1], grad_stream, kept_one, weights_one, cid
-    )
-
-    done_one = dense_grads(grad_both_one, grad_down_one)
-    grad_stream, done_two = lax.optimization_barrier((grad_stream, done_two))
-    grad_out_low = gather(lowered(grad_stream), True, cid["gather_full"])
+    (grad_low,) = gather([lowered(grad_stream)], True, cid["gather_full"])
+    grad_low, done_two = lax.optimization_barrier((grad_low, done_two))
+    done_two = dense_grads(done_two)
+    grad_stream, gain_two, grad_both_one, grad_down_one, done_attn = dense_backward(
+        stream_one,
+        norm_gains[1],
+        grad_stream,
+        grad_low,
+        kept_one,
+        weights_one,
+        cid,
+        done_attn,
+    )
+
+    one_wire = jnp.concatenate([grad_both_one, grad_down_one], axis=1)
+    grad_stream, one_wire, done_attn = lax.optimization_barrier(
+        (grad_stream, one_wire, done_attn)
+    )
+    done_one = reduce_high(one_wire)
+    (grad_out_low,) = gather([lowered(grad_stream)], True, cid["gather_full"])
     grad_recur_out = product_left(grad_out_low, mixed)
     grad_mixed = product(grad_out_low, output_full)
-    grad_mixed, done_attn = lax.optimization_barrier((grad_mixed, done_attn))
+    grad_mixed, done_attn, done_two = lax.optimization_barrier((grad_mixed, done_attn, done_two))
+    done_attn = summed_low(done_attn)
     grad_state = grad_mixed * gate_act
     grad_gating = lowered(gate_pull(grad_mixed * state)[0])
     decay_next = jnp.concatenate([decay[1:], jnp.ones((1, channels), jnp.float32)], axis=0)
@@ -955,22 +1105,39 @@
     partial, grad_in, grad_recur_out = lax.optimization_barrier(
         (partial, lowered(grad_in), lowered(grad_recur_out))
     )
-    grad_normed = scatter(partial, True, cid["scatter_full"])
-    stream_grad, gain_one = jax.vjp(rms_norm, stream_in, norm_gains[0])[1](grad_normed)
-    input_own = grad_stream + stream_grad
-    input_grad = gather(lowered(input_own), False, cid["gather_half"]).astype(jnp.float32)
-
-    in_grad = reduce_weight(grad_in)
-    rest_grad = jnp.concatenate(
+    blocks = high * LO
+    wire = jnp.concatenate(
         [
-            grad_recur_out.reshape(high * LO, weight_rows, channels),
-            lowered(grad_recur_gate).reshape(high * LO, gate_rows, channels),
-            lowered(grad_input_gate).reshape(high * LO, gate_rows, channels),
+            jnp.concatenate(
+                [
+                    grad_in.reshape(blocks, weight_rows, 2 * channels),
+                    grad_recur_out.reshape(blocks, weight_rows, channels),
+                ],
+                axis=2,
+            ),
+            jnp.concatenate(
+                [
+                    lowered(grad_recur_gate).reshape(blocks, gate_rows, channels),
+                    lowered(grad_input_gate).reshape(blocks, gate_rows, channels),
+                    jnp.zeros((blocks, gate_rows, channels), jnp.bfloat16),
+                ],
+                axis=2,
+            ),
+            grad_keyvalue.reshape(blocks, -1, 3 * channels),
         ],
         axis=1,
     )
-    rest_grad = joined(reduce_weight(rest_grad.reshape(-1, channels))).T
-    gains_sum, small = small_sums(
+    layer_own = lowered((stream_three + summed_four) * valid[:, None])
+    layer_own, both_low = lax.optimization_barrier((layer_own, both_low))
+    (layer_out,) = gather([layer_own], False, cid["gather_half"])
+    wire, done_one, layer_out = lax.optimization_barrier((wire, done_one, layer_out))
+    last = exchanged(reduce_high(wire.reshape(-1, 3 * channels)))
+    keyvalue_grad = jnp.sum(last[:, weight_rows + gate_rows :].astype(jnp.float32), axis=0)
+    last_rows, last_gates = (last[:, :weight_rows], last[:, weight_rows : weight_rows + gate_rows])
+    gain_one = jnp.sum(normed_one.astype(jnp.float32) * partial.astype(jnp.float32), axis=0)
+    gain_one = gain_one / norm_gains[0]
+    grad_normed, gains_sum, small = scatter_and_sums(
+        partial,
         jnp.concatenate(
             [jnp.stack([gain_one, gain_two, gain_three, gain_four]), jnp.zeros_like(norm_gains)]
         ),
@@ -978,26 +1145,30 @@
             [grad_taps, grad_conv_bias[None], grad_biases, grad_decay_param[None]], axis=0
         ),
         high,
-        cid["small_sums"],
-    )
+        cid["last"],
+    )
+    rms_local = functools.partial(rms_norm, gain=norm_gains[0])
+    stream_grad = jax.vjp(rms_local, stream_in)[1](grad_normed)[0]
+    (input_grad,) = gather([lowered(grad_stream + stream_grad)], False, cid["gather_half"])
     gains_sum = gains_sum[: norm_gains.shape[0]]
+    input_grad = input_grad.astype(jnp.float32)
     return (
         layer_out,
         input_grad,
         gains_sum,
-        joined(in_grad[:, :, :channels]),
-        joined(in_grad[:, :, channels:]),
+        joined(last_rows[:, :, :channels]),
+        joined(last_rows[:, :, channels : 2 * channels]),
         small[:CONV],
         small[CONV],
-        rest_grad[:, weight_rows : weight_rows + gate_rows],
-        rest_grad[:, weight_rows + gate_rows :],
+        joined(last_gates[:, :, :channels]).T,
+        joined(last_gates[:, :, channels : 2 * channels]).T,
         small[CONV + 1 : CONV + 3],
         small[CONV + 3],
-        rest_grad[:, :weight_rows],
-        *done_one,
-        done_attn[:weight_rows, :query_width].astype(jnp.float32),
-        done_attn[weight_rows:].reshape(keyvalue_weight.shape).astype(jnp.float32),
-        done_attn[:weight_rows, query_width:].astype(jnp.float32).T,
+        joined(last_rows[:, :, 2 * channels :]).T,
+        *dense_grads(done_one),
+        done_attn[:, :query_width],
+        keyvalue_grad.reshape(keyvalue_weight.shape),
+        done_attn[:, query_width:].T,
         *done_two,
     )
 

time: 844 us -> 774 us (0.917)
  matrix products: 152 us -> 99.7 us
  waiting for transfers between devices: 119 us -> 90.8 us
  local copies, waits for them, and re-layouts: 41.7 us -> 64.5 us
  Pallas kernels: 386 us -> 368 us
  other arithmetic: 88.2 us -> 97.1 us
    dot_general x4 -> x0, matrix products: 38.8 us -> none  [the longest x1 14.2 us: local(): jnp.einsum('hqk,kd->qhd', grad_scores, keys_ext, preferred_element_type=j...]
    pallas_call x20 -> x19, Pallas kernels: 364 us -> 337 us  [the longest x10 183 us: gather(): pl.pallas_call(functools.partial(gather_kernel, full, count), out_shape=[...]
    ppermute x11 -> x9, waiting for transfers between devices: 56.6 us -> 42.1 us  [swap_low(): lax.ppermute(block, 'seq', [(s, s // LO * LO + (1 - s % LO)) for s in ran...]
    ppermute x6, waiting for transfers between devices: 13.3 us -> 0.45 us  [shifted(): return lax.ppermute(block, 'seq', route)]
    slice x8 -> x9, local copies, waits for them, and re-layouts: 5.41 us -> 14.8 us  [the longest x2 7.18 us: dense_weights(): return (wide[:, :2 * width], wide[:, 2 * width:])]
    pallas_call x2, Pallas kernels: 22.1 us -> 31.4 us  [plane_scan(): pl.pallas_call(functools.partial(scan_kernel, high, reverse), out_shape=(...]
    unnamed x301 -> x345, local copies, waits for them, and re-layouts: 15.5 us -> 19.5 us
    all_gather x6 -> x4, waiting for transfers between devices: 24.9 us -> 27.6 us  [the longest x3 27.6 us: gather_high(): lax.all_gather(rows, 'seq', axis=0, tiled=True, axis_index_groups=high_gr...]
  transfers between devices with their start and end apart: 30 -> 25, of which waited for: 14 -> 11; matrix products, arithmetic and copies ran while one was open for 29% -> 26% of each run, Pallas kernels for 46% -> 46%
where the time goes in v2:
time: 774 us; the launch traced here: 765 us
  Pallas kernels  368 us (48%)
  matrix products  99.7 us (13%)
  other arithmetic  97.1 us (13%)
  waiting for transfers between devices  90.8 us (12%)
  local copies, waits for them, and re-layouts  64.5 us (8%)
  starting transfers between devices  27.5 us (4%)
  between operations  17.5 us (2%)
    pallas_call x10, Pallas kernels, gather(): pl.pallas_call(functools.partial(gather_kernel, full, count), out_shape=[...  183 us
    pallas_call x7, Pallas kernels, scatter(): pl.pallas_call(functools.partial(scatter_kernel, full, count), out_shape=...  121 us
    ppermute x9, waiting for transfers between devices, swap_low(): lax.ppermute(block, 'seq', [(s, s // LO * LO + (1 - s % LO)) for s in ran...  42.1 us
    dot_general x13, matrix products, product(): return jnp.dot(left, right, preferred_element_type=jnp.float32)  38.5 us
    pallas_call x2, Pallas kernels, plane_scan(): pl.pallas_call(functools.partial(scan_kernel, high, reverse), out_shape=(...  31.4 us
    dot_general x13, matrix products, product_right(): lax.dot_general(left, right, (((1,), (1,)), ((), ())), preferred_element_...  28.8 us
    all_gather x3, waiting for transfers between devices, gather_high(): lax.all_gather(rows, 'seq', axis=0, tiled=True, axis_index_groups=high_gr...  27.6 us
    dot_general x13, matrix products, product_left(): lax.dot_general(left, right, (((0,), (0,)), ((), ())), preferred_element_...  27.2 us
  transfers between devices with their start and end apart: 25, of which 11 were waited for; matrix products, arithmetic and copies ran while one was open for 26% of the time, Pallas kernels for 46%

profile of v2, /device:TPU:0, one launch (start us, length us, event | category | flops | bytes accessed | tf_op | source)
XLA Modules:
  0.0 765.4 jit_solution(1697330669759719350)
XLA Ops:
  11.2 2.9 collective-permute-start.1
  16.5 5.5 collective-permute-done.1
  30.9 38.3 %gather_full.5 = (bf16[8,128,1536]{2,1,0:T(8,128)(2,1)}, bf16[8,128,1536]{2,1,0:T(8,128)(2,1)}) custom-call(bf16[128,1536]{1,0:T(8,128)(2,1)} %fusion.62.refs_0_, bf16[128,1536]{1,0:T(8,128)(2,1)} %fusion.64.refs_1_), custom_call_target="tpu_custom_call" | custom-call | bytes 60000000 | tf_op jit(solution)/shard_map/gather_full/pallas_call | solution.py:238
  83.7 4.3 fusion.169
  88.0 3.7 collective-permute-start.2
  106.0 10.6 %scan.1 = (f32[1024,256]{1,0:T(8,128)S(1)}, f32[8,256]{1,0:T(8,128)S(1)}) custom-call(f32[1024,256]{1,0:T(8,128)S(1)} %get-tuple-element.203.decay_ref, f32[1024,256]{1,0:T(8,128)S(1)} %get-tuple-element.202.drive_ref, f32[8,256]{1,0:T(8,128)S(1)} %broadcast_in_dim.79.end_ref), custom_call_target="tpu_custom_call" | custom-call | bytes 33000000 | tf_op jit(solution)/shard_map/scan/pallas_call | solution.py:476
  118.1 17.1 %scatter_full.5 = f32[128,1536]{1,0:T(8,128)S(1)} custom-call(bf16[8,128,1536]{2,1,0:T(8,128)(2,1)S(1)} %bitcast.230), custom_call_target="tpu_custom_call" | custom-call | bytes 60000000 | tf_op jit(solution)/shard_map/scatter_full/pallas_call | solution.py:389
  137.4 18.5 %gather_full.6 = bf16[8,128,1536]{2,1,0:T(8,128)(2,1)} custom-call(bf16[128,1536]{1,0:T(8,128)(2,1)} %multiply_convert_fusion.8.refs_0_), custom_call_target="tpu_custom_call" | custom-call | bytes 60000000 | tf_op jit(solution)/shard_map/gather_full/pallas_call | solution.py:238
  155.9 27.6 %all-gather.8.cloned.1.call-done = bf16[1536,1728]{1,0:T(8,128)(2,1)} async-done(((bf16[384,1728]{1,0:T(8,128)(2,1)}), bf16[1536,1728]{1,0:T(8,128)(2,1)}) %all-gather.8.cloned.1.call-update) | async-done | bytes 5308432 | tf_op jit(solution)/shard_map/all_gather | solution.py:686
  183.5 4.0 slice.622
  187.6 3.1 slice.623
  194.0 6.2 fusion.170
  200.2 2.2 copy-done.41
  203.9 4.0 convolution_convert_fusion.3
  209.9 18.4 %scatter_full.6 = f32[128,1536]{1,0:T(8,128)S(1)} custom-call(bf16[8,128,1536]{2,1,0:T(8,128)(2,1)S(1)} %bitcast.238), custom_call_target="tpu_custom_call" | custom-call | bytes 60000000 | tf_op jit(solution)/shard_map/scatter_full/pallas_call | solution.py:389
  230.0 2.2 slice.629
  235.1 13.8 %gather_half.5 = bf16[4,128,1536]{2,1,0:T(8,128)(2,1)} custom-call(bf16[128,1536]{1,0:T(8,128)(2,1)} %multiply_convert_fusion.7.refs_0_), custom_call_target="tpu_custom_call" | custom-call | bytes 60000000 | tf_op jit(solution)/shard_map/gather_half/pallas_call | solution.py:238
  251.5 17.3 %collective-permute-done.6 = bf16[4,192,640]{2,1,0:T(8,128)(2,1)} collective-permute-done((bf16[4,192,640]{2,1,0:T(8,128)(2,1)}, bf16[4,192,640]{2,1,0:T(8,128)(2,1)}, u32[]{:S(2)}, u32[]{:S(2)}) %collective-permute-start.6) | collective-permute-done | bytes 983072 | tf_op jit(solution)/shard_map/ppermute | solution.py:668
  277.6 3.3 collective-permute-start.8
  282.1 2.5 copy.132
  284.6 3.5 fusion.171
  292.9 2.1 fusion
  295.1 3.3 fusion.25
  299.4 13.1 %scatter_half.2 = f32[128,1536]{1,0:T(8,128)S(1)} custom-call(bf16[4,128,1536]{2,1,0:T(8,128)(2,1)S(1)} %bitcast.234), custom_call_target="tpu_custom_call" | custom-call | bytes 60000000 | tf_op jit(solution)/shard_map/scatter_half/pallas_call | solution.py:389
  314.7 27.5 %gather_full.7 = bf16[8,128,1536]{2,1,0:T(8,128)(2,1)} custom-call(bf16[128,1536]{1,0:T(8,128)(2,1)} %multiply_convert_fusion.6.refs_0_), custom_call_target="tpu_custom_call" | custom-call | bytes 60000000 | tf_op jit(solution)/shard_map/gather_full/pallas_call | solution.py:238
  342.2 7.3 fusion.6
  349.6 4.0 fusion.21
  353.6 2.7 convolution_convert_fusion.9
  356.3 5.1 convolution_convert_fusion.1
  361.4 5.8 convolution_convert_fusion.7
  367.2 2.8 pad_maximum_fusion
  377.1 17.8 %scatter_full.7 = f32[128,1536]{1,0:T(8,128)S(1)} custom-call(bf16[8,128,1536]{2,1,0:T(8,128)(2,1)S(1)} %bitcast.235), custom_call_target="tpu_custom_call" | custom-call | bytes 60000000 | tf_op jit(solution)/shard_map/scatter_full/pallas_call | solution.py:389
  395.7 2.3 fusion.152
  398.0 14.4 %gather_half.6 = bf16[4,128,1536]{2,1,0:T(8,128)(2,1)} custom-call(bf16[128,1536]{1,0:T(8,128)(2,1)} %get-tuple-element.162.refs_0_), custom_call_target="tpu_custom_call" | custom-call | bytes 60000000 | tf_op jit(solution)/shard_map/gather_half/pallas_call | solution.py:238
  412.4 2.7 convolution_convert_fusion.16.grad_ref
  415.2 10.3 %attention_back.1 = (bf16[512,384]{1,0:T(8,128)(2,1)S(1)}, bf16[1536,256]{1,0:T(8,128)(2,1)S(1)}) custom-call(bf16[512,384]{1,0:T(8,128)(2,1)S(1)} %copy.143.query_ref, bf16[1536,256]{1,0:T(8,128)(2,1)S(1)} %maximum_maximum_fusion.ext_ref, bf16[512,384]{1,0:T(8,128)(2,1)S(1)} %convolution_convert_fusion.16.grad_ref, f32[8,512]{1,0:T(8,128)S(1)} %concatenate.186.log_ref, ...), custom_call_target="tpu_custom_call" | custom-call | bytes 60000000 | tf_op jit(solution)/shard_map/attention_back/pallas_call | solution.py:637
  429.8 16.6 %scatter_half.3 = f32[128,2304]{1,0:T(8,128)S(1)} custom-call(bf16[4,128,2304]{2,1,0:T(8,128)(2,1)S(1)} %bitcast.232), custom_call_target="tpu_custom_call" | custom-call | bytes 60000000 | tf_op jit(solution)/shard_map/scatter_half/pallas_call | solution.py:389
  446.5 5.6 convolution_convert_fusion.2
  458.2 19.8 %scatter_full.8 = f32[128,1536]{1,0:T(8,128)S(1)} custom-call(bf16[8,128,1536]{2,1,0:T(8,128)(2,1)S(1)} %bitcast.236), custom_call_target="tpu_custom_call" | custom-call | bytes 60000000 | tf_op jit(solution)/shard_map/scatter_full/pallas_call | solution.py:389
  478.9 4.5 reduce-scatter.5.cloned.1.call-done
  485.1 3.9 copy.151
  489.1 3.7 reshape_reshape.3
  498.0 17.7 %gather_full.8 = bf16[8,128,1536]{2,1,0:T(8,128)(2,1)} custom-call(bf16[128,1536]{1,0:T(8,128)(2,1)} %get-tuple-element.160.refs_0_), custom_call_target="tpu_custom_call" | custom-call | bytes 60000000 | tf_op jit(solution)/shard_map/gather_full/pallas_call | solution.py:238
  515.8 6.0 convolution_convert_fusion.8
  521.9 6.1 fusion.14
  528.0 6.1 convolution_convert_fusion
  534.0 6.0 convolution_convert_fusion.6
  543.8 17.9 %scatter_full.9 = f32[128,1536]{1,0:T(8,128)S(1)} custom-call(bf16[8,128,1536]{2,1,0:T(8,128)(2,1)S(1)} %bitcast.237), custom_call_target="tpu_custom_call" | custom-call | bytes 60000000 | tf_op jit(solution)/shard_map/scatter_full/pallas_call | solution.py:389
  561.9 2.9 pad_maximum_fusion.1
  566.2 2.6 broadcast_select_fusion.2
  571.0 13.9 %gather_half.8 = bf16[4,128,1536]{2,1,0:T(8,128)(2,1)} custom-call(bf16[128,1536]{1,0:T(8,128)(2,1)} %multiply_convert_fusion.5.refs_0_), custom_call_target="tpu_custom_call" | custom-call | bytes 60000000 | tf_op jit(solution)/shard_map/gather_half/pallas_call | solution.py:238
  585.6 6.0 gather_half.7
  599.0 17.9 %gather_full.9 = bf16[8,128,1536]{2,1,0:T(8,128)(2,1)} custom-call(bf16[128,1536]{1,0:T(8,128)(2,1)} %convert_element_type.299.refs_0_), custom_call_target="tpu_custom_call" | custom-call | bytes 60000000 | tf_op jit(solution)/shard_map/gather_full/pallas_call | solution.py:238
  616.8 3.1 fusion.172
  620.9 20.8 %scan_back.1 = (f32[1024,256]{1,0:T(8,128)S(1)}, f32[8,256]{1,0:T(8,128)}) custom-call(f32[1024,256]{1,0:T(8,128)S(1)} %concatenate.176.decay_ref, f32[1024,256]{1,0:T(8,128)S(1)} %get-tuple-element.185.drive_ref, f32[8,256]{1,0:T(8,128)S(1)} %broadcast_in_dim.92.end_ref), custom_call_target="tpu_custom_call" | custom-call | bytes 33000000 | tf_op jit(solution)/shard_map/scan_back/pallas_call | solution.py:476
  641.8 2.9 fusion.147
  646.5 2.3 multiply_reduce_fusion.5
  661.3 11.8 %reduce-scatter.9.cloned.1.call-done = bf16[384,1728]{1,0:T(8,128)(2,1)} async-done(((bf16[1536,1728]{1,0:T(8,128)(2,1)}), bf16[384,1728]{1,0:T(8,128)(2,1)}) %reduce-scatter.9.cloned.1.call-update) | async-done | bytes 1327120 | tf_op jit(solution)/shard_map/reduce_scatter | solution.py:690
  676.5 2.8 multiply_reduce_fusion
  680.2 22.9 %scatter_and_sums.1 = (f32[128,1536]{1,0:T(8,128)S(1)}, f32[8,1536]{1,0:T(8,128)S(1)}, f32[8,512]{1,0:T(8,128)S(1)}) custom-call(bf16[8,128,1536]{2,1,0:T(8,128)(2,1)S(1)} %bitcast.231, f32[8,1536]{1,0:T(8,128)S(1)} %concatenate.209.gains_ref, f32[8,256]{1,0:T(8,128)S(1)} %pad_maximum_fusion.28.rest_ref), custom_call_target="tpu_custom_call" | custom-call | bytes 60000000 | tf_op jit(solution)/shard_map/scatter_and_sums/pallas_call | solution.py:559
  705.5 14.9 %gather_half.9 = bf16[4,128,1536]{2,1,0:T(8,128)(2,1)} custom-call(bf16[128,1536]{1,0:T(8,128)(2,1)} %fusion.59.refs_0_), custom_call_target="tpu_custom_call" | custom-call | bytes 60000000 | tf_op jit(solution)/shard_map/gather_half/pallas_call | solution.py:238
  721.1 3.6 bitcast_convert_fusion
  727.6 13.9 %collective-permute-done.15 = bf16[192,1728]{1,0:T(8,128)(2,1)S(1)} collective-permute-done((bf16[192,1728]{1,0:T(8,128)(2,1)S(1)}, bf16[192,1728]{1,0:T(8,128)(2,1)S(1)}, u32[]{:S(2)}, u32[]{:S(2)}) %collective-permute-start.15) | collective-permute-done | bytes 663584 | tf_op jit(solution)/shard_map/ppermute | solution.py:668
  747.3 5.4 collective-permute-done.14
  (591 shorter events, 156.1 us)
Async XLA Ops:
  7.2 74.9 %all-gather.6.cloned.1.call-start = ((), (), s32[]{:S(2)}) async-start(), calls=%async_computation.4 | async-start | bytes 3194880 | tf_op jit(solution)/shard_map/all_gather | solution.py:686
  11.2 10.8 %collective-permute-start.1 = (bf16[208,768]{1,0:T(8,128)(2,1)}, bf16[208,768]{1,0:T(8,128)(2,1)}, u32[]{:S(2)}, u32[]{:S(2)}) collective-permute-start(bf16[208,768]{1,0:T(8,128)(2,1)} %broadcast_select_fusion.10), channel_id=1, source_target_pairs={{0,4},{4,0},{8,12},{12,8},{16,20},{20,16},{24,28},{28,24},{1,5},{5... | collective-permute-start | bytes 958472 | tf_op jit(solution)/shard_map/ppermute | solution.py:668
  24.1 45.2 %copy-start.153 = (f32[4,512]{1,0:T(4,128)S(1)}, f32[4,512]{1,0:T(4,128)}, u32[]{:S(2)}) copy-start(f32[4,512]{1,0:T(4,128)} %param.28) | copy-start | bytes 24580
  24.1 45.2 %copy-start.156 = (f32[2,512]{1,0:T(2,128)S(1)}, f32[2,512]{1,0:T(2,128)}, u32[]{:S(2)}) copy-start(f32[2,512]{1,0:T(2,128)} %param.32) | copy-start | bytes 12292
  24.1 159.4 %all-gather.8.cloned.1.call-start = ((), (), s32[]{:S(2)}) async-start(), calls=%async_computation.5 | async-start | bytes 6881280 | tf_op jit(solution)/shard_map/all_gather | solution.py:686
  25.1 45.9 %collective-permute-start = (bf16[192,1728]{1,0:T(8,128)(2,1)}, bf16[192,1728]{1,0:T(8,128)(2,1)}, u32[]{:S(2)}, u32[]{:S(2)}) collective-permute-start(bf16[192,1728]{1,0:T(8,128)(2,1)} %broadcast_select_fusion.6), channel_id=1, source_target_pairs={{0,4},{4,0},{8,12},{12,8},{16,20},{20,16},{24,28},{28,24},{1,5},{5... | collective-permute-start | bytes 1990664 | tf_op jit(solution)/shard_map/ppermute | solution.py:668
  27.8 41.4 %copy-start.157 = (f32[128]{0:T(128)}, f32[128]{0:T(128)S(1)}, u32[]{:S(2)}) copy-start(f32[128]{0:T(128)S(1)} %fusion.60) | copy-start | bytes 1540
  28.0 108.4 %copy-start.100 = (f32[1536]{0:T(1024)}, f32[1536]{0:T(1024)S(1)}, u32[]{:S(2)}) copy-start(f32[1536]{0:T(1024)S(1)} %get-tuple-element.151) | copy-start | bytes 18436
  28.0 206.2 %copy-start.102 = (f32[1536]{0:T(1024)}, f32[1536]{0:T(1024)S(1)}, u32[]{:S(2)}) copy-start(f32[1536]{0:T(1024)S(1)} %get-tuple-element.153) | copy-start | bytes 18436
  28.0 285.2 %copy-start.104 = (f32[1536]{0:T(1024)}, f32[1536]{0:T(1024)S(1)}, u32[]{:S(2)}) copy-start(f32[1536]{0:T(1024)S(1)} %get-tuple-element.150) | copy-start | bytes 18436
  28.1 41.9 %copy-start.144 = (f32[128]{0:T(128)}, f32[128]{0:T(128)S(1)}, u32[]{:S(2)}) copy-start(f32[128]{0:T(128)S(1)} %compare_convert_fusion.2) | copy-start | bytes 1540
  28.1 41.9 %copy-start.149 = (f32[128]{0:T(128)}, f32[128]{0:T(128)S(1)}, u32[]{:S(2)}) copy-start(f32[128]{0:T(128)S(1)} %fusion.136) | copy-start | bytes 1540
  70.0 34.7 %copy-start.119 = (f32[1,256]{1,0:T(1,128)}, f32[1,256]{1,0:T(1,128)S(1)}, u32[]{:S(2)}) copy-start(f32[1,256]{1,0:T(1,128)S(1)} %get-tuple-element.285) | copy-start | bytes 3076
  73.5 155.1 %all-gather.12.cloned.1.call-start = ((), (), s32[]{:S(2)}) async-start(), calls=%async_computation.11 | async-start | bytes 1966080 | tf_op jit(solution)/shard_map/all_gather | solution.py:950
  73.6 31.1 %copy-start.113 = (f32[1024]{0:T(1024)}, f32[1024]{0:T(1024)S(1)}, u32[]{:S(2)}) copy-start(f32[1024]{0:T(1024)S(1)} %compare_convert_fusion.1) | copy-start | bytes 12292
  73.7 29.0 %copy-start.106 = (f32[1024]{0:T(1024)}, f32[1024]{0:T(1024)S(1)}, u32[]{:S(2)}) copy-start(f32[1024]{0:T(1024)S(1)} %get-tuple-element.269) | copy-start | bytes 12292
  73.7 29.0 %copy-start.108 = (f32[1024]{0:T(1024)}, f32[1024]{0:T(1024)S(1)}, u32[]{:S(2)}) copy-start(f32[1024]{0:T(1024)S(1)} %get-tuple-element.270) | copy-start | bytes 12292
  73.7 29.0 %copy-start.110 = (f32[1024]{0:T(1024)}, f32[1024]{0:T(1024)S(1)}, u32[]{:S(2)}) copy-start(f32[1024]{0:T(1024)S(1)} %get-tuple-element.271) | copy-start | bytes 12292
  75.8 1.2 collective-permute-start.3
  76.8 27.9 %copy-start.128 = (f32[256]{0:T(256)}, f32[256]{0:T(256)S(1)}, u32[]{:S(2)}) copy-start(f32[256]{0:T(256)S(1)} %get-tuple-element.174) | copy-start | bytes 3076
  77.1 4.2 collective-permute-start.4
  87.9 28.7 %copy-start.24 = (f32[1024,512]{1,0:T(8,128)}, f32[1024,512]{1,0:T(8,128)S(1)}, u32[]{:S(2)}) copy-start(f32[1024,512]{1,0:T(8,128)S(1)} %fusion.169) | copy-start | bytes 6291460
  88.0 14.7 %collective-permute-start.2 = (f32[3,256]{1,0:T(4,128)S(1)}, f32[3,256]{1,0:T(4,128)S(1)}, u32[]{:S(2)}, u32[]{:S(2)}) collective-permute-start(f32[3,256]{1,0:T(4,128)S(1)} %slice.498), channel_id=1, source_target_pairs={{0,8},{4,12},{8,16},{12,20},{16,24},{20,28},{1,9},{5,13},{9,17},{1... | collective-permute-start | bytes 9224 | tf_op jit(solution)/shard_map/ppermute | solution.py:765
  102.2 89.1 %collective-permute-start.5 = (bf16[192,1728]{1,0:T(8,128)(2,1)}, bf16[192,1728]{1,0:T(8,128)(2,1)}, u32[]{:S(2)}, u32[]{:S(2)}) collective-permute-start(bf16[192,1728]{1,0:T(8,128)(2,1)} %broadcast_select_fusion.4), channel_id=1, source_target_pairs={{0,4},{4,0},{8,12},{12,8},{16,20},{20,16},{24,28},{28,24},{1,5},{5... | collective-permute-start | bytes 1990664 | tf_op jit(solution)/shard_map/ppermute | solution.py:668
  136.4 51.1 %copy-start.159 = (f32[128]{0:T(128)}, f32[128]{0:T(128)S(1)}, u32[]{:S(2)}) copy-start(f32[128]{0:T(128)S(1)} %get-tuple-element.170) | copy-start | bytes 1540
  136.4 91.9 %copy-start.9 = (f32[128,1536]{1,0:T(8,128)}, f32[128,1536]{1,0:T(8,128)S(1)}, u32[]{:S(2)}) copy-start(f32[128,1536]{1,0:T(8,128)S(1)} %get-tuple-element.171) | copy-start | bytes 2359300
  136.5 51.1 %copy-start.140 = (f32[128]{0:T(128)}, f32[128]{0:T(128)S(1)}, u32[]{:S(2)}) copy-start(f32[128]{0:T(128)S(1)} %fusion.137) | copy-start | bytes 1540
  190.7 151.5 %all-gather.10.cloned.1.call-start = ((), (), s32[]{:S(2)}) async-start(), calls=%async_computation.6 | async-start | bytes 6881280 | tf_op jit(solution)/shard_map/all_gather | solution.py:686
  228.3 255.1 %reduce-scatter.5.cloned.1.call-start = ((), (), s32[]{:S(2)}) async-start(), calls=%async_computation.7 | async-start | bytes 6881280 | tf_op jit(solution)/shard_map/reduce_scatter | solution.py:690
  228.6 84.0 %copy-start.14 = (f32[128,1536]{1,0:T(8,128)}, f32[128,1536]{1,0:T(8,128)S(1)}, u32[]{:S(2)}) copy-start(f32[128,1536]{1,0:T(8,128)S(1)} %get-tuple-element.169) | copy-start | bytes 2359300
  232.2 16.7 %collective-permute-start.9 = (bf16[4,192,384]{2,1,0:T(8,128)(2,1)S(1)}, bf16[4,192,384]{2,1,0:T(8,128)(2,1)S(1)}, u32[]{:S(2)}, u32[]{:S(2)}) collective-permute-start(bf16[4,192,384]{2,1,0:T(8,128)(2,1)S(1)} %slice.639), channel_id=1, source_target_pairs={{0,4},{4,0},{8,12},{12,8},{16,20},{20,16},{24,28},{28,24},{1,5},{5... | collective-permute-start | bytes 1769480 | tf_op jit(solution)/shard_map/ppermute | solution.py:668
  233.0 35.8 %collective-permute-start.6 = (bf16[4,192,640]{2,1,0:T(8,128)(2,1)}, bf16[4,192,640]{2,1,0:T(8,128)(2,1)}, u32[]{:S(2)}, u32[]{:S(2)}) collective-permute-start(bf16[4,192,640]{2,1,0:T(8,128)(2,1)} %slice.629), channel_id=1, source_target_pairs={{0,4},{4,0},{8,12},{12,8},{16,20},{20,16},{24,28},{28,24},{1,5},{5... | collective-permute-start | bytes 2949128 | tf_op jit(solution)/shard_map/ppermute | solution.py:668
  275.6 13.9 %collective-permute-start.7 = (bf16[512,256]{1,0:T(8,128)(2,1)}, bf16[512,256]{1,0:T(8,128)(2,1)}, u32[]{:S(2)}, u32[]{:S(2)}) collective-permute-start(bf16[512,256]{1,0:T(8,128)(2,1)} %pad_maximum_fusion.21), channel_id=1, source_target_pairs={{0,8},{4,12},{8,16},{12,20},{16,24},{20,28},{1,9},{5,13},{9,17},{1... | collective-permute-start | bytes 786440 | tf_op jit(solution)/shard_map/ppermute | solution.py:765
  277.6 11.9 %collective-permute-start.8 = (bf16[512,256]{1,0:T(8,128)(2,1)}, bf16[512,256]{1,0:T(8,128)(2,1)}, u32[]{:S(2)}, u32[]{:S(2)}) collective-permute-start(bf16[512,256]{1,0:T(8,128)(2,1)} %pad_maximum_fusion.21), channel_id=1, source_target_pairs={{0,4},{4,8},{8,12},{12,16},{16,20},{20,24},{24,28},{1,5},{5,9},{9,... | collective-permute-start | bytes 786440 | tf_op jit(solution)/shard_map/ppermute | solution.py:765
  370.1 171.8 %reduce-scatter.7.cloned.1.call-start = ((), (), s32[]{:S(2)}) async-start(), calls=%async_computation.8 | async-start | bytes 2949120 | tf_op jit(solution)/shard_map/reduce_scatter | solution.py:690
  373.1 21.8 %copy-start.12 = (f32[128,1536]{1,0:T(8,128)S(1)}, f32[128,1536]{1,0:T(8,128)}, u32[]{:S(2)}) copy-start(f32[128,1536]{1,0:T(8,128)} %copy-done.11) | copy-start | bytes 2359300
  373.1 21.8 %copy-start.105 = (f32[1536]{0:T(1024)S(1)}, f32[1536]{0:T(1024)}, u32[]{:S(2)}) copy-start(f32[1536]{0:T(1024)} %copy-done.104) | copy-start | bytes 18436
  373.1 21.8 %copy-start.148 = (f32[128]{0:T(128)S(1)}, f32[128]{0:T(128)}, u32[]{:S(2)}) copy-start(f32[128]{0:T(128)} %copy-done.147) | copy-start | bytes 1540
  452.1 26.8 %collective-permute-start.10 = (bf16[128,256]{1,0:T(8,128)(2,1)S(1)}, bf16[128,256]{1,0:T(8,128)(2,1)S(1)}, u32[]{:S(2)}, u32[]{:S(2)}) collective-permute-start(bf16[128,256]{1,0:T(8,128)(2,1)S(1)} %get-tuple-element.229), channel_id=1, source_target_pairs={{4,0},{8,4},{12,8},{16,12},{20,16},{24,20},{28,24},{5,1},{9,5},{13... | collective-permute-start | bytes 196616 | tf_op jit(solution)/shard_map/ppermute | solution.py:765
  453.4 25.5 %collective-permute-start.11 = (bf16[128,256]{1,0:T(8,128)(2,1)S(1)}, bf16[128,256]{1,0:T(8,128)(2,1)S(1)}, u32[]{:S(2)}, u32[]{:S(2)}) collective-permute-start(bf16[128,256]{1,0:T(8,128)(2,1)S(1)} %get-tuple-element.230), channel_id=1, source_target_pairs={{8,0},{12,4},{16,8},{20,12},{24,16},{28,20},{9,1},{13,5},{17,9},{2... | collective-permute-start | bytes 196616 | tf_op jit(solution)/shard_map/ppermute | solution.py:765
  483.5 189.6 %reduce-scatter.9.cloned.1.call-start = ((), (), s32[]{:S(2)}) async-start(), calls=%async_computation.9 | async-start | bytes 6881280 | tf_op jit(solution)/shard_map/reduce_scatter | solution.py:690
  534.0 27.6 %copy-start.10 = (f32[128,1536]{1,0:T(8,128)S(1)}, f32[128,1536]{1,0:T(8,128)}, u32[]{:S(2)}) copy-start(f32[128,1536]{1,0:T(8,128)} %copy-done.9) | copy-start | bytes 2359300
  534.0 27.6 %copy-start.101 = (f32[1536]{0:T(1024)S(1)}, f32[1536]{0:T(1024)}, u32[]{:S(2)}) copy-start(f32[1536]{0:T(1024)} %copy-done.100) | copy-start | bytes 18436
  566.1 32.1 %copy-start.32 = (f32[128,1536]{1,0:T(8,128)}, f32[128,1536]{1,0:T(8,128)S(1)}, u32[]{:S(2)}) copy-start(f32[128,1536]{1,0:T(8,128)S(1)} %fusion.57) | copy-start | bytes 2359300
  566.2 176.8 %reduce-scatter.11.cloned.1.call-start = ((), (), s32[]{:S(2)}) async-start(), calls=%async_computation.10 | async-start | bytes 3440640 | tf_op jit(solution)/shard_map/reduce_scatter | solution.py:690
  568.8 24.3 %collective-permute-start.12 = (bf16[192,1728]{1,0:T(8,128)(2,1)}, bf16[192,1728]{1,0:T(8,128)(2,1)}, u32[]{:S(2)}, u32[]{:S(2)}) collective-permute-start(bf16[192,1728]{1,0:T(8,128)(2,1)} %broadcast_select_fusion.2), channel_id=1, source_target_pairs={{0,4},{4,0},{8,12},{12,8},{16,20},{20,16},{24,28},{28,24},{1,5},{5... | collective-permute-start | bytes 1990664 | tf_op jit(solution)/shard_map/ppermute | solution.py:668
  620.0 21.7 %copy-start.17 = (f32[1024,128]{1,0:T(8,128)S(1)}, f32[1024,128]{1,0:T(8,128)}, u32[]{:S(2)}) copy-start(f32[1024,128]{1,0:T(8,128)} %copy-done.16) | copy-start | bytes 1572868
  620.0 21.7 %copy-start.19 = (f32[1024,128]{1,0:T(8,128)S(1)}, f32[1024,128]{1,0:T(8,128)}, u32[]{:S(2)}) copy-start(f32[1024,128]{1,0:T(8,128)} %copy-done.18) | copy-start | bytes 1572868
  620.0 21.7 %copy-start.23 = (f32[1024,256]{1,0:T(8,128)S(1)}, f32[1024,256]{1,0:T(8,128)}, u32[]{:S(2)}) copy-start(f32[1024,256]{1,0:T(8,128)} %copy-done.22) | copy-start | bytes 3145732
  620.0 21.7 %copy-start.27 = (f32[1024,128]{1,0:T(8,128)S(1)}, f32[1024,128]{1,0:T(8,128)}, u32[]{:S(2)}) copy-start(f32[1024,128]{1,0:T(8,128)} %copy-done.26) | copy-start | bytes 1572868
  620.0 21.7 %copy-start.29 = (f32[1024,128]{1,0:T(8,128)S(1)}, f32[1024,128]{1,0:T(8,128)}, u32[]{:S(2)}) copy-start(f32[1024,128]{1,0:T(8,128)} %copy-done.28) | copy-start | bytes 1572868
  620.0 21.7 %copy-start.114 = (f32[1024]{0:T(1024)S(1)}, f32[1024]{0:T(1024)}, u32[]{:S(2)}) copy-start(f32[1024]{0:T(1024)} %copy-done.113) | copy-start | bytes 12292
  620.0 21.7 %copy-start.120 = (f32[1,256]{1,0:T(1,128)S(1)}, f32[1,256]{1,0:T(1,128)}, u32[]{:S(2)}) copy-start(f32[1,256]{1,0:T(1,128)} %copy-done.119) | copy-start | bytes 3076
  620.0 21.7 %copy-start.127 = (f32[1,256]{1,0:T(1,128)S(1)}, f32[1,256]{1,0:T(1,128)}, u32[]{:S(2)}) copy-start(f32[1,256]{1,0:T(1,128)} %get-tuple-element.286) | copy-start | bytes 3076
  620.0 21.7 %copy-start.129 = (f32[256]{0:T(256)S(1)}, f32[256]{0:T(256)}, u32[]{:S(2)}) copy-start(f32[256]{0:T(256)} %copy-done.128) | copy-start | bytes 3076
  649.3 6.4 collective-permute-start.13
  674.9 50.8 %collective-permute-start.16 = (bf16[192,768]{1,0:T(8,128)(2,1)}, bf16[192,768]{1,0:T(8,128)(2,1)}, u32[]{:S(2)}, u32[]{:S(2)}) collective-permute-start(bf16[192,768]{1,0:T(8,128)(2,1)} %broadcast_select_fusion.12), channel_id=1, source_target_pairs={{0,4},{4,0},{8,12},{12,8},{16,20},{20,16},{24,28},{28,24},{1,5},{5... | collective-permute-start | bytes 884744 | tf_op jit(solution)/shard_map/ppermute | solution.py:668
  679.3 24.9 %copy-start.99 = (f32[1536]{0:T(1024)S(1)}, f32[1536]{0:T(1024)}, u32[]{:S(2)}) copy-start(f32[1536]{0:T(1024)} %copy-done.98) | copy-start | bytes 18436
  679.3 25.1 %copy-start.158 = (f32[128]{0:T(128)S(1)}, f32[128]{0:T(128)}, u32[]{:S(2)}) copy-start(f32[128]{0:T(128)} %copy-done.157) | copy-start | bytes 1540
  679.3 25.1 %copy-start.150 = (f32[128]{0:T(128)S(1)}, f32[128]{0:T(128)}, u32[]{:S(2)}) copy-start(f32[128]{0:T(128)} %copy-done.149) | copy-start | bytes 1540
  680.2 24.1 %copy-start.62 = (bf16[512,1536]{1,0:T(8,128)(2,1)S(1)}, bf16[512,1536]{1,0:T(8,128)(2,1)}, u32[]{:S(2)}) copy-start(bf16[512,1536]{1,0:T(8,128)(2,1)} %param.22) | copy-start | bytes 4718596
  680.2 24.3 %copy-start.33 = (f32[128,1536]{1,0:T(8,128)S(1)}, f32[128,1536]{1,0:T(8,128)}, u32[]{:S(2)}) copy-start(f32[128,1536]{1,0:T(8,128)} %copy-done.32) | copy-start | bytes 2359300
  724.7 16.8 %collective-permute-start.15 = (bf16[192,1728]{1,0:T(8,128)(2,1)S(1)}, bf16[192,1728]{1,0:T(8,128)(2,1)S(1)}, u32[]{:S(2)}, u32[]{:S(2)}) collective-permute-start(bf16[192,1728]{1,0:T(8,128)(2,1)S(1)} %broadcast_select_fusion), channel_id=1, source_target_pairs={{0,4},{4,0},{8,12},{12,8},{16,20},{20,16},{24,28},{28,24},{1,5},{5... | collective-permute-start | bytes 1990664 | tf_op jit(solution)/shard_map/ppermute | solution.py:668
  744.1 8.6 %collective-permute-start.14 = (bf16[224,768]{1,0:T(8,128)(2,1)S(1)}, bf16[224,768]{1,0:T(8,128)(2,1)S(1)}, u32[]{:S(2)}, u32[]{:S(2)}) collective-permute-start(bf16[224,768]{1,0:T(8,128)(2,1)S(1)} %broadcast_select_fusion.8), channel_id=1, source_target_pairs={{0,4},{4,0},{8,12},{12,8},{16,20},{20,16},{24,28},{28,24},{1,5},{5... | collective-permute-start | bytes 1032200 | tf_op jit(solution)/shard_map/ppermute | solution.py:668
  (131 other events, 780.4 us)
Sparse Core Ops, SparseCore 0:
  24.2 55.2 all-gather.5
  81.6 101.8 all-gather.7
  190.8 35.3 all-gather.11
  228.4 102.0 all-gather.9
  370.2 113.1 reduce-scatter.4
  485.6 56.2 reduce-scatter.6
  566.3 106.7 reduce-scatter.8
  675.4 57.5 reduce-scatter.10

commit v3 on v2

--- a/solution.py
+++ b/solution.py
@@ -1,4 +1,5 @@
 import functools
+import math
 
 import jax
 import jax.numpy as jnp
@@ -51,22 +52,6 @@
     reset = (slots != begin).astype(jnp.float32)
     valid = (segment < doc_lengths.shape[0]).astype(jnp.float32)
     return (segment, position, reset, valid)
-
-
-def rotate(values, position):
-    half_width = values.shape[-1] // 2
-    frequency = 10000.0 ** (-jnp.arange(half_width, dtype=jnp.float32) / half_width)
-    angle = position.astype(jnp.float32)[:, None] * frequency[None, :]
-    if values.ndim == 3:
-        angle = angle[:, None, :]
-    cosine = jnp.cos(angle)
-    sine = jnp.sin(angle)
-    first_half = values[..., :half_width]
-    second_half = values[..., half_width:]
-    return jnp.concatenate(
-        [first_half * cosine - second_half * sine, second_half * cosine + first_half * sine],
-        axis=-1,
-    )
 
 
 def convolve(extended, taps, bias, segment):
@@ -118,11 +103,16 @@
     return (a, b, c, across_a, across_b, across_c)
 
 
+def hail(devices):
+    for device in devices:
+        pl.semaphore_signal(
+            pltpu.get_barrier_semaphore(), inc=1, device_id=device, device_id_type=MESH
+        )
+
+
 def greet(devices):
-    barrier = pltpu.get_barrier_semaphore()
-    for device in devices:
-        pl.semaphore_signal(barrier, inc=1, device_id=device, device_id_type=MESH)
-    pl.semaphore_wait(barrier, len(devices))
+    hail(devices)
+    pl.semaphore_wait(pltpu.get_barrier_semaphore(), len(devices))
 
 
 def remote(src, dst, send_sem, recv_sem, slot, device):
@@ -283,19 +273,20 @@
         ]
     else:
         order = [(a, 1 - b, low), (a, 1 - b, high), (a, b, low), (a, b, high)]
-    core = []
-    for k, (pa, pb, part) in enumerate(order):
-        copy = remote(
-            part_ref.at[index(pa, pb, 1 - c), part],
-            cbuf.at[pair(pa, pb), part],
-            csend,
-            crecv,
-            k,
-            across_c,
-        )
-        copy.start()
-        core.append(copy)
-    yield
+    core = {}
+
+    def share(*which):
+        for k in which:
+            pa, pb, part = order[k]
+            core[k] = remote(
+                part_ref.at[index(pa, pb, 1 - c), part],
+                cbuf.at[pair(pa, pb), part],
+                csend,
+                crecv,
+                k,
+                across_c,
+            )
+            core[k].start()
 
     def summed(k):
         pa, pb, part = order[k]
@@ -313,13 +304,20 @@
         return copy
 
     if full:
+        yield
+        share(0, 1)
+        yield
+        share(2, 5)
         sx[0] = lowered(summed(0))
         x0 = go(sx.at[0], ax.at[0], 0, across_a)
         sy[0] = lowered(summed(1))
         y0 = go(sy.at[0], by.at[0], 1, across_b)
         yield
+        share(3, 4)
         sx[1] = lowered(summed(2))
         x1 = go(sx.at[1], ax.at[1], 2, across_a)
+        yield
+        share(6, 7)
         sy[1] = lowered(summed(3))
         y1 = go(sy.at[1], by.at[1], 3, across_b)
         yield
@@ -342,8 +340,8 @@
         total = total + by[1].astype(jnp.float32)
         last_x.wait_recv()
         out_ref[high] = total + rx[...].astype(jnp.float32)
-        yield
     else:
+        share(0, 1, 2, 3)
         sy[0] = lowered(summed(0))
         y0 = go(sy.at[0], by.at[0], 1, across_b)
         sy[1] = lowered(summed(1))
@@ -355,8 +353,7 @@
         total = summed(3)
         y1.wait_recv()
         out_ref[high] = total + by[1].astype(jnp.float32)
-        yield
-    for copy in core + sent:
+    for copy in [*core.values(), *sent]:
         copy.wait_send()
 
 
@@ -584,6 +581,230 @@
     )(lowered(partial).reshape(ways, rows, width), gains, rest)
 
 
+def gelu_parts(x):
+    inner = math.sqrt(2 / math.pi)
+    curve = jnp.tanh(inner * (x + 0.044715 * x * x * x))
+    half = 0.5 * (1 + curve)
+    slope = half + 0.5 * x * (1 - curve * curve) * inner * (1 + 3 * 0.044715 * x * x)
+    return (x * half, slope)
+
+
+def dense_kernel(mode, main, *refs):
+    forward, backward = (mode != "backward", mode != "forward")
+    refs = list(refs)
+
+    def take(count):
+        taken, refs[:] = (refs[:count], refs[count:])
+        return taken
+
+    (n_hbm,) = take(1)
+    g_hbm = take(1)[0] if backward else None
+    (w_hbm,) = take(1)
+    ab_hbm = take(1)[0] if mode == "backward" else None
+    (out_ref,) = take(1)
+    wire_hbm = take(1)[0] if backward else None
+    ab_out = take(1)[0] if mode == "forward" else None
+    p4_hbm = take(1)[0] if mode == "both" else None
+    n_v, w_v, hid_v, part_v = take(4)
+    g_v, low_v, wire_v = take(3) if backward else (None, None, None)
+    ab_v = take(1)[0] if mode != "both" else None
+    p4_v = take(1)[0] if mode == "both" else None
+    buffers = take(13)
+    (sems,) = take(1)
+    lanes = 128
+    both = 2 * main + lanes
+    tile = 256
+    rows = n_v.shape[0]
+    a, b = cube()[:2]
+    near = neighbours(True)
+    hail(near)
+    loads = [pltpu.make_async_copy(n_hbm, n_v, sems.at[0])]
+    loads.append(pltpu.make_async_copy(w_hbm, w_v, sems.at[1]))
+    if backward:
+        loads.append(pltpu.make_async_copy(g_hbm, g_v, sems.at[2]))
+    if mode == "backward":
+        loads.append(pltpu.make_async_copy(ab_hbm, ab_v, sems.at[3]))
+    for load in loads:
+        load.start()
+    for load in loads:
+        load.wait()
+
+    def work(pa, pb):
+        block = pa * 4 + pb * 2
+        at = pl.ds(pl.multiple_of(block * lanes, tile), tile)
+        if forward:
+            ab = product(n_v[at, :], w_v[:, :both])
+            if mode == "forward":
+                ab_v[at, :] = ab
+        else:
+            ab = ab_v[at, :]
+        gate, up, tail = (ab[:, :main], ab[:, main : 2 * main], ab[:, 2 * main :])
+        first = lax.broadcasted_iota(jnp.int32, tail.shape, 1) < lanes // 2
+        turned = pltpu.roll(tail, lanes // 2, 1)
+        act, slope = gelu_parts(gate)
+        tail_act, tail_slope = gelu_parts(tail)
+        hid_v[at, :main] = lowered(act * up)
+        hid_v[at, main:] = lowered(jnp.where(first, tail_act * turned, 0.0))
+        if backward:
+            grad = product(g_v[at, :], w_v[:, both:])
+            grad_main, grad_tail = (grad[:, :main], grad[:, main:])
+            low_v[at, :main] = lowered(grad_main * up * slope)
+            low_v[at, main : 2 * main] = lowered(grad_main * act)
+            turned_grad = pltpu.roll(grad_tail, lanes // 2, 1)
+            turned_act = pltpu.roll(tail_act, lanes // 2, 1)
+            low_v[at, 2 * main :] = lowered(
+                jnp.where(first, grad_tail * turned * tail_slope, turned_grad * turned_act)
+            )
+            part = lowered(product_right(low_v[at, :], w_v[:, :both]))
+        else:
+            part = lowered(product_right(hid_v[at, :], w_v[:, both:]))
+        part_v[pl.ds(block, 2)] = part.reshape(2, lanes, part.shape[1])
+
+    schedule = scatter_steps(True, part_v, out_ref, *buffers)
+    next(schedule)
+    for turn, (pa, pb) in enumerate(((1 - a, 1 - b), (1 - a, b), (a, 1 - b), (a, b))):
+        work(pa, pb)
+        if turn == 0:
+            pl.semaphore_wait(pltpu.get_barrier_semaphore(), len(near))
+        next(schedule)
+    stores = []
+
+    def store(src, dst, slot):
+        copy = pltpu.make_async_copy(src, dst, sems.at[slot])
+        copy.start()
+        stores.append(copy)
+
+    if mode == "forward":
+        store(ab_v, ab_out, 4)
+        next(schedule)
+    else:
+        depth = w_v.shape[0]
+
+        def grads(i, carry):
+            cols = pl.ds(pl.multiple_of(i * tile, tile), tile)
+            wire_v[cols, :both] = lowered(product_left(n_v[:, cols], low_v[...]))
+            wire_v[cols, both:] = lowered(product_left(g_v[:, cols], hid_v[...]))
+            return carry
+
+        split = depth // tile // 2
+        lax.fori_loop(0, split, grads, 0)
+        store(wire_v.at[pl.ds(0, split * tile)], wire_hbm.at[pl.ds(0, split * tile)], 4)
+        next(schedule)
+        lax.fori_loop(split, depth // tile, grads, 0)
+        rest = pl.ds(split * tile, depth - split * tile)
+        store(wire_v.at[rest], wire_hbm.at[rest], 5)
+    if mode == "both":
+
+        def onward(i, carry):
+            at = pl.ds(pl.multiple_of(i * tile, tile), tile)
+            p4_v[at, :] = lowered(product_right(hid_v[at, :], w_v[:, both:]))
+            return carry
+
+        lax.fori_loop(0, rows // tile, onward, 0)
+        store(p4_v, p4_hbm, 6)
+    next(schedule, None)
+    for copy in stores:
+        copy.wait()
+
+
+def dense_call(mode, normed, grad_low, weights, ab, collective_id):
+    rows, depth = normed.shape
+    columns = weights.shape[1]
+    main = (columns // 128 - 2) // 3 * 128
+    both = 2 * main + 128
+    backward = mode != "forward"
+    low = jnp.bfloat16
+    operands = [normed] + ([grad_low] if backward else []) + [weights]
+    shapes = [jax.ShapeDtypeStruct((rows // 8, depth), jnp.float32)]
+    scratch = [(normed.shape, low), (weights.shape, low), ((rows, columns - both), low)]
+    scratch += [((8, rows // 8, depth), low)]
+    if backward:
+        shapes.append(jax.ShapeDtypeStruct(weights.shape, low))
+        scratch += [(normed.shape, low), ((rows, both), low), (weights.shape, low)]
+    if mode == "forward":
+        shapes.append(jax.ShapeDtypeStruct((rows, both), jnp.float32))
+    if mode == "backward":
+        operands.append(ab)
+    if mode == "both":
+        shapes.append(jax.ShapeDtypeStruct((rows, depth), low))
+        scratch.append(((rows, depth), low))
+    else:
+        scratch.append(((rows, both), jnp.float32))
+    return pl.pallas_call(
+        functools.partial(dense_kernel, mode, main),
+        out_shape=shapes,
+        in_specs=[ANY] * len(operands),
+        out_specs=[VMEM] + [ANY] * (len(shapes) - 1),
+        scratch_shapes=[pltpu.VMEM(shape, kind) for shape, kind in scratch]
+        + scatter_scratch(8, rows // 8, depth)
+        + [pltpu.SemaphoreType.DMA((7,))],
+        name="dense_" + mode,
+        cost_estimate=pl.CostEstimate(
+            flops=0, bytes_accessed=100_000_000 if backward else 80_000_000, transcendentals=0
+        ),
+        compiler_params=pltpu.CompilerParams(
+            collective_id=collective_id, has_side_effects=True, vmem_limit_bytes=56 * 2**20
+        ),
+    )(*operands)
+
+
+def attention_kernel(
+    shift, query_ref, ext_ref, here_ref, there_ref, cos_ref, sin_ref, out_ref, rot_ref, log_ref
+):
+    tile = 256
+    rows, width = query_ref.shape
+    heads = width // HD
+    reach = shift + tile
+    scale = HD ** (-0.5)
+    log_ref[...] = jnp.zeros_like(log_ref)
+
+    def turn(n, carry):
+        h = n // (rows // tile)
+        first = pl.multiple_of(lax.rem(n, rows // tile) * tile, tile)
+        lanes = pl.ds(pl.multiple_of(h * HD, HD), HD)
+        at = pl.ds(first, tile)
+        seen = pl.ds(first, reach)
+        query = query_ref[at, lanes]
+        query = query * cos_ref[at, :] + pltpu.roll(query, HD // 2, 1) * sin_ref[at, :]
+        query = lowered(query)
+        rot_ref[at, lanes] = query
+        allowed = visible(shift, there_ref[seen, :], here_ref[0:1, at])
+        scores = jnp.where(allowed, product_right(ext_ref[seen, :HD], query) * scale, -1e30)
+        top = jnp.max(scores, axis=0, keepdims=True)
+        probs = jnp.exp(scores - top)
+        total = jnp.sum(probs, axis=0, keepdims=True)
+        log_ref[pl.ds(h, 1), at] = top + jnp.log(total)
+        out_ref[at, lanes] = lowered(product_left(lowered(probs / total), ext_ref[seen, HD:]))
+        return carry
+
+    lax.fori_loop(0, heads * (rows // tile), turn, 0)
+
+
+def visible(shift, there, here):
+    shape = (there.shape[0], here.shape[1])
+    distance = (
+        lax.broadcasted_iota(jnp.int32, shape, 1) - lax.broadcasted_iota(jnp.int32, shape, 0) + shift
+    )
+    return (there == here) & (distance >= 0) & (distance < WINDOW)
+
+
+def attention(query, extended, here, there, cosine, sine):
+    rows, width = query.shape
+    return pl.pallas_call(
+        functools.partial(attention_kernel, extended.shape[0] - rows),
+        out_shape=[
+            jax.ShapeDtypeStruct((rows, width), jnp.bfloat16),
+            jax.ShapeDtypeStruct((rows, width), jnp.bfloat16),
+            jax.ShapeDtypeStruct((8, rows), jnp.float32),
+        ],
+        in_specs=[VMEM] * 6,
+        out_specs=[VMEM] * 3,
+        name="attention",
+        cost_estimate=TEN_US,
+        compiler_params=pltpu.CompilerParams(vmem_limit_bytes=48 * 2**20),
+    )(query, extended, here, there, cosine, sine)
+
+
 def attention_back_kernel(
     shift, query_ref, ext_ref, grad_ref, log_ref, here_ref, there_ref, cos_ref, sin_ref, dquery_ref, dext_ref, total
 ):
@@ -604,14 +825,7 @@
         grad = grad_ref[at, lanes]
         keys = ext_ref[seen, :HD]
         values = ext_ref[seen, HD:]
-        distance = (
-            lax.broadcasted_iota(jnp.int32, (reach, tile), 1)
-            - lax.broadcasted_iota(jnp.int32, (reach, tile), 0)
-            + shift
-        )
-        allowed = (
-            (there_ref[seen, :] == here_ref[0:1, at]) & (distance >= 0) & (distance < WINDOW)
-        )
+        allowed = visible(shift, there_ref[seen, :], here_ref[0:1, at])
         scores = jnp.where(allowed, product_right(keys, query) * scale, -1e30)
         probs = jnp.exp(scores - log_ref[pl.ds(h, 1), at])
         grad_probs = product_right(values, grad)
@@ -628,12 +842,9 @@
     dext_ref[...] = lowered(total[...])
 
 
-def attention_back(query_rot, extended, grad, log_total, segment, key_segment, cosine, sine):
+def attention_back(query_rot, extended, grad, log_total, here, there, cosine, sine):
     rows, width = query_rot.shape
     seen = extended.shape[0]
-    log_rows = jnp.concatenate(
-        [log_total, jnp.zeros((8 - log_total.shape[0], rows), jnp.float32)], axis=0
-    )
     return pl.pallas_call(
         functools.partial(attention_back_kernel, seen - rows),
         out_shape=[
@@ -646,16 +857,7 @@
         name="attention_back",
         cost_estimate=EIGHTEEN_US,
         compiler_params=pltpu.CompilerParams(vmem_limit_bytes=48 * 2**20),
-    )(
-        query_rot,
-        extended,
-        grad,
-        log_rows,
-        jnp.broadcast_to(segment[None], (8, rows)),
-        key_segment[:, None],
-        cosine,
-        sine,
-    )
+    )(query_rot, extended, grad, log_total, here, there, cosine, sine)
 
 
 def stacked_by_low(mine, other):
@@ -674,8 +876,11 @@
 
 
 def swap_columns(*parts):
+    return swap_pieces([jnp.concatenate(each, axis=1) for each in zip(*map(split_columns, parts))])
+
+
+def swap_pieces(halves):
     lo = lax.rem(lax.axis_index("seq"), LO)
-    halves = [jnp.concatenate(each, axis=1) for each in zip(*map(split_columns, parts))]
     kept = jnp.where(lo == 0, halves[0], halves[1])
     given = jnp.where(lo == 0, halves[1], halves[0])
     both = stacked_by_low(kept, swap_low(given))
@@ -707,32 +912,6 @@
 
 def joined(blocks):
     return jnp.concatenate([blocks[l] for l in range(LO)], axis=1).astype(jnp.float32)
-
-
-def dense_forward(normed, weights):
-    gate_up, down = weights
-    width = down.shape[1]
-    both = product(normed, gate_up)
-    hidden = lowered(gated(both[:, :width], both[:, width:]))
-    return (lowered(product_right(hidden, down)), (normed, both, hidden))
-
-
-def dense_backward(stream, gain, grad_out, grad_low, kept, weights, cid, tied=()):
-    gate_up, down = weights
-    width = down.shape[1]
-    normed, both, hidden = kept
-    grad_down = product_left(grad_low, hidden)
-    grad_hidden = product(grad_low, down)
-    gate_grad, up_grad = jax.vjp(gated, both[:, :width], both[:, width:])[1](grad_hidden)
-    both_low = jnp.concatenate([lowered(gate_grad), lowered(up_grad)], axis=1)
-    grad_both = product_left(normed, both_low)
-    partial = product_right(both_low, gate_up)
-    partial, grad_both, grad_down, tied = lax.optimization_barrier(
-        (lowered(partial), lowered(grad_both), lowered(grad_down), tied)
-    )
-    (grad_normed,) = scatter([partial], True, cid["scatter_full"])
-    stream_grad, gain_grad = jax.vjp(rms_norm, stream, gain)[1](grad_normed)
-    return (grad_out + stream_grad, gain_grad, grad_both, grad_down, tied)
 
 
 def block_product(values, weight):
@@ -765,11 +944,6 @@
     return lax.ppermute(block, "seq", route)
 
 
-def score_block(query_rot, keys_ext, allowed, score_scale):
-    raw = jnp.einsum("qhd,kd->hqk", query_rot, keys_ext, preferred_element_type=jnp.float32)
-    return jnp.where(allowed[None], raw * score_scale, -1e30)
-
-
 CIDS = {
     "gather_full": 0,
     "gather_half": 1,
@@ -781,29 +955,61 @@
     "last": 7,
     "gather_narrow": 8,
     "gather_two": 9,
-    "scatter_two": 10,
+    "forward": 10,
+    "both": 11,
+    "backward": 12,
+    "gather_weight": 13,
+    "gather_seen": 14,
 }
 
 
+def dense_wire(gate, up, down):
+    pieces = []
+    for g, u, d in zip(*map(split_columns, (gate, up, down))):
+        main = g.shape[1] // 128 * 128
+        blank = jnp.zeros((d.shape[0], -d.shape[1] % 128), d.dtype)
+        pieces.append(
+            jnp.concatenate([g[:, :main], u[:, :main], g[:, main:], u[:, main:], d, blank], axis=1)
+        )
+    return pieces
+
+
 def dense_grads(both):
-    width = both.shape[1] // 3
-    both = exchanged(both)
+    columns = both.shape[2]
+    main = (columns // 128 - 2) // 3 * 128
+    tail = 64
+    ends = 2 * main
+
+    def part(first, last):
+        return jnp.concatenate([both[:, :, first : first + main], both[:, :, last : last + tail]], axis=2)
+
     return (
-        joined(both[:, :, :width]),
-        joined(both[:, :, width : 2 * width]),
-        joined(both[:, :, 2 * width :]).T,
+        joined(part(0, ends)),
+        joined(part(main, ends + tail)),
+        joined(both[:, :, ends + 2 * tail : ends + 3 * tail + main]).T,
     )
 
 
 def turns(position):
     half_width = HD // 2
     frequency = 10000.0 ** (-jnp.arange(half_width, dtype=jnp.float32) / half_width)
-    angle = position.astype(jnp.float32)[:, None] * frequency[None, :]
-    cosine, sine = (jnp.cos(angle), jnp.sin(angle))
-    return (
-        jnp.concatenate([cosine, cosine], axis=1),
-        jnp.concatenate([-sine, sine], axis=1),
-    )
+    angle = position.astype(jnp.float32)[:, None] * jnp.tile(frequency, 2)[None, :]
+    sign = jnp.where(jnp.arange(HD) < half_width, -1.0, 1.0)
+    return (jnp.cos(angle), jnp.sin(angle) * sign[None, :])
+
+
+def rotate(values, factors):
+    cosine, sine = factors
+    half_width = HD // 2
+    swapped = jnp.concatenate([values[..., half_width:], values[..., :half_width]], axis=-1)
+    return values * cosine + swapped * sine
+
+
+def rotate_back(values, factors):
+    cosine, sine = factors
+    half_width = HD // 2
+    swapped = jnp.concatenate([values[..., half_width:], values[..., :half_width]], axis=-1)
+    return values * cosine - swapped * sine
 
 
 def both_lows(lanes):
@@ -813,17 +1019,12 @@
     return both.reshape(-1, lanes.shape[2])
 
 
-def dense_weights(wide):
-    width = wide.shape[1] // 3
-    return (wide[:, : 2 * width], wide[:, 2 * width :])
-
-
-def summed_low(both):
+def swap_sums(grad):
     lo = lax.rem(lax.axis_index("seq"), LO)
-    both = both.reshape(LO, -1, both.shape[1])
-    kept = jnp.where(lo == 0, both[0], both[1])
-    given = jnp.where(lo == 0, both[1], both[0])
-    return kept.astype(jnp.float32) + swap_low(given).astype(jnp.float32)
+    pairs = grad.reshape(lax.axis_size("seq") // LO, LO, -1, grad.shape[1])
+    kept = jnp.where(lo == 0, pairs[:, 0], pairs[:, 1])
+    given = jnp.where(lo == 0, pairs[:, 1], pairs[:, 0])
+    return (kept.reshape(-1, grad.shape[1]), swap_low(given).reshape(-1, grad.shape[1]))
 
 
 def local(
@@ -881,50 +1082,44 @@
 
     gate_rows = recur_gate.shape[1]
     weight_rows = input_branch.shape[0]
+    attn_rows = jnp.concatenate([query_weight, attention_out.T], axis=1)
+    query_width = query_weight.shape[1]
+    third = lax.all_gather(
+        jnp.concatenate(
+            [attn_rows, keyvalue_weight.reshape(-1, attn_rows.shape[1])], axis=0
+        ),
+        "seq",
+        axis_index_groups=high_groups(),
+    )
+    own_tokens = lax.dynamic_slice_in_dim(tokens, tp * own_rows, own_rows, 0)
+    own_cotangent = lax.dynamic_slice_in_dim(cotangent, tp * own_rows, own_rows, 0)
+    stream_in = own_tokens.astype(jnp.float32)
+    grad_stream = own_cotangent.astype(jnp.float32) * valid[:, None]
+    (normed_one,) = gather([lowered(rms_norm(stream_in, norm_gains[0]))], True, cid["gather_full"])
     first = swap_columns(
         jnp.concatenate([input_branch, recur_gate.T], axis=0),
         jnp.concatenate([gate_branch, input_gate.T], axis=0),
         jnp.concatenate([recur_output.T, jnp.zeros_like(recur_gate.T)], axis=0),
     )
+    first, third, normed_one = lax.optimization_barrier((first, third, normed_one))
     first_full = gather_high(first).reshape(high * LO, weight_rows + gate_rows, 3 * channels)
     in_full = first_full[:, :weight_rows, : 2 * channels].reshape(-1, 2 * channels)
     output_full = first_full[:, :weight_rows, 2 * channels :].reshape(-1, channels)
     recur_full = first_full[:, weight_rows:, :channels].reshape(-1, channels)
     input_gate_full = first_full[:, weight_rows:, channels : 2 * channels].reshape(-1, channels)
-    second = swap_columns(dense_gate_one, dense_up_one, dense_down_one.T)
-
-    own_tokens = lax.dynamic_slice_in_dim(tokens, tp * own_rows, own_rows, 0)
-    own_cotangent = lax.dynamic_slice_in_dim(cotangent, tp * own_rows, own_rows, 0)
-    stream_in = own_tokens.astype(jnp.float32)
-    grad_stream = own_cotangent.astype(jnp.float32) * valid[:, None]
-    normed_one, grad_low = gather(
-        [lowered(rms_norm(stream_in, norm_gains[0])), lowered(grad_stream)],
-        True,
-        cid["gather_two"],
-    )
-    normed_one, second, query_weight, keyvalue_weight, attention_out = lax.optimization_barrier(
-        (normed_one, second, query_weight, keyvalue_weight, attention_out)
-    )
-    weights_one = dense_weights(gather_high(second))
+    third = both_lows(third)
+    second = swap_pieces(dense_wire(dense_gate_one, dense_up_one, dense_down_one.T))
+
+    (grad_low,) = gather([lowered(grad_stream)], True, cid["gather_full"])
+    normed_one, in_full, second, third, grad_low = lax.optimization_barrier(
+        (normed_one, in_full, second, third, grad_low)
+    )
+    weights_one = gather_high(second)
     both = product(normed_one, in_full)
     both, dense_gate_two, dense_up_two, dense_down_two = lax.optimization_barrier(
         (both, dense_gate_two, dense_up_two, dense_down_two)
     )
-
-    keyvalue_part = keyvalue_weight[None]
-    for step in (1, 2):
-        other = lax.ppermute(keyvalue_part, "tp", [(i, i ^ step) for i in range(ways)])
-        low_bit = lax.rem(tp // step, 2)
-        keyvalue_part = jnp.concatenate(
-            [
-                jnp.where(low_bit == 0, keyvalue_part, other),
-                jnp.where(low_bit == 0, other, keyvalue_part),
-            ],
-            axis=0,
-        )
-    keyvalue_part = keyvalue_part.reshape(weight_rows, keyvalue_weight.shape[1])
-    third = jnp.concatenate([query_weight, keyvalue_part, attention_out.T], axis=1)
-    fourth = swap_columns(dense_gate_two, dense_up_two, dense_down_two.T)
+    fourth = swap_pieces(dense_wire(dense_gate_two, dense_up_two, dense_down_two.T))
 
     branch = both[:, :channels]
     gating = both[:, channels:]
@@ -943,79 +1138,69 @@
     state, state_in = plane_scan(decay, drive, ones, high, False, cid["scan"])
     gate_act, gate_pull = jax.vjp(jax.nn.gelu, gating)
     mixed = lowered(state * gate_act)
+    mixed, fourth = lax.optimization_barrier((mixed, fourth))
     (summed,) = scatter([product_right(mixed, output_full)], True, cid["scatter_full"])
     stream_one = stream_in + summed
     (normed_two,) = gather([lowered(rms_norm(stream_one, norm_gains[1]))], True, cid["gather_full"])
-    normed_two, weights_one, third = lax.optimization_barrier((normed_two, weights_one, third))
-    third = lax.all_gather(third, "seq", axis_index_groups=high_groups())
-
-    partial, kept_one = dense_forward(normed_two, weights_one)
-    partial, fourth = lax.optimization_barrier((partial, fourth))
-    weights_two = dense_weights(gather_high(fourth))
-    query_width = query_weight.shape[1]
-    early_width = query_width + keyvalue_part.shape[1]
-    early_full = both_lows(third[:, :, :early_width])
-    query_full = early_full[:, :query_width]
-    keyvalue_full = early_full[:, query_width:]
-    attn_full = both_lows(third[:, :, early_width:])
-
-    (summed,) = scatter([partial], True, cid["scatter_full"])
+    third = third.reshape(high * LO, -1, third.shape[1])
+    query_full = third[:, :weight_rows, :query_width].reshape(-1, query_width)
+    attn_full = third[:, :weight_rows, query_width:].reshape(-1, third.shape[2] - query_width)
+    part_rows, part_width = keyvalue_weight.shape
+    (keyvalue_full,) = gather(
+        [third[:, weight_rows:].reshape(-1, part_width)], False, cid["gather_weight"]
+    )
+    keyvalue_full = keyvalue_full.reshape(ways, high * LO, part_rows, part_width)
+    keyvalue_full = keyvalue_full.transpose(1, 0, 2, 3).reshape(-1, part_width)
+    factors = turns(position)
+    own_factors = [lax.dynamic_slice_in_dim(each, tp * own_rows, own_rows, 0) for each in factors]
+    segment_rows = jnp.broadcast_to(segment[None], (8, shard_rows))
+    key_column = key_segment[:, None]
+    early = (keyvalue_full, query_full, attn_full, factors, own_factors, segment_rows, key_column)
+    normed_two, early = lax.optimization_barrier((normed_two, early))
+    keyvalue_full, query_full, attn_full, factors, own_factors, segment_rows, key_column = early
+    normed_two, weights_one, fourth = lax.optimization_barrier((normed_two, weights_one, fourth))
+    weights_two = gather_high(fourth)
+    summed, ab_one = dense_call("forward", normed_two, None, weights_one, None, cid["forward"])
     stream_two = stream_one + summed
 
     normed_own = lowered(rms_norm(stream_two, norm_gains[2]))
-    (normed_three,) = gather([normed_own], False, cid["gather_half"])
-    query = product(normed_three, query_full)
-    keyval = product(normed_three, keyvalue_full)
-    local_heads = query.shape[1] // HD
-    query_heads = query.reshape(shard_rows, local_heads, HD)
-    rotate_here = functools.partial(rotate, position=position)
-    query_rot = lowered(rotate_here(query_heads))
-    key_rot = lowered(rotate_here(keyval[:, :HD]))
+    keyval = product(normed_own, keyvalue_full)
+    key_rot = lowered(rotate(keyval[:, :HD], own_factors))
     packed = jnp.concatenate([key_rot, lowered(keyval[:, HD:])], axis=1)
     earlier = [shifted(packed, offset) for offset in range(halo_shards, 0, -1)]
-    extended = jnp.concatenate(earlier + [packed], axis=0)
-    keys_ext = extended[:, :HD]
-    values_ext = extended[:, HD:]
-    query_slots = first_slot + jnp.arange(shard_rows, dtype=jnp.int32)
-    key_slots = (
-        first_slot
-        - halo_shards * shard_rows
-        + jnp.arange((halo_shards + 1) * shard_rows, dtype=jnp.int32)
-    )
-    distance = query_slots[:, None] - key_slots[None, :]
-    allowed = (segment[:, None] == key_segment[None, :]) & (distance >= 0) & (distance < WINDOW)
-    score_scale = HD ** (-0.5)
-    scores = score_block(query_rot, keys_ext, allowed, score_scale)
-    row_top = jnp.max(scores, axis=-1, keepdims=True)
-    row_total = jnp.sum(jnp.exp(scores - row_top), axis=-1, keepdims=True)
-    log_total = row_top + jnp.log(row_total)
-    probs_low = lowered(jnp.exp(scores - row_top) / row_total)
-    attended = lowered(
-        jnp.einsum("hqk,kd->qhd", probs_low, values_ext, preferred_element_type=jnp.float32)
-    ).reshape(shard_rows, local_heads * HD)
+    normed_three, seen = gather(
+        [normed_own, jnp.concatenate(earlier + [packed], axis=1)], False, cid["gather_seen"]
+    )
+    extended = jnp.concatenate(
+        [seen[:, 2 * HD * k : 2 * HD * (k + 1)] for k in range(halo_shards + 1)], axis=0
+    )
+    query = product(normed_three, query_full)
+    attended, query_rot, log_total = attention(
+        query, extended, segment_rows, key_column, *factors
+    )
     (summed,) = scatter([product_right(attended, attn_full)], False, cid["scatter_half"])
     stream_three = stream_two + summed
 
     (normed_four,) = gather(
         [lowered(rms_norm(stream_three, norm_gains[3]))], True, cid["gather_full"]
     )
-    partial_four, kept_two = dense_forward(normed_four, weights_two)
-    grad_stream, gain_four, grad_both_two, grad_down_two, _ = dense_backward(
-        stream_three, norm_gains[3], grad_stream, grad_low, kept_two, weights_two, cid
-    )
-
-    done_two = reduce_high(jnp.concatenate([grad_both_two, grad_down_two], axis=1))
+    grad_normed, wire_two, partial_four = dense_call(
+        "both", normed_four, grad_low, weights_two, None, cid["both"]
+    )
+    done_two = reduce_high(wire_two)
+    stream_grad, gain_four = jax.vjp(rms_norm, stream_three, norm_gains[3])[1](grad_normed)
+    grad_stream = grad_stream + stream_grad
     (grad_attn_low,) = gather([lowered(grad_stream)], False, cid["gather_half"])
     grad_attn_out = product_left(grad_attn_low, attended)
     grad_attended = lowered(product(grad_attn_low, attn_full))
     grad_query_low, grad_ext = attention_back(
-        query_rot.reshape(shard_rows, local_heads * HD),
+        query_rot,
         extended,
         grad_attended,
-        log_total[:, :, 0],
-        segment,
-        key_segment,
-        *turns(position),
+        log_total,
+        segment_rows,
+        key_column,
+        *factors,
     )
     grad_query = product_left(normed_three, grad_query_low)
     grad_pieces = grad_ext.reshape(halo_shards + 1, shard_rows, 2 * HD)
@@ -1025,9 +1210,12 @@
     partial, grad_query, grad_attn_out = lax.optimization_barrier(
         (partial, lowered(grad_query), lowered(grad_attn_out))
     )
-    attn_wire = jnp.concatenate([grad_query, grad_attn_out], axis=1)
+    attn_kept, attn_given = swap_sums(jnp.concatenate([grad_query, grad_attn_out], axis=1))
     (summed,) = scatter([partial], False, cid["scatter_wide"])
-    summed, partial_four = lax.optimization_barrier((summed, partial_four))
+    summed, partial_four, attn_given = lax.optimization_barrier(
+        (summed, partial_four, attn_given)
+    )
+    attn_wire = lowered(attn_kept.astype(jnp.float32) + attn_given.astype(jnp.float32))
     (summed_four,) = scatter([partial_four], True, cid["scatter_full"])
     width = normed_own.shape[1]
     pieces = [
@@ -1037,47 +1225,36 @@
     for offset in range(1, halo_shards + 1):
         piece = shifted(lowered(pieces[halo_shards - offset]), -offset)
         keyvalue_total = keyvalue_total + piece.astype(jnp.float32)
-    keyvalue_total, attn_wire, done_two, summed_four = lax.optimization_barrier(
-        (keyvalue_total, attn_wire, done_two, summed_four)
-    )
-    done_attn = reduce_high(attn_wire)
-    own_position = lax.dynamic_slice_in_dim(position, tp * own_rows, own_rows, 0)
-    rotate_own = functools.partial(rotate, position=own_position)
-    key_grad = jax.vjp(rotate_own, keyvalue_total[:, :HD])[1](keyvalue_total[:, :HD])[0]
+    keyvalue_total, summed_four = lax.optimization_barrier((keyvalue_total, summed_four))
+    key_grad = rotate_back(keyvalue_total[:, :HD], own_factors)
     keyvalue_low = lowered(jnp.concatenate([key_grad, keyvalue_total[:, HD:]], axis=1))
     grad_normed = summed[:, :width] + product_right(keyvalue_low, keyvalue_full)
-    (keyvalue_grads,) = gather([keyvalue_low], False, cid["gather_narrow"])
-    part_rows = keyvalue_weight.shape[0]
-    ways_view = normed_three.reshape(shard_rows, high * LO, ways, part_rows)
-    ours_only = lax.dynamic_slice_in_dim(ways_view, tp, 1, 2).reshape(shard_rows, -1)
-    grad_keyvalue = lowered(product_left(ours_only, keyvalue_grads))
     stream_grad, gain_three = jax.vjp(rms_norm, stream_two, norm_gains[2])[1](grad_normed)
     grad_stream = grad_stream + stream_grad
 
     (grad_low,) = gather([lowered(grad_stream)], True, cid["gather_full"])
-    grad_low, done_two = lax.optimization_barrier((grad_low, done_two))
-    done_two = dense_grads(done_two)
-    grad_stream, gain_two, grad_both_one, grad_down_one, done_attn = dense_backward(
-        stream_one,
-        norm_gains[1],
-        grad_stream,
-        grad_low,
-        kept_one,
-        weights_one,
-        cid,
-        done_attn,
-    )
-
-    one_wire = jnp.concatenate([grad_both_one, grad_down_one], axis=1)
+    grad_low, attn_wire, done_two = lax.optimization_barrier((grad_low, attn_wire, done_two))
+    done_attn = reduce_high(attn_wire)
+    done_two = dense_grads(exchanged(done_two))
+    grad_normed, one_wire = dense_call(
+        "backward", normed_two, grad_low, weights_one, ab_one, cid["backward"]
+    )
+    stream_grad, gain_two = jax.vjp(rms_norm, stream_one, norm_gains[1])[1](grad_normed)
+    grad_stream = grad_stream + stream_grad
     grad_stream, one_wire, done_attn = lax.optimization_barrier(
         (grad_stream, one_wire, done_attn)
     )
+    grad_stream, keyvalue_low = lax.optimization_barrier((grad_stream, keyvalue_low))
     done_one = reduce_high(one_wire)
+    (keyvalue_grads,) = gather([keyvalue_low], False, cid["gather_narrow"])
+    grad_keyvalue = lowered(product_left(normed_three, keyvalue_grads))
+    grad_keyvalue = grad_keyvalue.reshape(high * LO, ways, part_rows, part_width)
+    grad_keyvalue = lax.dynamic_slice_in_dim(grad_keyvalue, tp, 1, 1)
     (grad_out_low,) = gather([lowered(grad_stream)], True, cid["gather_full"])
     grad_recur_out = product_left(grad_out_low, mixed)
     grad_mixed = product(grad_out_low, output_full)
     grad_mixed, done_attn, done_two = lax.optimization_barrier((grad_mixed, done_attn, done_two))
-    done_attn = summed_low(done_attn)
+    done_attn = done_attn.astype(jnp.float32)
     grad_state = grad_mixed * gate_act
     grad_gating = lowered(gate_pull(grad_mixed * state)[0])
     decay_next = jnp.concatenate([decay[1:], jnp.ones((1, channels), jnp.float32)], axis=0)
@@ -1128,7 +1305,7 @@
         axis=1,
     )
     layer_own = lowered((stream_three + summed_four) * valid[:, None])
-    layer_own, both_low = lax.optimization_barrier((layer_own, both_low))
+    layer_own, wire = lax.optimization_barrier((layer_own, wire))
     (layer_out,) = gather([layer_own], False, cid["gather_half"])
     wire, done_one, layer_out = lax.optimization_barrier((wire, done_one, layer_out))
     last = exchanged(reduce_high(wire.reshape(-1, 3 * channels)))
@@ -1149,8 +1326,11 @@
     )
     rms_local = functools.partial(rms_norm, gain=norm_gains[0])
     stream_grad = jax.vjp(rms_local, stream_in)[1](grad_normed)[0]
-    (input_grad,) = gather([lowered(grad_stream + stream_grad)], False, cid["gather_half"])
+    input_own = lowered(grad_stream + stream_grad)
+    done_one = exchanged(done_one)
+    (input_grad,) = gather([input_own], False, cid["gather_half"])
     gains_sum = gains_sum[: norm_gains.shape[0]]
+    input_grad, done_one = lax.optimization_barrier((input_grad, done_one))
     input_grad = input_grad.astype(jnp.float32)
     return (
         layer_out,

time: 774 us -> 695 us (0.90)
  Pallas kernels: 368 us -> 450 us
  matrix products: 99.7 us -> 33 us
  waiting for transfers between devices: 90.8 us -> 28.4 us
  local copies, waits for them, and re-layouts: 64.5 us -> 48.4 us
  other arithmetic: 97.1 us -> 84 us
    pallas_call x0 -> x4, Pallas kernels: none -> 94 us  [the longest x3 85.6 us: dense_call(): pl.pallas_call(functools.partial(dense_kernel, mode, main), out_shape=sha...]
    pallas_call x7 -> x4, Pallas kernels: 121 us -> 65.7 us  [scatter(): pl.pallas_call(functools.partial(scatter_kernel, full, count), out_shape=...]
    pallas_call x10 -> x12, Pallas kernels: 183 us -> 225 us  [gather(): pl.pallas_call(functools.partial(gather_kernel, full, count), out_shape=[...]
    dot_general x13 -> x9, matrix products: 38.5 us -> 11.7 us  [product(): return jnp.dot(left, right, preferred_element_type=jnp.float32)]
    ppermute x9 -> x8, waiting for transfers between devices: 42.1 us -> 18 us  [swap_low(): lax.ppermute(block, 'seq', [(s, s // LO * LO + (1 - s % LO)) for s in ran...]
    all_gather x3, waiting for transfers between devices: 27.6 us -> 7.78 us  [gather_high(): lax.all_gather(rows, 'seq', axis=0, tiled=True, axis_index_groups=high_gr...]
    dot_general x13 -> x9, matrix products: 28.8 us -> 10.7 us  [product_right(): lax.dot_general(left, right, (((1,), (1,)), ((), ())), preferred_element_...]
    reduce_scatter x4, waiting for transfers between devices: 18.2 us -> 0.59 us  [reduce_high(): lax.psum_scatter(lowered(grad), 'seq', scatter_dimension=0, tiled=True, a...]
  transfers between devices with their start and end apart: 25 -> 22, of which waited for: 11 -> 8; matrix products, arithmetic and copies ran while one was open for 26% -> 20% of each run, Pallas kernels for 46% -> 61%
where the time goes in v3:
time: 695 us; the launch traced here: 687 us
  Pallas kernels  450 us (65%)
  other arithmetic  84 us (12%)
  local copies, waits for them, and re-layouts  48.4 us (7%)
  matrix products  33 us (5%)
  waiting for transfers between devices  28.4 us (4%)
  starting transfers between devices  25.1 us (4%)
  between operations  17.2 us (2%)
    pallas_call x12, Pallas kernels, gather(): pl.pallas_call(functools.partial(gather_kernel, full, count), out_shape=[...  225 us
    pallas_call x3, Pallas kernels, dense_call(): pl.pallas_call(functools.partial(dense_kernel, mode, main), out_shape=sha...  85.6 us
    pallas_call x4, Pallas kernels, scatter(): pl.pallas_call(functools.partial(scatter_kernel, full, count), out_shape=...  65.7 us
    pallas_call x1, Pallas kernels, scatter_and_sums(): pl.pallas_call(functools.partial(last_kernel, high), out_shape=[jax.Shape...  28.5 us
    pallas_call x2, Pallas kernels, plane_scan(): pl.pallas_call(functools.partial(scan_kernel, high, reverse), out_shape=(...  27.8 us
    convert_element_type x17, other arithmetic, lowered(): return values.astype(jnp.bfloat16)  19 us
    unnamed x339, local copies, waits for them, and re-layouts  19 us
    ppermute x8, waiting for transfers between devices, swap_low(): lax.ppermute(block, 'seq', [(s, s // LO * LO + (1 - s % LO)) for s in ran...  18 us
  transfers between devices with their start and end apart: 22, of which 8 were waited for; matrix products, arithmetic and copies ran while one was open for 20% of the time, Pallas kernels for 61%

profile of v3, /device:TPU:0, one launch (start us, length us, event | category | flops | bytes accessed | tf_op | source)
XLA Modules:
  0.0 686.6 jit_solution(15363627347389588751)
XLA Ops:
  10.0 1.9 broadcast_select_fusion.11
  11.9 2.9 collective-permute-start
  21.3 30.4 %gather_full.6 = bf16[8,128,1536]{2,1,0:T(8,128)(2,1)} custom-call(bf16[128,1536]{1,0:T(8,128)(2,1)} %fusion.39.refs_0_), custom_call_target="tpu_custom_call" | custom-call | bytes 60000000 | tf_op jit(solution)/shard_map/gather_full/pallas_call | solution.py:228
  55.2 1.9 fusion.41.refs_0_
  57.2 1.8 collective-permute-start.2
  59.1 43.2 %gather_full.7 = bf16[8,128,1536]{2,1,0:T(8,128)(2,1)} custom-call(bf16[128,1536]{1,0:T(8,128)(2,1)} %fusion.41.refs_0_), custom_call_target="tpu_custom_call" | custom-call | bytes 60000000 | tf_op jit(solution)/shard_map/gather_full/pallas_call | solution.py:228
  107.1 1.5 select_bitcast_fusion.1
  108.5 1.7 pad_maximum_fusion.1
  110.2 1.6 slice.635
  115.1 3.7 fusion.152
  120.7 4.3 collective-permute-start.3
  127.9 3.6 fusion.131
  133.4 2.5 slice.656
  136.9 1.6 collective-permute-start.4
  139.2 8.9 %gather_half.6 = bf16[4,384,256]{2,1,0:T(8,128)(2,1)} custom-call(bf16[384,256]{1,0:T(8,128)(2,1)} %reshape.440.refs_0_), custom_call_target="tpu_custom_call" | custom-call | bytes 60000000 | tf_op jit(solution)/shard_map/gather_half/pallas_call | solution.py:228
  148.2 2.1 copy.69
  154.4 9.6 %scan.1 = (f32[1024,256]{1,0:T(8,128)S(1)}, f32[8,256]{1,0:T(8,128)S(1)}) custom-call(f32[1024,256]{1,0:T(8,128)S(1)} %get-tuple-element.246.decay_ref, f32[1024,256]{1,0:T(8,128)S(1)} %get-tuple-element.245.drive_ref, f32[8,256]{1,0:T(8,128)S(1)} %broadcast_in_dim.71.end_ref), custom_call_target="tpu_custom_call" | custom-call | bytes 33000000 | tf_op jit(solution)/shard_map/scan/pallas_call | solution.py:473
  167.8 2.3 convolution_convert_fusion
  170.1 17.8 %scatter_full.2 = f32[128,1536]{1,0:T(8,128)S(1)} custom-call(bf16[8,128,1536]{2,1,0:T(8,128)(2,1)S(1)} %bitcast.193), custom_call_target="tpu_custom_call" | custom-call | bytes 60000000 | tf_op jit(solution)/shard_map/scatter_full/pallas_call | solution.py:386
  190.9 18.2 %gather_full.8 = bf16[8,128,1536]{2,1,0:T(8,128)(2,1)} custom-call(bf16[128,1536]{1,0:T(8,128)(2,1)} %multiply_convert_fusion.4.refs_0_), custom_call_target="tpu_custom_call" | custom-call | bytes 60000000 | tf_op jit(solution)/shard_map/gather_full/pallas_call | solution.py:228
  209.2 7.5 %all-gather.8.cloned.1.call-done.refs_1_.refs_2_ = bf16[1536,1792]{1,0:T(8,128)(2,1)} async-done(((bf16[384,1792]{1,0:T(8,128)(2,1)}), bf16[1536,1792]{1,0:T(8,128)(2,1)}) %all-gather.8.cloned.1.call-update) | async-done | bytes 5505040 | tf_op jit(solution)/shard_map/all_gather | solution.py:891
  216.9 23.8 %dense_forward.1 = (f32[128,1536]{1,0:T(8,128)}, f32[1024,1152]{1,0:T(8,128)}) custom-call(bf16[1024,1536]{1,0:T(8,128)(2,1)} %bitcast.199, bf16[1536,1792]{1,0:T(8,128)(2,1)} %all-gather.8.cloned.1.call-done.refs_1_.refs_2_), custom_call_target="tpu_custom_call" | custom-call | bytes 80000000 | tf_op jit(solution)/shard_map/dense_forward/pallas_call | solution.py:733
  244.7 3.4 collective-permute-start.6
  248.2 1.7 collective-permute-done.6
  250.6 20.0 %gather_half.7 = (bf16[4,128,1536]{2,1,0:T(8,128)(2,1)}, bf16[4,128,768]{2,1,0:T(8,128)(2,1)}) custom-call(bf16[128,1536]{1,0:T(8,128)(2,1)} %copy-done.55, bf16[128,768]{1,0:T(8,128)(2,1)} %pad_maximum_fusion.19.refs_1_), custom_call_target="tpu_custom_call" | custom-call | bytes 60000000 | tf_op jit(solution)/shard_map/gather_half/pallas_call | solution.py:228
  273.7 8.4 %attention.1 = (bf16[512,384]{1,0:T(8,128)(2,1)S(1)}, bf16[512,384]{1,0:T(8,128)(2,1)S(1)}, f32[8,512]{1,0:T(8,128)S(1)}) custom-call(f32[512,384]{1,0:T(8,128)S(1)} %fusion.154.query_ref, bf16[1536,256]{1,0:T(8,128)(2,1)S(1)} %pad_maximum_fusion.9.ext_ref, s32[8,512]{1,0:T(8,128)S(1)} %broadcast_in_dim.76.here_ref, ...), custom_call_target="tpu_custom_call" | custom-call | bytes 33000000 | tf_op jit(solution)/shard_map/attention/pallas_call | solution.py:793
  283.2 13.1 %scatter_half.2 = f32[128,1536]{1,0:T(8,128)S(1)} custom-call(bf16[4,128,1536]{2,1,0:T(8,128)(2,1)S(1)} %bitcast.197), custom_call_target="tpu_custom_call" | custom-call | bytes 60000000 | tf_op jit(solution)/shard_map/scatter_half/pallas_call | solution.py:386
  297.3 2.0 multiply_convert_fusion.2.refs_0_
  299.3 19.9 %gather_full.9 = bf16[8,128,1536]{2,1,0:T(8,128)(2,1)} custom-call(bf16[128,1536]{1,0:T(8,128)(2,1)} %multiply_convert_fusion.2.refs_0_), custom_call_target="tpu_custom_call" | custom-call | bytes 60000000 | tf_op jit(solution)/shard_map/gather_full/pallas_call | solution.py:228
  319.5 30.8 %dense_both.1 = (f32[128,1536]{1,0:T(8,128)}, bf16[1536,1792]{1,0:T(8,128)(2,1)}, bf16[1024,1536]{1,0:T(8,128)(2,1)}) custom-call(bf16[1024,1536]{1,0:T(8,128)(2,1)} %bitcast.205, bf16[1024,1536]{1,0:T(8,128)(2,1)} %bitcast.204, bf16[1536,1792]{1,0:T(8,128)(2,1)} %all-gather.10.cloned.1.call-done.refs_2_), custom_call_target="tpu_custom_call" | custom-call | bytes 100000000 | tf_op jit(solution)/shard_map/dense_both/pallas_call | solution.py:733
  350.4 2.2 multiply_reduce_fusion.6
  352.6 2.5 fusion.127
  355.2 14.7 %gather_half.8 = bf16[4,128,1536]{2,1,0:T(8,128)(2,1)} custom-call(bf16[128,1536]{1,0:T(8,128)(2,1)} %get-tuple-element.202.refs_0_), custom_call_target="tpu_custom_call" | custom-call | bytes 60000000 | tf_op jit(solution)/shard_map/gather_half/pallas_call | solution.py:228
  369.9 2.9 convolution_convert_fusion.8.grad_ref
  372.8 9.9 %attention_back.1 = (bf16[512,384]{1,0:T(8,128)(2,1)S(1)}, bf16[1536,256]{1,0:T(8,128)(2,1)S(1)}) custom-call(bf16[512,384]{1,0:T(8,128)(2,1)S(1)} %copy-done.8, bf16[1536,256]{1,0:T(8,128)(2,1)S(1)} %copy-done.1, bf16[512,384]{1,0:T(8,128)(2,1)S(1)} %convolution_convert_fusion.8.grad_ref, f32[8,512]{1,0:T(8,128)S(1)} %get-tuple-element.133.log_ref, ...), custom_call_target="tpu_custom_call" | custom-call | bytes 60000000 | tf_op jit(solution)/shard_map/attention_back/pallas_call | solution.py:848
  387.1 1.5 collective-permute-start.7
  388.6 16.3 %scatter_half.3 = f32[128,2304]{1,0:T(8,128)S(1)} custom-call(bf16[4,128,2304]{2,1,0:T(8,128)(2,1)S(1)} %bitcast.195), custom_call_target="tpu_custom_call" | custom-call | bytes 60000000 | tf_op jit(solution)/shard_map/scatter_half/pallas_call | solution.py:386
  404.9 9.9 %collective-permute-done.7 = bf16[4,192,768]{2,1,0:T(8,128)(2,1)S(1)} collective-permute-done((bf16[4,192,768]{2,1,0:T(8,128)(2,1)S(1)}, bf16[4,192,768]{2,1,0:T(8,128)(2,1)S(1)}, u32[]{:S(2)}, u32[]{:S(2)}) %collective-permute-start.7) | collective-permute-done | bytes 1179680 | tf_op jit(solution)/shard_map/ppermute | solution.py:870
  419.4 2.0 copy-done.2
  421.5 18.4 %scatter_full.3 = f32[128,1536]{1,0:T(8,128)S(1)} custom-call(bf16[8,128,1536]{2,1,0:T(8,128)(2,1)S(1)} %bitcast.198), custom_call_target="tpu_custom_call" | custom-call | bytes 60000000 | tf_op jit(solution)/shard_map/scatter_full/pallas_call | solution.py:386
  444.2 18.2 %gather_full.10 = bf16[8,128,1536]{2,1,0:T(8,128)(2,1)} custom-call(bf16[128,1536]{1,0:T(8,128)(2,1)} %get-tuple-element.200.refs_0_), custom_call_target="tpu_custom_call" | custom-call | bytes 60000000 | tf_op jit(solution)/shard_map/gather_full/pallas_call | solution.py:228
  465.8 31.0 %dense_backward.1 = (f32[128,1536]{1,0:T(8,128)}, bf16[1536,1792]{1,0:T(8,128)(2,1)}) custom-call(bf16[1024,1536]{1,0:T(8,128)(2,1)} %bitcast.200, bf16[1024,1536]{1,0:T(8,128)(2,1)} %bitcast.206, bf16[1536,1792]{1,0:T(8,128)(2,1)} %all-gather.8.cloned.1.call-done.refs_1_.refs_2_, f32[1024,1152]{1,0:T(8,128)} %get-tuple-element.147.refs_3_), custom_call_target="tpu_custom_call" | custom-call | bytes 100000000 | tf_op jit(solution)/shard_map/dense_backward/pallas_call | solution.py:733
  496.9 2.0 multiply_reduce_fusion.8
  501.2 2.0 multiply_convert_fusion.1.refs_0_
  508.8 17.2 %gather_full.11 = bf16[8,128,1536]{2,1,0:T(8,128)(2,1)} custom-call(bf16[128,1536]{1,0:T(8,128)(2,1)} %convert_element_type.230.refs_0_), custom_call_target="tpu_custom_call" | custom-call | bytes 60000000 | tf_op jit(solution)/shard_map/gather_full/pallas_call | solution.py:228
  525.9 3.0 fusion.155
  529.0 1.6 fusion.11
  530.7 18.3 %scan_back.1 = (f32[1024,256]{1,0:T(8,128)S(1)}, f32[8,256]{1,0:T(8,128)}) custom-call(f32[1024,256]{1,0:T(8,128)S(1)} %concatenate.178.decay_ref, f32[1024,256]{1,0:T(8,128)S(1)} %get-tuple-element.218.drive_ref, f32[8,256]{1,0:T(8,128)S(1)} %broadcast_in_dim.82.end_ref), custom_call_target="tpu_custom_call" | custom-call | bytes 33000000 | tf_op jit(solution)/shard_map/scan_back/pallas_call | solution.py:473
  549.0 3.5 fusion.122
  554.9 2.9 multiply_reduce_fusion.5
  559.2 1.5 collective-permute-start.11
  560.8 6.1 gather_half.9
  566.9 1.4 convolution_convert_fusion.12
  577.4 1.9 convolution_convert_fusion.7
  580.2 3.6 convolution_convert_fusion.1
  583.8 1.8 convolution_convert_fusion.2
  585.6 2.9 pad_maximum_fusion
  588.5 13.8 %gather_half.10 = bf16[4,128,1536]{2,1,0:T(8,128)(2,1)} custom-call(bf16[128,1536]{1,0:T(8,128)(2,1)} %multiply_convert_fusion.1.refs_0_), custom_call_target="tpu_custom_call" | custom-call | bytes 60000000 | tf_op jit(solution)/shard_map/gather_half/pallas_call | solution.py:228
  605.0 2.8 multiply_reduce_fusion
  608.7 28.5 %scatter_and_sums.1 = (f32[128,1536]{1,0:T(8,128)S(1)}, f32[8,1536]{1,0:T(8,128)S(1)}, f32[8,512]{1,0:T(8,128)S(1)}) custom-call(bf16[8,128,1536]{2,1,0:T(8,128)(2,1)S(1)} %bitcast.194, f32[8,1536]{1,0:T(8,128)S(1)} %concatenate.197.gains_ref, f32[8,256]{1,0:T(8,128)S(1)} %pad_maximum_fusion.23.rest_ref), custom_call_target="tpu_custom_call" | custom-call | bytes 60000000 | tf_op jit(solution)/shard_map/scatter_and_sums/pallas_call | solution.py:556
  638.7 1.6 collective-permute-start.12
  641.3 14.0 %gather_half.11 = bf16[4,128,1536]{2,1,0:T(8,128)(2,1)} custom-call(bf16[128,1536]{1,0:T(8,128)(2,1)} %fusion.36.refs_0_), custom_call_target="tpu_custom_call" | custom-call | bytes 60000000 | tf_op jit(solution)/shard_map/gather_half/pallas_call | solution.py:228
  658.0 2.1 convert_element_type.244
  665.8 8.1 %collective-permute-done.13 = bf16[224,768]{1,0:T(8,128)(2,1)S(1)} collective-permute-done((bf16[224,768]{1,0:T(8,128)(2,1)S(1)}, bf16[224,768]{1,0:T(8,128)(2,1)S(1)}, u32[]{:S(2)}, u32[]{:S(2)}) %collective-permute-start.13) | collective-permute-done | bytes 344096 | tf_op jit(solution)/shard_map/ppermute | solution.py:870
  (565 shorter events, 107.2 us)
Async XLA Ops:
  7.2 46.8 %all-gather.12.cloned.1.call-start = ((), (), s32[]{:S(2)}) async-start(), calls=%async_computation.11 | async-start | bytes 1597440 | tf_op jit(solution)/shard_map/all_gather | solution.py:1087
  11.9 40.1 %collective-permute-start = (bf16[208,768]{1,0:T(8,128)(2,1)}, bf16[208,768]{1,0:T(8,128)(2,1)}, u32[]{:S(2)}, u32[]{:S(2)}) collective-permute-start(bf16[208,768]{1,0:T(8,128)(2,1)} %broadcast_select_fusion.11), channel_id=1, source_target_pairs={{0,4},{4,0},{8,12},{12,8},{16,20},{20,16},{24,28},{28,24},{1,5},{5... | collective-permute-start | bytes 958472 | tf_op jit(solution)/shard_map/ppermute | solution.py:870
  15.6 94.6 %all-gather.6.cloned.1.call-start = ((), (), s32[]{:S(2)}) async-start(), calls=%async_computation.4 | async-start | bytes 3194880 | tf_op jit(solution)/shard_map/all_gather | solution.py:891
  19.4 84.6 %collective-permute-start.1 = (bf16[192,1792]{1,0:T(8,128)(2,1)}, bf16[192,1792]{1,0:T(8,128)(2,1)}, u32[]{:S(2)}, u32[]{:S(2)}) collective-permute-start(bf16[192,1792]{1,0:T(8,128)(2,1)} %broadcast_select_fusion.7), channel_id=1, source_target_pairs={{0,4},{4,0},{8,12},{12,8},{16,20},{20,16},{24,28},{28,24},{1,5},{5... | collective-permute-start | bytes 2064392 | tf_op jit(solution)/shard_map/ppermute | solution.py:870
  19.6 32.1 %copy-start.156 = (f32[128]{0:T(128)}, f32[128]{0:T(128)S(1)}, u32[]{:S(2)}) copy-start(f32[128]{0:T(128)S(1)} %fusion.37) | copy-start | bytes 1540
  20.3 31.4 %copy-start.97 = (f32[1536]{0:T(1024)}, f32[1536]{0:T(1024)S(1)}, u32[]{:S(2)}) copy-start(f32[1536]{0:T(1024)S(1)} %get-tuple-element.192) | copy-start | bytes 18436
  20.3 31.4 %copy-start.150 = (f32[128]{0:T(128)}, f32[128]{0:T(128)S(1)}, u32[]{:S(2)}) copy-start(f32[128]{0:T(128)S(1)} %fusion.114) | copy-start | bytes 1540
  21.2 30.5 %copy-start.166 = (s32[4]{0:T(128)S(1)}, s32[4]{0:T(128)}, u32[]{:S(2)}) copy-start(s32[4]{0:T(128)} %param.24) | copy-start | bytes 52
  21.2 30.7 %copy-start.68 = (bf16[192,512]{1,0:T(8,128)(2,1)S(1)}, bf16[192,512]{1,0:T(8,128)(2,1)}, u32[]{:S(2)}) copy-start(bf16[192,512]{1,0:T(8,128)(2,1)} %param.27) | copy-start | bytes 589828
  21.2 30.7 %copy-start.69 = (bf16[192,512]{1,0:T(8,128)(2,1)S(1)}, bf16[192,512]{1,0:T(8,128)(2,1)}, u32[]{:S(2)}) copy-start(bf16[192,512]{1,0:T(8,128)(2,1)} %param.26) | copy-start | bytes 589828
  21.2 30.7 %copy-start.75 = (bf16[208,256]{1,0:T(8,128)(2,1)S(1)}, bf16[208,256]{1,0:T(8,128)(2,1)}, u32[]{:S(2)}) copy-start(bf16[208,256]{1,0:T(8,128)(2,1)} %copy-done.74) | copy-start | bytes 319492
  21.2 30.8 %copy-start.77 = (bf16[208,256]{1,0:T(8,128)(2,1)S(1)}, bf16[208,256]{1,0:T(8,128)(2,1)}, u32[]{:S(2)}) copy-start(bf16[208,256]{1,0:T(8,128)(2,1)} %copy-done.76) | copy-start | bytes 319492
  21.2 30.7 %copy-start.93 = (bf16[512,16]{0,1:T(8,128)(2,1)S(1)}, bf16[512,16]{0,1:T(8,128)(2,1)}, u32[]{:S(2)}) copy-start(bf16[512,16]{0,1:T(8,128)(2,1)} %param.31) | copy-start | bytes 49156
  21.2 30.7 %copy-start.94 = (bf16[512,16]{0,1:T(8,128)(2,1)S(1)}, bf16[512,16]{0,1:T(8,128)(2,1)}, u32[]{:S(2)}) copy-start(bf16[512,16]{0,1:T(8,128)(2,1)} %param.30) | copy-start | bytes 49156
  54.0 162.6 %all-gather.8.cloned.1.call-start = ((), (), s32[]{:S(2)}) async-start(), calls=%async_computation.5 | async-start | bytes 6881280 | tf_op jit(solution)/shard_map/all_gather | solution.py:891
  55.2 47.1 %copy-start.139 = (f32[128]{0:T(128)}, f32[128]{0:T(128)S(1)}, u32[]{:S(2)}) copy-start(f32[128]{0:T(128)S(1)} %compare_convert_fusion.2) | copy-start | bytes 1540
  57.2 49.3 %collective-permute-start.2 = (bf16[4,208,768]{2,1,0:T(8,128)(2,1)}, bf16[4,208,768]{2,1,0:T(8,128)(2,1)}, u32[]{:S(2)}, u32[]{:S(2)}) collective-permute-start(bf16[4,208,768]{2,1,0:T(8,128)(2,1)} %bitcast.235), channel_id=1, source_target_pairs={{0,4},{4,0},{8,12},{12,8},{16,20},{20,16},{24,28},{28,24},{1,5},{5... | collective-permute-start | bytes 3833864 | tf_op jit(solution)/shard_map/ppermute | solution.py:870
  59.1 43.2 %copy-start.162 = (f32[512]{0:T(512)S(1)}, f32[512]{0:T(512)}, u32[]{:S(2)}) copy-start(f32[512]{0:T(512)} %param.29) | copy-start | bytes 6148
  111.9 207.6 %all-gather.10.cloned.1.call-start = ((), (), s32[]{:S(2)}) async-start(), calls=%async_computation.6 | async-start | bytes 6881280 | tf_op jit(solution)/shard_map/all_gather | solution.py:891
  114.7 35.5 %copy-start.103 = (f32[1024]{0:T(1024)}, f32[1024]{0:T(1024)S(1)}, u32[]{:S(2)}) copy-start(f32[1024]{0:T(1024)S(1)} %get-tuple-element.311) | copy-start | bytes 12292
  114.7 35.5 %copy-start.105 = (f32[1024]{0:T(1024)}, f32[1024]{0:T(1024)S(1)}, u32[]{:S(2)}) copy-start(f32[1024]{0:T(1024)S(1)} %get-tuple-element.312) | copy-start | bytes 12292
  114.8 35.5 %copy-start.107 = (f32[1024]{0:T(1024)}, f32[1024]{0:T(1024)S(1)}, u32[]{:S(2)}) copy-start(f32[1024]{0:T(1024)S(1)} %get-tuple-element.313) | copy-start | bytes 12292
  120.7 29.6 %collective-permute-start.3 = (f32[3,256]{1,0:T(4,128)}, f32[3,256]{1,0:T(4,128)S(1)}, u32[]{:S(2)}, u32[]{:S(2)}) collective-permute-start(f32[3,256]{1,0:T(4,128)} %slice.524), channel_id=1, source_target_pairs={{0,8},{4,12},{8,16},{12,20},{16,24},{20,28},{1,9},{5,13},{9,17},{1... | collective-permute-start | bytes 9224 | tf_op jit(solution)/shard_map/ppermute | solution.py:944
  133.3 18.0 %copy-start.79 = (bf16[8,16,256]{2,1,0:T(8,128)(2,1)}, bf16[8,16,256]{2,1,0:T(8,128)(2,1)S(1)}, u32[]{:S(2)}) copy-start(bf16[8,16,256]{2,1,0:T(8,128)(2,1)S(1)} %get-tuple-element.222) | copy-start | bytes 196612
  136.9 28.3 %collective-permute-start.4 = (bf16[192,1792]{1,0:T(8,128)(2,1)}, bf16[192,1792]{1,0:T(8,128)(2,1)}, u32[]{:S(2)}, u32[]{:S(2)}) collective-permute-start(bf16[192,1792]{1,0:T(8,128)(2,1)} %broadcast_select_fusion.5), channel_id=1, source_target_pairs={{0,4},{4,0},{8,12},{12,8},{16,20},{20,16},{24,28},{28,24},{1,5},{5... | collective-permute-start | bytes 2064392 | tf_op jit(solution)/shard_map/ppermute | solution.py:870
  189.2 19.9 %copy-start.158 = (f32[128]{0:T(128)}, f32[128]{0:T(128)S(1)}, u32[]{:S(2)}) copy-start(f32[128]{0:T(128)S(1)} %get-tuple-element.208) | copy-start | bytes 1540
  189.2 19.9 %copy-start.135 = (f32[128]{0:T(128)}, f32[128]{0:T(128)S(1)}, u32[]{:S(2)}) copy-start(f32[128]{0:T(128)S(1)} %fusion.115) | copy-start | bytes 1540
  190.9 18.2 %copy-start.134 = (s32[512]{0:T(512)S(1)}, s32[512]{0:T(512)}, u32[]{:S(2)}) copy-start(s32[512]{0:T(512)} %compare_select_fusion.5) | copy-start | bytes 6148
  216.7 245.7 %reduce-scatter.5.cloned.1.call-start = ((), (), s32[]{:S(2)}) async-start(), calls=%async_computation.7 | async-start | bytes 6881280 | tf_op jit(solution)/shard_map/reduce_scatter | solution.py:895
  216.9 23.9 %copy-start.10 = (f32[128,1536]{1,0:T(8,128)S(1)}, f32[128,1536]{1,0:T(8,128)}, u32[]{:S(2)}) copy-start(f32[128,1536]{1,0:T(8,128)} %copy-done.9) | copy-start | bytes 2359300
  243.4 4.9 collective-permute-start.5
  244.7 5.3 collective-permute-start.6
  350.3 149.8 %reduce-scatter.7.cloned.1.call-start = ((), (), s32[]{:S(2)}) async-start(), calls=%async_computation.8 | async-start | bytes 1474560 | tf_op jit(solution)/shard_map/reduce_scatter | solution.py:895
  387.1 27.7 %collective-permute-start.7 = (bf16[4,192,768]{2,1,0:T(8,128)(2,1)S(1)}, bf16[4,192,768]{2,1,0:T(8,128)(2,1)S(1)}, u32[]{:S(2)}, u32[]{:S(2)}) collective-permute-start(bf16[4,192,768]{2,1,0:T(8,128)(2,1)S(1)} %get-tuple-element.226), channel_id=1, source_target_pairs={{0,4},{4,0},{8,12},{12,8},{16,20},{20,16},{24,28},{28,24},{1,5},{5... | collective-permute-start | bytes 3538952 | tf_op jit(solution)/shard_map/ppermute | solution.py:870
  415.5 24.5 %collective-permute-start.8 = (bf16[128,256]{1,0:T(8,128)(2,1)}, bf16[128,256]{1,0:T(8,128)(2,1)S(1)}, u32[]{:S(2)}, u32[]{:S(2)}) collective-permute-start(bf16[128,256]{1,0:T(8,128)(2,1)} %get-tuple-element.259), channel_id=1, source_target_pairs={{4,0},{8,4},{12,8},{16,12},{20,16},{24,20},{28,24},{5,1},{9,5},{13... | collective-permute-start | bytes 196616 | tf_op jit(solution)/shard_map/ppermute | solution.py:944
  416.8 23.9 %collective-permute-start.9 = (bf16[128,256]{1,0:T(8,128)(2,1)S(1)}, bf16[128,256]{1,0:T(8,128)(2,1)}, u32[]{:S(2)}, u32[]{:S(2)}) collective-permute-start(bf16[128,256]{1,0:T(8,128)(2,1)S(1)} %get-tuple-element.260), channel_id=1, source_target_pairs={{8,0},{12,4},{16,8},{20,12},{24,16},{28,20},{9,1},{13,5},{17,9},{2... | collective-permute-start | bytes 196616 | tf_op jit(solution)/shard_map/ppermute | solution.py:944
  421.4 20.2 %copy-start.82 = (f32[128,128]{1,0:T(8,128)S(1)}, f32[128,128]{1,0:T(8,128)}, u32[]{:S(2)}) copy-start(f32[128,128]{1,0:T(8,128)} %get-tuple-element.119) | copy-start | bytes 196612
  421.4 20.2 %copy-start.84 = (f32[128,128]{1,0:T(8,128)S(1)}, f32[128,128]{1,0:T(8,128)}, u32[]{:S(2)}) copy-start(f32[128,128]{1,0:T(8,128)} %get-tuple-element.118) | copy-start | bytes 196612
  421.4 20.3 %copy-start.14 = (f32[128,1536]{1,0:T(8,128)S(1)}, f32[128,1536]{1,0:T(8,128)}, u32[]{:S(2)}) copy-start(f32[128,1536]{1,0:T(8,128)} %copy-done.12) | copy-start | bytes 2359300
  421.4 20.3 %copy-start.35 = (bf16[4,8,48,256]{3,2,0,1:T(8,128)(2,1)S(1)}, bf16[4,8,48,256]{3,2,0,1:T(8,128)(2,1)}, u32[]{:S(2)}) copy-start(bf16[4,8,48,256]{3,2,0,1:T(8,128)(2,1)} %copy.69) | copy-start | bytes 2359300
  421.4 20.3 %copy-start.101 = (f32[1536]{0:T(1024)S(1)}, f32[1536]{0:T(1024)}, u32[]{:S(2)}) copy-start(f32[1536]{0:T(1024)} %get-tuple-element.193) | copy-start | bytes 18436
  421.5 20.3 %copy-start.138 = (f32[128]{0:T(128)S(1)}, f32[128]{0:T(128)}, u32[]{:S(2)}) copy-start(f32[128]{0:T(128)} %copy-done.137) | copy-start | bytes 1540
  462.5 140.3 %reduce-scatter.9.cloned.1.call-start = ((), (), s32[]{:S(2)}) async-start(), calls=%async_computation.9 | async-start | bytes 6881280 | tf_op jit(solution)/shard_map/reduce_scatter | solution.py:895
  465.0 38.2 %collective-permute-start.10 = (bf16[192,1792]{1,0:T(8,128)(2,1)}, bf16[192,1792]{1,0:T(8,128)(2,1)}, u32[]{:S(2)}, u32[]{:S(2)}) collective-permute-start(bf16[192,1792]{1,0:T(8,128)(2,1)} %broadcast_select_fusion.3), channel_id=1, source_target_pairs={{0,4},{4,0},{8,12},{12,8},{16,20},{20,16},{24,28},{28,24},{1,5},{5... | collective-permute-start | bytes 2064392 | tf_op jit(solution)/shard_map/ppermute | solution.py:870
  465.8 31.0 %copy-start.11 = (f32[128,1536]{1,0:T(8,128)S(1)}, f32[128,1536]{1,0:T(8,128)}, u32[]{:S(2)}) copy-start(f32[128,1536]{1,0:T(8,128)} %copy-done.9) | copy-start | bytes 2359300
  465.8 31.0 %copy-start.136 = (f32[128]{0:T(128)S(1)}, f32[128]{0:T(128)}, u32[]{:S(2)}) copy-start(f32[128]{0:T(128)} %copy-done.135) | copy-start | bytes 1540
  500.1 162.5 %reduce-scatter.11.cloned.1.call-start = ((), (), s32[]{:S(2)}) async-start(), calls=%async_computation.10 | async-start | bytes 3440640 | tf_op jit(solution)/shard_map/reduce_scatter | solution.py:895
  529.0 20.0 %copy-start.31 = (f32[1024,128]{1,0:T(8,128)S(1)}, f32[1024,128]{1,0:T(8,128)}, u32[]{:S(2)}) copy-start(f32[1024,128]{1,0:T(8,128)} %copy-done.30) | copy-start | bytes 1572868
  529.0 20.0 %copy-start.33 = (f32[1024,128]{1,0:T(8,128)S(1)}, f32[1024,128]{1,0:T(8,128)}, u32[]{:S(2)}) copy-start(f32[1024,128]{1,0:T(8,128)} %copy-done.32) | copy-start | bytes 1572868
  530.6 18.4 %copy-start.16 = (f32[1024,128]{1,0:T(8,128)S(1)}, f32[1024,128]{1,0:T(8,128)}, u32[]{:S(2)}) copy-start(f32[1024,128]{1,0:T(8,128)} %copy-done.15) | copy-start | bytes 1572868
  530.6 18.4 %copy-start.18 = (f32[1024,128]{1,0:T(8,128)S(1)}, f32[1024,128]{1,0:T(8,128)}, u32[]{:S(2)}) copy-start(f32[1024,128]{1,0:T(8,128)} %copy-done.17) | copy-start | bytes 1572868
  530.6 18.4 %copy-start.25 = (f32[1024,256]{1,0:T(8,128)S(1)}, f32[1024,256]{1,0:T(8,128)}, u32[]{:S(2)}) copy-start(f32[1024,256]{1,0:T(8,128)} %copy-done.24) | copy-start | bytes 3145732
  530.6 18.4 %copy-start.112 = (f32[1024]{0:T(1024)S(1)}, f32[1024]{0:T(1024)}, u32[]{:S(2)}) copy-start(f32[1024]{0:T(1024)} %compare_convert_fusion.1) | copy-start | bytes 12292
  530.6 18.4 %copy-start.117 = (f32[1,256]{1,0:T(1,128)S(1)}, f32[1,256]{1,0:T(1,128)}, u32[]{:S(2)}) copy-start(f32[1,256]{1,0:T(1,128)} %get-tuple-element.326) | copy-start | bytes 3076
  530.6 18.4 %copy-start.122 = (f32[1,256]{1,0:T(1,128)S(1)}, f32[1,256]{1,0:T(1,128)}, u32[]{:S(2)}) copy-start(f32[1,256]{1,0:T(1,128)} %get-tuple-element.327) | copy-start | bytes 3076
  530.6 18.4 %copy-start.124 = (f32[256]{0:T(256)S(1)}, f32[256]{0:T(256)}, u32[]{:S(2)}) copy-start(f32[256]{0:T(256)} %get-tuple-element.212) | copy-start | bytes 3076
  530.6 18.4 %copy-start.125 = (f32[256]{0:T(256)S(1)}, f32[256]{0:T(256)}, u32[]{:S(2)}) copy-start(f32[256]{0:T(256)} %get-tuple-element.213) | copy-start | bytes 3076
  559.2 20.8 %collective-permute-start.11 = (f32[3,256]{1,0:T(4,128)S(1)}, f32[3,256]{1,0:T(4,128)S(1)}, u32[]{:S(2)}, u32[]{:S(2)}) collective-permute-start(f32[3,256]{1,0:T(4,128)S(1)} %pad_add_fusion.1), channel_id=1, source_target_pairs={{8,0},{12,4},{16,8},{20,12},{24,16},{28,20},{9,1},{13,5},{17,9},{2... | collective-permute-start | bytes 9224 | tf_op jit(solution)/shard_map/ppermute | solution.py:944
  608.6 29.8 %copy-start.64 = (bf16[512,1536]{1,0:T(8,128)(2,1)S(1)}, bf16[512,1536]{1,0:T(8,128)(2,1)}, u32[]{:S(2)}) copy-start(bf16[512,1536]{1,0:T(8,128)(2,1)} %param.22) | copy-start | bytes 4718596
  608.6 29.7 %copy-start.98 = (f32[1536]{0:T(1024)S(1)}, f32[1536]{0:T(1024)}, u32[]{:S(2)}) copy-start(f32[1536]{0:T(1024)} %copy-done.97) | copy-start | bytes 18436
  608.7 29.9 %copy-start.157 = (f32[128]{0:T(128)S(1)}, f32[128]{0:T(128)}, u32[]{:S(2)}) copy-start(f32[128]{0:T(128)} %copy-done.156) | copy-start | bytes 1540
  608.7 30.0 %copy-start.44 = (bf16[384,1792]{1,0:T(8,128)(2,1)S(1)}, bf16[384,1792]{1,0:T(8,128)(2,1)}, u32[]{:S(2)}) copy-start(bf16[384,1792]{1,0:T(8,128)(2,1)} %reduce-scatter.9.cloned.1.call-done) | copy-start | bytes 4128772
  638.7 17.8 %collective-permute-start.12 = (bf16[192,1792]{1,0:T(8,128)(2,1)S(1)}, bf16[192,1792]{1,0:T(8,128)(2,1)S(1)}, u32[]{:S(2)}, u32[]{:S(2)}) collective-permute-start(bf16[192,1792]{1,0:T(8,128)(2,1)S(1)} %broadcast_select_fusion.1), channel_id=1, source_target_pairs={{0,4},{4,0},{8,12},{12,8},{16,20},{20,16},{24,28},{28,24},{1,5},{5... | collective-permute-start | bytes 2064392 | tf_op jit(solution)/shard_map/ppermute | solution.py:870
  663.8 10.2 %collective-permute-start.13 = (bf16[224,768]{1,0:T(8,128)(2,1)S(1)}, bf16[224,768]{1,0:T(8,128)(2,1)S(1)}, u32[]{:S(2)}, u32[]{:S(2)}) collective-permute-start(bf16[224,768]{1,0:T(8,128)(2,1)S(1)} %broadcast_select_fusion.9), channel_id=1, source_target_pairs={{0,4},{4,0},{8,12},{12,8},{16,20},{20,16},{24,28},{28,24},{1,5},{5... | collective-permute-start | bytes 1032200 | tf_op jit(solution)/shard_map/ppermute | solution.py:870
  (125 other events, 451.4 us)
Sparse Core Ops, SparseCore 0:
  15.7 32.4 all-gather.11
  54.2 55.2 all-gather.5
  112.0 104.6 all-gather.7
  218.7 100.7 all-gather.9
  350.4 104.5 reduce-scatter.4
  462.6 33.0 reduce-scatter.6
  500.2 102.4 reduce-scatter.8
  605.1 57.5 reduce-scatter.10

commit v4 on v3

--- a/solution.py
+++ b/solution.py
@@ -208,27 +208,28 @@
     mine.wait()
 
 
-def gather_kernel(full, count, *refs):
+def gather_kernel(spans, *refs):
+    count = len(spans)
     in_refs, out_refs = (refs[:count], refs[count : 2 * count])
     send_sem, recv_sem, local_sem = refs[2 * count :]
-    greet(neighbours(full))
+    greet(neighbours(any(spans)))
     in_turn(
         *[
             gather_steps(
-                full, in_refs[k], out_refs[k], send_sem.at[k], recv_sem.at[k], local_sem.at[k]
+                spans[k], in_refs[k], out_refs[k], send_sem.at[k], recv_sem.at[k], local_sem.at[k]
             )
             for k in range(count)
         ]
     )
 
 
-def gather(blocks, full, collective_id):
-    ways = 8 if full else 4
+def gather(blocks, spans, collective_id):
     count = len(blocks)
+    ways = [8 if span else 4 for span in spans]
     results = pl.pallas_call(
-        functools.partial(gather_kernel, full, count),
+        functools.partial(gather_kernel, spans),
         out_shape=[
-            jax.ShapeDtypeStruct((ways, *block.shape), block.dtype) for block in blocks
+            jax.ShapeDtypeStruct((n, *block.shape), block.dtype) for n, block in zip(ways, blocks)
         ],
         in_specs=[ANY] * count,
         out_specs=[ANY] * count,
@@ -237,13 +238,13 @@
             pltpu.SemaphoreType.DMA((count, 13)),
             pltpu.SemaphoreType.DMA((count,)),
         ],
-        name="gather_full" if full else "gather_half",
+        name="gather_full" if any(spans) else "gather_half",
         cost_estimate=EIGHTEEN_US,
         compiler_params=pltpu.CompilerParams(collective_id=collective_id, has_side_effects=True),
     )(*blocks)
     return [
-        result.reshape(ways * block.shape[0], block.shape[1])
-        for result, block in zip(results, blocks)
+        result.reshape(n * block.shape[0], block.shape[1])
+        for n, result, block in zip(ways, results, blocks)
     ]
 
 
@@ -540,28 +541,30 @@
     return [(lax.rem(seq // LO + k, high) * LO + lax.rem(seq, LO), tp) for k in range(1, high)]
 
 
-def last_kernel(high, part_ref, gains_ref, rest_ref, out_ref, gains_out, rest_out, *more):
+def last_kernel(high, part_ref, gains_ref, rest_ref, in_ref, out_ref, gains_out, rest_out, all_ref, *more):
     greet(high_peers(high) + neighbours(True))
     in_turn(
+        small_steps(high, gains_ref, rest_ref, gains_out, rest_out, *more[13:21]),
         scatter_steps(True, part_ref, out_ref, *more[:13]),
-        small_steps(high, gains_ref, rest_ref, gains_out, rest_out, *more[13:]),
-    )
-
-
-def scatter_and_sums(partial, gains, rest, high, collective_id):
+        gather_steps(False, in_ref, all_ref, *more[21:]),
+    )
+
+
+def scatter_and_sums(partial, gains, rest, block, high, collective_id):
     slots = 2 * (high - 1) + 4
     ways = 8
     width = partial.shape[1]
     rows = partial.shape[0] // ways
-    return pl.pallas_call(
+    *sums, gathered = pl.pallas_call(
         functools.partial(last_kernel, high),
         out_shape=[
             jax.ShapeDtypeStruct((rows, width), jnp.float32),
             jax.ShapeDtypeStruct(gains.shape, jnp.float32),
             jax.ShapeDtypeStruct((rest.shape[0], LO * rest.shape[1]), jnp.float32),
+            jax.ShapeDtypeStruct((4, *block.shape), block.dtype),
         ],
-        in_specs=[VMEM] * 3,
-        out_specs=[VMEM] * 3,
+        in_specs=[VMEM] * 3 + [ANY],
+        out_specs=[VMEM] * 3 + [ANY],
         scratch_shapes=scatter_scratch(ways, rows, width)
         + [
             pltpu.VMEM((high - 1, *gains.shape), jnp.float32),
@@ -572,13 +575,17 @@
             pltpu.VMEM(rest.shape, jnp.float32),
             pltpu.SemaphoreType.DMA((slots,)),
             pltpu.SemaphoreType.DMA((slots,)),
+            pltpu.SemaphoreType.DMA((13,)),
+            pltpu.SemaphoreType.DMA((13,)),
+            pltpu.SemaphoreType.DMA,
         ],
         name="scatter_and_sums",
         cost_estimate=EIGHTEEN_US,
         compiler_params=pltpu.CompilerParams(
             collective_id=collective_id, has_side_effects=True, vmem_limit_bytes=40 * 2**20
         ),
-    )(lowered(partial).reshape(ways, rows, width), gains, rest)
+    )(lowered(partial).reshape(ways, rows, width), gains, rest, block)
+    return (*sums, gathered.reshape(-1, block.shape[1]))
 
 
 def gelu_parts(x):
@@ -590,53 +597,82 @@
 
 
 def dense_kernel(mode, main, *refs):
-    forward, backward = (mode != "backward", mode != "forward")
     refs = list(refs)
 
-    def take(count):
-        taken, refs[:] = (refs[:count], refs[count:])
-        return taken
-
-    (n_hbm,) = take(1)
-    g_hbm = take(1)[0] if backward else None
-    (w_hbm,) = take(1)
-    ab_hbm = take(1)[0] if mode == "backward" else None
-    (out_ref,) = take(1)
-    wire_hbm = take(1)[0] if backward else None
-    ab_out = take(1)[0] if mode == "forward" else None
-    p4_hbm = take(1)[0] if mode == "both" else None
-    n_v, w_v, hid_v, part_v = take(4)
-    g_v, low_v, wire_v = take(3) if backward else (None, None, None)
-    ab_v = take(1)[0] if mode != "both" else None
-    p4_v = take(1)[0] if mode == "both" else None
-    buffers = take(13)
-    (sems,) = take(1)
+    def take(wanted=True):
+        return refs.pop(0) if wanted else None
+
+    grads = mode in ("both", "backward")
+    fresh = mode in ("both", "forward")
+    n_hbm = take(mode != "product")
+    g_hbm = take(grads)
+    w_hbm = take()
+    ab_hbm = take(mode == "backward")
+    hid_in = take(mode == "product")
+    out_ref = take()
+    wire_hbm = take(grads)
+    ab_out = take(mode == "forward")
+    hid_out = take(mode == "both")
+    w_v, hid_v, part_v = (take(), take(), take())
+    n_v = take(mode != "product")
+    g_v, low_v, wire_v = (take(grads), take(grads), take(grads))
+    ab_v = take(mode in ("forward", "backward"))
+    buffers = [take() for _ in range(13)]
+    sems = take()
     lanes = 128
     both = 2 * main + lanes
     tile = 256
-    rows = n_v.shape[0]
     a, b = cube()[:2]
     near = neighbours(True)
     hail(near)
-    loads = [pltpu.make_async_copy(n_hbm, n_v, sems.at[0])]
-    loads.append(pltpu.make_async_copy(w_hbm, w_v, sems.at[1]))
-    if backward:
-        loads.append(pltpu.make_async_copy(g_hbm, g_v, sems.at[2]))
-    if mode == "backward":
-        loads.append(pltpu.make_async_copy(ab_hbm, ab_v, sems.at[3]))
-    for load in loads:
-        load.start()
-    for load in loads:
-        load.wait()
-
-    def work(pa, pb):
+    up_part, down_part = (pl.ds(0, both), pl.ds(both, w_v.shape[1] - both))
+    loads = {}
+
+    def load(name, src, dst):
+        loads[name] = pltpu.make_async_copy(src, dst, sems.at[len(loads)])
+        loads[name].start()
+
+    def need(*names):
+        for name in names:
+            if name in loads:
+                loads.pop(name).wait()
+
+    tiles = ((1 - a, 1 - b), (1 - a, b), (a, 1 - b), (a, b))
+
+    def rows_of(pa, pb):
+        return pl.ds(pl.multiple_of((pa * 4 + pb * 2) * lanes, tile), tile)
+
+    def load_rows(turn, **pairs):
+        at = rows_of(*tiles[turn])
+        for name, (src, dst) in pairs.items():
+            if src is not None:
+                load(f"{name}{turn}", src.at[at], dst.at[at])
+
+    for turn in range(4):
+        load_rows(turn, n=(n_hbm, n_v), hid=(hid_in, hid_v), ab=(ab_hbm, ab_v))
+        if turn == 0 and mode != "product":
+            load("up", w_hbm.at[:, up_part], w_v.at[:, up_part])
+        load_rows(turn, g=(g_hbm, g_v))
+        if turn == 0:
+            load("down", w_hbm.at[:, down_part], w_v.at[:, down_part])
+
+    def work(turn):
+        pa, pb = tiles[turn]
         block = pa * 4 + pb * 2
-        at = pl.ds(pl.multiple_of(block * lanes, tile), tile)
-        if forward:
+        at = rows_of(pa, pb)
+        if mode == "product":
+            need(f"hid{turn}", "down")
+            part = lowered(product_right(hid_v[at, :], w_v[:, both:]))
+            part_v[pl.ds(block, 2)] = part.reshape(2, lanes, part.shape[1])
+            return
+        need(f"n{turn}")
+        if fresh:
+            need("up")
             ab = product(n_v[at, :], w_v[:, :both])
             if mode == "forward":
                 ab_v[at, :] = ab
         else:
+            need(f"ab{turn}")
             ab = ab_v[at, :]
         gate, up, tail = (ab[:, :main], ab[:, main : 2 * main], ab[:, 2 * main :])
         first = lax.broadcasted_iota(jnp.int32, tail.shape, 1) < lanes // 2
@@ -645,7 +681,8 @@
         tail_act, tail_slope = gelu_parts(tail)
         hid_v[at, :main] = lowered(act * up)
         hid_v[at, main:] = lowered(jnp.where(first, tail_act * turned, 0.0))
-        if backward:
+        need(f"g{turn}", "down")
+        if grads:
             grad = product(g_v[at, :], w_v[:, both:])
             grad_main, grad_tail = (grad[:, :main], grad[:, main:])
             low_v[at, :main] = lowered(grad_main * up * slope)
@@ -655,6 +692,7 @@
             low_v[at, 2 * main :] = lowered(
                 jnp.where(first, grad_tail * turned * tail_slope, turned_grad * turned_act)
             )
+            need("up")
             part = lowered(product_right(low_v[at, :], w_v[:, :both]))
         else:
             part = lowered(product_right(hid_v[at, :], w_v[:, both:]))
@@ -662,8 +700,8 @@
 
     schedule = scatter_steps(True, part_v, out_ref, *buffers)
     next(schedule)
-    for turn, (pa, pb) in enumerate(((1 - a, 1 - b), (1 - a, b), (a, 1 - b), (a, b))):
-        work(pa, pb)
+    for turn in range(4):
+        work(turn)
         if turn == 0:
             pl.semaphore_wait(pltpu.get_barrier_semaphore(), len(near))
         next(schedule)
@@ -674,73 +712,75 @@
         copy.start()
         stores.append(copy)
 
+    if mode == "both":
+        store(hid_v, hid_out, 16)
     if mode == "forward":
-        store(ab_v, ab_out, 4)
-        next(schedule)
-    else:
+        store(ab_v, ab_out, 16)
+    if grads:
         depth = w_v.shape[0]
 
-        def grads(i, carry):
+        def weight_grads(i, carry):
             cols = pl.ds(pl.multiple_of(i * tile, tile), tile)
             wire_v[cols, :both] = lowered(product_left(n_v[:, cols], low_v[...]))
             wire_v[cols, both:] = lowered(product_left(g_v[:, cols], hid_v[...]))
             return carry
 
         split = depth // tile // 2
-        lax.fori_loop(0, split, grads, 0)
-        store(wire_v.at[pl.ds(0, split * tile)], wire_hbm.at[pl.ds(0, split * tile)], 4)
+        lax.fori_loop(0, split, weight_grads, 0)
+        store(wire_v.at[pl.ds(0, split * tile)], wire_hbm.at[pl.ds(0, split * tile)], 17)
         next(schedule)
-        lax.fori_loop(split, depth // tile, grads, 0)
+        lax.fori_loop(split, depth // tile, weight_grads, 0)
         rest = pl.ds(split * tile, depth - split * tile)
-        store(wire_v.at[rest], wire_hbm.at[rest], 5)
-    if mode == "both":
-
-        def onward(i, carry):
-            at = pl.ds(pl.multiple_of(i * tile, tile), tile)
-            p4_v[at, :] = lowered(product_right(hid_v[at, :], w_v[:, both:]))
-            return carry
-
-        lax.fori_loop(0, rows // tile, onward, 0)
-        store(p4_v, p4_hbm, 6)
+        store(wire_v.at[rest], wire_hbm.at[rest], 18)
+    else:
+        next(schedule)
     next(schedule, None)
     for copy in stores:
         copy.wait()
 
 
-def dense_call(mode, normed, grad_low, weights, ab, collective_id):
-    rows, depth = normed.shape
-    columns = weights.shape[1]
+def dense_call(mode, rows_in, grad_low, weights, ab, collective_id):
+    rows = rows_in.shape[0]
+    depth, columns = weights.shape
     main = (columns // 128 - 2) // 3 * 128
     both = 2 * main + 128
-    backward = mode != "forward"
+    grads = mode in ("both", "backward")
     low = jnp.bfloat16
-    operands = [normed] + ([grad_low] if backward else []) + [weights]
-    shapes = [jax.ShapeDtypeStruct((rows // 8, depth), jnp.float32)]
-    scratch = [(normed.shape, low), (weights.shape, low), ((rows, columns - both), low)]
-    scratch += [((8, rows // 8, depth), low)]
-    if backward:
-        shapes.append(jax.ShapeDtypeStruct(weights.shape, low))
-        scratch += [(normed.shape, low), ((rows, both), low), (weights.shape, low)]
-    if mode == "forward":
-        shapes.append(jax.ShapeDtypeStruct((rows, both), jnp.float32))
+    wide = ((rows, depth), low)
+    hidden = ((rows, columns - both), low)
+    if mode == "product":
+        operands = [weights, rows_in]
+    else:
+        operands = [rows_in] + ([grad_low] if grads else []) + [weights]
     if mode == "backward":
         operands.append(ab)
-    if mode == "both":
-        shapes.append(jax.ShapeDtypeStruct((rows, depth), low))
-        scratch.append(((rows, depth), low))
-    else:
+    extra = {
+        "forward": [((rows, both), jnp.float32)],
+        "backward": [(weights.shape, low)],
+        "both": [(weights.shape, low), hidden],
+        "product": [],
+    }[mode]
+    scratch = [(weights.shape, low), hidden, ((8, rows // 8, depth), low)]
+    if mode != "product":
+        scratch.append(wide)
+    if grads:
+        scratch += [wide, ((rows, both), low), (weights.shape, low)]
+    if mode in ("forward", "backward"):
         scratch.append(((rows, both), jnp.float32))
     return pl.pallas_call(
         functools.partial(dense_kernel, mode, main),
-        out_shape=shapes,
+        out_shape=[
+            jax.ShapeDtypeStruct(shape, kind)
+            for shape, kind in [((rows // 8, depth), jnp.float32)] + extra
+        ],
         in_specs=[ANY] * len(operands),
-        out_specs=[VMEM] + [ANY] * (len(shapes) - 1),
+        out_specs=[VMEM] + [ANY] * len(extra),
         scratch_shapes=[pltpu.VMEM(shape, kind) for shape, kind in scratch]
         + scatter_scratch(8, rows // 8, depth)
-        + [pltpu.SemaphoreType.DMA((7,))],
+        + [pltpu.SemaphoreType.DMA((19,))],
         name="dense_" + mode,
         cost_estimate=pl.CostEstimate(
-            flops=0, bytes_accessed=100_000_000 if backward else 80_000_000, transcendentals=0
+            flops=0, bytes_accessed=100_000_000 if grads else 75_000_000, transcendentals=0
         ),
         compiler_params=pltpu.CompilerParams(
             collective_id=collective_id, has_side_effects=True, vmem_limit_bytes=56 * 2**20
@@ -960,6 +1000,7 @@
     "backward": 12,
     "gather_weight": 13,
     "gather_seen": 14,
+    "product": 15,
 }
 
 
@@ -1084,42 +1125,45 @@
     weight_rows = input_branch.shape[0]
     attn_rows = jnp.concatenate([query_weight, attention_out.T], axis=1)
     query_width = query_weight.shape[1]
-    third = lax.all_gather(
-        jnp.concatenate(
-            [attn_rows, keyvalue_weight.reshape(-1, attn_rows.shape[1])], axis=0
-        ),
-        "seq",
-        axis_index_groups=high_groups(),
-    )
+    third = jnp.concatenate(
+        [attn_rows, keyvalue_weight.reshape(-1, attn_rows.shape[1])], axis=0
+    )
+
     own_tokens = lax.dynamic_slice_in_dim(tokens, tp * own_rows, own_rows, 0)
     own_cotangent = lax.dynamic_slice_in_dim(cotangent, tp * own_rows, own_rows, 0)
     stream_in = own_tokens.astype(jnp.float32)
     grad_stream = own_cotangent.astype(jnp.float32) * valid[:, None]
-    (normed_one,) = gather([lowered(rms_norm(stream_in, norm_gains[0]))], True, cid["gather_full"])
     first = swap_columns(
         jnp.concatenate([input_branch, recur_gate.T], axis=0),
         jnp.concatenate([gate_branch, input_gate.T], axis=0),
         jnp.concatenate([recur_output.T, jnp.zeros_like(recur_gate.T)], axis=0),
     )
-    first, third, normed_one = lax.optimization_barrier((first, third, normed_one))
-    first_full = gather_high(first).reshape(high * LO, weight_rows + gate_rows, 3 * channels)
+    normed_own = lowered(rms_norm(stream_in, norm_gains[0]))
+    grad_own = lowered(grad_stream)
+    first, normed_own, grad_own, dense_gate_one = lax.optimization_barrier(
+        (first, normed_own, grad_own, dense_gate_one)
+    )
+    third_rows = third.shape[0]
+    early_wires = lax.all_gather(
+        jnp.concatenate([third, first], axis=0), "seq", axis_index_groups=high_groups()
+    )
+    normed_one, grad_low = gather([normed_own, grad_own], [True, True], cid["gather_two"])
+    second = swap_pieces(dense_wire(dense_gate_one, dense_up_one, dense_down_one.T))
+    second, dense_gate_two = lax.optimization_barrier((second, dense_gate_two))
+    fourth = swap_pieces(dense_wire(dense_gate_two, dense_up_two, dense_down_two.T))
+    normed_one, early_wires, grad_low, second, fourth = lax.optimization_barrier(
+        (normed_one, early_wires, grad_low, second, fourth)
+    )
+    third = early_wires[:, :third_rows]
+    first_full = early_wires[:, third_rows:]
+    first_full = first_full.reshape(high * LO, weight_rows + gate_rows, 3 * channels)
     in_full = first_full[:, :weight_rows, : 2 * channels].reshape(-1, 2 * channels)
     output_full = first_full[:, :weight_rows, 2 * channels :].reshape(-1, channels)
     recur_full = first_full[:, weight_rows:, :channels].reshape(-1, channels)
     input_gate_full = first_full[:, weight_rows:, channels : 2 * channels].reshape(-1, channels)
+    weights_one = gather_high(second)
     third = both_lows(third)
-    second = swap_pieces(dense_wire(dense_gate_one, dense_up_one, dense_down_one.T))
-
-    (grad_low,) = gather([lowered(grad_stream)], True, cid["gather_full"])
-    normed_one, in_full, second, third, grad_low = lax.optimization_barrier(
-        (normed_one, in_full, second, third, grad_low)
-    )
-    weights_one = gather_high(second)
     both = product(normed_one, in_full)
-    both, dense_gate_two, dense_up_two, dense_down_two = lax.optimization_barrier(
-        (both, dense_gate_two, dense_up_two, dense_down_two)
-    )
-    fourth = swap_pieces(dense_wire(dense_gate_two, dense_up_two, dense_down_two.T))
 
     branch = both[:, :channels]
     gating = both[:, channels:]
@@ -1138,16 +1182,17 @@
     state, state_in = plane_scan(decay, drive, ones, high, False, cid["scan"])
     gate_act, gate_pull = jax.vjp(jax.nn.gelu, gating)
     mixed = lowered(state * gate_act)
-    mixed, fourth = lax.optimization_barrier((mixed, fourth))
+    mixed, third = lax.optimization_barrier((mixed, third))
     (summed,) = scatter([product_right(mixed, output_full)], True, cid["scatter_full"])
     stream_one = stream_in + summed
-    (normed_two,) = gather([lowered(rms_norm(stream_one, norm_gains[1]))], True, cid["gather_full"])
     third = third.reshape(high * LO, -1, third.shape[1])
     query_full = third[:, :weight_rows, :query_width].reshape(-1, query_width)
     attn_full = third[:, :weight_rows, query_width:].reshape(-1, third.shape[2] - query_width)
     part_rows, part_width = keyvalue_weight.shape
-    (keyvalue_full,) = gather(
-        [third[:, weight_rows:].reshape(-1, part_width)], False, cid["gather_weight"]
+    normed_two, keyvalue_full = gather(
+        [lowered(rms_norm(stream_one, norm_gains[1])), third[:, weight_rows:].reshape(-1, part_width)],
+        [True, False],
+        cid["gather_weight"],
     )
     keyvalue_full = keyvalue_full.reshape(ways, high * LO, part_rows, part_width)
     keyvalue_full = keyvalue_full.transpose(1, 0, 2, 3).reshape(-1, part_width)
@@ -1169,7 +1214,7 @@
     packed = jnp.concatenate([key_rot, lowered(keyval[:, HD:])], axis=1)
     earlier = [shifted(packed, offset) for offset in range(halo_shards, 0, -1)]
     normed_three, seen = gather(
-        [normed_own, jnp.concatenate(earlier + [packed], axis=1)], False, cid["gather_seen"]
+        [normed_own, jnp.concatenate(earlier + [packed], axis=1)], [False, False], cid["gather_seen"]
     )
     extended = jnp.concatenate(
         [seen[:, 2 * HD * k : 2 * HD * (k + 1)] for k in range(halo_shards + 1)], axis=0
@@ -1182,15 +1227,15 @@
     stream_three = stream_two + summed
 
     (normed_four,) = gather(
-        [lowered(rms_norm(stream_three, norm_gains[3]))], True, cid["gather_full"]
-    )
-    grad_normed, wire_two, partial_four = dense_call(
+        [lowered(rms_norm(stream_three, norm_gains[3]))], [True], cid["gather_full"]
+    )
+    grad_normed, wire_two, hidden_two = dense_call(
         "both", normed_four, grad_low, weights_two, None, cid["both"]
     )
     done_two = reduce_high(wire_two)
     stream_grad, gain_four = jax.vjp(rms_norm, stream_three, norm_gains[3])[1](grad_normed)
     grad_stream = grad_stream + stream_grad
-    (grad_attn_low,) = gather([lowered(grad_stream)], False, cid["gather_half"])
+    (grad_attn_low,) = gather([lowered(grad_stream)], [False], cid["gather_half"])
     grad_attn_out = product_left(grad_attn_low, attended)
     grad_attended = lowered(product(grad_attn_low, attn_full))
     grad_query_low, grad_ext = attention_back(
@@ -1212,11 +1257,6 @@
     )
     attn_kept, attn_given = swap_sums(jnp.concatenate([grad_query, grad_attn_out], axis=1))
     (summed,) = scatter([partial], False, cid["scatter_wide"])
-    summed, partial_four, attn_given = lax.optimization_barrier(
-        (summed, partial_four, attn_given)
-    )
-    attn_wire = lowered(attn_kept.astype(jnp.float32) + attn_given.astype(jnp.float32))
-    (summed_four,) = scatter([partial_four], True, cid["scatter_full"])
     width = normed_own.shape[1]
     pieces = [
         summed[:, width + 2 * HD * k : width + 2 * HD * (k + 1)] for k in range(halo_shards + 1)
@@ -1225,16 +1265,16 @@
     for offset in range(1, halo_shards + 1):
         piece = shifted(lowered(pieces[halo_shards - offset]), -offset)
         keyvalue_total = keyvalue_total + piece.astype(jnp.float32)
-    keyvalue_total, summed_four = lax.optimization_barrier((keyvalue_total, summed_four))
+    keyvalue_total, attn_given = lax.optimization_barrier((keyvalue_total, attn_given))
+    done_attn = reduce_high(attn_kept.astype(jnp.float32) + attn_given.astype(jnp.float32))
     key_grad = rotate_back(keyvalue_total[:, :HD], own_factors)
     keyvalue_low = lowered(jnp.concatenate([key_grad, keyvalue_total[:, HD:]], axis=1))
     grad_normed = summed[:, :width] + product_right(keyvalue_low, keyvalue_full)
     stream_grad, gain_three = jax.vjp(rms_norm, stream_two, norm_gains[2])[1](grad_normed)
     grad_stream = grad_stream + stream_grad
 
-    (grad_low,) = gather([lowered(grad_stream)], True, cid["gather_full"])
-    grad_low, attn_wire, done_two = lax.optimization_barrier((grad_low, attn_wire, done_two))
-    done_attn = reduce_high(attn_wire)
+    (grad_low,) = gather([lowered(grad_stream)], [True], cid["gather_full"])
+    grad_low, done_two = lax.optimization_barrier((grad_low, done_two))
     done_two = dense_grads(exchanged(done_two))
     grad_normed, one_wire = dense_call(
         "backward", normed_two, grad_low, weights_one, ab_one, cid["backward"]
@@ -1246,11 +1286,13 @@
     )
     grad_stream, keyvalue_low = lax.optimization_barrier((grad_stream, keyvalue_low))
     done_one = reduce_high(one_wire)
-    (keyvalue_grads,) = gather([keyvalue_low], False, cid["gather_narrow"])
+    (keyvalue_grads,) = gather([keyvalue_low], [False], cid["gather_narrow"])
     grad_keyvalue = lowered(product_left(normed_three, keyvalue_grads))
     grad_keyvalue = grad_keyvalue.reshape(high * LO, ways, part_rows, part_width)
     grad_keyvalue = lax.dynamic_slice_in_dim(grad_keyvalue, tp, 1, 1)
-    (grad_out_low,) = gather([lowered(grad_stream)], True, cid["gather_full"])
+    (grad_out_low,) = gather([lowered(grad_stream)], [True], cid["gather_full"])
+    grad_out_low, hidden_two = lax.optimization_barrier((grad_out_low, hidden_two))
+    (summed_four,) = dense_call("product", hidden_two, None, weights_two, None, cid["product"])
     grad_recur_out = product_left(grad_out_low, mixed)
     grad_mixed = product(grad_out_low, output_full)
     grad_mixed, done_attn, done_two = lax.optimization_barrier((grad_mixed, done_attn, done_two))
@@ -1304,16 +1346,12 @@
         ],
         axis=1,
     )
+    wire, done_one, summed_four = lax.optimization_barrier((wire, done_one, summed_four))
     layer_own = lowered((stream_three + summed_four) * valid[:, None])
-    layer_own, wire = lax.optimization_barrier((layer_own, wire))
-    (layer_out,) = gather([layer_own], False, cid["gather_half"])
-    wire, done_one, layer_out = lax.optimization_barrier((wire, done_one, layer_out))
-    last = exchanged(reduce_high(wire.reshape(-1, 3 * channels)))
-    keyvalue_grad = jnp.sum(last[:, weight_rows + gate_rows :].astype(jnp.float32), axis=0)
-    last_rows, last_gates = (last[:, :weight_rows], last[:, weight_rows : weight_rows + gate_rows])
+    last = reduce_high(wire.reshape(-1, 3 * channels))
     gain_one = jnp.sum(normed_one.astype(jnp.float32) * partial.astype(jnp.float32), axis=0)
     gain_one = gain_one / norm_gains[0]
-    grad_normed, gains_sum, small = scatter_and_sums(
+    grad_normed, gains_sum, small, layer_out = scatter_and_sums(
         partial,
         jnp.concatenate(
             [jnp.stack([gain_one, gain_two, gain_three, gain_four]), jnp.zeros_like(norm_gains)]
@@ -1321,6 +1359,7 @@
         jnp.concatenate(
             [grad_taps, grad_conv_bias[None], grad_biases, grad_decay_param[None]], axis=0
         ),
+        layer_own,
         high,
         cid["last"],
     )
@@ -1328,10 +1367,13 @@
     stream_grad = jax.vjp(rms_local, stream_in)[1](grad_normed)[0]
     input_own = lowered(grad_stream + stream_grad)
     done_one = exchanged(done_one)
-    (input_grad,) = gather([input_own], False, cid["gather_half"])
+    (input_grad,) = gather([input_own], [False], cid["gather_half"])
     gains_sum = gains_sum[: norm_gains.shape[0]]
-    input_grad, done_one = lax.optimization_barrier((input_grad, done_one))
+    input_grad, done_one, last = lax.optimization_barrier((input_grad, done_one, last))
     input_grad = input_grad.astype(jnp.float32)
+    last = exchanged(last)
+    keyvalue_grad = jnp.sum(last[:, weight_rows + gate_rows :].astype(jnp.float32), axis=0)
+    last_rows, last_gates = (last[:, :weight_rows], last[:, weight_rows : weight_rows + gate_rows])
     return (
         layer_out,
         input_grad,

time: 695 us -> 658 us (0.947)
  Pallas kernels: 450 us -> 389 us
  waiting for transfers between devices: 28.4 us -> 89.2 us
  other arithmetic: 84 us -> 71.2 us
  local copies, waits for them, and re-layouts: 48.4 us -> 37.8 us
  matrix products: 33 us -> 24 us
    pallas_call x15 -> x13, Pallas kernels: 310 us -> 272 us  [the longest x9 176 us: gather(): pl.pallas_call(functools.partial(gather_kernel, spans), out_shape=[jax.Sh...]
    pallas_call x4 -> x3, Pallas kernels: 65.7 us -> 47.2 us  [scatter(): pl.pallas_call(functools.partial(scatter_kernel, full, count), out_shape=...]
    ppermute x8, waiting for transfers between devices: 18 us -> 36.3 us  [swap_low(): lax.ppermute(block, 'seq', [(s, s // LO * LO + (1 - s % LO)) for s in ran...]
    ppermute x6, waiting for transfers between devices: 1.89 us -> 19.6 us  [shifted(): return lax.ppermute(block, 'seq', route)]
    reduce_scatter x4, waiting for transfers between devices: 0.59 us -> 15.5 us  [reduce_high(): lax.psum_scatter(lowered(grad), 'seq', scatter_dimension=0, tiled=True, a...]
    all_gather x1, waiting for transfers between devices: 0.01 us -> 11 us  [local(): lax.all_gather(jnp.concatenate([third, first], axis=0), 'seq', axis_index...]
    pallas_call x2, Pallas kernels: 27.8 us -> 20.1 us  [plane_scan(): pl.pallas_call(functools.partial(scan_kernel, high, reverse), out_shape=(...]
    unnamed x339 -> x299, local copies, waits for them, and re-layouts: 19 us -> 12.8 us
  transfers between devices with their start and end apart: 22 -> 21, of which waited for: 8 -> 15; matrix products, arithmetic and copies ran while one was open for 20% -> 17% of each run, Pallas kernels for 61% -> 56%
where the time goes in v4:
time: 658 us; the launch traced here: 651 us
  Pallas kernels  389 us (59%)
  waiting for transfers between devices  89.2 us (14%)
  other arithmetic  71.2 us (11%)
  local copies, waits for them, and re-layouts  37.8 us (6%)
  matrix products  24 us (4%)
  starting transfers between devices  23 us (3%)
  between operations  17.1 us (3%)
    pallas_call x9, Pallas kernels, gather(): pl.pallas_call(functools.partial(gather_kernel, spans), out_shape=[jax.Sh...  176 us
    pallas_call x4, Pallas kernels, dense_call(): pl.pallas_call(functools.partial(dense_kernel, mode, main), out_shape=[ja...  96.1 us
    pallas_call x3, Pallas kernels, scatter(): pl.pallas_call(functools.partial(scatter_kernel, full, count), out_shape=...  47.2 us
    ppermute x8, waiting for transfers between devices, swap_low(): lax.ppermute(block, 'seq', [(s, s // LO * LO + (1 - s % LO)) for s in ran...  36.3 us
    pallas_call x1, Pallas kernels, scatter_and_sums(): pl.pallas_call(functools.partial(last_kernel, high), out_shape=[jax.Shape...  31.6 us
    pallas_call x2, Pallas kernels, plane_scan(): pl.pallas_call(functools.partial(scan_kernel, high, reverse), out_shape=(...  20.1 us
    ppermute x6, waiting for transfers between devices, shifted(): return lax.ppermute(block, 'seq', route)  19.6 us
    convert_element_type x16, other arithmetic, lowered(): return values.astype(jnp.bfloat16)  17.4 us
  transfers between devices with their start and end apart: 21, of which 15 were waited for; matrix products, arithmetic and copies ran while one was open for 17% of the time, Pallas kernels for 56%

profile of v4, /device:TPU:0, one launch (start us, length us, event | category | flops | bytes accessed | tf_op | source)
XLA Modules:
  0.0 651.4 jit_solution(7943519347505898264)
XLA Ops:
  10.6 3.0 collective-permute-start
  15.7 1.9 fusion.41.refs_1_
  17.5 3.6 collective-permute-done
  24.4 1.8 collective-permute-start.1
  26.6 14.5 %collective-permute-done.1 = bf16[192,1792]{1,0:T(8,128)(2,1)S(1)} collective-permute-done((bf16[192,1792]{1,0:T(8,128)(2,1)S(1)}, bf16[192,1792]{1,0:T(8,128)(2,1)S(1)}, u32[]{:S(2)}, u32[]{:S(2)}) %collective-permute-start.1) | collective-permute-done | bytes 688160 | tf_op jit(solution)/shard_map/ppermute | solution.py:910
  44.9 41.7 %gather_full.5 = (bf16[8,128,1536]{2,1,0:T(8,128)(2,1)}, bf16[8,128,1536]{2,1,0:T(8,128)(2,1)}) custom-call(bf16[128,1536]{1,0:T(8,128)(2,1)} %fusion.39.refs_0_, bf16[128,1536]{1,0:T(8,128)(2,1)} %fusion.41.refs_1_), custom_call_target="tpu_custom_call" | custom-call | bytes 60000000 | tf_op jit(solution)/shard_map/gather_full/pallas_call | solution.py:229
  88.0 11.0 %all-gather.9.cloned.1.call-done = bf16[2496,768]{1,0:T(8,128)(2,1)} async-done(((bf16[624,768]{1,0:T(8,128)(2,1)}), bf16[2496,768]{1,0:T(8,128)(2,1)}) %all-gather.9.cloned.1.call-update) | async-done | bytes 3833872 | tf_op jit(solution)/shard_map/all_gather | solution.py:1147
  103.0 1.9 slice.538
  105.1 2.6 copy-done.49
  107.7 1.8 fusion.151
  111.4 1.6 collective-permute-start.4
  116.3 9.4 %scan.1 = (f32[1024,256]{1,0:T(8,128)S(1)}, f32[8,256]{1,0:T(8,128)S(1)}) custom-call(f32[1024,256]{1,0:T(8,128)S(1)} %get-tuple-element.247.decay_ref, f32[1024,256]{1,0:T(8,128)S(1)} %get-tuple-element.246.drive_ref, f32[8,256]{1,0:T(8,128)S(1)} %broadcast_in_dim.71.end_ref), custom_call_target="tpu_custom_call" | custom-call | bytes 33000000 | tf_op jit(solution)/shard_map/scan/pallas_call | solution.py:474
  126.1 15.1 %collective-permute-done.4 = bf16[4,208,768]{2,1,0:T(8,128)(2,1)S(1)} collective-permute-done((bf16[4,208,768]{2,1,0:T(8,128)(2,1)S(1)}, bf16[4,208,768]{2,1,0:T(8,128)(2,1)S(1)}, u32[]{:S(2)}, u32[]{:S(2)}) %collective-permute-start.4) | collective-permute-done | bytes 1277984 | tf_op jit(solution)/shard_map/ppermute | solution.py:910
  142.9 17.1 %scatter_full.1 = f32[128,1536]{1,0:T(8,128)S(1)} custom-call(bf16[8,128,1536]{2,1,0:T(8,128)(2,1)S(1)} %bitcast.190), custom_call_target="tpu_custom_call" | custom-call | bytes 60000000 | tf_op jit(solution)/shard_map/scatter_full/pallas_call | solution.py:387
  161.5 1.7 reshape.436.refs_1_
  166.4 23.5 %gather_full.6 = (bf16[8,128,1536]{2,1,0:T(8,128)(2,1)}, bf16[4,384,256]{2,1,0:T(8,128)(2,1)}) custom-call(bf16[128,1536]{1,0:T(8,128)(2,1)} %multiply_convert_fusion.4.refs_0_, bf16[384,256]{1,0:T(8,128)(2,1)} %reshape.436.refs_1_), custom_call_target="tpu_custom_call" | custom-call | bytes 60000000 | tf_op jit(solution)/shard_map/gather_full/pallas_call | solution.py:229
  189.9 2.1 copy.70
  192.0 3.4 fusion.130
  195.4 6.7 %all-gather.5.cloned.1.call-done.refs_1_.refs_2_ = bf16[1536,1792]{1,0:T(8,128)(2,1)} async-done(((bf16[384,1792]{1,0:T(8,128)(2,1)}), bf16[1536,1792]{1,0:T(8,128)(2,1)}) %all-gather.5.cloned.1.call-update) | async-done | bytes 5505040 | tf_op jit(solution)/shard_map/all_gather | solution.py:931
  202.5 22.9 %dense_forward.1 = (f32[128,1536]{1,0:T(8,128)}, f32[1024,1152]{1,0:T(8,128)}) custom-call(bf16[1024,1536]{1,0:T(8,128)(2,1)} %bitcast.197, bf16[1536,1792]{1,0:T(8,128)(2,1)} %all-gather.5.cloned.1.call-done.refs_1_.refs_2_), custom_call_target="tpu_custom_call" | custom-call | bytes 75000000 | tf_op jit(solution)/shard_map/dense_forward/pallas_call | solution.py:770
  230.1 3.4 collective-permute-start.6
  233.7 1.7 collective-permute-done.6
  236.1 20.0 %gather_half.4 = (bf16[4,128,1536]{2,1,0:T(8,128)(2,1)}, bf16[4,128,768]{2,1,0:T(8,128)(2,1)}) custom-call(bf16[128,1536]{1,0:T(8,128)(2,1)} %copy-done.46, bf16[128,768]{1,0:T(8,128)(2,1)} %pad_maximum_fusion.19.refs_1_), custom_call_target="tpu_custom_call" | custom-call | bytes 60000000 | tf_op jit(solution)/shard_map/gather_half/pallas_call | solution.py:229
  259.2 8.6 %attention.1 = (bf16[512,384]{1,0:T(8,128)(2,1)S(1)}, bf16[512,384]{1,0:T(8,128)(2,1)S(1)}, f32[8,512]{1,0:T(8,128)S(1)}) custom-call(f32[512,384]{1,0:T(8,128)S(1)} %fusion.153.query_ref, bf16[1536,256]{1,0:T(8,128)(2,1)S(1)} %pad_maximum_fusion.10.ext_ref, s32[8,512]{1,0:T(8,128)S(1)} %broadcast_in_dim.76.here_ref, ...), custom_call_target="tpu_custom_call" | custom-call | bytes 33000000 | tf_op jit(solution)/shard_map/attention/pallas_call | solution.py:833
  268.9 13.1 %scatter_half.2 = f32[128,1536]{1,0:T(8,128)S(1)} custom-call(bf16[4,128,1536]{2,1,0:T(8,128)(2,1)S(1)} %bitcast.194), custom_call_target="tpu_custom_call" | custom-call | bytes 60000000 | tf_op jit(solution)/shard_map/scatter_half/pallas_call | solution.py:387
  283.0 2.0 multiply_convert_fusion.2.refs_0_
  285.0 20.0 %gather_full.7 = bf16[8,128,1536]{2,1,0:T(8,128)(2,1)} custom-call(bf16[128,1536]{1,0:T(8,128)(2,1)} %multiply_convert_fusion.2.refs_0_), custom_call_target="tpu_custom_call" | custom-call | bytes 60000000 | tf_op jit(solution)/shard_map/gather_full/pallas_call | solution.py:229
  305.0 27.1 %dense_both.1 = (f32[128,1536]{1,0:T(8,128)}, bf16[1536,1792]{1,0:T(8,128)(2,1)}, bf16[1024,640]{1,0:T(8,128)(2,1)}) custom-call(bf16[1024,1536]{1,0:T(8,128)(2,1)} %bitcast.196, bf16[1024,1536]{1,0:T(8,128)(2,1)} %bitcast.226, bf16[1536,1792]{1,0:T(8,128)(2,1)} %all-gather.7.cloned.1.call-done.refs_2_.refs_0_), custom_call_target="tpu_custom_call" | custom-call | bytes 100000000 | tf_op jit(solution)/shard_map/dense_both/pallas_call | solution.py:770
  332.2 2.2 multiply_reduce_fusion.6
  334.4 2.5 fusion.126
  337.0 14.4 %gather_half.5 = bf16[4,128,1536]{2,1,0:T(8,128)(2,1)} custom-call(bf16[128,1536]{1,0:T(8,128)(2,1)} %get-tuple-element.204.refs_0_), custom_call_target="tpu_custom_call" | custom-call | bytes 60000000 | tf_op jit(solution)/shard_map/gather_half/pallas_call | solution.py:229
  351.4 2.8 convolution_convert_fusion.8.grad_ref
  354.3 9.8 %attention_back.1 = (bf16[512,384]{1,0:T(8,128)(2,1)S(1)}, bf16[1536,256]{1,0:T(8,128)(2,1)S(1)}) custom-call(bf16[512,384]{1,0:T(8,128)(2,1)S(1)} %copy-done.8, bf16[1536,256]{1,0:T(8,128)(2,1)S(1)} %copy-done.1, bf16[512,384]{1,0:T(8,128)(2,1)S(1)} %convolution_convert_fusion.8.grad_ref, f32[8,512]{1,0:T(8,128)S(1)} %get-tuple-element.137.log_ref, ...), custom_call_target="tpu_custom_call" | custom-call | bytes 60000000 | tf_op jit(solution)/shard_map/attention_back/pallas_call | solution.py:888
  368.3 1.6 broadcast_select_fusion
  370.8 17.0 %scatter_half.3 = f32[128,2304]{1,0:T(8,128)S(1)} custom-call(bf16[4,128,2304]{2,1,0:T(8,128)(2,1)S(1)} %bitcast.192), custom_call_target="tpu_custom_call" | custom-call | bytes 60000000 | tf_op jit(solution)/shard_map/scatter_half/pallas_call | solution.py:387
  392.4 6.5 %collective-permute-done.7 = bf16[128,256]{1,0:T(8,128)(2,1)S(1)} collective-permute-done((bf16[128,256]{1,0:T(8,128)(2,1)}, bf16[128,256]{1,0:T(8,128)(2,1)S(1)}, u32[]{:S(2)}, u32[]{:S(2)}) %collective-permute-start.7) | collective-permute-done | bytes 65568 | tf_op jit(solution)/shard_map/ppermute | solution.py:984
  399.6 4.9 collective-permute-done.8
  405.4 2.6 fusion.1
  409.4 2.6 multiply_reduce_fusion.7
  413.3 17.6 %gather_full.8 = bf16[8,128,1536]{2,1,0:T(8,128)(2,1)} custom-call(bf16[128,1536]{1,0:T(8,128)(2,1)} %get-tuple-element.202.refs_0_), custom_call_target="tpu_custom_call" | custom-call | bytes 60000000 | tf_op jit(solution)/shard_map/gather_full/pallas_call | solution.py:229
  430.9 5.8 reduce-scatter.5.cloned.1.call-done
  436.7 25.8 %dense_backward.1 = (f32[128,1536]{1,0:T(8,128)}, bf16[1536,1792]{1,0:T(8,128)(2,1)}) custom-call(bf16[1024,1536]{1,0:T(8,128)(2,1)} %bitcast.198, bf16[1024,1536]{1,0:T(8,128)(2,1)} %bitcast.199, bf16[1536,1792]{1,0:T(8,128)(2,1)} %all-gather.5.cloned.1.call-done.refs_1_.refs_2_, f32[1024,1152]{1,0:T(8,128)} %get-tuple-element.146.refs_3_), custom_call_target="tpu_custom_call" | custom-call | bytes 100000000 | tf_op jit(solution)/shard_map/dense_backward/pallas_call | solution.py:770
  462.6 2.0 multiply_reduce_fusion.8
  464.9 3.3 reduce-scatter.7.cloned.1.call-done
  470.5 18.1 %gather_full.9 = bf16[8,128,1536]{2,1,0:T(8,128)(2,1)} custom-call(bf16[128,1536]{1,0:T(8,128)(2,1)} %convert_element_type.229.refs_0_), custom_call_target="tpu_custom_call" | custom-call | bytes 60000000 | tf_op jit(solution)/shard_map/gather_full/pallas_call | solution.py:229
  490.6 6.0 gather_half.6
  496.7 2.0 fusion
  499.4 1.7 reshape.465
  501.1 20.4 %dense_product.1 = f32[128,1536]{1,0:T(8,128)} custom-call(bf16[1536,1792]{1,0:T(8,128)(2,1)} %all-gather.7.cloned.1.call-done.refs_2_.refs_0_, bf16[1024,640]{1,0:T(8,128)(2,1)} %get-tuple-element.164.refs_1_), custom_call_target="tpu_custom_call" | custom-call | bytes 75000000 | tf_op jit(solution)/shard_map/dense_product/pallas_call | solution.py:770
  529.3 10.7 %scan_back.1 = (f32[1024,256]{1,0:T(8,128)S(1)}, f32[8,256]{1,0:T(8,128)}) custom-call(f32[1024,256]{1,0:T(8,128)S(1)} %concatenate.172.decay_ref, f32[1024,256]{1,0:T(8,128)S(1)} %get-tuple-element.220.drive_ref, f32[8,256]{1,0:T(8,128)S(1)} %broadcast_in_dim.82.end_ref), custom_call_target="tpu_custom_call" | custom-call | bytes 33000000 | tf_op jit(solution)/shard_map/scan_back/pallas_call | solution.py:474
  540.1 3.5 fusion.75
  545.7 2.3 multiply_reduce_fusion.5
  551.5 6.3 collective-permute-done.11
  557.9 1.8 convolution_convert_fusion.1
  559.8 1.8 convolution_convert_fusion.2
  561.6 1.9 pad_maximum_fusion
  563.5 4.3 reduce-scatter.9.cloned.1.call-done
  569.6 2.8 multiply_reduce_fusion
  574.7 31.6 %scatter_and_sums.1 = (f32[128,1536]{1,0:T(8,128)S(1)}, f32[8,1536]{1,0:T(8,128)S(1)}, f32[8,512]{1,0:T(8,128)S(1)}, bf16[4,128,1536]{2,1,0:T(8,128)(2,1)S(1)}) custom-call(bf16[8,128,1536]{2,1,0:T(8,128)(2,1)S(1)} %bitcast.191, f32[8,1536]{1,0:T(8,128)S(1)} %concatenate.190.gains_ref, f32[8,256]{1,0:T(8,128)S(1)} %pad_maximum_fusion.23.rest_ref, ...), custom_call_target="tpu_custom_call" | custom-call | bytes 60000000 | tf_op jit(solution)/shard_map/scatter_and_sums/pallas_call | solution.py:558
  609.8 14.4 %gather_half.7 = bf16[4,128,1536]{2,1,0:T(8,128)(2,1)} custom-call(bf16[128,1536]{1,0:T(8,128)(2,1)} %fusion.36.refs_0_), custom_call_target="tpu_custom_call" | custom-call | bytes 60000000 | tf_op jit(solution)/shard_map/gather_half/pallas_call | solution.py:229
  625.7 2.0 reduce-scatter.11.cloned.1.call-done
  628.8 1.6 collective-permute-start.13
  630.4 2.1 convert_element_type.244
  635.7 3.1 collective-permute-done.13
  (524 shorter events, 91.4 us)
Async XLA Ops:
  7.2 91.7 %all-gather.9.cloned.1.call-start = ((), (), s32[]{:S(2)}) async-start(), calls=%async_computation.10 | async-start | bytes 4792320 | tf_op jit(solution)/shard_map/all_gather | solution.py:1147
  9.3 11.8 %copy-start.59 = (bf16[192,512]{1,0:T(8,128)(2,1)S(1)}, bf16[192,512]{1,0:T(8,128)(2,1)}, u32[]{:S(2)}) copy-start(bf16[192,512]{1,0:T(8,128)(2,1)} %param.27) | copy-start | bytes 589828
  9.3 11.8 %copy-start.60 = (bf16[192,512]{1,0:T(8,128)(2,1)S(1)}, bf16[192,512]{1,0:T(8,128)(2,1)}, u32[]{:S(2)}) copy-start(bf16[192,512]{1,0:T(8,128)(2,1)} %param.26) | copy-start | bytes 589828
  9.4 11.8 %copy-start.81 = (bf16[512,16]{0,1:T(8,128)(2,1)S(1)}, bf16[512,16]{0,1:T(8,128)(2,1)}, u32[]{:S(2)}) copy-start(bf16[512,16]{0,1:T(8,128)(2,1)} %param.31) | copy-start | bytes 49156
  9.4 11.7 %copy-start.82 = (bf16[512,16]{0,1:T(8,128)(2,1)S(1)}, bf16[512,16]{0,1:T(8,128)(2,1)}, u32[]{:S(2)}) copy-start(bf16[512,16]{0,1:T(8,128)(2,1)} %param.30) | copy-start | bytes 49156
  10.6 10.5 %collective-permute-start = (bf16[208,768]{1,0:T(8,128)(2,1)S(1)}, bf16[208,768]{1,0:T(8,128)(2,1)S(1)}, u32[]{:S(2)}, u32[]{:S(2)}) collective-permute-start(bf16[208,768]{1,0:T(8,128)(2,1)S(1)} %broadcast_select_fusion.11), channel_id=1, source_target_pairs={{0,4},{4,0},{8,12},{12,8},{16,20},{20,16},{24,28},{28,24},{1,5},{5... | collective-permute-start | bytes 958472 | tf_op jit(solution)/shard_map/ppermute | solution.py:910
  22.5 179.7 %all-gather.5.cloned.1.call-start = ((), (), s32[]{:S(2)}) async-start(), calls=%async_computation.4 | async-start | bytes 6881280 | tf_op jit(solution)/shard_map/all_gather | solution.py:931
  24.4 16.7 %collective-permute-start.1 = (bf16[192,1792]{1,0:T(8,128)(2,1)S(1)}, bf16[192,1792]{1,0:T(8,128)(2,1)S(1)}, u32[]{:S(2)}, u32[]{:S(2)}) collective-permute-start(bf16[192,1792]{1,0:T(8,128)(2,1)S(1)} %broadcast_select_fusion.7), channel_id=1, source_target_pairs={{0,4},{4,0},{8,12},{12,8},{16,20},{20,16},{24,28},{28,24},{1,5},{5... | collective-permute-start | bytes 2064392 | tf_op jit(solution)/shard_map/ppermute | solution.py:910
  43.4 43.2 %collective-permute-start.2 = (bf16[192,1792]{1,0:T(8,128)(2,1)S(1)}, bf16[192,1792]{1,0:T(8,128)(2,1)S(1)}, u32[]{:S(2)}, u32[]{:S(2)}) collective-permute-start(bf16[192,1792]{1,0:T(8,128)(2,1)S(1)} %broadcast_select_fusion.5), channel_id=1, source_target_pairs={{0,4},{4,0},{8,12},{12,8},{16,20},{20,16},{24,28},{28,24},{1,5},{5... | collective-permute-start | bytes 2064392 | tf_op jit(solution)/shard_map/ppermute | solution.py:910
  86.7 12.4 %copy-start.143 = (f32[512]{0:T(512)S(1)}, f32[512]{0:T(512)}, u32[]{:S(2)}) copy-start(f32[512]{0:T(512)} %param.29) | copy-start | bytes 6148
  86.7 12.5 %copy-start.134 = (f32[512]{0:T(512)S(1)}, f32[512]{0:T(512)}, u32[]{:S(2)}) copy-start(f32[512]{0:T(512)} %param.33) | copy-start | bytes 6148
  86.7 13.2 %copy-start.133 = (f32[4,512]{1,0:T(4,128)S(1)}, f32[4,512]{1,0:T(4,128)}, u32[]{:S(2)}) copy-start(f32[4,512]{1,0:T(4,128)} %param.28) | copy-start | bytes 24580
  86.7 13.1 %copy-start.136 = (f32[2,512]{1,0:T(2,128)S(1)}, f32[2,512]{1,0:T(2,128)}, u32[]{:S(2)}) copy-start(f32[2,512]{1,0:T(2,128)} %param.32) | copy-start | bytes 12292
  99.0 206.1 %all-gather.7.cloned.1.call-start = ((), (), s32[]{:S(2)}) async-start(), calls=%async_computation.5 | async-start | bytes 6881280 | tf_op jit(solution)/shard_map/all_gather | solution.py:931
  99.9 15.0 %copy-start.108 = (f32[256]{0:T(256)}, f32[256]{0:T(256)S(1)}, u32[]{:S(2)}) copy-start(f32[256]{0:T(256)S(1)} %get-tuple-element.214) | copy-start | bytes 3076
  100.0 12.9 %copy-start.111 = (f32[1,256]{1,0:T(1,128)}, f32[1,256]{1,0:T(1,128)S(1)}, u32[]{:S(2)}) copy-start(f32[1,256]{1,0:T(1,128)S(1)} %get-tuple-element.308) | copy-start | bytes 3076
  100.0 12.9 %copy-start.113 = (f32[1,256]{1,0:T(1,128)}, f32[1,256]{1,0:T(1,128)S(1)}, u32[]{:S(2)}) copy-start(f32[1,256]{1,0:T(1,128)S(1)} %get-tuple-element.309) | copy-start | bytes 3076
  100.0 12.9 %copy-start.115 = (f32[1,256]{1,0:T(1,128)}, f32[1,256]{1,0:T(1,128)S(1)}, u32[]{:S(2)}) copy-start(f32[1,256]{1,0:T(1,128)S(1)} %get-tuple-element.310) | copy-start | bytes 3076
  100.0 12.9 %copy-start.117 = (f32[1,256]{1,0:T(1,128)}, f32[1,256]{1,0:T(1,128)S(1)}, u32[]{:S(2)}) copy-start(f32[1,256]{1,0:T(1,128)S(1)} %get-tuple-element.311) | copy-start | bytes 3076
  100.0 14.9 %copy-start.101 = (f32[1,256]{1,0:T(1,128)}, f32[1,256]{1,0:T(1,128)S(1)}, u32[]{:S(2)}) copy-start(f32[1,256]{1,0:T(1,128)S(1)} %get-tuple-element.323) | copy-start | bytes 3076
  100.0 14.9 %copy-start.106 = (f32[1,256]{1,0:T(1,128)}, f32[1,256]{1,0:T(1,128)S(1)}, u32[]{:S(2)}) copy-start(f32[1,256]{1,0:T(1,128)S(1)} %get-tuple-element.324) | copy-start | bytes 3076
  102.7 12.2 %copy-start.96 = (f32[1024]{0:T(1024)}, f32[1024]{0:T(1024)S(1)}, u32[]{:S(2)}) copy-start(f32[1024]{0:T(1024)S(1)} %compare_convert_fusion.1) | copy-start | bytes 12292
  109.5 16.2 %copy-start.24 = (f32[1024,512]{1,0:T(8,128)}, f32[1024,512]{1,0:T(8,128)S(1)}, u32[]{:S(2)}) copy-start(f32[1024,512]{1,0:T(8,128)S(1)} %fusion.151) | copy-start | bytes 6291460
  109.5 3.4 collective-permute-start.3
  111.3 30.5 %copy-start.47 = (bf16[8,192,256]{2,1,0:T(8,128)(2,1)}, bf16[8,192,256]{2,1,0:T(8,128)(2,1)S(1)}, u32[]{:S(2)}) copy-start(bf16[8,192,256]{2,1,0:T(8,128)(2,1)S(1)} %slice.668) | copy-start | bytes 2359300
  111.4 29.9 %collective-permute-start.4 = (bf16[4,208,768]{2,1,0:T(8,128)(2,1)S(1)}, bf16[4,208,768]{2,1,0:T(8,128)(2,1)S(1)}, u32[]{:S(2)}, u32[]{:S(2)}) collective-permute-start(bf16[4,208,768]{2,1,0:T(8,128)(2,1)S(1)} %slice.561), channel_id=1, source_target_pairs={{0,4},{4,0},{8,12},{12,8},{16,20},{20,16},{24,28},{28,24},{1,5},{5... | collective-permute-start | bytes 3833864 | tf_op jit(solution)/shard_map/ppermute | solution.py:910
  126.1 15.7 %copy-start.44 = (bf16[1024,256]{1,0:T(8,128)(2,1)}, bf16[1024,256]{1,0:T(8,128)(2,1)S(1)}, u32[]{:S(2)}) copy-start(bf16[1024,256]{1,0:T(8,128)(2,1)S(1)} %multiply_convert_fusion) | copy-start | bytes 1572868
  141.8 19.0 %copy-start.19 = (bf16[4,2,208,768]{3,2,1,0:T(8,128)(2,1)}, bf16[4,2,208,768]{3,2,1,0:T(8,128)(2,1)S(1)}, u32[]{:S(2)}) copy-start(bf16[4,2,208,768]{3,2,1,0:T(8,128)(2,1)S(1)} %copy.69) | copy-start | bytes 7667716
  164.6 27.4 %copy-start.139 = (f32[128]{0:T(128)}, f32[128]{0:T(128)S(1)}, u32[]{:S(2)}) copy-start(f32[128]{0:T(128)S(1)} %get-tuple-element.210) | copy-start | bytes 1540
  164.7 27.4 %copy-start.120 = (f32[128]{0:T(128)}, f32[128]{0:T(128)S(1)}, u32[]{:S(2)}) copy-start(f32[128]{0:T(128)S(1)} %fusion.115) | copy-start | bytes 1540
  202.2 234.5 %reduce-scatter.5.cloned.1.call-start = ((), (), s32[]{:S(2)}) async-start(), calls=%async_computation.6 | async-start | bytes 6881280 | tf_op jit(solution)/shard_map/reduce_scatter | solution.py:935
  202.5 22.9 %copy-start.10 = (f32[128,1536]{1,0:T(8,128)S(1)}, f32[128,1536]{1,0:T(8,128)}, u32[]{:S(2)}) copy-start(f32[128,1536]{1,0:T(8,128)} %copy-done.9) | copy-start | bytes 2359300
  228.8 4.9 collective-permute-start.5
  230.1 5.3 collective-permute-start.6
  268.9 13.1 %copy-start.13 = (f32[128,1536]{1,0:T(8,128)S(1)}, f32[128,1536]{1,0:T(8,128)}, u32[]{:S(2)}) copy-start(f32[128,1536]{1,0:T(8,128)} %copy-done.12) | copy-start | bytes 2359300
  332.1 136.1 %reduce-scatter.7.cloned.1.call-start = ((), (), s32[]{:S(2)}) async-start(), calls=%async_computation.7 | async-start | bytes 1474560 | tf_op jit(solution)/shard_map/reduce_scatter | solution.py:935
  369.9 35.5 %collective-permute-start.9 = (bf16[4,192,768]{2,1,0:T(8,128)(2,1)}, bf16[4,192,768]{2,1,0:T(8,128)(2,1)}, u32[]{:S(2)}, u32[]{:S(2)}) collective-permute-start(bf16[4,192,768]{2,1,0:T(8,128)(2,1)} %get-tuple-element.227), channel_id=1, source_target_pairs={{0,4},{4,0},{8,12},{12,8},{16,20},{20,16},{24,28},{28,24},{1,5},{5... | collective-permute-start | bytes 3538952 | tf_op jit(solution)/shard_map/ppermute | solution.py:910
  388.5 10.4 %collective-permute-start.7 = (bf16[128,256]{1,0:T(8,128)(2,1)}, bf16[128,256]{1,0:T(8,128)(2,1)S(1)}, u32[]{:S(2)}, u32[]{:S(2)}) collective-permute-start(bf16[128,256]{1,0:T(8,128)(2,1)} %get-tuple-element.260), channel_id=1, source_target_pairs={{4,0},{8,4},{12,8},{16,12},{20,16},{24,20},{28,24},{5,1},{9,5},{13... | collective-permute-start | bytes 196616 | tf_op jit(solution)/shard_map/ppermute | solution.py:984
  389.8 14.7 %collective-permute-start.8 = (bf16[128,256]{1,0:T(8,128)(2,1)S(1)}, bf16[128,256]{1,0:T(8,128)(2,1)}, u32[]{:S(2)}, u32[]{:S(2)}) collective-permute-start(bf16[128,256]{1,0:T(8,128)(2,1)S(1)} %get-tuple-element.261), channel_id=1, source_target_pairs={{8,0},{12,4},{16,8},{20,12},{24,16},{28,20},{9,1},{13,5},{17,9},{2... | collective-permute-start | bytes 196616 | tf_op jit(solution)/shard_map/ppermute | solution.py:984
  391.2 14.2 %copy-start.38 = (bf16[4,1,192,768]{3,2,1,0:T(8,128)(2,1)S(1)}, bf16[4,1,192,768]{3,2,1,0:T(8,128)(2,1)}, u32[]{:S(2)}) copy-start(bf16[4,1,192,768]{3,2,1,0:T(8,128)(2,1)} %get-tuple-element.226) | copy-start | bytes 3538948
  408.0 159.8 %reduce-scatter.9.cloned.1.call-start = ((), (), s32[]{:S(2)}) async-start(), calls=%async_computation.8 | async-start | bytes 6881280 | tf_op jit(solution)/shard_map/reduce_scatter | solution.py:935
  436.7 25.9 %copy-start.11 = (f32[128,1536]{1,0:T(8,128)S(1)}, f32[128,1536]{1,0:T(8,128)}, u32[]{:S(2)}) copy-start(f32[128,1536]{1,0:T(8,128)} %copy-done.9) | copy-start | bytes 2359300
  436.7 25.9 %copy-start.121 = (f32[128]{0:T(128)S(1)}, f32[128]{0:T(128)}, u32[]{:S(2)}) copy-start(f32[128]{0:T(128)} %copy-done.120) | copy-start | bytes 1540
  468.3 159.4 %reduce-scatter.11.cloned.1.call-start = ((), (), s32[]{:S(2)}) async-start(), calls=%async_computation.9 | async-start | bytes 3440640 | tf_op jit(solution)/shard_map/reduce_scatter | solution.py:935
  470.5 18.1 %copy-start.37 = (bf16[384,1792]{1,0:T(8,128)(2,1)S(1)}, bf16[384,1792]{1,0:T(8,128)(2,1)}, u32[]{:S(2)}) copy-start(bf16[384,1792]{1,0:T(8,128)(2,1)} %reduce-scatter.5.cloned.1.call-done) | copy-start | bytes 4128772
  489.5 34.1 %collective-permute-start.10 = (bf16[192,1792]{1,0:T(8,128)(2,1)}, bf16[192,1792]{1,0:T(8,128)(2,1)}, u32[]{:S(2)}, u32[]{:S(2)}) collective-permute-start(bf16[192,1792]{1,0:T(8,128)(2,1)} %broadcast_select_fusion.3), channel_id=1, source_target_pairs={{0,4},{4,0},{8,12},{12,8},{16,20},{20,16},{24,28},{28,24},{1,5},{5... | collective-permute-start | bytes 2064392 | tf_op jit(solution)/shard_map/ppermute | solution.py:910
  501.1 20.4 %copy-start.48 = (bf16[8,192,256]{2,1,0:T(8,128)(2,1)S(1)}, bf16[8,192,256]{2,1,0:T(8,128)(2,1)}, u32[]{:S(2)}) copy-start(bf16[8,192,256]{2,1,0:T(8,128)(2,1)} %copy-done.47) | copy-start | bytes 2359300
  501.1 20.4 %copy-start.51 = (bf16[8,128,1536]{2,1,0:T(8,128)(2,1)S(1)}, bf16[8,128,1536]{2,1,0:T(8,128)(2,1)}, u32[]{:S(2)}) copy-start(bf16[8,128,1536]{2,1,0:T(8,128)(2,1)} %gather_full.9) | copy-start | bytes 9437188
  528.3 11.7 %copy-start.27 = (f32[1024,128]{1,0:T(8,128)S(1)}, f32[1024,128]{1,0:T(8,128)}, u32[]{:S(2)}) copy-start(f32[1024,128]{1,0:T(8,128)} %copy-done.26) | copy-start | bytes 1572868
  528.3 11.7 %copy-start.29 = (f32[1024,128]{1,0:T(8,128)S(1)}, f32[1024,128]{1,0:T(8,128)}, u32[]{:S(2)}) copy-start(f32[1024,128]{1,0:T(8,128)} %copy-done.28) | copy-start | bytes 1572868
  529.2 10.8 %copy-start.16 = (f32[1024,128]{1,0:T(8,128)S(1)}, f32[1024,128]{1,0:T(8,128)}, u32[]{:S(2)}) copy-start(f32[1024,128]{1,0:T(8,128)} %copy-done.15) | copy-start | bytes 1572868
  529.2 10.8 %copy-start.18 = (f32[1024,128]{1,0:T(8,128)S(1)}, f32[1024,128]{1,0:T(8,128)}, u32[]{:S(2)}) copy-start(f32[1024,128]{1,0:T(8,128)} %copy-done.17) | copy-start | bytes 1572868
  529.2 10.8 %copy-start.23 = (f32[1024,256]{1,0:T(8,128)S(1)}, f32[1024,256]{1,0:T(8,128)}, u32[]{:S(2)}) copy-start(f32[1024,256]{1,0:T(8,128)} %copy-done.22) | copy-start | bytes 3145732
  529.2 10.8 %copy-start.97 = (f32[1024]{0:T(1024)S(1)}, f32[1024]{0:T(1024)}, u32[]{:S(2)}) copy-start(f32[1024]{0:T(1024)} %copy-done.96) | copy-start | bytes 12292
  529.2 10.8 %copy-start.102 = (f32[1,256]{1,0:T(1,128)S(1)}, f32[1,256]{1,0:T(1,128)}, u32[]{:S(2)}) copy-start(f32[1,256]{1,0:T(1,128)} %copy-done.101) | copy-start | bytes 3076
  529.2 10.8 %copy-start.107 = (f32[1,256]{1,0:T(1,128)S(1)}, f32[1,256]{1,0:T(1,128)}, u32[]{:S(2)}) copy-start(f32[1,256]{1,0:T(1,128)} %copy-done.106) | copy-start | bytes 3076
  529.2 10.8 %copy-start.109 = (f32[256]{0:T(256)S(1)}, f32[256]{0:T(256)}, u32[]{:S(2)}) copy-start(f32[256]{0:T(256)} %copy-done.108) | copy-start | bytes 3076
  529.2 10.8 %copy-start.110 = (f32[256]{0:T(256)S(1)}, f32[256]{0:T(256)}, u32[]{:S(2)}) copy-start(f32[256]{0:T(256)} %get-tuple-element.215) | copy-start | bytes 3076
  529.2 10.8 %copy-start.127 = (f32[1,256]{1,0:T(1,128)S(1)}, f32[1,256]{1,0:T(1,128)}, u32[]{:S(2)}) copy-start(f32[1,256]{1,0:T(1,128)} %slice.599) | copy-start | bytes 3076
  548.5 9.3 %collective-permute-start.11 = (f32[3,256]{1,0:T(4,128)S(1)}, f32[3,256]{1,0:T(4,128)S(1)}, u32[]{:S(2)}, u32[]{:S(2)}) collective-permute-start(f32[3,256]{1,0:T(4,128)S(1)} %pad_add_fusion.1), channel_id=1, source_target_pairs={{8,0},{12,4},{16,8},{20,12},{24,16},{28,20},{9,1},{13,5},{17,9},{2... | collective-permute-start | bytes 9224 | tf_op jit(solution)/shard_map/ppermute | solution.py:984
  574.7 32.9 %copy-start.35 = (bf16[384,1792]{1,0:T(8,128)(2,1)S(1)}, bf16[384,1792]{1,0:T(8,128)(2,1)}, u32[]{:S(2)}) copy-start(bf16[384,1792]{1,0:T(8,128)(2,1)} %reduce-scatter.9.cloned.1.call-done) | copy-start | bytes 4128772
  607.6 17.8 %collective-permute-start.12 = (bf16[192,1792]{1,0:T(8,128)(2,1)S(1)}, bf16[192,1792]{1,0:T(8,128)(2,1)S(1)}, u32[]{:S(2)}, u32[]{:S(2)}) collective-permute-start(bf16[192,1792]{1,0:T(8,128)(2,1)S(1)} %broadcast_select_fusion.1), channel_id=1, source_target_pairs={{0,4},{4,0},{8,12},{12,8},{16,20},{20,16},{24,28},{28,24},{1,5},{5... | collective-permute-start | bytes 2064392 | tf_op jit(solution)/shard_map/ppermute | solution.py:910
  609.8 15.6 %copy-start.36 = (bf16[384,1792]{1,0:T(8,128)(2,1)S(1)}, bf16[384,1792]{1,0:T(8,128)(2,1)}, u32[]{:S(2)}) copy-start(bf16[384,1792]{1,0:T(8,128)(2,1)} %reduce-scatter.9.cloned.1.call-done) | copy-start | bytes 4128772
  628.8 10.0 %collective-permute-start.13 = (bf16[224,768]{1,0:T(8,128)(2,1)S(1)}, bf16[224,768]{1,0:T(8,128)(2,1)S(1)}, u32[]{:S(2)}, u32[]{:S(2)}) collective-permute-start(bf16[224,768]{1,0:T(8,128)(2,1)S(1)} %broadcast_select_fusion.9), channel_id=1, source_target_pairs={{0,4},{4,0},{8,12},{12,8},{16,20},{20,16},{24,28},{28,24},{1,5},{5... | collective-permute-start | bytes 1032200 | tf_op jit(solution)/shard_map/ppermute | solution.py:910
  (104 other events, 299.7 us)
Sparse Core Ops, SparseCore 0:
  22.6 76.3 all-gather.8
  100.5 101.6 all-gather.4
  203.7 100.7 all-gather.6
  332.3 104.4 reduce-scatter.4
  439.5 28.7 reduce-scatter.6
  470.4 97.3 reduce-scatter.8
  570.7 56.9 reduce-scatter.10

commit v5 on v4

--- a/solution.py
+++ b/solution.py
@@ -317,10 +317,10 @@
         share(3, 4)
         sx[1] = lowered(summed(2))
         x1 = go(sx.at[1], ax.at[1], 2, across_a)
+        sy[1] = lowered(summed(3))
+        y1 = go(sy.at[1], by.at[1], 3, across_b)
         yield
         share(6, 7)
-        sy[1] = lowered(summed(3))
-        y1 = go(sy.at[1], by.at[1], 3, across_b)
         yield
         total = summed(4)
         x0.wait_recv()
@@ -705,6 +705,7 @@
         if turn == 0:
             pl.semaphore_wait(pltpu.get_barrier_semaphore(), len(near))
         next(schedule)
+    next(schedule)
     stores = []
 
     def store(src, dst, slot):
@@ -717,23 +718,12 @@
     if mode == "forward":
         store(ab_v, ab_out, 16)
     if grads:
-        depth = w_v.shape[0]
-
-        def weight_grads(i, carry):
-            cols = pl.ds(pl.multiple_of(i * tile, tile), tile)
+        half = w_v.shape[0] // 2
+        for part in range(2):
+            cols = pl.ds(part * half, half)
             wire_v[cols, :both] = lowered(product_left(n_v[:, cols], low_v[...]))
             wire_v[cols, both:] = lowered(product_left(g_v[:, cols], hid_v[...]))
-            return carry
-
-        split = depth // tile // 2
-        lax.fori_loop(0, split, weight_grads, 0)
-        store(wire_v.at[pl.ds(0, split * tile)], wire_hbm.at[pl.ds(0, split * tile)], 17)
-        next(schedule)
-        lax.fori_loop(split, depth // tile, weight_grads, 0)
-        rest = pl.ds(split * tile, depth - split * tile)
-        store(wire_v.at[rest], wire_hbm.at[rest], 18)
-    else:
-        next(schedule)
+            store(wire_v.at[cols], wire_hbm.at[cols], 17 + part)
     next(schedule, None)
     for copy in stores:
         copy.wait()
@@ -1347,7 +1337,7 @@
         axis=1,
     )
     wire, done_one, summed_four = lax.optimization_barrier((wire, done_one, summed_four))
-    layer_own = lowered((stream_three + summed_four) * valid[:, None])
+    layer_own = lowered(stream_three + summed_four)
     last = reduce_high(wire.reshape(-1, 3 * channels))
     gain_one = jnp.sum(normed_one.astype(jnp.float32) * partial.astype(jnp.float32), axis=0)
     gain_one = gain_one / norm_gains[0]
@@ -1369,8 +1359,11 @@
     done_one = exchanged(done_one)
     (input_grad,) = gather([input_own], [False], cid["gather_half"])
     gains_sum = gains_sum[: norm_gains.shape[0]]
-    input_grad, done_one, last = lax.optimization_barrier((input_grad, done_one, last))
+    input_grad, layer_out, done_one, last = lax.optimization_barrier(
+        (input_grad, layer_out, done_one, last)
+    )
     input_grad = input_grad.astype(jnp.float32)
+    layer_out = jnp.where(segment[:, None] < doc_lengths.shape[0], layer_out, 0)
     last = exchanged(last)
     keyvalue_grad = jnp.sum(last[:, weight_rows + gate_rows :].astype(jnp.float32), axis=0)
     last_rows, last_gates = (last[:, :weight_rows], last[:, weight_rows : weight_rows + gate_rows])

time: 658 us -> 656 us (level)
  transfers between devices with their start and end apart: 21 -> 21, of which waited for: 15 -> 16; matrix products, arithmetic and copies ran while one was open for 17% -> 17% of each run, Pallas kernels for 56% -> 55%
where the time goes in v5:
time: 656 us; the launch traced here: 650 us
  Pallas kernels  385 us (59%)
  waiting for transfers between devices  89.5 us (14%)
  other arithmetic  72.5 us (11%)
  local copies, waits for them, and re-layouts  36.4 us (6%)
  starting transfers between devices  24.7 us (4%)
  matrix products  24 us (4%)
  between operations  17.1 us (3%)
    pallas_call x9, Pallas kernels, gather(): pl.pallas_call(functools.partial(gather_kernel, spans), out_shape=[jax.Sh...  175 us
    pallas_call x4, Pallas kernels, dense_call(): pl.pallas_call(functools.partial(dense_kernel, mode, main), out_shape=[ja...  94.3 us
    pallas_call x3, Pallas kernels, scatter(): pl.pallas_call(functools.partial(scatter_kernel, full, count), out_shape=...  47.4 us
    ppermute x8, waiting for transfers between devices, swap_low(): lax.ppermute(block, 'seq', [(s, s // LO * LO + (1 - s % LO)) for s in ran...  35.4 us
    pallas_call x1, Pallas kernels, scatter_and_sums(): pl.pallas_call(functools.partial(last_kernel, high), out_shape=[jax.Shape...  30.1 us
    pallas_call x2, Pallas kernels, plane_scan(): pl.pallas_call(functools.partial(scan_kernel, high, reverse), out_shape=(...  20.7 us
    ppermute x6, waiting for transfers between devices, shifted(): return lax.ppermute(block, 'seq', route)  18.7 us
    reduce_scatter x4, waiting for transfers between devices, reduce_high(): lax.psum_scatter(lowered(grad), 'seq', scatter_dimension=0, tiled=True, a...  17.7 us
  transfers between devices with their start and end apart: 21, of which 16 were waited for; matrix products, arithmetic and copies ran while one was open for 17% of the time, Pallas kernels for 55%

profile of v5, /device:TPU:0, one launch (start us, length us, event | category | flops | bytes accessed | tf_op | source)
XLA Modules:
  0.0 649.6 jit_solution(11362698104222253373)
XLA Ops:
  10.6 3.0 collective-permute-start
  15.7 1.9 fusion.41.refs_1_
  17.5 3.6 collective-permute-done
  24.4 1.8 collective-permute-start.1
  26.6 14.5 %collective-permute-done.1 = bf16[192,1792]{1,0:T(8,128)(2,1)S(1)} collective-permute-done((bf16[192,1792]{1,0:T(8,128)(2,1)S(1)}, bf16[192,1792]{1,0:T(8,128)(2,1)S(1)}, u32[]{:S(2)}, u32[]{:S(2)}) %collective-permute-start.1) | collective-permute-done | bytes 688160 | tf_op jit(solution)/shard_map/ppermute | solution.py:900
  44.9 41.7 %gather_full.5 = (bf16[8,128,1536]{2,1,0:T(8,128)(2,1)}, bf16[8,128,1536]{2,1,0:T(8,128)(2,1)}) custom-call(bf16[128,1536]{1,0:T(8,128)(2,1)} %fusion.39.refs_0_, bf16[128,1536]{1,0:T(8,128)(2,1)} %fusion.41.refs_1_), custom_call_target="tpu_custom_call" | custom-call | bytes 60000000 | tf_op jit(solution)/shard_map/gather_full/pallas_call | solution.py:229
  88.0 11.0 %all-gather.9.cloned.1.call-done = bf16[2496,768]{1,0:T(8,128)(2,1)} async-done(((bf16[624,768]{1,0:T(8,128)(2,1)}), bf16[2496,768]{1,0:T(8,128)(2,1)}) %all-gather.9.cloned.1.call-update) | async-done | bytes 3833872 | tf_op jit(solution)/shard_map/all_gather | solution.py:1137
  103.1 1.9 slice.535
  105.1 2.6 copy-done.49
  107.7 1.8 fusion.151
  109.5 1.6 collective-permute-start.3
  116.4 9.3 %scan.1 = (f32[1024,256]{1,0:T(8,128)S(1)}, f32[8,256]{1,0:T(8,128)S(1)}) custom-call(f32[1024,256]{1,0:T(8,128)S(1)} %get-tuple-element.251.decay_ref, f32[1024,256]{1,0:T(8,128)S(1)} %get-tuple-element.250.drive_ref, f32[8,256]{1,0:T(8,128)S(1)} %broadcast_in_dim.81.end_ref), custom_call_target="tpu_custom_call" | custom-call | bytes 33000000 | tf_op jit(solution)/shard_map/scan/pallas_call | solution.py:474
  126.2 15.2 %collective-permute-done.4 = bf16[4,208,768]{2,1,0:T(8,128)(2,1)S(1)} collective-permute-done((bf16[4,208,768]{2,1,0:T(8,128)(2,1)S(1)}, bf16[4,208,768]{2,1,0:T(8,128)(2,1)S(1)}, u32[]{:S(2)}, u32[]{:S(2)}) %collective-permute-start.4) | collective-permute-done | bytes 1277984 | tf_op jit(solution)/shard_map/ppermute | solution.py:900
  143.0 17.1 %scatter_full.1 = f32[128,1536]{1,0:T(8,128)S(1)} custom-call(bf16[8,128,1536]{2,1,0:T(8,128)(2,1)S(1)} %bitcast.190), custom_call_target="tpu_custom_call" | custom-call | bytes 60000000 | tf_op jit(solution)/shard_map/scatter_full/pallas_call | solution.py:387
  161.6 1.7 reshape.444.refs_1_
  166.5 23.6 %gather_full.6 = (bf16[8,128,1536]{2,1,0:T(8,128)(2,1)}, bf16[4,384,256]{2,1,0:T(8,128)(2,1)}) custom-call(bf16[128,1536]{1,0:T(8,128)(2,1)} %multiply_convert_fusion.3.refs_0_, bf16[384,256]{1,0:T(8,128)(2,1)} %reshape.444.refs_1_), custom_call_target="tpu_custom_call" | custom-call | bytes 60000000 | tf_op jit(solution)/shard_map/gather_full/pallas_call | solution.py:229
  190.0 2.1 copy.70
  192.1 3.4 fusion.130
  195.5 6.6 %all-gather.5.cloned.1.call-done.refs_1_.refs_2_ = bf16[1536,1792]{1,0:T(8,128)(2,1)} async-done(((bf16[384,1792]{1,0:T(8,128)(2,1)}), bf16[1536,1792]{1,0:T(8,128)(2,1)}) %all-gather.5.cloned.1.call-update) | async-done | bytes 5505040 | tf_op jit(solution)/shard_map/all_gather | solution.py:921
  202.8 22.9 %dense_forward.1 = (f32[128,1536]{1,0:T(8,128)}, f32[1024,1152]{1,0:T(8,128)}) custom-call(bf16[1024,1536]{1,0:T(8,128)(2,1)} %bitcast.197, bf16[1536,1792]{1,0:T(8,128)(2,1)} %all-gather.5.cloned.1.call-done.refs_1_.refs_2_), custom_call_target="tpu_custom_call" | custom-call | bytes 75000000 | tf_op jit(solution)/shard_map/dense_forward/pallas_call | solution.py:760
  230.4 3.4 collective-permute-start.6
  233.9 1.8 collective-permute-done.6
  236.4 20.0 %gather_half.4 = (bf16[4,128,1536]{2,1,0:T(8,128)(2,1)}, bf16[4,128,768]{2,1,0:T(8,128)(2,1)}) custom-call(bf16[128,1536]{1,0:T(8,128)(2,1)} %copy-done.46, bf16[128,768]{1,0:T(8,128)(2,1)} %pad_maximum_fusion.19.refs_1_), custom_call_target="tpu_custom_call" | custom-call | bytes 60000000 | tf_op jit(solution)/shard_map/gather_half/pallas_call | solution.py:229
  259.4 8.3 %attention.1 = (bf16[512,384]{1,0:T(8,128)(2,1)S(1)}, bf16[512,384]{1,0:T(8,128)(2,1)S(1)}, f32[8,512]{1,0:T(8,128)S(1)}) custom-call(f32[512,384]{1,0:T(8,128)S(1)} %fusion.153.query_ref, bf16[1536,256]{1,0:T(8,128)(2,1)S(1)} %pad_maximum_fusion.10.ext_ref, s32[8,512]{1,0:T(8,128)S(1)} %broadcast_in_dim.85.here_ref, ...), custom_call_target="tpu_custom_call" | custom-call | bytes 33000000 | tf_op jit(solution)/shard_map/attention/pallas_call | solution.py:823
  268.9 13.1 %scatter_half.2 = f32[128,1536]{1,0:T(8,128)S(1)} custom-call(bf16[4,128,1536]{2,1,0:T(8,128)(2,1)S(1)} %bitcast.194), custom_call_target="tpu_custom_call" | custom-call | bytes 60000000 | tf_op jit(solution)/shard_map/scatter_half/pallas_call | solution.py:387
  283.0 2.0 multiply_convert_fusion.1.refs_0_
  285.0 20.0 %gather_full.7 = bf16[8,128,1536]{2,1,0:T(8,128)(2,1)} custom-call(bf16[128,1536]{1,0:T(8,128)(2,1)} %multiply_convert_fusion.1.refs_0_), custom_call_target="tpu_custom_call" | custom-call | bytes 60000000 | tf_op jit(solution)/shard_map/gather_full/pallas_call | solution.py:229
  305.0 26.4 %dense_both.1 = (f32[128,1536]{1,0:T(8,128)}, bf16[1536,1792]{1,0:T(8,128)(2,1)}, bf16[1024,640]{1,0:T(8,128)(2,1)}) custom-call(bf16[1024,1536]{1,0:T(8,128)(2,1)} %bitcast.196, bf16[1024,1536]{1,0:T(8,128)(2,1)} %bitcast.226, bf16[1536,1792]{1,0:T(8,128)(2,1)} %all-gather.7.cloned.1.call-done.refs_2_.refs_0_), custom_call_target="tpu_custom_call" | custom-call | bytes 100000000 | tf_op jit(solution)/shard_map/dense_both/pallas_call | solution.py:760
  331.5 2.2 multiply_reduce_fusion.6
  333.8 2.5 fusion.126
  336.3 14.1 %gather_half.5 = bf16[4,128,1536]{2,1,0:T(8,128)(2,1)} custom-call(bf16[128,1536]{1,0:T(8,128)(2,1)} %get-tuple-element.208.refs_0_), custom_call_target="tpu_custom_call" | custom-call | bytes 60000000 | tf_op jit(solution)/shard_map/gather_half/pallas_call | solution.py:229
  350.4 2.8 convolution_convert_fusion.8.grad_ref
  353.3 9.9 %attention_back.1 = (bf16[512,384]{1,0:T(8,128)(2,1)S(1)}, bf16[1536,256]{1,0:T(8,128)(2,1)S(1)}) custom-call(bf16[512,384]{1,0:T(8,128)(2,1)S(1)} %copy-done.8, bf16[1536,256]{1,0:T(8,128)(2,1)S(1)} %copy-done.1, bf16[512,384]{1,0:T(8,128)(2,1)S(1)} %convolution_convert_fusion.8.grad_ref, f32[8,512]{1,0:T(8,128)S(1)} %get-tuple-element.138.log_ref, ...), custom_call_target="tpu_custom_call" | custom-call | bytes 60000000 | tf_op jit(solution)/shard_map/attention_back/pallas_call | solution.py:878
  367.4 1.6 broadcast_select_fusion.1
  370.1 17.2 %scatter_half.3 = f32[128,2304]{1,0:T(8,128)S(1)} custom-call(bf16[4,128,2304]{2,1,0:T(8,128)(2,1)S(1)} %bitcast.192), custom_call_target="tpu_custom_call" | custom-call | bytes 60000000 | tf_op jit(solution)/shard_map/scatter_half/pallas_call | solution.py:387
  391.9 6.5 collective-permute-done.7
  399.0 4.8 collective-permute-done.8
  404.7 2.6 fusion.1
  408.7 2.6 multiply_reduce_fusion.7
  412.6 17.5 %gather_full.8 = bf16[8,128,1536]{2,1,0:T(8,128)(2,1)} custom-call(bf16[128,1536]{1,0:T(8,128)(2,1)} %get-tuple-element.206.refs_0_), custom_call_target="tpu_custom_call" | custom-call | bytes 60000000 | tf_op jit(solution)/shard_map/gather_full/pallas_call | solution.py:229
  430.1 5.8 reduce-scatter.5.cloned.1.call-done
  435.9 24.6 %dense_backward.1 = (f32[128,1536]{1,0:T(8,128)}, bf16[1536,1792]{1,0:T(8,128)(2,1)}) custom-call(bf16[1024,1536]{1,0:T(8,128)(2,1)} %bitcast.198, bf16[1024,1536]{1,0:T(8,128)(2,1)} %bitcast.199, bf16[1536,1792]{1,0:T(8,128)(2,1)} %all-gather.5.cloned.1.call-done.refs_1_.refs_2_, f32[1024,1152]{1,0:T(8,128)} %get-tuple-element.147.refs_3_), custom_call_target="tpu_custom_call" | custom-call | bytes 100000000 | tf_op jit(solution)/shard_map/dense_backward/pallas_call | solution.py:760
  460.6 2.0 multiply_reduce_fusion.8
  462.9 4.6 reduce-scatter.7.cloned.1.call-done
  469.7 18.1 %gather_full.9 = bf16[8,128,1536]{2,1,0:T(8,128)(2,1)} custom-call(bf16[128,1536]{1,0:T(8,128)(2,1)} %convert_element_type.231.refs_0_), custom_call_target="tpu_custom_call" | custom-call | bytes 60000000 | tf_op jit(solution)/shard_map/gather_full/pallas_call | solution.py:229
  489.9 6.0 gather_half.6
  495.9 2.0 fusion
  498.6 1.7 reshape.473
  500.4 20.4 %dense_product.1 = f32[128,1536]{1,0:T(8,128)} custom-call(bf16[1536,1792]{1,0:T(8,128)(2,1)} %all-gather.7.cloned.1.call-done.refs_2_.refs_0_, bf16[1024,640]{1,0:T(8,128)(2,1)} %get-tuple-element.165.refs_1_), custom_call_target="tpu_custom_call" | custom-call | bytes 75000000 | tf_op jit(solution)/shard_map/dense_product/pallas_call | solution.py:760
  528.5 11.4 %scan_back.1 = (f32[1024,256]{1,0:T(8,128)S(1)}, f32[8,256]{1,0:T(8,128)}) custom-call(f32[1024,256]{1,0:T(8,128)S(1)} %concatenate.180.decay_ref, f32[1024,256]{1,0:T(8,128)S(1)} %get-tuple-element.224.drive_ref, f32[8,256]{1,0:T(8,128)S(1)} %broadcast_in_dim.151.end_ref), custom_call_target="tpu_custom_call" | custom-call | bytes 33000000 | tf_op jit(solution)/shard_map/scan_back/pallas_call | solution.py:474
  540.1 3.5 fusion.75
  545.7 2.3 multiply_reduce_fusion.5
  551.5 5.6 collective-permute-done.11
  557.2 1.8 convolution_convert_fusion.1
  559.1 1.8 convolution_convert_fusion.2
  560.9 1.8 pad_maximum_fusion
  562.8 4.2 reduce-scatter.9.cloned.1.call-done
  568.8 2.8 multiply_reduce_fusion
  573.9 30.1 %scatter_and_sums.1 = (f32[128,1536]{1,0:T(8,128)S(1)}, f32[8,1536]{1,0:T(8,128)S(1)}, f32[8,512]{1,0:T(8,128)S(1)}, bf16[4,128,1536]{2,1,0:T(8,128)(2,1)S(1)}) custom-call(bf16[8,128,1536]{2,1,0:T(8,128)(2,1)S(1)} %bitcast.191, f32[8,1536]{1,0:T(8,128)S(1)} %concatenate.190.gains_ref, f32[8,256]{1,0:T(8,128)S(1)} %pad_maximum_fusion.23.rest_ref, ...), custom_call_target="tpu_custom_call" | custom-call | bytes 60000000 | tf_op jit(solution)/shard_map/scatter_and_sums/pallas_call | solution.py:558
  605.3 1.9 collective-permute-start.12
  608.4 13.8 %gather_half.7 = bf16[4,128,1536]{2,1,0:T(8,128)(2,1)} custom-call(bf16[128,1536]{1,0:T(8,128)(2,1)} %fusion.36.refs_0_), custom_call_target="tpu_custom_call" | custom-call | bytes 60000000 | tf_op jit(solution)/shard_map/gather_half/pallas_call | solution.py:229
  623.9 3.1 reduce-scatter.11.cloned.1.call-done
  629.6 2.1 convert_element_type.246
  636.2 1.9 collective-permute-done.13
  (524 shorter events, 92.8 us)
Async XLA Ops:
  7.2 91.7 %all-gather.9.cloned.1.call-start = ((), (), s32[]{:S(2)}) async-start(), calls=%async_computation.10 | async-start | bytes 4792320 | tf_op jit(solution)/shard_map/all_gather | solution.py:1137
  9.3 11.8 %copy-start.59 = (bf16[192,512]{1,0:T(8,128)(2,1)S(1)}, bf16[192,512]{1,0:T(8,128)(2,1)}, u32[]{:S(2)}) copy-start(bf16[192,512]{1,0:T(8,128)(2,1)} %param.27) | copy-start | bytes 589828
  9.3 11.8 %copy-start.60 = (bf16[192,512]{1,0:T(8,128)(2,1)S(1)}, bf16[192,512]{1,0:T(8,128)(2,1)}, u32[]{:S(2)}) copy-start(bf16[192,512]{1,0:T(8,128)(2,1)} %param.26) | copy-start | bytes 589828
  9.4 11.8 %copy-start.81 = (bf16[512,16]{0,1:T(8,128)(2,1)S(1)}, bf16[512,16]{0,1:T(8,128)(2,1)}, u32[]{:S(2)}) copy-start(bf16[512,16]{0,1:T(8,128)(2,1)} %param.31) | copy-start | bytes 49156
  9.4 11.7 %copy-start.82 = (bf16[512,16]{0,1:T(8,128)(2,1)S(1)}, bf16[512,16]{0,1:T(8,128)(2,1)}, u32[]{:S(2)}) copy-start(bf16[512,16]{0,1:T(8,128)(2,1)} %param.30) | copy-start | bytes 49156
  10.6 10.5 %collective-permute-start = (bf16[208,768]{1,0:T(8,128)(2,1)S(1)}, bf16[208,768]{1,0:T(8,128)(2,1)S(1)}, u32[]{:S(2)}, u32[]{:S(2)}) collective-permute-start(bf16[208,768]{1,0:T(8,128)(2,1)S(1)} %broadcast_select_fusion.12), channel_id=1, source_target_pairs={{0,4},{4,0},{8,12},{12,8},{16,20},{20,16},{24,28},{28,24},{1,5},{5... | collective-permute-start | bytes 958472 | tf_op jit(solution)/shard_map/ppermute | solution.py:900
  22.5 179.7 %all-gather.5.cloned.1.call-start = ((), (), s32[]{:S(2)}) async-start(), calls=%async_computation.4 | async-start | bytes 6881280 | tf_op jit(solution)/shard_map/all_gather | solution.py:921
  24.4 16.7 %collective-permute-start.1 = (bf16[192,1792]{1,0:T(8,128)(2,1)S(1)}, bf16[192,1792]{1,0:T(8,128)(2,1)S(1)}, u32[]{:S(2)}, u32[]{:S(2)}) collective-permute-start(bf16[192,1792]{1,0:T(8,128)(2,1)S(1)} %broadcast_select_fusion.8), channel_id=1, source_target_pairs={{0,4},{4,0},{8,12},{12,8},{16,20},{20,16},{24,28},{28,24},{1,5},{5... | collective-permute-start | bytes 2064392 | tf_op jit(solution)/shard_map/ppermute | solution.py:900
  43.4 43.2 %collective-permute-start.2 = (bf16[192,1792]{1,0:T(8,128)(2,1)S(1)}, bf16[192,1792]{1,0:T(8,128)(2,1)S(1)}, u32[]{:S(2)}, u32[]{:S(2)}) collective-permute-start(bf16[192,1792]{1,0:T(8,128)(2,1)S(1)} %broadcast_select_fusion.6), channel_id=1, source_target_pairs={{0,4},{4,0},{8,12},{12,8},{16,20},{20,16},{24,28},{28,24},{1,5},{5... | collective-permute-start | bytes 2064392 | tf_op jit(solution)/shard_map/ppermute | solution.py:900
  86.7 12.4 %copy-start.143 = (f32[512]{0:T(512)S(1)}, f32[512]{0:T(512)}, u32[]{:S(2)}) copy-start(f32[512]{0:T(512)} %param.29) | copy-start | bytes 6148
  86.7 12.5 %copy-start.131 = (f32[512]{0:T(512)S(1)}, f32[512]{0:T(512)}, u32[]{:S(2)}) copy-start(f32[512]{0:T(512)} %param.33) | copy-start | bytes 6148
  86.7 13.1 %copy-start.130 = (f32[4,512]{1,0:T(4,128)S(1)}, f32[4,512]{1,0:T(4,128)}, u32[]{:S(2)}) copy-start(f32[4,512]{1,0:T(4,128)} %param.28) | copy-start | bytes 24580
  86.8 13.1 %copy-start.136 = (f32[2,512]{1,0:T(2,128)S(1)}, f32[2,512]{1,0:T(2,128)}, u32[]{:S(2)}) copy-start(f32[2,512]{1,0:T(2,128)} %param.32) | copy-start | bytes 12292
  99.0 206.1 %all-gather.7.cloned.1.call-start = ((), (), s32[]{:S(2)}) async-start(), calls=%async_computation.5 | async-start | bytes 6881280 | tf_op jit(solution)/shard_map/all_gather | solution.py:921
  99.9 15.1 %copy-start.108 = (f32[256]{0:T(256)}, f32[256]{0:T(256)S(1)}, u32[]{:S(2)}) copy-start(f32[256]{0:T(256)S(1)} %get-tuple-element.218) | copy-start | bytes 3076
  100.0 13.0 %copy-start.111 = (f32[1,256]{1,0:T(1,128)}, f32[1,256]{1,0:T(1,128)S(1)}, u32[]{:S(2)}) copy-start(f32[1,256]{1,0:T(1,128)S(1)} %get-tuple-element.312) | copy-start | bytes 3076
  100.0 13.0 %copy-start.113 = (f32[1,256]{1,0:T(1,128)}, f32[1,256]{1,0:T(1,128)S(1)}, u32[]{:S(2)}) copy-start(f32[1,256]{1,0:T(1,128)S(1)} %get-tuple-element.313) | copy-start | bytes 3076
  100.0 13.0 %copy-start.115 = (f32[1,256]{1,0:T(1,128)}, f32[1,256]{1,0:T(1,128)S(1)}, u32[]{:S(2)}) copy-start(f32[1,256]{1,0:T(1,128)S(1)} %get-tuple-element.314) | copy-start | bytes 3076
  100.0 13.0 %copy-start.117 = (f32[1,256]{1,0:T(1,128)}, f32[1,256]{1,0:T(1,128)S(1)}, u32[]{:S(2)}) copy-start(f32[1,256]{1,0:T(1,128)S(1)} %get-tuple-element.315) | copy-start | bytes 3076
  100.0 15.0 %copy-start.101 = (f32[1,256]{1,0:T(1,128)}, f32[1,256]{1,0:T(1,128)S(1)}, u32[]{:S(2)}) copy-start(f32[1,256]{1,0:T(1,128)S(1)} %get-tuple-element.327) | copy-start | bytes 3076
  100.0 15.0 %copy-start.106 = (f32[1,256]{1,0:T(1,128)}, f32[1,256]{1,0:T(1,128)S(1)}, u32[]{:S(2)}) copy-start(f32[1,256]{1,0:T(1,128)S(1)} %get-tuple-element.328) | copy-start | bytes 3076
  102.7 12.3 %copy-start.96 = (f32[1024]{0:T(1024)}, f32[1024]{0:T(1024)S(1)}, u32[]{:S(2)}) copy-start(f32[1024]{0:T(1024)S(1)} %compare_convert_fusion.1) | copy-start | bytes 12292
  109.5 16.2 %copy-start.24 = (f32[1024,512]{1,0:T(8,128)}, f32[1024,512]{1,0:T(8,128)S(1)}, u32[]{:S(2)}) copy-start(f32[1024,512]{1,0:T(8,128)S(1)} %fusion.151) | copy-start | bytes 6291460
  109.5 3.5 collective-permute-start.3
  111.4 30.5 %copy-start.47 = (bf16[8,192,256]{2,1,0:T(8,128)(2,1)}, bf16[8,192,256]{2,1,0:T(8,128)(2,1)S(1)}, u32[]{:S(2)}) copy-start(bf16[8,192,256]{2,1,0:T(8,128)(2,1)S(1)} %slice.667) | copy-start | bytes 2359300
  111.4 29.9 %collective-permute-start.4 = (bf16[4,208,768]{2,1,0:T(8,128)(2,1)S(1)}, bf16[4,208,768]{2,1,0:T(8,128)(2,1)S(1)}, u32[]{:S(2)}, u32[]{:S(2)}) collective-permute-start(bf16[4,208,768]{2,1,0:T(8,128)(2,1)S(1)} %slice.560), channel_id=1, source_target_pairs={{0,4},{4,0},{8,12},{12,8},{16,20},{20,16},{24,28},{28,24},{1,5},{5... | collective-permute-start | bytes 3833864 | tf_op jit(solution)/shard_map/ppermute | solution.py:900
  126.1 15.8 %copy-start.44 = (bf16[1024,256]{1,0:T(8,128)(2,1)}, bf16[1024,256]{1,0:T(8,128)(2,1)S(1)}, u32[]{:S(2)}) copy-start(bf16[1024,256]{1,0:T(8,128)(2,1)S(1)} %multiply_convert_fusion) | copy-start | bytes 1572868
  141.9 19.0 %copy-start.19 = (bf16[4,2,208,768]{3,2,1,0:T(8,128)(2,1)}, bf16[4,2,208,768]{3,2,1,0:T(8,128)(2,1)S(1)}, u32[]{:S(2)}) copy-start(bf16[4,2,208,768]{3,2,1,0:T(8,128)(2,1)S(1)} %copy.69) | copy-start | bytes 7667716
  164.7 27.4 %copy-start.139 = (f32[128]{0:T(128)}, f32[128]{0:T(128)S(1)}, u32[]{:S(2)}) copy-start(f32[128]{0:T(128)S(1)} %get-tuple-element.214) | copy-start | bytes 1540
  164.7 27.4 %copy-start.120 = (f32[128]{0:T(128)}, f32[128]{0:T(128)S(1)}, u32[]{:S(2)}) copy-start(f32[128]{0:T(128)S(1)} %fusion.115) | copy-start | bytes 1540
  202.2 233.7 %reduce-scatter.5.cloned.1.call-start = ((), (), s32[]{:S(2)}) async-start(), calls=%async_computation.6 | async-start | bytes 6881280 | tf_op jit(solution)/shard_map/reduce_scatter | solution.py:925
  202.8 22.9 %copy-start.10 = (f32[128,1536]{1,0:T(8,128)S(1)}, f32[128,1536]{1,0:T(8,128)}, u32[]{:S(2)}) copy-start(f32[128,1536]{1,0:T(8,128)} %copy-done.9) | copy-start | bytes 2359300
  229.1 4.8 collective-permute-start.5
  230.4 5.3 collective-permute-start.6
  268.9 13.1 %copy-start.13 = (f32[128,1536]{1,0:T(8,128)S(1)}, f32[128,1536]{1,0:T(8,128)}, u32[]{:S(2)}) copy-start(f32[128,1536]{1,0:T(8,128)} %copy-done.12) | copy-start | bytes 2359300
  331.5 136.1 %reduce-scatter.7.cloned.1.call-start = ((), (), s32[]{:S(2)}) async-start(), calls=%async_computation.7 | async-start | bytes 1474560 | tf_op jit(solution)/shard_map/reduce_scatter | solution.py:925
  368.9 35.7 %collective-permute-start.9 = (bf16[4,192,768]{2,1,0:T(8,128)(2,1)}, bf16[4,192,768]{2,1,0:T(8,128)(2,1)}, u32[]{:S(2)}, u32[]{:S(2)}) collective-permute-start(bf16[4,192,768]{2,1,0:T(8,128)(2,1)} %get-tuple-element.231), channel_id=1, source_target_pairs={{0,4},{4,0},{8,12},{12,8},{16,20},{20,16},{24,28},{28,24},{1,5},{5... | collective-permute-start | bytes 3538952 | tf_op jit(solution)/shard_map/ppermute | solution.py:900
  388.0 10.3 %collective-permute-start.7 = (bf16[128,256]{1,0:T(8,128)(2,1)}, bf16[128,256]{1,0:T(8,128)(2,1)S(1)}, u32[]{:S(2)}, u32[]{:S(2)}) collective-permute-start(bf16[128,256]{1,0:T(8,128)(2,1)} %get-tuple-element.264), channel_id=1, source_target_pairs={{4,0},{8,4},{12,8},{16,12},{20,16},{24,20},{28,24},{5,1},{9,5},{13... | collective-permute-start | bytes 196616 | tf_op jit(solution)/shard_map/ppermute | solution.py:974
  389.3 14.5 %collective-permute-start.8 = (bf16[128,256]{1,0:T(8,128)(2,1)S(1)}, bf16[128,256]{1,0:T(8,128)(2,1)}, u32[]{:S(2)}, u32[]{:S(2)}) collective-permute-start(bf16[128,256]{1,0:T(8,128)(2,1)S(1)} %get-tuple-element.265), channel_id=1, source_target_pairs={{8,0},{12,4},{16,8},{20,12},{24,16},{28,20},{9,1},{13,5},{17,9},{2... | collective-permute-start | bytes 196616 | tf_op jit(solution)/shard_map/ppermute | solution.py:974
  390.7 14.0 %copy-start.38 = (bf16[4,1,192,768]{3,2,1,0:T(8,128)(2,1)S(1)}, bf16[4,1,192,768]{3,2,1,0:T(8,128)(2,1)}, u32[]{:S(2)}) copy-start(bf16[4,1,192,768]{3,2,1,0:T(8,128)(2,1)} %get-tuple-element.230) | copy-start | bytes 3538948
  407.3 159.7 %reduce-scatter.9.cloned.1.call-start = ((), (), s32[]{:S(2)}) async-start(), calls=%async_computation.8 | async-start | bytes 6881280 | tf_op jit(solution)/shard_map/reduce_scatter | solution.py:925
  435.9 24.7 %copy-start.11 = (f32[128,1536]{1,0:T(8,128)S(1)}, f32[128,1536]{1,0:T(8,128)}, u32[]{:S(2)}) copy-start(f32[128,1536]{1,0:T(8,128)} %copy-done.9) | copy-start | bytes 2359300
  435.9 24.7 %copy-start.121 = (f32[128]{0:T(128)S(1)}, f32[128]{0:T(128)}, u32[]{:S(2)}) copy-start(f32[128]{0:T(128)} %copy-done.120) | copy-start | bytes 1540
  467.5 159.4 %reduce-scatter.11.cloned.1.call-start = ((), (), s32[]{:S(2)}) async-start(), calls=%async_computation.9 | async-start | bytes 3440640 | tf_op jit(solution)/shard_map/reduce_scatter | solution.py:925
  469.7 18.1 %copy-start.37 = (bf16[384,1792]{1,0:T(8,128)(2,1)S(1)}, bf16[384,1792]{1,0:T(8,128)(2,1)}, u32[]{:S(2)}) copy-start(bf16[384,1792]{1,0:T(8,128)(2,1)} %reduce-scatter.5.cloned.1.call-done) | copy-start | bytes 4128772
  488.7 34.1 %collective-permute-start.10 = (bf16[192,1792]{1,0:T(8,128)(2,1)}, bf16[192,1792]{1,0:T(8,128)(2,1)}, u32[]{:S(2)}, u32[]{:S(2)}) collective-permute-start(bf16[192,1792]{1,0:T(8,128)(2,1)} %broadcast_select_fusion.4), channel_id=1, source_target_pairs={{0,4},{4,0},{8,12},{12,8},{16,20},{20,16},{24,28},{28,24},{1,5},{5... | collective-permute-start | bytes 2064392 | tf_op jit(solution)/shard_map/ppermute | solution.py:900
  500.3 20.4 %copy-start.48 = (bf16[8,192,256]{2,1,0:T(8,128)(2,1)S(1)}, bf16[8,192,256]{2,1,0:T(8,128)(2,1)}, u32[]{:S(2)}) copy-start(bf16[8,192,256]{2,1,0:T(8,128)(2,1)} %copy-done.47) | copy-start | bytes 2359300
  500.4 20.4 %copy-start.51 = (bf16[8,128,1536]{2,1,0:T(8,128)(2,1)S(1)}, bf16[8,128,1536]{2,1,0:T(8,128)(2,1)}, u32[]{:S(2)}) copy-start(bf16[8,128,1536]{2,1,0:T(8,128)(2,1)} %gather_full.9) | copy-start | bytes 9437188
  527.6 12.4 %copy-start.27 = (f32[1024,128]{1,0:T(8,128)S(1)}, f32[1024,128]{1,0:T(8,128)}, u32[]{:S(2)}) copy-start(f32[1024,128]{1,0:T(8,128)} %copy-done.26) | copy-start | bytes 1572868
  527.6 12.4 %copy-start.29 = (f32[1024,128]{1,0:T(8,128)S(1)}, f32[1024,128]{1,0:T(8,128)}, u32[]{:S(2)}) copy-start(f32[1024,128]{1,0:T(8,128)} %copy-done.28) | copy-start | bytes 1572868
  528.4 11.6 %copy-start.16 = (f32[1024,128]{1,0:T(8,128)S(1)}, f32[1024,128]{1,0:T(8,128)}, u32[]{:S(2)}) copy-start(f32[1024,128]{1,0:T(8,128)} %copy-done.15) | copy-start | bytes 1572868
  528.4 11.6 %copy-start.18 = (f32[1024,128]{1,0:T(8,128)S(1)}, f32[1024,128]{1,0:T(8,128)}, u32[]{:S(2)}) copy-start(f32[1024,128]{1,0:T(8,128)} %copy-done.17) | copy-start | bytes 1572868
  528.4 11.6 %copy-start.23 = (f32[1024,256]{1,0:T(8,128)S(1)}, f32[1024,256]{1,0:T(8,128)}, u32[]{:S(2)}) copy-start(f32[1024,256]{1,0:T(8,128)} %copy-done.22) | copy-start | bytes 3145732
  528.5 11.6 %copy-start.97 = (f32[1024]{0:T(1024)S(1)}, f32[1024]{0:T(1024)}, u32[]{:S(2)}) copy-start(f32[1024]{0:T(1024)} %copy-done.96) | copy-start | bytes 12292
  528.5 11.6 %copy-start.102 = (f32[1,256]{1,0:T(1,128)S(1)}, f32[1,256]{1,0:T(1,128)}, u32[]{:S(2)}) copy-start(f32[1,256]{1,0:T(1,128)} %copy-done.101) | copy-start | bytes 3076
  528.5 11.6 %copy-start.107 = (f32[1,256]{1,0:T(1,128)S(1)}, f32[1,256]{1,0:T(1,128)}, u32[]{:S(2)}) copy-start(f32[1,256]{1,0:T(1,128)} %copy-done.106) | copy-start | bytes 3076
  528.5 11.6 %copy-start.109 = (f32[256]{0:T(256)S(1)}, f32[256]{0:T(256)}, u32[]{:S(2)}) copy-start(f32[256]{0:T(256)} %copy-done.108) | copy-start | bytes 3076
  528.5 11.6 %copy-start.110 = (f32[256]{0:T(256)S(1)}, f32[256]{0:T(256)}, u32[]{:S(2)}) copy-start(f32[256]{0:T(256)} %get-tuple-element.219) | copy-start | bytes 3076
  528.5 11.6 %copy-start.124 = (f32[1,256]{1,0:T(1,128)S(1)}, f32[1,256]{1,0:T(1,128)}, u32[]{:S(2)}) copy-start(f32[1,256]{1,0:T(1,128)} %slice.599) | copy-start | bytes 3076
  548.5 8.5 %collective-permute-start.11 = (f32[3,256]{1,0:T(4,128)S(1)}, f32[3,256]{1,0:T(4,128)S(1)}, u32[]{:S(2)}, u32[]{:S(2)}) collective-permute-start(f32[3,256]{1,0:T(4,128)S(1)} %pad_add_fusion.1), channel_id=1, source_target_pairs={{8,0},{12,4},{16,8},{20,12},{24,16},{28,20},{9,1},{13,5},{17,9},{2... | collective-permute-start | bytes 9224 | tf_op jit(solution)/shard_map/ppermute | solution.py:974
  573.9 31.3 %copy-start.35 = (bf16[384,1792]{1,0:T(8,128)(2,1)S(1)}, bf16[384,1792]{1,0:T(8,128)(2,1)}, u32[]{:S(2)}) copy-start(bf16[384,1792]{1,0:T(8,128)(2,1)} %reduce-scatter.9.cloned.1.call-done) | copy-start | bytes 4128772
  605.3 18.4 %collective-permute-start.12 = (bf16[192,1792]{1,0:T(8,128)(2,1)S(1)}, bf16[192,1792]{1,0:T(8,128)(2,1)S(1)}, u32[]{:S(2)}, u32[]{:S(2)}) collective-permute-start(bf16[192,1792]{1,0:T(8,128)(2,1)S(1)} %broadcast_select_fusion.2), channel_id=1, source_target_pairs={{0,4},{4,0},{8,12},{12,8},{16,20},{20,16},{24,28},{28,24},{1,5},{5... | collective-permute-start | bytes 2064392 | tf_op jit(solution)/shard_map/ppermute | solution.py:900
  608.4 15.2 %copy-start.36 = (bf16[384,1792]{1,0:T(8,128)(2,1)S(1)}, bf16[384,1792]{1,0:T(8,128)(2,1)}, u32[]{:S(2)}) copy-start(bf16[384,1792]{1,0:T(8,128)(2,1)} %reduce-scatter.9.cloned.1.call-done) | copy-start | bytes 4128772
  628.1 10.0 %collective-permute-start.13 = (bf16[224,768]{1,0:T(8,128)(2,1)S(1)}, bf16[224,768]{1,0:T(8,128)(2,1)S(1)}, u32[]{:S(2)}, u32[]{:S(2)}) collective-permute-start(bf16[224,768]{1,0:T(8,128)(2,1)S(1)} %broadcast_select_fusion.10), channel_id=1, source_target_pairs={{0,4},{4,0},{8,12},{12,8},{16,20},{20,16},{24,28},{28,24},{1,5},{5... | collective-permute-start | bytes 1032200 | tf_op jit(solution)/shard_map/ppermute | solution.py:900
  (104 other events, 302.2 us)
Sparse Core Ops, SparseCore 0:
  22.6 76.3 all-gather.8
  100.5 101.6 all-gather.4
  203.7 100.7 all-gather.6
  331.6 104.3 reduce-scatter.4
  438.7 28.8 reduce-scatter.6
  469.7 97.3 reduce-scatter.8
  569.9 56.9 reduce-scatter.10

commit v6 on v5

--- a/solution.py
+++ b/solution.py
@@ -1271,9 +1271,7 @@
     )
     stream_grad, gain_two = jax.vjp(rms_norm, stream_one, norm_gains[1])[1](grad_normed)
     grad_stream = grad_stream + stream_grad
-    grad_stream, one_wire, done_attn = lax.optimization_barrier(
-        (grad_stream, one_wire, done_attn)
-    )
+    grad_stream, one_wire = lax.optimization_barrier((grad_stream, one_wire))
     grad_stream, keyvalue_low = lax.optimization_barrier((grad_stream, keyvalue_low))
     done_one = reduce_high(one_wire)
     (keyvalue_grads,) = gather([keyvalue_low], [False], cid["gather_narrow"])

time: 656 us -> 656 us (level)
  transfers between devices with their start and end apart: 21 -> 21, of which waited for: 16 -> 15; matrix products, arithmetic and copies ran while one was open for 17% -> 18% of each run, Pallas kernels for 55% -> 55%
where the time goes in v6:
time: 656 us; the launch traced here: 650 us
  Pallas kernels  385 us (59%)
  waiting for transfers between devices  86.1 us (13%)
  other arithmetic  73.8 us (11%)
  local copies, waits for them, and re-layouts  37 us (6%)
  matrix products  25.9 us (4%)
  starting transfers between devices  24.9 us (4%)
  between operations  17.1 us (3%)
    pallas_call x9, Pallas kernels, gather(): pl.pallas_call(functools.partial(gather_kernel, spans), out_shape=[jax.Sh...  174 us
    pallas_call x4, Pallas kernels, dense_call(): pl.pallas_call(functools.partial(dense_kernel, mode, main), out_shape=[ja...  93.9 us
    pallas_call x3, Pallas kernels, scatter(): pl.pallas_call(functools.partial(scatter_kernel, full, count), out_shape=...  47.4 us
    ppermute x8, waiting for transfers between devices, swap_low(): lax.ppermute(block, 'seq', [(s, s // LO * LO + (1 - s % LO)) for s in ran...  35.6 us
    pallas_call x1, Pallas kernels, scatter_and_sums(): pl.pallas_call(functools.partial(last_kernel, high), out_shape=[jax.Shape...  30.3 us
    pallas_call x2, Pallas kernels, plane_scan(): pl.pallas_call(functools.partial(scan_kernel, high, reverse), out_shape=(...  20.8 us
    ppermute x6, waiting for transfers between devices, shifted(): return lax.ppermute(block, 'seq', route)  17.6 us
    convert_element_type x16, other arithmetic, lowered(): return values.astype(jnp.bfloat16)  17.3 us
  transfers between devices with their start and end apart: 21, of which 15 were waited for; matrix products, arithmetic and copies ran while one was open for 18% of the time, Pallas kernels for 55%

profile of v6, /device:TPU:0, one launch (start us, length us, event | category | flops | bytes accessed | tf_op | source)
XLA Modules:
  0.0 649.6 jit_solution(3374026025337933746)
XLA Ops:
  10.6 3.0 collective-permute-start
  15.7 1.9 fusion.41.refs_1_
  17.5 3.6 collective-permute-done
  24.4 1.8 collective-permute-start.1
  26.6 14.5 %collective-permute-done.1 = bf16[192,1792]{1,0:T(8,128)(2,1)S(1)} collective-permute-done((bf16[192,1792]{1,0:T(8,128)(2,1)S(1)}, bf16[192,1792]{1,0:T(8,128)(2,1)S(1)}, u32[]{:S(2)}, u32[]{:S(2)}) %collective-permute-start.1) | collective-permute-done | bytes 688160 | tf_op jit(solution)/shard_map/ppermute | solution.py:900
  44.9 41.7 %gather_full.5 = (bf16[8,128,1536]{2,1,0:T(8,128)(2,1)}, bf16[8,128,1536]{2,1,0:T(8,128)(2,1)}) custom-call(bf16[128,1536]{1,0:T(8,128)(2,1)} %fusion.39.refs_0_, bf16[128,1536]{1,0:T(8,128)(2,1)} %fusion.41.refs_1_), custom_call_target="tpu_custom_call" | custom-call | bytes 60000000 | tf_op jit(solution)/shard_map/gather_full/pallas_call | solution.py:229
  88.0 11.0 %all-gather.9.cloned.1.call-done = bf16[2496,768]{1,0:T(8,128)(2,1)} async-done(((bf16[624,768]{1,0:T(8,128)(2,1)}), bf16[2496,768]{1,0:T(8,128)(2,1)}) %all-gather.9.cloned.1.call-update) | async-done | bytes 3833872 | tf_op jit(solution)/shard_map/all_gather | solution.py:1137
  103.1 1.9 slice.535
  105.1 2.6 copy-done.49
  107.7 1.8 fusion.151
  116.4 9.4 %scan.1 = (f32[1024,256]{1,0:T(8,128)S(1)}, f32[8,256]{1,0:T(8,128)S(1)}) custom-call(f32[1024,256]{1,0:T(8,128)S(1)} %get-tuple-element.249.decay_ref, f32[1024,256]{1,0:T(8,128)S(1)} %get-tuple-element.248.drive_ref, f32[8,256]{1,0:T(8,128)S(1)} %broadcast_in_dim.81.end_ref), custom_call_target="tpu_custom_call" | custom-call | bytes 33000000 | tf_op jit(solution)/shard_map/scan/pallas_call | solution.py:474
  126.2 15.1 %collective-permute-done.4 = bf16[4,208,768]{2,1,0:T(8,128)(2,1)S(1)} collective-permute-done((bf16[4,208,768]{2,1,0:T(8,128)(2,1)S(1)}, bf16[4,208,768]{2,1,0:T(8,128)(2,1)S(1)}, u32[]{:S(2)}, u32[]{:S(2)}) %collective-permute-start.4) | collective-permute-done | bytes 1277984 | tf_op jit(solution)/shard_map/ppermute | solution.py:900
  143.0 17.1 %scatter_full.1 = f32[128,1536]{1,0:T(8,128)S(1)} custom-call(bf16[8,128,1536]{2,1,0:T(8,128)(2,1)S(1)} %bitcast.190), custom_call_target="tpu_custom_call" | custom-call | bytes 60000000 | tf_op jit(solution)/shard_map/scatter_full/pallas_call | solution.py:387
  161.6 1.7 reshape.444.refs_1_
  166.5 23.6 %gather_full.6 = (bf16[8,128,1536]{2,1,0:T(8,128)(2,1)}, bf16[4,384,256]{2,1,0:T(8,128)(2,1)}) custom-call(bf16[128,1536]{1,0:T(8,128)(2,1)} %multiply_convert_fusion.3.refs_0_, bf16[384,256]{1,0:T(8,128)(2,1)} %reshape.444.refs_1_), custom_call_target="tpu_custom_call" | custom-call | bytes 60000000 | tf_op jit(solution)/shard_map/gather_full/pallas_call | solution.py:229
  190.0 2.1 copy.70
  192.1 3.4 fusion.130
  195.5 6.6 %all-gather.5.cloned.1.call-done.refs_1_.refs_2_ = bf16[1536,1792]{1,0:T(8,128)(2,1)} async-done(((bf16[384,1792]{1,0:T(8,128)(2,1)}), bf16[1536,1792]{1,0:T(8,128)(2,1)}) %all-gather.5.cloned.1.call-update) | async-done | bytes 5505040 | tf_op jit(solution)/shard_map/all_gather | solution.py:921
  202.8 22.9 %dense_forward.1 = (f32[128,1536]{1,0:T(8,128)}, f32[1024,1152]{1,0:T(8,128)}) custom-call(bf16[1024,1536]{1,0:T(8,128)(2,1)} %bitcast.197, bf16[1536,1792]{1,0:T(8,128)(2,1)} %all-gather.5.cloned.1.call-done.refs_1_.refs_2_), custom_call_target="tpu_custom_call" | custom-call | bytes 75000000 | tf_op jit(solution)/shard_map/dense_forward/pallas_call | solution.py:760
  230.4 3.4 collective-permute-start.6
  233.9 1.8 collective-permute-done.6
  236.4 20.0 %gather_half.4 = (bf16[4,128,1536]{2,1,0:T(8,128)(2,1)}, bf16[4,128,768]{2,1,0:T(8,128)(2,1)}) custom-call(bf16[128,1536]{1,0:T(8,128)(2,1)} %copy-done.46, bf16[128,768]{1,0:T(8,128)(2,1)} %pad_maximum_fusion.19.refs_1_), custom_call_target="tpu_custom_call" | custom-call | bytes 60000000 | tf_op jit(solution)/shard_map/gather_half/pallas_call | solution.py:229
  259.4 8.3 %attention.1 = (bf16[512,384]{1,0:T(8,128)(2,1)S(1)}, bf16[512,384]{1,0:T(8,128)(2,1)S(1)}, f32[8,512]{1,0:T(8,128)S(1)}) custom-call(f32[512,384]{1,0:T(8,128)S(1)} %fusion.153.query_ref, bf16[1536,256]{1,0:T(8,128)(2,1)S(1)} %pad_maximum_fusion.10.ext_ref, s32[8,512]{1,0:T(8,128)S(1)} %broadcast_in_dim.85.here_ref, ...), custom_call_target="tpu_custom_call" | custom-call | bytes 33000000 | tf_op jit(solution)/shard_map/attention/pallas_call | solution.py:823
  268.9 13.1 %scatter_half.2 = f32[128,1536]{1,0:T(8,128)S(1)} custom-call(bf16[4,128,1536]{2,1,0:T(8,128)(2,1)S(1)} %bitcast.194), custom_call_target="tpu_custom_call" | custom-call | bytes 60000000 | tf_op jit(solution)/shard_map/scatter_half/pallas_call | solution.py:387
  283.0 2.0 multiply_convert_fusion.1.refs_0_
  285.0 20.0 %gather_full.7 = bf16[8,128,1536]{2,1,0:T(8,128)(2,1)} custom-call(bf16[128,1536]{1,0:T(8,128)(2,1)} %multiply_convert_fusion.1.refs_0_), custom_call_target="tpu_custom_call" | custom-call | bytes 60000000 | tf_op jit(solution)/shard_map/gather_full/pallas_call | solution.py:229
  305.0 26.4 %dense_both.1 = (f32[128,1536]{1,0:T(8,128)}, bf16[1536,1792]{1,0:T(8,128)(2,1)}, bf16[1024,640]{1,0:T(8,128)(2,1)}) custom-call(bf16[1024,1536]{1,0:T(8,128)(2,1)} %bitcast.196, bf16[1024,1536]{1,0:T(8,128)(2,1)} %bitcast.226, bf16[1536,1792]{1,0:T(8,128)(2,1)} %all-gather.7.cloned.1.call-done.refs_2_.refs_0_), custom_call_target="tpu_custom_call" | custom-call | bytes 100000000 | tf_op jit(solution)/shard_map/dense_both/pallas_call | solution.py:760
  331.5 2.2 multiply_reduce_fusion.6
  333.8 2.5 fusion.126
  336.3 14.1 %gather_half.5 = bf16[4,128,1536]{2,1,0:T(8,128)(2,1)} custom-call(bf16[128,1536]{1,0:T(8,128)(2,1)} %get-tuple-element.206.refs_0_), custom_call_target="tpu_custom_call" | custom-call | bytes 60000000 | tf_op jit(solution)/shard_map/gather_half/pallas_call | solution.py:229
  350.4 2.8 convolution_convert_fusion.8.grad_ref
  353.3 9.8 %attention_back.1 = (bf16[512,384]{1,0:T(8,128)(2,1)S(1)}, bf16[1536,256]{1,0:T(8,128)(2,1)S(1)}) custom-call(bf16[512,384]{1,0:T(8,128)(2,1)S(1)} %copy-done.8, bf16[1536,256]{1,0:T(8,128)(2,1)S(1)} %copy-done.1, bf16[512,384]{1,0:T(8,128)(2,1)S(1)} %convolution_convert_fusion.8.grad_ref, f32[8,512]{1,0:T(8,128)S(1)} %get-tuple-element.137.log_ref, ...), custom_call_target="tpu_custom_call" | custom-call | bytes 60000000 | tf_op jit(solution)/shard_map/attention_back/pallas_call | solution.py:878
  370.1 17.2 %scatter_half.3 = f32[128,2304]{1,0:T(8,128)S(1)} custom-call(bf16[4,128,2304]{2,1,0:T(8,128)(2,1)S(1)} %bitcast.192), custom_call_target="tpu_custom_call" | custom-call | bytes 60000000 | tf_op jit(solution)/shard_map/scatter_half/pallas_call | solution.py:387
  391.9 6.5 collective-permute-done.7
  399.0 4.8 collective-permute-done.8
  404.7 2.6 fusion.1
  408.7 2.6 multiply_reduce_fusion.7
  412.6 17.5 %gather_full.8 = bf16[8,128,1536]{2,1,0:T(8,128)(2,1)} custom-call(bf16[128,1536]{1,0:T(8,128)(2,1)} %get-tuple-element.204.refs_0_), custom_call_target="tpu_custom_call" | custom-call | bytes 60000000 | tf_op jit(solution)/shard_map/gather_full/pallas_call | solution.py:229
  430.1 5.8 reduce-scatter.5.cloned.1.call-done
  435.9 24.6 %dense_backward.1 = (f32[128,1536]{1,0:T(8,128)}, bf16[1536,1792]{1,0:T(8,128)(2,1)}) custom-call(bf16[1024,1536]{1,0:T(8,128)(2,1)} %bitcast.198, bf16[1024,1536]{1,0:T(8,128)(2,1)} %bitcast.199, bf16[1536,1792]{1,0:T(8,128)(2,1)} %all-gather.5.cloned.1.call-done.refs_1_.refs_2_, f32[1024,1152]{1,0:T(8,128)} %get-tuple-element.146.refs_3_), custom_call_target="tpu_custom_call" | custom-call | bytes 100000000 | tf_op jit(solution)/shard_map/dense_backward/pallas_call | solution.py:760
  460.6 2.0 multiply_reduce_fusion.8
  465.2 17.7 %gather_full.9 = bf16[8,128,1536]{2,1,0:T(8,128)(2,1)} custom-call(bf16[128,1536]{1,0:T(8,128)(2,1)} %convert_element_type.227.refs_0_), custom_call_target="tpu_custom_call" | custom-call | bytes 60000000 | tf_op jit(solution)/shard_map/gather_full/pallas_call | solution.py:229
  485.3 6.0 gather_half.6
  491.3 2.0 fusion
  494.1 1.7 reshape.473
  495.8 20.0 %dense_product.1 = f32[128,1536]{1,0:T(8,128)} custom-call(bf16[1536,1792]{1,0:T(8,128)(2,1)} %all-gather.7.cloned.1.call-done.refs_2_.refs_0_, bf16[1024,640]{1,0:T(8,128)(2,1)} %get-tuple-element.163.refs_1_), custom_call_target="tpu_custom_call" | custom-call | bytes 75000000 | tf_op jit(solution)/shard_map/dense_product/pallas_call | solution.py:760
  515.8 2.0 fusion.154
  517.8 1.9 convolution_convert_fusion.7
  524.5 2.1 fusion.49
  526.7 11.5 %scan_back.1 = (f32[1024,256]{1,0:T(8,128)S(1)}, f32[8,256]{1,0:T(8,128)}) custom-call(f32[1024,256]{1,0:T(8,128)S(1)} %concatenate.180.decay_ref, f32[1024,256]{1,0:T(8,128)S(1)} %get-tuple-element.222.drive_ref, f32[8,256]{1,0:T(8,128)S(1)} %broadcast_in_dim.151.end_ref), custom_call_target="tpu_custom_call" | custom-call | bytes 33000000 | tf_op jit(solution)/shard_map/scan_back/pallas_call | solution.py:474
  538.3 3.5 fusion.75
  544.5 2.3 multiply_reduce_fusion.5
  550.4 4.4 collective-permute-done.11
  554.9 1.8 convolution_convert_fusion.1
  556.8 1.8 convolution_convert_fusion.2
  558.7 1.8 pad_maximum_fusion
  560.5 6.5 %reduce-scatter.9.cloned.1.call-done = bf16[384,1792]{1,0:T(8,128)(2,1)} async-done(((bf16[1536,1792]{1,0:T(8,128)(2,1)}), bf16[384,1792]{1,0:T(8,128)(2,1)}) %reduce-scatter.9.cloned.1.call-update) | async-done | bytes 1376272 | tf_op jit(solution)/shard_map/reduce_scatter | solution.py:925
  568.8 2.8 multiply_reduce_fusion
  573.9 30.3 %scatter_and_sums.1 = (f32[128,1536]{1,0:T(8,128)S(1)}, f32[8,1536]{1,0:T(8,128)S(1)}, f32[8,512]{1,0:T(8,128)S(1)}, bf16[4,128,1536]{2,1,0:T(8,128)(2,1)S(1)}) custom-call(bf16[8,128,1536]{2,1,0:T(8,128)(2,1)S(1)} %bitcast.191, f32[8,1536]{1,0:T(8,128)S(1)} %concatenate.190.gains_ref, f32[8,256]{1,0:T(8,128)S(1)} %pad_maximum_fusion.23.rest_ref, ...), custom_call_target="tpu_custom_call" | custom-call | bytes 60000000 | tf_op jit(solution)/shard_map/scatter_and_sums/pallas_call | solution.py:558
  605.4 1.6 collective-permute-start.12
  608.3 13.7 %gather_half.7 = bf16[4,128,1536]{2,1,0:T(8,128)(2,1)} custom-call(bf16[128,1536]{1,0:T(8,128)(2,1)} %fusion.36.refs_0_), custom_call_target="tpu_custom_call" | custom-call | bytes 60000000 | tf_op jit(solution)/shard_map/gather_half/pallas_call | solution.py:229
  624.1 2.9 reduce-scatter.11.cloned.1.call-done
  629.7 2.1 convert_element_type.246
  636.3 1.8 collective-permute-done.13
  (528 shorter events, 94.7 us)
Async XLA Ops:
  7.2 91.7 %all-gather.9.cloned.1.call-start = ((), (), s32[]{:S(2)}) async-start(), calls=%async_computation.10 | async-start | bytes 4792320 | tf_op jit(solution)/shard_map/all_gather | solution.py:1137
  9.3 11.8 %copy-start.59 = (bf16[192,512]{1,0:T(8,128)(2,1)S(1)}, bf16[192,512]{1,0:T(8,128)(2,1)}, u32[]{:S(2)}) copy-start(bf16[192,512]{1,0:T(8,128)(2,1)} %param.27) | copy-start | bytes 589828
  9.3 11.8 %copy-start.60 = (bf16[192,512]{1,0:T(8,128)(2,1)S(1)}, bf16[192,512]{1,0:T(8,128)(2,1)}, u32[]{:S(2)}) copy-start(bf16[192,512]{1,0:T(8,128)(2,1)} %param.26) | copy-start | bytes 589828
  9.4 11.8 %copy-start.83 = (bf16[512,16]{0,1:T(8,128)(2,1)S(1)}, bf16[512,16]{0,1:T(8,128)(2,1)}, u32[]{:S(2)}) copy-start(bf16[512,16]{0,1:T(8,128)(2,1)} %param.31) | copy-start | bytes 49156
  9.4 11.7 %copy-start.84 = (bf16[512,16]{0,1:T(8,128)(2,1)S(1)}, bf16[512,16]{0,1:T(8,128)(2,1)}, u32[]{:S(2)}) copy-start(bf16[512,16]{0,1:T(8,128)(2,1)} %param.30) | copy-start | bytes 49156
  10.6 10.5 %collective-permute-start = (bf16[208,768]{1,0:T(8,128)(2,1)S(1)}, bf16[208,768]{1,0:T(8,128)(2,1)S(1)}, u32[]{:S(2)}, u32[]{:S(2)}) collective-permute-start(bf16[208,768]{1,0:T(8,128)(2,1)S(1)} %broadcast_select_fusion.12), channel_id=1, source_target_pairs={{0,4},{4,0},{8,12},{12,8},{16,20},{20,16},{24,28},{28,24},{1,5},{5... | collective-permute-start | bytes 958472 | tf_op jit(solution)/shard_map/ppermute | solution.py:900
  22.5 179.7 %all-gather.5.cloned.1.call-start = ((), (), s32[]{:S(2)}) async-start(), calls=%async_computation.4 | async-start | bytes 6881280 | tf_op jit(solution)/shard_map/all_gather | solution.py:921
  24.4 16.7 %collective-permute-start.1 = (bf16[192,1792]{1,0:T(8,128)(2,1)S(1)}, bf16[192,1792]{1,0:T(8,128)(2,1)S(1)}, u32[]{:S(2)}, u32[]{:S(2)}) collective-permute-start(bf16[192,1792]{1,0:T(8,128)(2,1)S(1)} %broadcast_select_fusion.8), channel_id=1, source_target_pairs={{0,4},{4,0},{8,12},{12,8},{16,20},{20,16},{24,28},{28,24},{1,5},{5... | collective-permute-start | bytes 2064392 | tf_op jit(solution)/shard_map/ppermute | solution.py:900
  43.4 43.2 %collective-permute-start.2 = (bf16[192,1792]{1,0:T(8,128)(2,1)S(1)}, bf16[192,1792]{1,0:T(8,128)(2,1)S(1)}, u32[]{:S(2)}, u32[]{:S(2)}) collective-permute-start(bf16[192,1792]{1,0:T(8,128)(2,1)S(1)} %broadcast_select_fusion.6), channel_id=1, source_target_pairs={{0,4},{4,0},{8,12},{12,8},{16,20},{20,16},{24,28},{28,24},{1,5},{5... | collective-permute-start | bytes 2064392 | tf_op jit(solution)/shard_map/ppermute | solution.py:900
  86.7 12.4 %copy-start.145 = (f32[512]{0:T(512)S(1)}, f32[512]{0:T(512)}, u32[]{:S(2)}) copy-start(f32[512]{0:T(512)} %param.29) | copy-start | bytes 6148
  86.7 12.5 %copy-start.133 = (f32[512]{0:T(512)S(1)}, f32[512]{0:T(512)}, u32[]{:S(2)}) copy-start(f32[512]{0:T(512)} %param.33) | copy-start | bytes 6148
  86.7 13.1 %copy-start.132 = (f32[4,512]{1,0:T(4,128)S(1)}, f32[4,512]{1,0:T(4,128)}, u32[]{:S(2)}) copy-start(f32[4,512]{1,0:T(4,128)} %param.28) | copy-start | bytes 24580
  86.7 13.1 %copy-start.138 = (f32[2,512]{1,0:T(2,128)S(1)}, f32[2,512]{1,0:T(2,128)}, u32[]{:S(2)}) copy-start(f32[2,512]{1,0:T(2,128)} %param.32) | copy-start | bytes 12292
  99.0 206.1 %all-gather.7.cloned.1.call-start = ((), (), s32[]{:S(2)}) async-start(), calls=%async_computation.5 | async-start | bytes 6881280 | tf_op jit(solution)/shard_map/all_gather | solution.py:921
  99.9 15.1 %copy-start.110 = (f32[256]{0:T(256)}, f32[256]{0:T(256)S(1)}, u32[]{:S(2)}) copy-start(f32[256]{0:T(256)S(1)} %get-tuple-element.216) | copy-start | bytes 3076
  100.0 13.0 %copy-start.113 = (f32[1,256]{1,0:T(1,128)}, f32[1,256]{1,0:T(1,128)S(1)}, u32[]{:S(2)}) copy-start(f32[1,256]{1,0:T(1,128)S(1)} %get-tuple-element.310) | copy-start | bytes 3076
  100.0 13.0 %copy-start.115 = (f32[1,256]{1,0:T(1,128)}, f32[1,256]{1,0:T(1,128)S(1)}, u32[]{:S(2)}) copy-start(f32[1,256]{1,0:T(1,128)S(1)} %get-tuple-element.311) | copy-start | bytes 3076
  100.0 13.0 %copy-start.117 = (f32[1,256]{1,0:T(1,128)}, f32[1,256]{1,0:T(1,128)S(1)}, u32[]{:S(2)}) copy-start(f32[1,256]{1,0:T(1,128)S(1)} %get-tuple-element.312) | copy-start | bytes 3076
  100.0 13.0 %copy-start.119 = (f32[1,256]{1,0:T(1,128)}, f32[1,256]{1,0:T(1,128)S(1)}, u32[]{:S(2)}) copy-start(f32[1,256]{1,0:T(1,128)S(1)} %get-tuple-element.313) | copy-start | bytes 3076
  100.0 15.0 %copy-start.103 = (f32[1,256]{1,0:T(1,128)}, f32[1,256]{1,0:T(1,128)S(1)}, u32[]{:S(2)}) copy-start(f32[1,256]{1,0:T(1,128)S(1)} %get-tuple-element.325) | copy-start | bytes 3076
  100.0 15.0 %copy-start.108 = (f32[1,256]{1,0:T(1,128)}, f32[1,256]{1,0:T(1,128)S(1)}, u32[]{:S(2)}) copy-start(f32[1,256]{1,0:T(1,128)S(1)} %get-tuple-element.326) | copy-start | bytes 3076
  102.7 12.3 %copy-start.98 = (f32[1024]{0:T(1024)}, f32[1024]{0:T(1024)S(1)}, u32[]{:S(2)}) copy-start(f32[1024]{0:T(1024)S(1)} %compare_convert_fusion.1) | copy-start | bytes 12292
  109.5 16.3 %copy-start.24 = (f32[1024,512]{1,0:T(8,128)}, f32[1024,512]{1,0:T(8,128)S(1)}, u32[]{:S(2)}) copy-start(f32[1024,512]{1,0:T(8,128)S(1)} %fusion.151) | copy-start | bytes 6291460
  109.5 3.5 collective-permute-start.3
  111.4 30.5 %copy-start.47 = (bf16[8,192,256]{2,1,0:T(8,128)(2,1)}, bf16[8,192,256]{2,1,0:T(8,128)(2,1)S(1)}, u32[]{:S(2)}) copy-start(bf16[8,192,256]{2,1,0:T(8,128)(2,1)S(1)} %slice.667) | copy-start | bytes 2359300
  111.5 29.9 %collective-permute-start.4 = (bf16[4,208,768]{2,1,0:T(8,128)(2,1)S(1)}, bf16[4,208,768]{2,1,0:T(8,128)(2,1)S(1)}, u32[]{:S(2)}, u32[]{:S(2)}) collective-permute-start(bf16[4,208,768]{2,1,0:T(8,128)(2,1)S(1)} %slice.560), channel_id=1, source_target_pairs={{0,4},{4,0},{8,12},{12,8},{16,20},{20,16},{24,28},{28,24},{1,5},{5... | collective-permute-start | bytes 3833864 | tf_op jit(solution)/shard_map/ppermute | solution.py:900
  126.2 15.7 %copy-start.44 = (bf16[1024,256]{1,0:T(8,128)(2,1)}, bf16[1024,256]{1,0:T(8,128)(2,1)S(1)}, u32[]{:S(2)}) copy-start(bf16[1024,256]{1,0:T(8,128)(2,1)S(1)} %multiply_convert_fusion) | copy-start | bytes 1572868
  141.9 19.0 %copy-start.19 = (bf16[4,2,208,768]{3,2,1,0:T(8,128)(2,1)}, bf16[4,2,208,768]{3,2,1,0:T(8,128)(2,1)S(1)}, u32[]{:S(2)}) copy-start(bf16[4,2,208,768]{3,2,1,0:T(8,128)(2,1)S(1)} %copy.69) | copy-start | bytes 7667716
  164.7 27.4 %copy-start.141 = (f32[128]{0:T(128)}, f32[128]{0:T(128)S(1)}, u32[]{:S(2)}) copy-start(f32[128]{0:T(128)S(1)} %get-tuple-element.212) | copy-start | bytes 1540
  164.7 27.4 %copy-start.122 = (f32[128]{0:T(128)}, f32[128]{0:T(128)S(1)}, u32[]{:S(2)}) copy-start(f32[128]{0:T(128)S(1)} %fusion.115) | copy-start | bytes 1540
  202.2 233.7 %reduce-scatter.5.cloned.1.call-start = ((), (), s32[]{:S(2)}) async-start(), calls=%async_computation.6 | async-start | bytes 6881280 | tf_op jit(solution)/shard_map/reduce_scatter | solution.py:925
  202.8 22.9 %copy-start.10 = (f32[128,1536]{1,0:T(8,128)S(1)}, f32[128,1536]{1,0:T(8,128)}, u32[]{:S(2)}) copy-start(f32[128,1536]{1,0:T(8,128)} %copy-done.9) | copy-start | bytes 2359300
  229.1 4.8 collective-permute-start.5
  230.4 5.3 collective-permute-start.6
  268.9 13.1 %copy-start.13 = (f32[128,1536]{1,0:T(8,128)S(1)}, f32[128,1536]{1,0:T(8,128)}, u32[]{:S(2)}) copy-start(f32[128,1536]{1,0:T(8,128)} %copy-done.12) | copy-start | bytes 2359300
  331.5 193.0 %reduce-scatter.7.cloned.1.call-start = ((), (), s32[]{:S(2)}) async-start(), calls=%async_computation.7 | async-start | bytes 1474560 | tf_op jit(solution)/shard_map/reduce_scatter | solution.py:925
  368.9 35.7 %collective-permute-start.9 = (bf16[4,192,768]{2,1,0:T(8,128)(2,1)}, bf16[4,192,768]{2,1,0:T(8,128)(2,1)}, u32[]{:S(2)}, u32[]{:S(2)}) collective-permute-start(bf16[4,192,768]{2,1,0:T(8,128)(2,1)} %get-tuple-element.229), channel_id=1, source_target_pairs={{0,4},{4,0},{8,12},{12,8},{16,20},{20,16},{24,28},{28,24},{1,5},{5... | collective-permute-start | bytes 3538952 | tf_op jit(solution)/shard_map/ppermute | solution.py:900
  388.0 10.4 %collective-permute-start.7 = (bf16[128,256]{1,0:T(8,128)(2,1)}, bf16[128,256]{1,0:T(8,128)(2,1)S(1)}, u32[]{:S(2)}, u32[]{:S(2)}) collective-permute-start(bf16[128,256]{1,0:T(8,128)(2,1)} %get-tuple-element.262), channel_id=1, source_target_pairs={{4,0},{8,4},{12,8},{16,12},{20,16},{24,20},{28,24},{5,1},{9,5},{13... | collective-permute-start | bytes 196616 | tf_op jit(solution)/shard_map/ppermute | solution.py:974
  389.3 14.5 %collective-permute-start.8 = (bf16[128,256]{1,0:T(8,128)(2,1)S(1)}, bf16[128,256]{1,0:T(8,128)(2,1)}, u32[]{:S(2)}, u32[]{:S(2)}) collective-permute-start(bf16[128,256]{1,0:T(8,128)(2,1)S(1)} %get-tuple-element.263), channel_id=1, source_target_pairs={{8,0},{12,4},{16,8},{20,12},{24,16},{28,20},{9,1},{13,5},{17,9},{2... | collective-permute-start | bytes 196616 | tf_op jit(solution)/shard_map/ppermute | solution.py:974
  390.7 14.0 %copy-start.38 = (bf16[4,1,192,768]{3,2,1,0:T(8,128)(2,1)S(1)}, bf16[4,1,192,768]{3,2,1,0:T(8,128)(2,1)}, u32[]{:S(2)}) copy-start(bf16[4,1,192,768]{3,2,1,0:T(8,128)(2,1)} %get-tuple-element.228) | copy-start | bytes 3538948
  407.3 159.7 %reduce-scatter.9.cloned.1.call-start = ((), (), s32[]{:S(2)}) async-start(), calls=%async_computation.8 | async-start | bytes 6881280 | tf_op jit(solution)/shard_map/reduce_scatter | solution.py:925
  435.9 24.6 %copy-start.11 = (f32[128,1536]{1,0:T(8,128)S(1)}, f32[128,1536]{1,0:T(8,128)}, u32[]{:S(2)}) copy-start(f32[128,1536]{1,0:T(8,128)} %copy-done.9) | copy-start | bytes 2359300
  435.9 24.7 %copy-start.123 = (f32[128]{0:T(128)S(1)}, f32[128]{0:T(128)}, u32[]{:S(2)}) copy-start(f32[128]{0:T(128)} %copy-done.122) | copy-start | bytes 1540
  462.9 164.0 %reduce-scatter.11.cloned.1.call-start = ((), (), s32[]{:S(2)}) async-start(), calls=%async_computation.9 | async-start | bytes 3440640 | tf_op jit(solution)/shard_map/reduce_scatter | solution.py:925
  465.2 17.7 %copy-start.37 = (bf16[384,1792]{1,0:T(8,128)(2,1)S(1)}, bf16[384,1792]{1,0:T(8,128)(2,1)}, u32[]{:S(2)}) copy-start(bf16[384,1792]{1,0:T(8,128)(2,1)} %reduce-scatter.5.cloned.1.call-done) | copy-start | bytes 4128772
  483.8 35.9 %collective-permute-start.10 = (bf16[192,1792]{1,0:T(8,128)(2,1)}, bf16[192,1792]{1,0:T(8,128)(2,1)}, u32[]{:S(2)}, u32[]{:S(2)}) collective-permute-start(bf16[192,1792]{1,0:T(8,128)(2,1)} %broadcast_select_fusion.4), channel_id=1, source_target_pairs={{0,4},{4,0},{8,12},{12,8},{16,20},{20,16},{24,28},{28,24},{1,5},{5... | collective-permute-start | bytes 2064392 | tf_op jit(solution)/shard_map/ppermute | solution.py:900
  495.8 20.0 %copy-start.48 = (bf16[8,192,256]{2,1,0:T(8,128)(2,1)S(1)}, bf16[8,192,256]{2,1,0:T(8,128)(2,1)}, u32[]{:S(2)}) copy-start(bf16[8,192,256]{2,1,0:T(8,128)(2,1)} %copy-done.47) | copy-start | bytes 2359300
  495.8 20.0 %copy-start.51 = (bf16[8,128,1536]{2,1,0:T(8,128)(2,1)S(1)}, bf16[8,128,1536]{2,1,0:T(8,128)(2,1)}, u32[]{:S(2)}) copy-start(bf16[8,128,1536]{2,1,0:T(8,128)(2,1)} %gather_full.9) | copy-start | bytes 9437188
  524.4 13.7 %copy-start.27 = (f32[1024,128]{1,0:T(8,128)S(1)}, f32[1024,128]{1,0:T(8,128)}, u32[]{:S(2)}) copy-start(f32[1024,128]{1,0:T(8,128)} %copy-done.26) | copy-start | bytes 1572868
  524.5 13.7 %copy-start.29 = (f32[1024,128]{1,0:T(8,128)S(1)}, f32[1024,128]{1,0:T(8,128)}, u32[]{:S(2)}) copy-start(f32[1024,128]{1,0:T(8,128)} %copy-done.28) | copy-start | bytes 1572868
  526.6 11.6 %copy-start.16 = (f32[1024,128]{1,0:T(8,128)S(1)}, f32[1024,128]{1,0:T(8,128)}, u32[]{:S(2)}) copy-start(f32[1024,128]{1,0:T(8,128)} %copy-done.15) | copy-start | bytes 1572868
  526.6 11.6 %copy-start.18 = (f32[1024,128]{1,0:T(8,128)S(1)}, f32[1024,128]{1,0:T(8,128)}, u32[]{:S(2)}) copy-start(f32[1024,128]{1,0:T(8,128)} %copy-done.17) | copy-start | bytes 1572868
  526.6 11.6 %copy-start.23 = (f32[1024,256]{1,0:T(8,128)S(1)}, f32[1024,256]{1,0:T(8,128)}, u32[]{:S(2)}) copy-start(f32[1024,256]{1,0:T(8,128)} %copy-done.22) | copy-start | bytes 3145732
  526.6 11.6 %copy-start.99 = (f32[1024]{0:T(1024)S(1)}, f32[1024]{0:T(1024)}, u32[]{:S(2)}) copy-start(f32[1024]{0:T(1024)} %copy-done.98) | copy-start | bytes 12292
  526.6 11.6 %copy-start.104 = (f32[1,256]{1,0:T(1,128)S(1)}, f32[1,256]{1,0:T(1,128)}, u32[]{:S(2)}) copy-start(f32[1,256]{1,0:T(1,128)} %copy-done.103) | copy-start | bytes 3076
  526.6 11.6 %copy-start.109 = (f32[1,256]{1,0:T(1,128)S(1)}, f32[1,256]{1,0:T(1,128)}, u32[]{:S(2)}) copy-start(f32[1,256]{1,0:T(1,128)} %copy-done.108) | copy-start | bytes 3076
  526.7 11.6 %copy-start.111 = (f32[256]{0:T(256)S(1)}, f32[256]{0:T(256)}, u32[]{:S(2)}) copy-start(f32[256]{0:T(256)} %copy-done.110) | copy-start | bytes 3076
  526.7 11.6 %copy-start.112 = (f32[256]{0:T(256)S(1)}, f32[256]{0:T(256)}, u32[]{:S(2)}) copy-start(f32[256]{0:T(256)} %get-tuple-element.217) | copy-start | bytes 3076
  526.7 11.6 %copy-start.126 = (f32[1,256]{1,0:T(1,128)S(1)}, f32[1,256]{1,0:T(1,128)}, u32[]{:S(2)}) copy-start(f32[1,256]{1,0:T(1,128)} %slice.599) | copy-start | bytes 3076
  547.4 7.4 %collective-permute-start.11 = (f32[3,256]{1,0:T(4,128)S(1)}, f32[3,256]{1,0:T(4,128)S(1)}, u32[]{:S(2)}, u32[]{:S(2)}) collective-permute-start(f32[3,256]{1,0:T(4,128)S(1)} %pad_add_fusion.1), channel_id=1, source_target_pairs={{8,0},{12,4},{16,8},{20,12},{24,16},{28,20},{9,1},{13,5},{17,9},{2... | collective-permute-start | bytes 9224 | tf_op jit(solution)/shard_map/ppermute | solution.py:974
  573.9 31.5 %copy-start.35 = (bf16[384,1792]{1,0:T(8,128)(2,1)S(1)}, bf16[384,1792]{1,0:T(8,128)(2,1)}, u32[]{:S(2)}) copy-start(bf16[384,1792]{1,0:T(8,128)(2,1)} %reduce-scatter.9.cloned.1.call-done) | copy-start | bytes 4128772
  605.4 18.4 %collective-permute-start.12 = (bf16[192,1792]{1,0:T(8,128)(2,1)S(1)}, bf16[192,1792]{1,0:T(8,128)(2,1)S(1)}, u32[]{:S(2)}, u32[]{:S(2)}) collective-permute-start(bf16[192,1792]{1,0:T(8,128)(2,1)S(1)} %broadcast_select_fusion.2), channel_id=1, source_target_pairs={{0,4},{4,0},{8,12},{12,8},{16,20},{20,16},{24,28},{28,24},{1,5},{5... | collective-permute-start | bytes 2064392 | tf_op jit(solution)/shard_map/ppermute | solution.py:900
  608.3 15.5 %copy-start.36 = (bf16[384,1792]{1,0:T(8,128)(2,1)S(1)}, bf16[384,1792]{1,0:T(8,128)(2,1)}, u32[]{:S(2)}) copy-start(bf16[384,1792]{1,0:T(8,128)(2,1)} %reduce-scatter.9.cloned.1.call-done) | copy-start | bytes 4128772
  628.1 10.0 %collective-permute-start.13 = (bf16[224,768]{1,0:T(8,128)(2,1)S(1)}, bf16[224,768]{1,0:T(8,128)(2,1)S(1)}, u32[]{:S(2)}, u32[]{:S(2)}) collective-permute-start(bf16[224,768]{1,0:T(8,128)(2,1)S(1)} %broadcast_select_fusion.10), channel_id=1, source_target_pairs={{0,4},{4,0},{8,12},{12,8},{16,20},{20,16},{24,28},{28,24},{1,5},{5... | collective-permute-start | bytes 1032200 | tf_op jit(solution)/shard_map/ppermute | solution.py:900
  (106 other events, 313.0 us)
Sparse Core Ops, SparseCore 0:
  22.6 76.3 all-gather.8
  100.5 101.6 all-gather.4
  203.7 100.7 all-gather.6
  331.6 104.3 reduce-scatter.4
  438.7 28.8 reduce-scatter.6
  469.7 97.3 reduce-scatter.8
  569.9 57.0 reduce-scatter.10
